TPU v7x, 32 devices: a whole 2x2x4 slice. The times are simulated.
32 devices in a mesh: section: 2 (over y), tp: 4 (over z), rep: 4 (over x, core).
Axes of the slice: x: 2, y: 2, z: 4, core: 2. Of those that a mesh axis runs over, the one named last changes fastest.
Arguments:
- prompt: bfloat16 [768, 2560], P('rep', 'tp'), parts along dimension 0, may hold values from -6 to 6
- block_sizes: int32 [32], P('rep'), parts along dimension 0, may hold values from 1 to 48, 192 in all
- w_query_down: bfloat16 [2, 2560, 768], P('section', None, 'tp'), may hold values from -0.125 to 0.125
- w_query: bfloat16 [2, 768, 2560], P('section', None, 'tp'), may hold values from -0.21875 to 0.21875
- w_latent: bfloat16 [2, 2560, 544], P('section', None, 'tp'), may hold values from -0.125 to 0.125
- w_keys: bfloat16 [2, 512, 2048], P('section', None, 'tp'), may hold values from -0.25 to 0.25
- w_values: bfloat16 [2, 512, 2048], P('section', None, 'tp'), may hold values from -0.25 to 0.25
- w_out: bfloat16 [2, 2048, 2560], P('section', 'tp'), may hold values from -1.5 to 1.5
Outputs:
- latent_cache: bfloat16 [2, 768, 544], P('section', ('rep', 'tp')), parts along dimension 1
- layer_ends: bfloat16 [2, 32, 2560], P('section', 'rep', 'tp'), parts along dimension 1
There are 4 independent parts, one for each index of `rep`. A program takes and returns all parts, laid end to end along the dimension named above; an argument that names none is the same for every part. Nothing has to cross between parts.
Inputs may be any that keep to these rules, and one draw needn't show every extreme that they name: `block_sizes`: the block sizes sum to 192, and the largest is exactly 48.
All inputs are finite; a program needn't handle non-finite values.
Results may differ from a plain program's by a relative error of at most 0.017.
Values may be sent and summed in bfloat16 or wider, within the bound.
No kernel may reach another device: no remote copies, remote signals or barrier semaphores. Data moves between devices by JAX's collectives and lax.ppermute only.
A program may use at most 64 MiB of HBM per device.

v0:
```python
import jax
import jax.numpy as jnp
from jax import lax
from jax.sharding import PartitionSpec as P

TOKENS = 192
BLOCKS = 8
BLOCK_MOST = 48
NOPE_DIM = 128
ROPE_DIM = 32
VALUE_DIM = 128
LATENT = 512


EPSILON = 1e-06


def from_behind(block, axis, distance):
    devices = range(lax.axis_size(axis))
    route = [(i - distance, i) for i in devices if i - distance in devices]
    return lax.ppermute(block, axis, route)


def rms_rows(values):
    return values * lax.rsqrt(jnp.mean(values * values, axis=-1, keepdims=True) + EPSILON)


def rotate(values, positions):
    half_width = values.shape[-1] // 2
    frequency = 10000.0 ** (-2.0 * jnp.arange(half_width, dtype=jnp.float32) / values.shape[-1])
    angles = positions.astype(jnp.float32)[:, None] * frequency[None, :]
    if values.ndim == 3:
        angles = angles[:, None, :]
    cosine = jnp.cos(angles)
    sine_part = jnp.sin(angles)
    first_half = values[..., :half_width]
    second = values[..., half_width:]
    return jnp.concatenate(
        [first_half * cosine - second * sine_part, first_half * sine_part + second * cosine],
        axis=-1,
    )


def local(prompt, block_sizes, w_query_down, w_query, w_latent, w_keys, w_values, w_out):
    section_count = lax.axis_size("section")
    section_id = lax.axis_index("section")
    tp_id = lax.axis_index("tp")
    tp_count = lax.axis_size("tp")
    share_cols = prompt.shape[1]
    down_weight = w_query_down[0]
    query_weight = w_query[0]
    latent_weight = w_latent[0]
    key_weight = w_keys[0]
    value_weight = w_values[0]
    out_weight = w_out[0]
    head_count = query_weight.shape[1] // (NOPE_DIM + ROPE_DIM)
    starts = jnp.cumsum(block_sizes) - block_sizes
    block_ids = jnp.arange(BLOCKS, dtype=jnp.int32)
    scale_factor = (NOPE_DIM + ROPE_DIM) ** (-0.5)
    key_index = jnp.arange(TOKENS, dtype=jnp.int32)
    prompt_pad = jnp.concatenate(
        [prompt, jnp.zeros((BLOCK_MOST, share_cols), jnp.bfloat16)], axis=0
    )
    buffer_rows = TOKENS + BLOCK_MOST
    buffers = (
        jnp.zeros((buffer_rows, LATENT + ROPE_DIM), jnp.bfloat16),
        jnp.zeros((buffer_rows, head_count * NOPE_DIM), jnp.bfloat16),
        jnp.zeros((buffer_rows, head_count * VALUE_DIM), jnp.bfloat16),
    )
    ends_init = jnp.zeros((BLOCKS + 1, share_cols), jnp.bfloat16)
    tick_count = BLOCKS + section_count - 1

    def locate(tick):
        block_now = tick - section_id
        active = jnp.logical_and(block_now >= 0, block_now < BLOCKS)
        picked = block_ids == block_now
        first_row = jnp.where(active, jnp.sum(jnp.where(picked, starts, 0)), TOKENS)
        row_total = jnp.where(active, jnp.sum(jnp.where(picked, block_sizes, 0)), 1)
        end_slot = jnp.where(active, block_now, BLOCKS)
        return (first_row, row_total, end_slot)

    def compute(rows_in, first_row, state_buffers):
        cache, key_buffer, value_buffer = state_buffers
        positions = first_row + jnp.arange(BLOCK_MOST, dtype=jnp.int32)
        normed = rms_rows(rows_in.astype(jnp.float32)).astype(jnp.bfloat16)
        down_part = jnp.dot(normed, down_weight, preferred_element_type=jnp.float32)
        latent_part = jnp.dot(normed, latent_weight, preferred_element_type=jnp.float32)
        down_full, latent = (
            lax.all_gather(down_part, "tp", axis=1, tiled=True),
            lax.all_gather(latent_part, "tp", axis=1, tiled=True),
        )
        compressed = rms_rows(down_full).astype(jnp.bfloat16)
        queries = jnp.dot(compressed, query_weight, preferred_element_type=jnp.float32).reshape(
            BLOCK_MOST, head_count, NOPE_DIM + ROPE_DIM
        )
        queries = jnp.concatenate(
            [queries[..., :NOPE_DIM], rotate(queries[..., NOPE_DIM:], positions)], axis=-1
        ).astype(jnp.bfloat16)
        fresh_rows = jnp.concatenate(
            [rms_rows(latent[:, :LATENT]), rotate(latent[:, LATENT:], positions)], axis=-1
        ).astype(jnp.bfloat16)
        new_keys = jnp.dot(
            fresh_rows[:, :LATENT], key_weight, preferred_element_type=jnp.float32
        ).astype(jnp.bfloat16)
        new_values = jnp.dot(
            fresh_rows[:, :LATENT], value_weight, preferred_element_type=jnp.float32
        ).astype(jnp.bfloat16)
        cache = lax.dynamic_update_slice_in_dim(cache, fresh_rows, first_row, 0)
        key_buffer = lax.dynamic_update_slice_in_dim(key_buffer, new_keys, first_row, 0)
        value_buffer = lax.dynamic_update_slice_in_dim(value_buffer, new_values, first_row, 0)
        key_rows = key_buffer[:TOKENS].reshape(TOKENS, head_count, NOPE_DIM)
        scores = jnp.einsum(
            "ihd,jhd->hij", queries[..., :NOPE_DIM], key_rows, preferred_element_type=jnp.float32
        )
        scores = scores + jnp.einsum(
            "ihr,jr->hij",
            queries[..., NOPE_DIM:],
            cache[:TOKENS, LATENT:],
            preferred_element_type=jnp.float32,
        )
        visible = key_index[None, :] <= positions[:, None]
        powered = jnp.where(visible[None], jnp.exp(scores * scale_factor), 0.0)
        attention = (powered / jnp.sum(powered, axis=-1, keepdims=True)).astype(jnp.bfloat16)
        value_rows = value_buffer[:TOKENS].reshape(TOKENS, head_count, VALUE_DIM)
        mixed_rows = jnp.einsum(
            "hij,jhv->ihv", attention, value_rows, preferred_element_type=jnp.float32
        ).astype(jnp.bfloat16)
        partial_value = jnp.dot(
            mixed_rows.reshape(BLOCK_MOST, head_count * VALUE_DIM),
            out_weight,
            preferred_element_type=jnp.float32,
        )
        return (partial_value, (cache, key_buffer, value_buffer))

    def record(ends_buf, new_share, row_total, end_slot):
        row_value = lax.dynamic_slice_in_dim(new_share, row_total - 1, 1, 0)
        return lax.dynamic_update_slice_in_dim(ends_buf, row_value, end_slot, 0)

    full_prompt = lax.all_gather(prompt_pad, "tp", axis=1, tiled=True)

    def advance(tick, state_tuple):
        incoming, state_buffers, ends_buf = state_tuple
        first_row, row_total, end_slot = locate(tick)
        own_rows = lax.dynamic_slice_in_dim(full_prompt, first_row, BLOCK_MOST, 0)
        rows_in = jnp.where(section_id == 0, own_rows, incoming)
        partial_value, state_buffers = compute(rows_in, first_row, state_buffers)
        summed = lax.psum(partial_value.astype(jnp.bfloat16), "tp").astype(jnp.float32)
        new_rows = (rows_in.astype(jnp.float32) + summed).astype(jnp.bfloat16)
        new_share = lax.dynamic_slice_in_dim(new_rows, tp_id * share_cols, share_cols, 1)
        ends_buf = record(ends_buf, new_share, row_total, end_slot)
        passed = from_behind(new_rows, "section", 1)
        return (passed, state_buffers, ends_buf)

    start_rows = jnp.zeros((BLOCK_MOST, full_prompt.shape[1]), jnp.bfloat16)
    final_state = lax.fori_loop(0, tick_count, advance, (start_rows, buffers, ends_init))
    cache = final_state[1][0]
    ends_buf = final_state[2]
    own_count = TOKENS // tp_count
    own_cache = lax.dynamic_slice_in_dim(cache, tp_id * own_count, own_count, 0)
    return (own_cache[None], ends_buf[:BLOCKS][None])


def solution(mesh):
    in_specs = (
        P("rep", "tp"),
        P("rep"),
        P("section", None, "tp"),
        P("section", None, "tp"),
        P("section", None, "tp"),
        P("section", None, "tp"),
        P("section", None, "tp"),
        P("section", "tp", None),
    )
    out_specs = (P("section", ("rep", "tp"), None), P("section", "rep", "tp"))
    return jax.shard_map(local, mesh=mesh, in_specs=in_specs, out_specs=out_specs, check_vma=False)
```

profile of v0, /device:TPU:4, one launch (start us, length us, event | category | flops | bytes accessed | tf_op | source)
XLA Modules:
  0.0 906.0 jit_solution(16084966877128177667)
XLA Ops:
  12.2 2.5 copy.67
  15.8 25.9 %all-gather.10.cloned.1.call-done = bf16[240,2560]{1,0:T(8,128)(2,1)} async-done(((bf16[240,640]{1,0:T(8,128)(2,1)}), bf16[240,2560]{1,0:T(8,128)(2,1)}) %all-gather.10.cloned.1.call-update) | async-done | bytes 1228816 | tf_op jit(solution)/shard_map/all_gather | solution.py:139
  44.5 851.5 %while.27 = (s32[]{:T(128)}, bf16[48,2560]{1,0:T(8,128)(2,1)S(1)}, bf16[240,544]{0,1:T(8,128)(2,1)}, bf16[240,512]{1,0:T(8,128)(2,1)}, bf16[240,512]{1,0:T(8,128...) while((s32[]{:T(128)}, bf16[48,2560]{1,0:T(8,128)(2,1)S(1)}, ...), condition=%wide.region_9.10_spmd.clone, body=%wide.region_1.9_spmd.clone.sunk | while | flops 327882208 | bytes 19493144 | solution.py:155
  49.9 13.6 %all-gather.6 = f32[4,192,48]{1,2,0:T(8,128)S(1)} all-gather(f32[1,192,48]{1,2,0:T(8,128)S(1)} %convolution_bitcast_fusion.6), channel_id=1, replica_groups=mesh['section'=2,'tp'=4,'rep'=4] {'tp'}, dimensions={0}, use_global_device_ids=true | all-gather | bytes 184320 | tf_op jit(solution)/shard_map/while/body/eval_jaxpr/all_gather | solution.py:89
  68.9 13.6 %all-gather.7 = f32[4,136,48]{1,2,0:T(8,128)S(1)} all-gather(f32[1,136,48]{1,2,0:T(8,128)S(1)} %convolution_bitcast_fusion.7), channel_id=1, replica_groups=mesh['section'=2,'tp'=4,'rep'=4] {'tp'}, dimensions={0}, use_global_device_ids=true | all-gather | bytes 130560 | tf_op jit(solution)/shard_map/while/body/eval_jaxpr/all_gather | solution.py:90
  85.2 2.9 dynamic_update_slice.64
  94.5 34.7 %all-reduce.3.cloned.1.call-done = bf16[48,2560]{1,0:T(8,128)(2,1)} async-done(((bf16[48,2560]{1,0:T(8,128)(2,1)}), bf16[48,2560]{1,0:T(8,128)(2,1)}) %all-reduce.3.cloned.1.call-update) | async-done | bytes 245776 | tf_op jit(solution)/shard_map/while/body/eval_jaxpr/psum | solution.py:147
  134.8 3.4 collective-permute-done
  143.6 13.8 %all-gather.6 = f32[4,192,48]{1,2,0:T(8,128)S(1)} all-gather(f32[1,192,48]{1,2,0:T(8,128)S(1)} %convolution_bitcast_fusion.6), channel_id=1, replica_groups=mesh['section'=2,'tp'=4,'rep'=4] {'tp'}, dimensions={0}, use_global_device_ids=true | all-gather | bytes 184320 | tf_op jit(solution)/shard_map/while/body/eval_jaxpr/all_gather | solution.py:89
  162.9 13.6 %all-gather.7 = f32[4,136,48]{1,2,0:T(8,128)S(1)} all-gather(f32[1,136,48]{1,2,0:T(8,128)S(1)} %convolution_bitcast_fusion.7), channel_id=1, replica_groups=mesh['section'=2,'tp'=4,'rep'=4] {'tp'}, dimensions={0}, use_global_device_ids=true | all-gather | bytes 130560 | tf_op jit(solution)/shard_map/while/body/eval_jaxpr/all_gather | solution.py:90
  179.1 3.1 dynamic_update_slice.64
  188.8 35.0 %all-reduce.3.cloned.1.call-done = bf16[48,2560]{1,0:T(8,128)(2,1)} async-done(((bf16[48,2560]{1,0:T(8,128)(2,1)}), bf16[48,2560]{1,0:T(8,128)(2,1)}) %all-reduce.3.cloned.1.call-update) | async-done | bytes 245776 | tf_op jit(solution)/shard_map/while/body/eval_jaxpr/psum | solution.py:147
  229.6 3.4 collective-permute-done
  238.3 13.8 %all-gather.6 = f32[4,192,48]{1,2,0:T(8,128)S(1)} all-gather(f32[1,192,48]{1,2,0:T(8,128)S(1)} %convolution_bitcast_fusion.6), channel_id=1, replica_groups=mesh['section'=2,'tp'=4,'rep'=4] {'tp'}, dimensions={0}, use_global_device_ids=true | all-gather | bytes 184320 | tf_op jit(solution)/shard_map/while/body/eval_jaxpr/all_gather | solution.py:89
  257.6 13.6 %all-gather.7 = f32[4,136,48]{1,2,0:T(8,128)S(1)} all-gather(f32[1,136,48]{1,2,0:T(8,128)S(1)} %convolution_bitcast_fusion.7), channel_id=1, replica_groups=mesh['section'=2,'tp'=4,'rep'=4] {'tp'}, dimensions={0}, use_global_device_ids=true | all-gather | bytes 130560 | tf_op jit(solution)/shard_map/while/body/eval_jaxpr/all_gather | solution.py:90
  273.8 3.6 dynamic_update_slice.64
  284.0 35.1 %all-reduce.3.cloned.1.call-done = bf16[48,2560]{1,0:T(8,128)(2,1)} async-done(((bf16[48,2560]{1,0:T(8,128)(2,1)}), bf16[48,2560]{1,0:T(8,128)(2,1)}) %all-reduce.3.cloned.1.call-update) | async-done | bytes 245776 | tf_op jit(solution)/shard_map/while/body/eval_jaxpr/psum | solution.py:147
  324.7 3.4 collective-permute-done
  333.5 13.8 %all-gather.6 = f32[4,192,48]{1,2,0:T(8,128)S(1)} all-gather(f32[1,192,48]{1,2,0:T(8,128)S(1)} %convolution_bitcast_fusion.6), channel_id=1, replica_groups=mesh['section'=2,'tp'=4,'rep'=4] {'tp'}, dimensions={0}, use_global_device_ids=true | all-gather | bytes 184320 | tf_op jit(solution)/shard_map/while/body/eval_jaxpr/all_gather | solution.py:89
  352.7 13.6 %all-gather.7 = f32[4,136,48]{1,2,0:T(8,128)S(1)} all-gather(f32[1,136,48]{1,2,0:T(8,128)S(1)} %convolution_bitcast_fusion.7), channel_id=1, replica_groups=mesh['section'=2,'tp'=4,'rep'=4] {'tp'}, dimensions={0}, use_global_device_ids=true | all-gather | bytes 130560 | tf_op jit(solution)/shard_map/while/body/eval_jaxpr/all_gather | solution.py:90
  369.0 3.6 dynamic_update_slice.64
  379.1 35.1 %all-reduce.3.cloned.1.call-done = bf16[48,2560]{1,0:T(8,128)(2,1)} async-done(((bf16[48,2560]{1,0:T(8,128)(2,1)}), bf16[48,2560]{1,0:T(8,128)(2,1)}) %all-reduce.3.cloned.1.call-update) | async-done | bytes 245776 | tf_op jit(solution)/shard_map/while/body/eval_jaxpr/psum | solution.py:147
  419.9 3.4 collective-permute-done
  428.7 13.8 %all-gather.6 = f32[4,192,48]{1,2,0:T(8,128)S(1)} all-gather(f32[1,192,48]{1,2,0:T(8,128)S(1)} %convolution_bitcast_fusion.6), channel_id=1, replica_groups=mesh['section'=2,'tp'=4,'rep'=4] {'tp'}, dimensions={0}, use_global_device_ids=true | all-gather | bytes 184320 | tf_op jit(solution)/shard_map/while/body/eval_jaxpr/all_gather | solution.py:89
  447.9 13.6 %all-gather.7 = f32[4,136,48]{1,2,0:T(8,128)S(1)} all-gather(f32[1,136,48]{1,2,0:T(8,128)S(1)} %convolution_bitcast_fusion.7), channel_id=1, replica_groups=mesh['section'=2,'tp'=4,'rep'=4] {'tp'}, dimensions={0}, use_global_device_ids=true | all-gather | bytes 130560 | tf_op jit(solution)/shard_map/while/body/eval_jaxpr/all_gather | solution.py:90
  464.1 3.6 dynamic_update_slice.64
  474.3 35.0 %all-reduce.3.cloned.1.call-done = bf16[48,2560]{1,0:T(8,128)(2,1)} async-done(((bf16[48,2560]{1,0:T(8,128)(2,1)}), bf16[48,2560]{1,0:T(8,128)(2,1)}) %all-reduce.3.cloned.1.call-update) | async-done | bytes 245776 | tf_op jit(solution)/shard_map/while/body/eval_jaxpr/psum | solution.py:147
  515.0 3.4 collective-permute-done
  523.8 13.8 %all-gather.6 = f32[4,192,48]{1,2,0:T(8,128)S(1)} all-gather(f32[1,192,48]{1,2,0:T(8,128)S(1)} %convolution_bitcast_fusion.6), channel_id=1, replica_groups=mesh['section'=2,'tp'=4,'rep'=4] {'tp'}, dimensions={0}, use_global_device_ids=true | all-gather | bytes 184320 | tf_op jit(solution)/shard_map/while/body/eval_jaxpr/all_gather | solution.py:89
  543.0 13.6 %all-gather.7 = f32[4,136,48]{1,2,0:T(8,128)S(1)} all-gather(f32[1,136,48]{1,2,0:T(8,128)S(1)} %convolution_bitcast_fusion.7), channel_id=1, replica_groups=mesh['section'=2,'tp'=4,'rep'=4] {'tp'}, dimensions={0}, use_global_device_ids=true | all-gather | bytes 130560 | tf_op jit(solution)/shard_map/while/body/eval_jaxpr/all_gather | solution.py:90
  559.2 3.6 dynamic_update_slice.64
  569.4 34.1 %all-reduce.3.cloned.1.call-done = bf16[48,2560]{1,0:T(8,128)(2,1)} async-done(((bf16[48,2560]{1,0:T(8,128)(2,1)}), bf16[48,2560]{1,0:T(8,128)(2,1)}) %all-reduce.3.cloned.1.call-update) | async-done | bytes 245776 | tf_op jit(solution)/shard_map/while/body/eval_jaxpr/psum | solution.py:147
  609.2 3.4 collective-permute-done
  618.0 13.8 %all-gather.6 = f32[4,192,48]{1,2,0:T(8,128)S(1)} all-gather(f32[1,192,48]{1,2,0:T(8,128)S(1)} %convolution_bitcast_fusion.6), channel_id=1, replica_groups=mesh['section'=2,'tp'=4,'rep'=4] {'tp'}, dimensions={0}, use_global_device_ids=true | all-gather | bytes 184320 | tf_op jit(solution)/shard_map/while/body/eval_jaxpr/all_gather | solution.py:89
  637.2 13.6 %all-gather.7 = f32[4,136,48]{1,2,0:T(8,128)S(1)} all-gather(f32[1,136,48]{1,2,0:T(8,128)S(1)} %convolution_bitcast_fusion.7), channel_id=1, replica_groups=mesh['section'=2,'tp'=4,'rep'=4] {'tp'}, dimensions={0}, use_global_device_ids=true | all-gather | bytes 130560 | tf_op jit(solution)/shard_map/while/body/eval_jaxpr/all_gather | solution.py:90
  653.5 2.9 dynamic_update_slice.64
  663.0 35.0 %all-reduce.3.cloned.1.call-done = bf16[48,2560]{1,0:T(8,128)(2,1)} async-done(((bf16[48,2560]{1,0:T(8,128)(2,1)}), bf16[48,2560]{1,0:T(8,128)(2,1)}) %all-reduce.3.cloned.1.call-update) | async-done | bytes 245776 | tf_op jit(solution)/shard_map/while/body/eval_jaxpr/psum | solution.py:147
  703.7 3.4 collective-permute-done
  712.5 13.8 %all-gather.6 = f32[4,192,48]{1,2,0:T(8,128)S(1)} all-gather(f32[1,192,48]{1,2,0:T(8,128)S(1)} %convolution_bitcast_fusion.6), channel_id=1, replica_groups=mesh['section'=2,'tp'=4,'rep'=4] {'tp'}, dimensions={0}, use_global_device_ids=true | all-gather | bytes 184320 | tf_op jit(solution)/shard_map/while/body/eval_jaxpr/all_gather | solution.py:89
  731.7 13.6 %all-gather.7 = f32[4,136,48]{1,2,0:T(8,128)S(1)} all-gather(f32[1,136,48]{1,2,0:T(8,128)S(1)} %convolution_bitcast_fusion.7), channel_id=1, replica_groups=mesh['section'=2,'tp'=4,'rep'=4] {'tp'}, dimensions={0}, use_global_device_ids=true | all-gather | bytes 130560 | tf_op jit(solution)/shard_map/while/body/eval_jaxpr/all_gather | solution.py:90
  748.0 2.9 dynamic_update_slice.64
  757.5 35.0 %all-reduce.3.cloned.1.call-done = bf16[48,2560]{1,0:T(8,128)(2,1)} async-done(((bf16[48,2560]{1,0:T(8,128)(2,1)}), bf16[48,2560]{1,0:T(8,128)(2,1)}) %all-reduce.3.cloned.1.call-update) | async-done | bytes 245776 | tf_op jit(solution)/shard_map/while/body/eval_jaxpr/psum | solution.py:147
  798.2 3.4 collective-permute-done
  806.9 13.8 %all-gather.6 = f32[4,192,48]{1,2,0:T(8,128)S(1)} all-gather(f32[1,192,48]{1,2,0:T(8,128)S(1)} %convolution_bitcast_fusion.6), channel_id=1, replica_groups=mesh['section'=2,'tp'=4,'rep'=4] {'tp'}, dimensions={0}, use_global_device_ids=true | all-gather | bytes 184320 | tf_op jit(solution)/shard_map/while/body/eval_jaxpr/all_gather | solution.py:89
  826.2 13.6 %all-gather.7 = f32[4,136,48]{1,2,0:T(8,128)S(1)} all-gather(f32[1,136,48]{1,2,0:T(8,128)S(1)} %convolution_bitcast_fusion.7), channel_id=1, replica_groups=mesh['section'=2,'tp'=4,'rep'=4] {'tp'}, dimensions={0}, use_global_device_ids=true | all-gather | bytes 130560 | tf_op jit(solution)/shard_map/while/body/eval_jaxpr/all_gather | solution.py:90
  842.4 2.9 dynamic_update_slice.64
  851.9 35.0 %all-reduce.3.cloned.1.call-done = bf16[48,2560]{1,0:T(8,128)(2,1)} async-done(((bf16[48,2560]{1,0:T(8,128)(2,1)}), bf16[48,2560]{1,0:T(8,128)(2,1)}) %all-reduce.3.cloned.1.call-update) | async-done | bytes 245776 | tf_op jit(solution)/shard_map/while/body/eval_jaxpr/psum | solution.py:147
  892.6 3.4 collective-permute-done
  (457 shorter events, 230.0 us)
Async XLA Ops:
  7.2 34.6 %all-gather.10.cloned.1.call-start = ((), (), s32[]{:S(2)}) async-start(), calls=%async_computation | async-start | bytes 1536000 | tf_op jit(solution)/shard_map/all_gather | solution.py:139
  12.1 32.3 %copy-start = (bf16[1,512,2560]{2,1,0:T(8,128)(2,1)S(1)}, bf16[1,512,2560]{2,1,0:T(8,128)(2,1)}, u32[]{:S(2)}) copy-start(bf16[1,512,2560]{2,1,0:T(8,128)(2,1)} %param.17) | copy-start | bytes 7864324
  44.5 84.7 %all-reduce.3.cloned.1.call-start = ((), (), s32[]{:S(2)}) async-start(), calls=%async_computation.1 | async-start | bytes 491520 | tf_op jit(solution)/shard_map/while/body/eval_jaxpr/psum | solution.py:147
  82.7 1.5 copy-start.1
  82.7 1.7 copy-start.4
  82.7 5.4 copy-start.2
  88.5 6.0 copy-start.3
  130.2 8.1 collective-permute-start
  138.3 85.6 %all-reduce.3.cloned.1.call-start = ((), (), s32[]{:S(2)}) async-start(), calls=%async_computation.1 | async-start | bytes 491520 | tf_op jit(solution)/shard_map/while/body/eval_jaxpr/psum | solution.py:147
  176.6 1.7 copy-start.4
  176.6 5.6 copy-start.2
  182.8 6.0 copy-start.3
  224.9 8.1 collective-permute-start
  233.0 86.1 %all-reduce.3.cloned.1.call-start = ((), (), s32[]{:S(2)}) async-start(), calls=%async_computation.1 | async-start | bytes 491520 | tf_op jit(solution)/shard_map/while/body/eval_jaxpr/psum | solution.py:147
  271.3 1.7 copy-start.4
  271.3 6.0 copy-start.2
  277.9 6.0 copy-start.3
  320.0 8.1 collective-permute-start
  328.1 86.1 %all-reduce.3.cloned.1.call-start = ((), (), s32[]{:S(2)}) async-start(), calls=%async_computation.1 | async-start | bytes 491520 | tf_op jit(solution)/shard_map/while/body/eval_jaxpr/psum | solution.py:147
  366.5 1.7 copy-start.4
  366.5 6.0 copy-start.2
  373.0 6.0 copy-start.3
  415.2 8.1 collective-permute-start
  423.3 86.0 %all-reduce.3.cloned.1.call-start = ((), (), s32[]{:S(2)}) async-start(), calls=%async_computation.1 | async-start | bytes 491520 | tf_op jit(solution)/shard_map/while/body/eval_jaxpr/psum | solution.py:147
  461.6 1.7 copy-start.4
  461.6 6.0 copy-start.2
  468.2 6.0 copy-start.3
  510.3 8.1 collective-permute-start
  518.4 85.1 %all-reduce.3.cloned.1.call-start = ((), (), s32[]{:S(2)}) async-start(), calls=%async_computation.1 | async-start | bytes 491520 | tf_op jit(solution)/shard_map/while/body/eval_jaxpr/psum | solution.py:147
  556.7 1.7 copy-start.4
  556.7 6.0 copy-start.2
  563.3 6.0 copy-start.3
  604.5 8.1 collective-permute-start
  612.6 85.4 %all-reduce.3.cloned.1.call-start = ((), (), s32[]{:S(2)}) async-start(), calls=%async_computation.1 | async-start | bytes 491520 | tf_op jit(solution)/shard_map/while/body/eval_jaxpr/psum | solution.py:147
  651.0 1.7 copy-start.4
  651.0 5.4 copy-start.2
  656.9 6.0 copy-start.3
  699.0 8.1 collective-permute-start
  707.1 85.3 %all-reduce.3.cloned.1.call-start = ((), (), s32[]{:S(2)}) async-start(), calls=%async_computation.1 | async-start | bytes 491520 | tf_op jit(solution)/shard_map/while/body/eval_jaxpr/psum | solution.py:147
  745.5 1.7 copy-start.4
  745.5 5.4 copy-start.2
  751.4 6.0 copy-start.3
  793.5 8.1 collective-permute-start
  801.6 85.3 %all-reduce.3.cloned.1.call-start = ((), (), s32[]{:S(2)}) async-start(), calls=%async_computation.1 | async-start | bytes 491520 | tf_op jit(solution)/shard_map/while/body/eval_jaxpr/psum | solution.py:147
  839.9 1.7 copy-start.4
  839.9 5.4 copy-start.2
  845.8 6.0 copy-start.3
  887.9 8.1 collective-permute-start
  (8 other events, 12.2 us)
Sparse Core Ops, SparseCore 0:
  9.6 32.1 all-gather.9
  94.6 34.5 all-reduce.2
  189.0 34.8 all-reduce.2
  284.1 34.9 all-reduce.2
  379.2 34.8 all-reduce.2
  474.4 34.8 all-reduce.2
  569.5 33.9 all-reduce.2
  663.1 34.8 all-reduce.2
  757.6 34.8 all-reduce.2
  852.0 34.8 all-reduce.2
where the time goes:
time: 913 us; the launch traced here: 906 us
  waiting for transfers between devices  371 us (41%)
  blocking collectives  246 us (27%)
  local copies, waits for them, and re-layouts  92.1 us (10%)
  matrix products  91.3 us (10%)
  other arithmetic  66.3 us (7%)
  between operations  14 us (2%)
  loops' own time  13.8 us (2%)
  starting transfers between devices  11.7 us (1%)
    psum x9, waiting for transfers between devices, advance(): lax.psum(partial_value.astype(jnp.bfloat16), 'tp').astype(jnp.float32)  314 us
    all_gather x9, blocking collectives, compute(): lax.all_gather(down_part, 'tp', axis=1, tiled=True)  124 us
    all_gather x9, blocking collectives, compute(): lax.all_gather(latent_part, 'tp', axis=1, tiled=True)  122 us
    ppermute x9, waiting for transfers between devices, from_behind(): return lax.ppermute(block, axis, route)  30.7 us
    dynamic_update_slice x9, local copies, waits for them, and re-layouts, compute(): cache = lax.dynamic_update_slice_in_dim(cache, fresh_rows, first_row, 0)  29.1 us
    all_gather x1, waiting for transfers between devices, local(): full_prompt = lax.all_gather(prompt_pad, 'tp', axis=1, tiled=True)  25.9 us
  transfers between devices with their start and end apart: 19, of which 19 were waited for; matrix products, arithmetic and copies ran while one was open for 3% of the time, Pallas kernels for 0%

commit v1 on v0

v1 whole, which is shorter than its diff:
```python
import jax
import jax.numpy as jnp
from jax import lax
from jax.sharding import PartitionSpec as P

NOPE_DIM = 128
ROPE_DIM = 32
VALUE_DIM = 128
LATENT = 512
EPSILON = 1e-06
F32 = jnp.float32
BF16 = jnp.bfloat16


def rms_rows(values):
    return values * lax.rsqrt(jnp.mean(values * values, axis=-1, keepdims=True) + EPSILON)


def rotate(values, positions):
    half_width = values.shape[-1] // 2
    frequency = 10000.0 ** (-2.0 * jnp.arange(half_width, dtype=F32) / values.shape[-1])
    angles = positions.astype(F32)[:, None] * frequency[None, :]
    if values.ndim == 3:
        angles = angles[:, None, :]
    cosine = jnp.cos(angles)
    sine_part = jnp.sin(angles)
    first_half = values[..., :half_width]
    second = values[..., half_width:]
    return jnp.concatenate(
        [first_half * cosine - second * sine_part, first_half * sine_part + second * cosine],
        axis=-1,
    )


def dot(a, b):
    return jnp.dot(a, b, preferred_element_type=F32)


def local(prompt, block_sizes, w_query_down, w_query, w_latent, w_keys, w_values, w_out):
    sections = lax.axis_size("section")
    section_id = lax.axis_index("section")
    tp_id = lax.axis_index("tp")
    tp_count = lax.axis_size("tp")
    tokens, share_cols = prompt.shape
    share_rows = tokens // tp_count
    down_weight, query_weight, latent_weight = w_query_down[0], w_query[0], w_latent[0]
    key_weight, value_weight, out_weight = w_keys[0], w_values[0], w_out[0]
    down_cols, latent_cols = down_weight.shape[1], latent_weight.shape[1]
    head_count = query_weight.shape[1] // (NOPE_DIM + ROPE_DIM)
    scale_factor = (NOPE_DIM + ROPE_DIM) ** (-0.5)
    all_positions = jnp.arange(tokens, dtype=jnp.int32)
    end_rows = jnp.cumsum(block_sizes) - 1

    def shift(array, distance, routes):
        pairs = [
            (a * tp_count + i, b * tp_count + (i + distance) % tp_count)
            for a, b in routes
            for i in range(tp_count)
        ]
        return lax.ppermute(array, ("section", "tp"), pairs)

    def gather(array, where, axis):
        routes = [(s, s) for s in where]
        width = array.shape[axis]
        shape = list(array.shape)
        shape[axis] = width * tp_count
        whole = jnp.zeros(shape, array.dtype)
        for k in range(tp_count):
            piece = array if k == 0 else shift(array, k, routes)
            whole = lax.dynamic_update_slice_in_dim(
                whole, piece, lax.rem(tp_id - k + tp_count, tp_count) * width, axis
            )
        return whole

    def keys_and_values(cache):
        plain = cache[:, :LATENT]
        keys = dot(plain, key_weight).astype(BF16).reshape(tokens, head_count, NOPE_DIM)
        values = dot(plain, value_weight).astype(BF16).reshape(tokens, head_count, VALUE_DIM)
        return keys, values

    def attend(compressed, positions, cache):
        keys, values = keys_and_values(cache)
        rows = compressed.shape[0]
        queries = dot(compressed, query_weight).reshape(rows, head_count, NOPE_DIM + ROPE_DIM)
        queries = jnp.concatenate(
            [queries[..., :NOPE_DIM], rotate(queries[..., NOPE_DIM:], positions)], axis=-1
        ).astype(BF16)
        scores = jnp.einsum("ihd,jhd->hij", queries[..., :NOPE_DIM], keys, preferred_element_type=F32)
        scores = scores + jnp.einsum(
            "ihr,jr->hij", queries[..., NOPE_DIM:], cache[:, LATENT:], preferred_element_type=F32
        )
        visible = all_positions[None, :] <= positions[:, None]
        powered = jnp.where(visible[None], jnp.exp(scores * scale_factor), 0.0)
        attention = (powered / jnp.sum(powered, axis=-1, keepdims=True)).astype(BF16)
        mixed = jnp.einsum("hij,jhv->ihv", attention, values, preferred_element_type=F32)
        return dot(mixed.astype(BF16).reshape(rows, head_count * VALUE_DIM), out_weight)

    def layer(hidden, own_share, tick):
        normed = rms_rows(hidden.astype(F32)).astype(BF16)
        parts = jnp.concatenate(
            [dot(normed, down_weight).astype(BF16), dot(normed, latent_weight).astype(BF16)], axis=1
        )
        whole = gather(parts[None], [tick], 0).astype(F32)
        down = jnp.concatenate([whole[m, :, :down_cols] for m in range(tp_count)], axis=1)
        latent = jnp.concatenate([whole[m, :, down_cols:] for m in range(tp_count)], axis=1)
        compressed = rms_rows(down).astype(BF16)
        cache = jnp.concatenate(
            [rms_rows(latent[:, :LATENT]), rotate(latent[:, LATENT:], all_positions)], axis=-1
        ).astype(BF16)
        partial = attend(compressed, all_positions, cache)
        start = tp_id * share_cols
        mine = lax.dynamic_slice_in_dim(partial, start, share_cols, 1) + own_share.astype(F32)
        partial = lax.dynamic_update_slice_in_dim(partial, mine, start, 1).astype(BF16)
        return partial, cache

    def pass_on(partial, tick):
        ends = jnp.take(partial, end_rows, axis=0)
        total = 0.0
        for k in range(tp_count):
            first = lax.rem(tp_id + k, tp_count) * share_rows
            block = lax.dynamic_slice_in_dim(partial, first, share_rows, 0)
            block = jnp.concatenate([block, ends], axis=0)
            total = total + shift(block, k, [(tick, tick + 1)]).astype(F32)
        total = total.astype(BF16)
        return total[:share_rows], total[share_rows:]

    own_cache = jnp.zeros((share_rows, LATENT + ROPE_DIM), BF16)
    own_ends = jnp.zeros((block_sizes.shape[0], share_cols), BF16)
    last = sections - 1
    latent_whole = gather(latent_weight, range(1, sections), 1) if last else latent_weight
    hidden, own_share = gather(prompt, [0], 1), prompt
    for tick in range(last):
        partial, cache = layer(hidden, own_share, tick)
        mine = lax.dynamic_slice_in_dim(cache, tp_id * share_rows, share_rows, 0)
        own_cache = jnp.where(section_id == tick, mine, own_cache)
        rows, ends = pass_on(partial, tick)
        ends_share = lax.dynamic_slice_in_dim(ends, tp_id * share_cols, share_cols, 1)
        own_ends = jnp.where(section_id == tick, shift(ends_share, 0, [(tick + 1, tick)]), own_ends)
        if tick + 1 < last:
            hidden = gather(rows, [tick + 1], 0)
            own_share = lax.dynamic_slice_in_dim(hidden, tp_id * share_cols, share_cols, 1)

    row_positions = tp_id * share_rows + jnp.arange(share_rows, dtype=jnp.int32)
    latent = dot(rms_rows(rows.astype(F32)).astype(BF16), latent_whole)
    fresh = jnp.concatenate(
        [rms_rows(latent[:, :LATENT]), rotate(latent[:, LATENT:], row_positions)], axis=-1
    ).astype(BF16)
    own_cache = jnp.where(section_id == last, fresh, own_cache)
    down = dot(rms_rows(ends.astype(F32)).astype(BF16), down_weight).astype(BF16)
    down = jnp.pad(down, ((0, 0), (0, fresh.shape[1] - down_cols)))
    whole = gather(jnp.concatenate([fresh, down], axis=0)[None], [last], 0)
    cache = whole[:, :share_rows].reshape(tokens, LATENT + ROPE_DIM)
    down = jnp.concatenate([whole[m, share_rows:, :down_cols] for m in range(tp_count)], axis=1)
    compressed = rms_rows(down.astype(F32)).astype(BF16)
    partial = attend(compressed, end_rows, cache).astype(BF16)
    total = ends_share.astype(F32)
    for k in range(tp_count):
        start = lax.rem(tp_id + k, tp_count) * share_cols
        block = lax.dynamic_slice_in_dim(partial, start, share_cols, 1)
        total = total + (shift(block, k, [(last, last)]) if k else block).astype(F32)
    own_ends = jnp.where(section_id == last, total.astype(BF16), own_ends)
    return (own_cache[None], own_ends[None])


def solution(mesh):
    in_specs = (
        P("rep", "tp"),
        P("rep"),
        P("section", None, "tp"),
        P("section", None, "tp"),
        P("section", None, "tp"),
        P("section", None, "tp"),
        P("section", None, "tp"),
        P("section", "tp", None),
    )
    out_specs = (P("section", ("rep", "tp"), None), P("section", "rep", "tp"))
    return jax.shard_map(local, mesh=mesh, in_specs=in_specs, out_specs=out_specs, check_vma=False)
```

time: 913 us -> 180 us (0.20)
  waiting for transfers between devices: 371 us -> 72.9 us
  blocking collectives: 246 us -> 0 us
  matrix products: 91.3 us -> 15.5 us
  local copies, waits for them, and re-layouts: 92.1 us -> 26.9 us
  other arithmetic: 66.3 us -> 14.3 us
  starting transfers between devices: 11.7 us -> 48.2 us
  loops' own time: 13.8 us -> 0 us
  between operations: 14 us -> 1.5 us
    psum x9 -> x0, waiting for transfers between devices: 314 us -> none  [advance(): lax.psum(partial_value.astype(jnp.bfloat16), 'tp').astype(jnp.float32)]
    all_gather x18 -> x0, blocking collectives: 246 us -> none  [the longest x9 124 us: compute(): lax.all_gather(down_part, 'tp', axis=1, tiled=True)]
    dot_general x81 -> x17, matrix products: 91.3 us -> 15.5 us  [the longest x12 11.8 us: dot(): return jnp.dot(a, b, preferred_element_type=F32)]
    dynamic_update_slice x36 -> x14, local copies, waits for them, and re-layouts: 59.4 us -> 10.7 us  [gather(): lax.dynamic_update_slice_in_dim(whole, piece, lax.rem(tp_id - k + tp_coun...]
    ppermute x9 -> x20, waiting for transfers between devices: 30.7 us -> 72.9 us  [shift(): return lax.ppermute(array, ('section', 'tp'), pairs)]
    ppermute x9 -> x20, starting transfers between devices: 11.6 us -> 48.2 us  [shift(): return lax.ppermute(array, ('section', 'tp'), pairs)]
    all_gather x1 -> x0, waiting for transfers between devices: 25.9 us -> none  [local(): full_prompt = lax.all_gather(prompt_pad, 'tp', axis=1, tiled=True)]
    reduce_sum x18 -> x0, other arithmetic: 23 us -> none  [the longest x9 11.7 us: locate(): row_total = jnp.where(active, jnp.sum(jnp.where(picked, block_sizes, 0)), 1)]
  transfers between devices with their start and end apart: 19 -> 20, of which waited for: 19 -> 6; matrix products, arithmetic and copies ran while one was open for 3% -> 29% of each run, Pallas kernels for 0% -> 0%
where the time goes in v1:
time: 180 us; the launch traced here: 179 us
  waiting for transfers between devices  72.9 us (41%)
  starting transfers between devices  48.2 us (27%)
  local copies, waits for them, and re-layouts  26.9 us (15%)
  matrix products  15.5 us (9%)
  other arithmetic  14.3 us (8%)
    ppermute x20, waiting for transfers between devices, shift(): return lax.ppermute(array, ('section', 'tp'), pairs)  72.9 us
    ppermute x20, starting transfers between devices, shift(): return lax.ppermute(array, ('section', 'tp'), pairs)  48.2 us
    dot_general x12, matrix products, dot(): return jnp.dot(a, b, preferred_element_type=F32)  11.8 us
    dynamic_update_slice x14, local copies, waits for them, and re-layouts, gather(): lax.dynamic_update_slice_in_dim(whole, piece, lax.rem(tp_id - k + tp_coun...  10.7 us
    reduce_sum x7, other arithmetic, rms_rows(): jnp.mean(values * values, axis=-1, keepdims=True) + EPSILON  3.85 us
  transfers between devices with their start and end apart: 20, of which 6 were waited for; matrix products, arithmetic and copies ran while one was open for 29% of the time, Pallas kernels for 0%

profile of v1, /device:TPU:4, one launch (start us, length us, event | category | flops | bytes accessed | tf_op | source)
XLA Modules:
  0.0 179.2 jit_solution(18035569483916212203)
XLA Ops:
  0.7 1.5 collective-permute-start
  3.5 3.5 %collective-permute-start.10 = (bf16[2560,136]{0,1:T(8,128)(2,1)}, bf16[2560,136]{0,1:T(8,128)(2,1)}, u32[]{:S(2)}, u32[]{:S(2)}) collective-permute-start(bf16[2560,136]{0,1:T(8,128)(2,1)} %bitcast.145), channel_id=1, source_target_pairs={{16,20},{20,24},{24,28},{28,16},{17,21},{21,25},{25,29},{29,17},{1... | collective-permute-start | bytes 2088968 | tf_op jit(solution)/shard_map/ppermute | solution.py:60
  9.6 1.7 broadcast_in_dim.96
  12.2 1.0 broadcast_in_dim.55
  15.2 1.8 constant_dynamic-update-slice_fusion.14
  18.5 1.5 fusion.3
  20.0 1.9 %convolution_convert_fusion.7 = bf16[192,136]{0,1:T(8,128)(2,1)S(1)} fusion(bf16[192,2560]{1,0:T(8,128)(2,1)} %constant_dynamic-update-slice_fusion.12, f32[192]{0:T(256)S(1)} %add_rsqrt_fusion.2, bf16[1,2560,136]{1,2,0:T(8,128)(2,1)} %param.12), kind=kOutput, calls=%fused_computation.25 | convolution fusion | flops 135194112 | bytes 1732352 | tf_op jit(solution)/shard_map/dot_general | solution.py:36
  21.9 1.7 convolution_convert_fusion.6
  23.9 1.3 collective-permute-start.3
  25.2 1.3 collective-permute-start.4
  26.6 2.3 %copy.93 = bf16[1,768,640]{1,2,0:T(8,128)(2,1)} copy(bf16[1,768,640]{2,1,0:T(8,128)(2,1)} %param.11) | data formatting | bytes 1966080 | tf_op args[3]
  31.7 1.0 slice_bitcast_fusion.7
  33.6 1.2 multiply_cosine_fusion
  34.8 0.9 copy.98
  35.7 1.6 copy.99
  37.3 1.5 copy.96
  38.8 1.5 copy.97
  40.3 1.5 multiply_reduce_fusion.1
  41.8 1.4 multiply_convert_fusion.1
  43.5 1.0 fusion.8
  45.4 1.2 fusion.7
  46.6 1.8 %fusion.10 = bf16[4,24,8,128]{3,2,1,0:T(8,128)(2,1)S(1)} fusion(f32[4,192,192]{1,2,0:T(8,128)} %fusion.7, bf16[24,4,8,128]{3,2,1,0:T(8,128)(2,1)} %fusion.8), kind=kOutput, calls=%fused_computation.21 | convolution fusion | flops 38142912 | bytes 983040 | tf_op jit(solution)/shard_map/hij,jhv->ihv/dot_general | solution.py:95
  49.5 1.0 convert_element_type.166
  50.5 2.1 %gather_fusion = bf16[8,2560]{1,0:T(8,128)(2,1)S(1)} fusion(bf16[192,2560]{1,0:T(8,128)(2,1)} %convert_element_type.166, s32[1024]{0:T(1024)} %pad_clamp_fusion), kind=kCustom, calls=%fused_computation | custom fusion | bytes 81952 | tf_op jit(solution)/shard_map/jit(_take)/gather | solution.py:117
  52.7 1.5 constant_dynamic-slice_fusion.7
  54.3 1.3 collective-permute-start.6
  55.6 1.3 collective-permute-start.7
  56.9 1.3 collective-permute-start.8
  58.2 1.3 collective-permute-start.9
  59.6 41.0 %collective-permute-done.6 = bf16[56,2560]{1,0:T(8,128)(2,1)S(1)} collective-permute-done((bf16[56,2560]{1,0:T(8,128)(2,1)S(1)}, bf16[56,2560]{1,0:T(8,128)(2,1)S(1)}, u32[]{:S(2)}, u32[]{:S(2)}) %collective-permute-start.6) | collective-permute-done | bytes 286752 | tf_op jit(solution)/shard_map/ppermute | solution.py:60
  100.6 2.0 %collective-permute-start.11 = (bf16[2560,136]{0,1:T(8,128)(2,1)S(1)}, bf16[2560,136]{0,1:T(8,128)(2,1)S(1)}, u32[]{:S(2)}, u32[]{:S(2)}) collective-permute-start(bf16[2560,136]{0,1:T(8,128)(2,1)S(1)} %bitcast.146), channel_id=1, source_target_pairs={{16,24},{20,28},{24,16},{28,20},{17,25},{21,29},{25,17},{29,21},{1... | collective-permute-start | bytes 2088968 | tf_op jit(solution)/shard_map/ppermute | solution.py:60
  102.7 1.9 %collective-permute-start.12 = (bf16[2560,136]{0,1:T(8,128)(2,1)S(1)}, bf16[2560,136]{0,1:T(8,128)(2,1)S(1)}, u32[]{:S(2)}, u32[]{:S(2)}) collective-permute-start(bf16[2560,136]{0,1:T(8,128)(2,1)S(1)} %bitcast.147), channel_id=1, source_target_pairs={{16,28},{20,16},{24,20},{28,24},{17,29},{21,17},{25,21},{29,25},{1... | collective-permute-start | bytes 2088968 | tf_op jit(solution)/shard_map/ppermute | solution.py:60
  105.5 2.0 %constant_dynamic-update-slice_fusion.6 = bf16[2560,544]{0,1:T(8,128)(2,1)} fusion(bf16[2560,544]{0,1:T(8,128)(2,1)} %constant_dynamic-update-slice_fusion.7, bf16[2560,136]{0,1:T(8,128)(2,1)} %collective-permute-done.10, s32[]{:T(128)S(6)} %select_n.141), kind=kLoop, calls=%fused_computation.163 | loop fusion | bytes 1392644 | tf_op jit(solution)/shard_map/dynamic_update_slice | solution.py:70
  107.5 22.1 %collective-permute-done.11 = bf16[2560,136]{0,1:T(8,128)(2,1)S(1)} collective-permute-done((bf16[2560,136]{0,1:T(8,128)(2,1)S(1)}, bf16[2560,136]{0,1:T(8,128)(2,1)S(1)}, u32[]{:S(2)}, u32[]{:S(2)}) %collective-permute-start.11) | collective-permute-done | bytes 696352 | tf_op jit(solution)/shard_map/ppermute | solution.py:60
  130.5 4.9 %collective-permute-done.12 = bf16[2560,136]{0,1:T(8,128)(2,1)S(1)} collective-permute-done((bf16[2560,136]{0,1:T(8,128)(2,1)S(1)}, bf16[2560,136]{0,1:T(8,128)(2,1)S(1)}, u32[]{:S(2)}, u32[]{:S(2)}) %collective-permute-start.12) | collective-permute-done | bytes 696352 | tf_op jit(solution)/shard_map/ppermute | solution.py:60
  135.4 0.9 constant_dynamic-update-slice_fusion.4
  136.3 2.7 %fusion.33 = f32[48,544]{1,0:T(8,128)S(1)} fusion(bf16[2560,544]{0,1:T(8,128)(2,1)} %constant_dynamic-update-slice_fusion.4, f32[48]{0:T(128)S(1)} %add_rsqrt_fusion.6, bf16[56,2560]{1,0:T(8,128)(2,1)S(1)} %add_convert_fusion), kind=kOutput, calls=%fused_computation.64 | convolution fusion | flops 134062080 | bytes 3136000 | tf_op jit(solution)/shard_map/dot_general | solution.py:36
  139.9 11.6 %collective-permute-start.13 = (bf16[1,56,544]{2,1,0:T(8,128)(2,1)S(1)}, bf16[1,56,544]{2,1,0:T(8,128)(2,1)S(1)}, u32[]{:S(2)}, u32[]{:S(2)}) collective-permute-start(bf16[1,56,544]{2,1,0:T(8,128)(2,1)S(1)} %get-tuple-element.9), channel_id=1, source_target_pairs={{16,20},{20,24},{24,28},{28,16},{17,21},{21,25},{25,29},{29,17},{1... | collective-permute-start | bytes 182792 | tf_op jit(solution)/shard_map/ppermute | solution.py:60
  151.6 1.3 collective-permute-start.19
  152.9 3.1 %collective-permute-start.14 = (bf16[1,56,544]{2,1,0:T(8,128)(2,1)S(1)}, bf16[1,56,544]{2,1,0:T(8,128)(2,1)S(1)}, u32[]{:S(2)}, u32[]{:S(2)}) collective-permute-start(bf16[1,56,544]{2,1,0:T(8,128)(2,1)S(1)} %get-tuple-element.9), channel_id=1, source_target_pairs={{16,24},{20,28},{24,16},{28,20},{17,25},{21,29},{25,17},{29,21},{1... | collective-permute-start | bytes 182792 | tf_op jit(solution)/shard_map/ppermute | solution.py:60
  156.0 3.1 %collective-permute-start.15 = (bf16[1,56,544]{2,1,0:T(8,128)(2,1)S(1)}, bf16[1,56,544]{2,1,0:T(8,128)(2,1)S(1)}, u32[]{:S(2)}, u32[]{:S(2)}) collective-permute-start(bf16[1,56,544]{2,1,0:T(8,128)(2,1)S(1)} %get-tuple-element.9), channel_id=1, source_target_pairs={{16,28},{20,16},{24,20},{28,24},{17,29},{21,17},{25,21},{29,25},{1... | collective-permute-start | bytes 182792 | tf_op jit(solution)/shard_map/ppermute | solution.py:60
  159.1 1.9 %collective-permute-done.14 = bf16[1,56,544]{2,1,0:T(8,128)(2,1)S(1)} collective-permute-done((bf16[1,56,544]{2,1,0:T(8,128)(2,1)S(1)}, bf16[1,56,544]{2,1,0:T(8,128)(2,1)S(1)}, u32[]{:S(2)}, u32[]{:S(2)}) %collective-permute-start.14) | collective-permute-done | bytes 60960 | tf_op jit(solution)/shard_map/ppermute | solution.py:60
  161.1 1.2 collective-permute-done.15
  162.6 1.3 fusion.11
  165.7 2.6 %collective-permute-start.16 = (bf16[8,640]{1,0:T(8,128)(2,1)S(1)}, bf16[8,640]{1,0:T(8,128)(2,1)S(1)}, u32[]{:S(2)}, u32[]{:S(2)}) collective-permute-start(bf16[8,640]{1,0:T(8,128)(2,1)S(1)} %get-tuple-element.34), channel_id=1, source_target_pairs={{16,20},{20,24},{24,28},{28,16},{17,21},{21,25},{25,29},{29,17},{1... | collective-permute-start | bytes 30728 | tf_op jit(solution)/shard_map/ppermute | solution.py:60
  168.3 4.7 %collective-permute-start.17 = (bf16[8,640]{1,0:T(8,128)(2,1)S(1)}, bf16[8,640]{1,0:T(8,128)(2,1)S(1)}, u32[]{:S(2)}, u32[]{:S(2)}) collective-permute-start(bf16[8,640]{1,0:T(8,128)(2,1)S(1)} %get-tuple-element.36), channel_id=1, source_target_pairs={{16,24},{20,28},{24,16},{28,20},{17,25},{21,29},{25,17},{29,21},{1... | collective-permute-start | bytes 30728 | tf_op jit(solution)/shard_map/ppermute | solution.py:60
  173.0 3.0 %collective-permute-start.18 = (bf16[8,640]{1,0:T(8,128)(2,1)S(1)}, bf16[8,640]{1,0:T(8,128)(2,1)S(1)}, u32[]{:S(2)}, u32[]{:S(2)}) collective-permute-start(bf16[8,640]{1,0:T(8,128)(2,1)S(1)} %get-tuple-element.35), channel_id=1, source_target_pairs={{16,28},{20,16},{24,20},{28,24},{17,29},{21,17},{25,21},{29,25},{1... | collective-permute-start | bytes 30728 | tf_op jit(solution)/shard_map/ppermute | solution.py:60
  176.8 1.8 collective-permute-done.18
  (151 shorter events, 20.7 us)
Async XLA Ops:
  0.6 47.8 %copy-start = (bf16[1,512,2560]{2,1,0:T(8,128)(2,1)S(1)}, bf16[1,512,2560]{2,1,0:T(8,128)(2,1)}, u32[]{:S(2)}) copy-start(bf16[1,512,2560]{2,1,0:T(8,128)(2,1)} %param.15) | copy-start | bytes 7864324
  0.6 12.6 %copy-start.8 = (bf16[192,640]{1,0:T(8,128)(2,1)S(1)}, bf16[192,640]{1,0:T(8,128)(2,1)}, u32[]{:S(2)}) copy-start(bf16[192,640]{1,0:T(8,128)(2,1)} %param.8) | copy-start | bytes 737284
  0.7 14.6 %collective-permute-start = (bf16[192,640]{1,0:T(8,128)(2,1)}, bf16[192,640]{1,0:T(8,128)(2,1)}, u32[]{:S(2)}, u32[]{:S(2)}) collective-permute-start(bf16[192,640]{1,0:T(8,128)(2,1)} %param.8), channel_id=1, source_target_pairs={{0,4},{4,8},{8,12},{12,0},{1,5},{5,9},{9,13},{13,1},{2,6},{6,10},{... | collective-permute-start | bytes 737288 | tf_op jit(solution)/shard_map/ppermute | solution.py:60
  2.1 14.9 %collective-permute-start.1 = (bf16[192,640]{1,0:T(8,128)(2,1)}, bf16[192,640]{1,0:T(8,128)(2,1)S(1)}, u32[]{:S(2)}, u32[]{:S(2)}) collective-permute-start(bf16[192,640]{1,0:T(8,128)(2,1)} %param.8), channel_id=1, source_target_pairs={{0,8},{4,12},{8,0},{12,4},{1,9},{5,13},{9,1},{13,5},{2,10},{6,14},... | collective-permute-start | bytes 737288 | tf_op jit(solution)/shard_map/ppermute | solution.py:60
  2.8 14.9 %collective-permute-start.2 = (bf16[192,640]{1,0:T(8,128)(2,1)}, bf16[192,640]{1,0:T(8,128)(2,1)S(1)}, u32[]{:S(2)}, u32[]{:S(2)}) collective-permute-start(bf16[192,640]{1,0:T(8,128)(2,1)} %param.8), channel_id=1, source_target_pairs={{0,12},{4,0},{8,4},{12,8},{1,13},{5,1},{9,5},{13,9},{2,14},{6,2},{... | collective-permute-start | bytes 737288 | tf_op jit(solution)/shard_map/ppermute | solution.py:60
  3.5 102.0 %collective-permute-start.10 = (bf16[2560,136]{0,1:T(8,128)(2,1)}, bf16[2560,136]{0,1:T(8,128)(2,1)}, u32[]{:S(2)}, u32[]{:S(2)}) collective-permute-start(bf16[2560,136]{0,1:T(8,128)(2,1)} %bitcast.145), channel_id=1, source_target_pairs={{16,20},{20,24},{24,28},{28,16},{17,21},{21,25},{25,29},{29,17},{1... | collective-permute-start | bytes 2088968 | tf_op jit(solution)/shard_map/ppermute | solution.py:60
  15.2 6.7 %copy-start.6 = (bf16[1,2560,192]{1,2,0:T(8,128)(2,1)S(1)}, bf16[1,2560,192]{1,2,0:T(8,128)(2,1)}, u32[]{:S(2)}) copy-start(bf16[1,2560,192]{1,2,0:T(8,128)(2,1)} %param.10) | copy-start | bytes 2949124
  23.9 5.6 %collective-permute-start.3 = (bf16[1,192,328]{2,1,0:T(8,128)(2,1)S(1)}, bf16[1,192,328]{2,1,0:T(8,128)(2,1)}, u32[]{:S(2)}, u32[]{:S(2)}) collective-permute-start(bf16[1,192,328]{2,1,0:T(8,128)(2,1)S(1)} %get-tuple-element.11), channel_id=1, source_target_pairs={{0,4},{4,8},{8,12},{12,0},{1,5},{5,9},{9,13},{13,1},{2,6},{6,10},{... | collective-permute-start | bytes 377864 | tf_op jit(solution)/shard_map/ppermute | solution.py:60
  25.2 5.3 %collective-permute-start.4 = (bf16[1,192,328]{2,1,0:T(8,128)(2,1)S(1)}, bf16[1,192,328]{2,1,0:T(8,128)(2,1)}, u32[]{:S(2)}, u32[]{:S(2)}) collective-permute-start(bf16[1,192,328]{2,1,0:T(8,128)(2,1)S(1)} %get-tuple-element.11), channel_id=1, source_target_pairs={{0,8},{4,12},{8,0},{12,4},{1,9},{5,13},{9,1},{13,5},{2,10},{6,14},... | collective-permute-start | bytes 377864 | tf_op jit(solution)/shard_map/ppermute | solution.py:60
  26.6 7.1 %copy-start.27 = (f32[16]{0:T(128)}, f32[16]{0:T(128)S(1)}, u32[]{:S(2)}) copy-start(f32[16]{0:T(128)S(1)} %multiply_power_fusion) | copy-start | bytes 196
  28.9 2.6 %collective-permute-start.5 = (bf16[1,192,328]{2,1,0:T(8,128)(2,1)S(1)}, bf16[1,192,328]{2,1,0:T(8,128)(2,1)S(1)}, u32[]{:S(2)}, u32[]{:S(2)}) collective-permute-start(bf16[1,192,328]{2,1,0:T(8,128)(2,1)S(1)} %get-tuple-element.11), channel_id=1, source_target_pairs={{0,12},{4,0},{8,4},{12,8},{1,13},{5,1},{9,5},{13,9},{2,14},{6,2},{... | collective-permute-start | bytes 377864 | tf_op jit(solution)/shard_map/ppermute | solution.py:60
  31.7 1.9 %copy-start.14 = (f32[192,192]{1,0:T(8,128)}, f32[192,192]{1,0:T(8,128)S(1)}, u32[]{:S(2)}) copy-start(f32[192,192]{1,0:T(8,128)S(1)} %get-tuple-element.14) | copy-start | bytes 442372
  31.7 1.9 %copy-start.16 = (f32[192,192]{1,0:T(8,128)}, f32[192,192]{1,0:T(8,128)S(1)}, u32[]{:S(2)}) copy-start(f32[192,192]{1,0:T(8,128)S(1)} %get-tuple-element.15) | copy-start | bytes 442372
  31.7 11.5 %copy-start.3 = (bf16[1,512,512]{2,1,0:T(8,128)(2,1)S(1)}, bf16[1,512,512]{2,1,0:T(8,128)(2,1)}, u32[]{:S(2)}) copy-start(bf16[1,512,512]{2,1,0:T(8,128)(2,1)} %param.13) | copy-start | bytes 1572868
  32.7 9.0 %copy-start.5 = (f32[192,136]{1,0:T(8,128)}, f32[192,136]{1,0:T(8,128)S(1)}, u32[]{:S(2)}) copy-start(f32[192,136]{1,0:T(8,128)S(1)} %get-tuple-element.16) | copy-start | bytes 313348
  40.2 3.3 %copy-start.4 = (bf16[1,512,512]{2,1,0:T(8,128)(2,1)S(1)}, bf16[1,512,512]{2,1,0:T(8,128)(2,1)}, u32[]{:S(2)}) copy-start(bf16[1,512,512]{2,1,0:T(8,128)(2,1)} %param.14) | copy-start | bytes 1572868
  40.2 4.2 %copy-start.1 = (bf16[1,768,640]{1,2,0:T(8,128)(2,1)S(1)}, bf16[1,768,640]{1,2,0:T(8,128)(2,1)}, u32[]{:S(2)}) copy-start(bf16[1,768,640]{1,2,0:T(8,128)(2,1)} %copy.93) | copy-start | bytes 2949124
  40.2 4.2 %copy-start.11 = (f32[192,192]{1,0:T(8,128)S(1)}, f32[192,192]{1,0:T(8,128)}, u32[]{:S(2)}) copy-start(f32[192,192]{1,0:T(8,128)} %copy-done.10) | copy-start | bytes 442372
  40.3 4.2 %copy-start.13 = (f32[192,192]{1,0:T(8,128)S(1)}, f32[192,192]{1,0:T(8,128)}, u32[]{:S(2)}) copy-start(f32[192,192]{1,0:T(8,128)} %copy-done.12) | copy-start | bytes 442372
  40.3 4.2 %copy-start.15 = (f32[192,192]{1,0:T(8,128)S(1)}, f32[192,192]{1,0:T(8,128)}, u32[]{:S(2)}) copy-start(f32[192,192]{1,0:T(8,128)} %copy-done.14) | copy-start | bytes 442372
  40.3 4.2 %copy-start.17 = (f32[192,192]{1,0:T(8,128)S(1)}, f32[192,192]{1,0:T(8,128)}, u32[]{:S(2)}) copy-start(f32[192,192]{1,0:T(8,128)} %copy-done.16) | copy-start | bytes 442372
  40.3 4.2 %copy-start.30 = (f32[192]{0:T(256)S(1)}, f32[192]{0:T(256)}, u32[]{:S(2)}) copy-start(f32[192]{0:T(256)} %add_rsqrt_fusion) | copy-start | bytes 2308
  41.8 3.3 %copy-start.23 = (f32[192,16]{0,1:T(8,128)S(1)}, f32[192,16]{0,1:T(8,128)}, u32[]{:S(2)}) copy-start(f32[192,16]{0,1:T(8,128)} %copy.99) | copy-start | bytes 36868
  41.8 3.3 %copy-start.24 = (bf16[192,16]{0,1:T(8,128)(2,1)S(1)}, bf16[192,16]{0,1:T(8,128)(2,1)}, u32[]{:S(2)}) copy-start(bf16[192,16]{0,1:T(8,128)(2,1)} %copy.96) | copy-start | bytes 18436
  41.8 3.3 %copy-start.25 = (bf16[192,16]{0,1:T(8,128)(2,1)S(1)}, bf16[192,16]{0,1:T(8,128)(2,1)}, u32[]{:S(2)}) copy-start(bf16[192,16]{0,1:T(8,128)(2,1)} %copy.97) | copy-start | bytes 18436
  43.2 2.2 %copy-start.22 = (pred[192,192]{0,1:T(8,128)(4,1)S(1)}, pred[192,192]{0,1:T(8,128)(4,1)}, u32[]{:S(2)}) copy-start(pred[192,192]{0,1:T(8,128)(4,1)} %iota_compare_fusion) | copy-start | bytes 110596
  49.4 3.2 %copy-start.31 = (pred[8]{0:T(512)(128)(4,1)S(1)}, pred[8]{0:T(512)(128)(4,1)}, u32[]{:S(2)}) copy-start(pred[8]{0:T(512)(128)(4,1)} %compare_and_fusion) | copy-start | bytes 28
  50.5 9.0 %copy-start.28 = (f32[16]{0:T(128)S(1)}, f32[16]{0:T(128)}, u32[]{:S(2)}) copy-start(f32[16]{0:T(128)} %copy-done.27) | copy-start | bytes 196
  50.5 9.0 %copy-start.29 = (f32[8]{0:T(128)S(1)}, f32[8]{0:T(128)}, u32[]{:S(2)}) copy-start(f32[8]{0:T(128)} %get-tuple-element.51) | copy-start | bytes 100
  52.6 48.0 %copy-start.19 = (bf16[1,2560,136]{1,2,0:T(8,128)(2,1)S(1)}, bf16[1,2560,136]{1,2,0:T(8,128)(2,1)}, u32[]{:S(2)}) copy-start(bf16[1,2560,136]{1,2,0:T(8,128)(2,1)} %param.12) | copy-start | bytes 2088964
  52.7 52.4 %copy-start.7 = (bf16[1,2560,192]{1,2,0:T(8,128)(2,1)S(1)}, bf16[1,2560,192]{1,2,0:T(8,128)(2,1)}, u32[]{:S(2)}) copy-start(bf16[1,2560,192]{1,2,0:T(8,128)(2,1)} %param.10) | copy-start | bytes 2949124
  54.3 46.3 %collective-permute-start.6 = (bf16[56,2560]{1,0:T(8,128)(2,1)S(1)}, bf16[56,2560]{1,0:T(8,128)(2,1)S(1)}, u32[]{:S(2)}, u32[]{:S(2)}) collective-permute-start(bf16[56,2560]{1,0:T(8,128)(2,1)S(1)} %get-tuple-element.39), channel_id=1, source_target_pairs={{0,16},{4,20},{8,24},{12,28},{1,17},{5,21},{9,25},{13,29},{2,18},{... | collective-permute-start | bytes 860168 | tf_op jit(solution)/shard_map/ppermute | solution.py:60
  55.6 47.1 %collective-permute-start.7 = (bf16[56,2560]{1,0:T(8,128)(2,1)S(1)}, bf16[56,2560]{1,0:T(8,128)(2,1)S(1)}, u32[]{:S(2)}, u32[]{:S(2)}) collective-permute-start(bf16[56,2560]{1,0:T(8,128)(2,1)S(1)} %get-tuple-element.40), channel_id=1, source_target_pairs={{0,20},{4,24},{8,28},{12,16},{1,21},{5,25},{9,29},{13,17},{2,22},{... | collective-permute-start | bytes 860168 | tf_op jit(solution)/shard_map/ppermute | solution.py:60
  56.9 47.7 %collective-permute-start.8 = (bf16[56,2560]{1,0:T(8,128)(2,1)S(1)}, bf16[56,2560]{1,0:T(8,128)(2,1)S(1)}, u32[]{:S(2)}, u32[]{:S(2)}) collective-permute-start(bf16[56,2560]{1,0:T(8,128)(2,1)S(1)} %get-tuple-element.41), channel_id=1, source_target_pairs={{0,24},{4,28},{8,16},{12,20},{1,25},{5,29},{9,17},{13,21},{2,26},{... | collective-permute-start | bytes 860168 | tf_op jit(solution)/shard_map/ppermute | solution.py:60
  58.2 46.4 %collective-permute-start.9 = (bf16[56,2560]{1,0:T(8,128)(2,1)S(1)}, bf16[56,2560]{1,0:T(8,128)(2,1)S(1)}, u32[]{:S(2)}, u32[]{:S(2)}) collective-permute-start(bf16[56,2560]{1,0:T(8,128)(2,1)S(1)} %get-tuple-element.42), channel_id=1, source_target_pairs={{0,28},{4,16},{8,20},{12,24},{1,29},{5,17},{9,21},{13,25},{2,30},{... | collective-permute-start | bytes 860168 | tf_op jit(solution)/shard_map/ppermute | solution.py:60
  100.6 29.0 %collective-permute-start.11 = (bf16[2560,136]{0,1:T(8,128)(2,1)S(1)}, bf16[2560,136]{0,1:T(8,128)(2,1)S(1)}, u32[]{:S(2)}, u32[]{:S(2)}) collective-permute-start(bf16[2560,136]{0,1:T(8,128)(2,1)S(1)} %bitcast.146), channel_id=1, source_target_pairs={{16,24},{20,28},{24,16},{28,20},{17,25},{21,29},{25,17},{29,21},{1... | collective-permute-start | bytes 2088968 | tf_op jit(solution)/shard_map/ppermute | solution.py:60
  102.7 32.7 %collective-permute-start.12 = (bf16[2560,136]{0,1:T(8,128)(2,1)S(1)}, bf16[2560,136]{0,1:T(8,128)(2,1)S(1)}, u32[]{:S(2)}, u32[]{:S(2)}) collective-permute-start(bf16[2560,136]{0,1:T(8,128)(2,1)S(1)} %bitcast.147), channel_id=1, source_target_pairs={{16,28},{20,16},{24,20},{28,24},{17,29},{21,17},{25,21},{29,25},{1... | collective-permute-start | bytes 2088968 | tf_op jit(solution)/shard_map/ppermute | solution.py:60
  139.1 25.8 %copy-start.26 = (pred[8,192]{1,0:T(8,128)(4,1)S(1)}, pred[8,192]{1,0:T(8,128)(4,1)}, u32[]{:S(2)}) copy-start(pred[8,192]{1,0:T(8,128)(4,1)} %iota_compare_fusion.2) | copy-start | bytes 4612
  139.8 24.3 %copy-start.2 = (bf16[1,768,640]{1,2,0:T(8,128)(2,1)S(1)}, bf16[1,768,640]{1,2,0:T(8,128)(2,1)}, u32[]{:S(2)}) copy-start(bf16[1,768,640]{1,2,0:T(8,128)(2,1)} %copy.93) | copy-start | bytes 2949124
  139.9 19.2 %collective-permute-start.13 = (bf16[1,56,544]{2,1,0:T(8,128)(2,1)S(1)}, bf16[1,56,544]{2,1,0:T(8,128)(2,1)S(1)}, u32[]{:S(2)}, u32[]{:S(2)}) collective-permute-start(bf16[1,56,544]{2,1,0:T(8,128)(2,1)S(1)} %get-tuple-element.9), channel_id=1, source_target_pairs={{16,20},{20,24},{24,28},{28,16},{17,21},{21,25},{25,29},{29,17},{1... | collective-permute-start | bytes 182792 | tf_op jit(solution)/shard_map/ppermute | solution.py:60
  151.6 25.2 %collective-permute-start.19 = (bf16[8,640]{1,0:T(8,128)(2,1)S(1)}, bf16[8,640]{1,0:T(8,128)(2,1)S(1)}, u32[]{:S(2)}, u32[]{:S(2)}) collective-permute-start(bf16[8,640]{1,0:T(8,128)(2,1)S(1)} %constant_dynamic-slice_fusion.2), channel_id=1, source_target_pairs={{16,0},{20,4},{24,8},{28,12},{17,1},{21,5},{25,9},{29,13},{18,2},{... | collective-permute-start | bytes 30728 | tf_op jit(solution)/shard_map/ppermute | solution.py:60
  152.9 8.2 %collective-permute-start.14 = (bf16[1,56,544]{2,1,0:T(8,128)(2,1)S(1)}, bf16[1,56,544]{2,1,0:T(8,128)(2,1)S(1)}, u32[]{:S(2)}, u32[]{:S(2)}) collective-permute-start(bf16[1,56,544]{2,1,0:T(8,128)(2,1)S(1)} %get-tuple-element.9), channel_id=1, source_target_pairs={{16,24},{20,28},{24,16},{28,20},{17,25},{21,29},{25,17},{29,21},{1... | collective-permute-start | bytes 182792 | tf_op jit(solution)/shard_map/ppermute | solution.py:60
  156.0 6.2 %collective-permute-start.15 = (bf16[1,56,544]{2,1,0:T(8,128)(2,1)S(1)}, bf16[1,56,544]{2,1,0:T(8,128)(2,1)S(1)}, u32[]{:S(2)}, u32[]{:S(2)}) collective-permute-start(bf16[1,56,544]{2,1,0:T(8,128)(2,1)S(1)} %get-tuple-element.9), channel_id=1, source_target_pairs={{16,28},{20,16},{24,20},{28,24},{17,29},{21,17},{25,21},{29,25},{1... | collective-permute-start | bytes 182792 | tf_op jit(solution)/shard_map/ppermute | solution.py:60
  162.6 13.5 %copy-start.20 = (bf16[192,16]{1,0:T(8,128)(2,1)S(1)}, bf16[192,16]{1,0:T(8,128)(2,1)}, u32[]{:S(2)}) copy-start(bf16[192,16]{1,0:T(8,128)(2,1)} %get-tuple-element.47) | copy-start | bytes 18436
  162.6 13.5 %copy-start.21 = (bf16[192,16]{1,0:T(8,128)(2,1)S(1)}, bf16[192,16]{1,0:T(8,128)(2,1)}, u32[]{:S(2)}) copy-start(bf16[192,16]{1,0:T(8,128)(2,1)} %get-tuple-element.48) | copy-start | bytes 18436
  165.7 11.1 %collective-permute-start.16 = (bf16[8,640]{1,0:T(8,128)(2,1)S(1)}, bf16[8,640]{1,0:T(8,128)(2,1)S(1)}, u32[]{:S(2)}, u32[]{:S(2)}) collective-permute-start(bf16[8,640]{1,0:T(8,128)(2,1)S(1)} %get-tuple-element.34), channel_id=1, source_target_pairs={{16,20},{20,24},{24,28},{28,16},{17,21},{21,25},{25,29},{29,17},{1... | collective-permute-start | bytes 30728 | tf_op jit(solution)/shard_map/ppermute | solution.py:60
  168.3 8.5 %collective-permute-start.17 = (bf16[8,640]{1,0:T(8,128)(2,1)S(1)}, bf16[8,640]{1,0:T(8,128)(2,1)S(1)}, u32[]{:S(2)}, u32[]{:S(2)}) collective-permute-start(bf16[8,640]{1,0:T(8,128)(2,1)S(1)} %get-tuple-element.36), channel_id=1, source_target_pairs={{16,24},{20,28},{24,16},{28,20},{17,25},{21,29},{25,17},{29,21},{1... | collective-permute-start | bytes 30728 | tf_op jit(solution)/shard_map/ppermute | solution.py:60
  173.0 5.6 %collective-permute-start.18 = (bf16[8,640]{1,0:T(8,128)(2,1)S(1)}, bf16[8,640]{1,0:T(8,128)(2,1)S(1)}, u32[]{:S(2)}, u32[]{:S(2)}) collective-permute-start(bf16[8,640]{1,0:T(8,128)(2,1)S(1)} %get-tuple-element.35), channel_id=1, source_target_pairs={{16,28},{20,16},{24,20},{28,24},{17,29},{21,17},{25,21},{29,25},{1... | collective-permute-start | bytes 30728 | tf_op jit(solution)/shard_map/ppermute | solution.py:60
  (4 other events, 5.1 us)

commit v2 on v1

--- a/solution.py
+++ b/solution.py
@@ -1,6 +1,8 @@
 import jax
 import jax.numpy as jnp
 from jax import lax
+from jax.experimental import pallas as pl
+from jax.experimental.pallas import tpu as pltpu
 from jax.sharding import PartitionSpec as P
 
 NOPE_DIM = 128
@@ -162,7 +164,269 @@
     return (own_cache[None], own_ends[None])
 
 
+ROW_WIDTH = LATENT + ROPE_DIM
+HEAD_WIDTH = NOPE_DIM + ROPE_DIM
+SMEM = pl.BlockSpec(memory_space=pltpu.SMEM)
+VMEM = pl.BlockSpec(memory_space=pltpu.VMEM)
+
+
+def call(kernel, out_shape, args, scratch=(), flops=0):
+    many = isinstance(out_shape, list)
+    moved = sum(a.size * a.dtype.itemsize for a in args)
+    return pl.pallas_call(
+        kernel,
+        out_shape=out_shape,
+        in_specs=[SMEM] + [VMEM] * (len(args) - 1),
+        out_specs=[VMEM] * len(out_shape) if many else VMEM,
+        scratch_shapes=list(scratch),
+        compiler_params=pltpu.CompilerParams(vmem_limit_bytes=40 * 2**20),
+        cost_estimate=pl.CostEstimate(flops=flops, bytes_accessed=moved, transcendentals=0),
+    )(*args)
+
+
+def dot_t(a, b):
+    return lax.dot_general(a, b, (((1,), (1,)), ((), ())), preferred_element_type=F32)
+
+
+def unit(values):
+    return lax.rsqrt(jnp.mean(values * values, axis=-1, keepdims=True) + EPSILON)
+
+
+def turn(pair, cosine, sine):
+    half = pair.shape[1] // 2
+    a, b = pair[:, :half], pair[:, half:]
+    return jnp.concatenate([a * cosine - b * sine, a * sine + b * cosine], axis=1)
+
+
+def down_kernel(ids, own, one, two, three, w_down, w_latent, out):
+    tp = ids[1]
+    share = own.shape[1]
+    squares, down, latent = 0.0, 0.0, 0.0
+    for k, ref in enumerate((own, one, two, three)):
+        rows = pl.ds(pl.multiple_of((tp ^ k) * share, share), share)
+        piece = ref[...]
+        wide = piece.astype(F32)
+        squares = squares + jnp.sum(wide * wide, axis=1, keepdims=True)
+        down = down + dot(piece, w_down[rows, :])
+        latent = latent + dot(piece, w_latent[rows, :])
+    scale = lax.rsqrt(squares / (4 * share) + EPSILON)
+    out[...] = jnp.concatenate([down * scale, latent * scale], axis=1).astype(BF16)
+
+
+def attend_rows(compressed, cache, seen, cosine, sine, w_query, w_keys, w_values):
+    queries = dot(compressed, w_query[...])
+    plain, turned = cache[:, :LATENT], cache[:, LATENT:]
+    keys = dot(plain, w_keys[...]).astype(BF16)
+    values = dot(plain, w_values[...]).astype(BF16)
+    mixed = []
+    for head in range(queries.shape[1] // HEAD_WIDTH):
+        query = queries[:, head * HEAD_WIDTH : (head + 1) * HEAD_WIDTH]
+        query = jnp.concatenate(
+            [query[:, :NOPE_DIM], turn(query[:, NOPE_DIM:], cosine, sine)], axis=1
+        ).astype(BF16)
+        key = jnp.concatenate([keys[:, head * NOPE_DIM : (head + 1) * NOPE_DIM], turned], axis=1)
+        scores = dot_t(query, key) * HEAD_WIDTH**-0.5
+        powered = jnp.where(seen, jnp.exp(scores), 0.0)
+        attention = (powered / jnp.sum(powered, axis=1, keepdims=True)).astype(BF16)
+        mixed.append(dot(attention, values[:, head * VALUE_DIM : (head + 1) * VALUE_DIM]))
+    return jnp.concatenate(mixed, axis=1).astype(BF16)
+
+
+def layer_kernel(
+    ids, ends, own, one, two, three, share, cosine, sine, w_query, w_keys, w_values, w_out,
+    out0, out1, out2, out3, own_cache, stack, total, cached,
+):
+    tp = ids[1]
+    tokens, width = share.shape
+    block = tokens // 4
+    down_cols = w_query.shape[0] // 4
+    for k, ref in enumerate((own, one, two, three)):
+        stack[k] = ref[...]
+    pieces = [stack[tp ^ m].astype(F32) for m in range(4)]
+    down = jnp.concatenate([p[:, :down_cols] for p in pieces], axis=1)
+    latent = jnp.concatenate([p[:, down_cols:] for p in pieces], axis=1)
+    compressed = (down * unit(down)).astype(BF16)
+    plain = latent[:, :LATENT]
+    cache = jnp.concatenate(
+        [plain * unit(plain), turn(latent[:, LATENT:], cosine[...], sine[...])], axis=1
+    ).astype(BF16)
+    cached[...] = cache
+    own_cache[...] = cached[pl.ds(pl.multiple_of(tp * block, block), block), :]
+    seen = lax.broadcasted_iota(jnp.int32, (tokens, tokens), 0) >= lax.broadcasted_iota(
+        jnp.int32, (tokens, tokens), 1
+    )
+    mixed = attend_rows(
+        compressed, cache, seen, cosine[...], sine[...], w_query, w_keys, w_values
+    )
+    chosen = (
+        lax.broadcasted_iota(jnp.int32, (ends.shape[0], tokens), 1) == ends[...]
+    ).astype(BF16)
+    rows = jnp.concatenate([mixed, dot(chosen, mixed).astype(BF16)], axis=0)
+    total[...] = dot(rows, w_out[...])
+    mine = pl.ds(pl.multiple_of(tp * width, 128), width)
+    added = jnp.concatenate([share[...].astype(F32), dot(chosen, share[...])], axis=0)
+    total[:, mine] += added
+    last = total[tokens:, :]
+    for k, out in enumerate((out0, out1, out2, out3)):
+        part = total[pl.ds(pl.multiple_of((tp ^ k) * block, block), block), :]
+        out[...] = jnp.concatenate([part, last], axis=0).astype(BF16)
+
+
+def latent_kernel(
+    ids, one, two, three, four, cosine, sine, quarter0, quarter1, quarter2, quarter3, w_down,
+    out, own_ends, hidden,
+):
+    tp, rep = ids[1], ids[2]
+    block = cosine.shape[0]
+    width = own_ends.shape[1]
+    rows = one[...].astype(F32) + two[...].astype(F32) + three[...].astype(F32) + four[...].astype(F32)
+    narrow = rows.astype(BF16)
+    rows = narrow.astype(F32)
+    hidden[...] = rows
+    scale = unit(rows)
+    count = w_down.shape[1]
+    parts = []
+    for source in range(4):
+        total = 0.0
+        for step, quarter in enumerate((quarter0, quarter1, quarter2, quarter3)):
+            columns = pl.ds(pl.multiple_of((rep ^ step) * width, 128), width)
+            piece = hidden[0:block, columns].astype(BF16)
+            total = total + dot_t(piece, quarter[source])
+        parts.append(total)
+    latent = jnp.concatenate(parts, axis=1) * scale[:block]
+    plain = latent[:, :LATENT]
+    fresh = jnp.concatenate(
+        [plain * unit(plain), turn(latent[:, LATENT:], cosine[...], sine[...])], axis=1
+    )
+    down = dot(narrow[block:, :], w_down[...]) * scale[block:]
+    down = jnp.concatenate([down, jnp.zeros((down.shape[0], ROW_WIDTH - count), F32)], axis=1)
+    out[...] = jnp.concatenate([fresh, down], axis=0).astype(BF16)
+    mine = pl.ds(pl.multiple_of(tp * width, 128), width)
+    own_ends[...] = hidden[block:, mine].astype(BF16)
+
+
+def ends_kernel(
+    ids, ends, own, one, two, three, cosine, sine, w_query, w_keys, w_values, w_out,
+    out0, out1, out2, out3, stack, total,
+):
+    tp = ids[1]
+    count = ends.shape[0]
+    block = own.shape[0] - count
+    down_cols = w_query.shape[0] // 4
+    width = out0.shape[1]
+    for k, ref in enumerate((own, one, two, three)):
+        stack[k] = ref[...].astype(F32)
+    pieces = [stack[tp ^ m] for m in range(4)]
+    cache = jnp.concatenate([p[:block] for p in pieces], axis=0).astype(BF16)
+    down = jnp.concatenate([p[block:, :down_cols] for p in pieces], axis=1)
+    compressed = (down * unit(down)).astype(BF16)
+    seen = lax.broadcasted_iota(jnp.int32, (count, 4 * block), 1) <= ends[...]
+    mixed = attend_rows(
+        compressed, cache, seen, cosine[...], sine[...], w_query, w_keys, w_values
+    )
+    total[...] = dot(mixed, w_out[...])
+    for k, out in enumerate((out0, out1, out2, out3)):
+        columns = pl.ds(pl.multiple_of((tp ^ k) * width, 128), width)
+        out[...] = total[:, columns].astype(BF16)
+
+
+def local_two(prompt, block_sizes, w_query_down, w_query, w_latent, w_keys, w_values, w_out):
+    section, tp, rep = (lax.axis_index(a) for a in ("section", "tp", "rep"))
+    ids = jnp.stack([section, tp, rep]).astype(jnp.int32)
+    tokens, share = prompt.shape
+    block = tokens // 4
+    count = block_sizes.shape[0]
+    w_down, w_up, w_lat = w_query_down[0], w_query[0], w_latent[0]
+    w_key, w_value, w_final = w_keys[0], w_values[0], w_out[0]
+    down_cols, latent_cols = w_down.shape[1], w_lat.shape[1]
+    model = 4 * share
+    ends = (jnp.cumsum(block_sizes) - 1).astype(jnp.int32)[:, None]
+    frequency = 10000.0 ** (-2.0 * jnp.arange(ROPE_DIM // 2, dtype=F32) / ROPE_DIM)
+
+    def tables(positions):
+        angles = positions.astype(F32) * frequency[None, :]
+        return jnp.cos(angles), jnp.sin(angles)
+
+    cosine, sine = tables(jnp.arange(tokens)[:, None])
+    own_cosine, own_sine = tables(tp * block + jnp.arange(block)[:, None])
+    end_cosine, end_sine = tables(ends)
+
+    def within(array, k):
+        pairs = [(s * 4 + i, s * 4 + (i ^ k)) for s in range(2) for i in range(4)]
+        return lax.ppermute(array, ("section", "tp"), pairs)
+
+    def onward(array, k):
+        pairs = [(i, 4 + (i ^ k)) for i in range(4)] + [(4 + i, i) for i in range(4)]
+        return lax.ppermute(array, ("section", "tp"), pairs)
+
+    def over_rep(array, k):
+        return lax.ppermute(array, "rep", [(i, i ^ k) for i in range(4)])
+
+    quarter = lax.dynamic_slice_in_dim(w_lat, rep * share, share, 0).T
+    quarter = jnp.pad(quarter, ((0, tokens - latent_cols), (0, 0)))
+    sent = jnp.where(section == 0, prompt, quarter)
+    shares = [sent] + [within(sent, k) for k in (1, 2, 3)]
+    parts = call(
+        down_kernel,
+        jax.ShapeDtypeStruct((tokens, down_cols + latent_cols), BF16),
+        [ids, *shares, w_down, w_lat],
+        flops=2 * tokens * model * (down_cols + latent_cols),
+    )
+    pieces = [parts] + [within(parts, k) for k in (1, 2, 3)]
+
+    ordered = jnp.stack([p[:latent_cols] for p in shares])
+    ordered = jnp.stack([lax.dynamic_index_in_dim(ordered, tp ^ m, 0, False) for m in range(4)])
+    across = over_rep(ordered, 2)
+    both = jnp.stack([ordered, across])
+
+    message = jax.ShapeDtypeStruct((block + count, model), BF16)
+    *blocks, first_cache = call(
+        layer_kernel,
+        [message] * 4 + [jax.ShapeDtypeStruct((block, ROW_WIDTH), BF16)],
+        [ids, ends, *pieces, prompt, cosine, sine, w_up, w_key, w_value, w_final],
+        [
+            pltpu.VMEM((4, tokens, down_cols + latent_cols), BF16),
+            pltpu.VMEM((tokens + count, model), F32),
+            pltpu.VMEM((tokens, ROW_WIDTH), BF16),
+        ],
+        flops=2 * tokens * (w_up.size + w_key.size + w_value.size + w_final.size),
+    )
+    arrived = [onward(blocks[k], k) for k in (3, 2, 1, 0)]
+    near = over_rep(both, 1)
+    quarters = [both[0], near[0], both[1], near[1]]
+    fresh, ends_share = call(
+        latent_kernel,
+        [
+            jax.ShapeDtypeStruct((block + count, ROW_WIDTH), BF16),
+            jax.ShapeDtypeStruct((count, share), BF16),
+        ],
+        [ids, *arrived, own_cosine, own_sine, *quarters, w_down],
+        [pltpu.VMEM((block + count, model), F32)],
+        flops=2 * block * model * ROW_WIDTH,
+    )
+    pieces = [fresh] + [within(fresh, k) for k in (1, 2, 3)]
+    first_ends = onward(ends_share, 0)
+    outs = call(
+        ends_kernel,
+        [jax.ShapeDtypeStruct((count, share), BF16)] * 4,
+        [ids, ends, *pieces, end_cosine, end_sine, w_up, w_key, w_value, w_final],
+        [
+            pltpu.VMEM((4, block + count, ROW_WIDTH), F32),
+            pltpu.VMEM((count, model), F32),
+        ],
+        flops=2 * tokens * (w_key.size + w_value.size),
+    )
+    total = ends_share.astype(F32) + outs[0].astype(F32)
+    for k in (1, 2, 3):
+        total = total + within(outs[k], k).astype(F32)
+    own_ends = jnp.where(section == 0, first_ends, total.astype(BF16))
+    own_cache = jnp.where(section == 0, first_cache, fresh[:block])
+    return (own_cache[None], own_ends[None])
+
+
 def solution(mesh):
+    sizes = [mesh.shape[a] for a in ("section", "tp", "rep")]
+    body = local_two if sizes == [2, 4, 4] else local
     in_specs = (
         P("rep", "tp"),
         P("rep"),
@@ -174,4 +438,4 @@
         P("section", "tp", None),
     )
     out_specs = (P("section", ("rep", "tp"), None), P("section", "rep", "tp"))
-    return jax.shard_map(local, mesh=mesh, in_specs=in_specs, out_specs=out_specs, check_vma=False)
+    return jax.shard_map(body, mesh=mesh, in_specs=in_specs, out_specs=out_specs, check_vma=False)

time: 180 us -> 132 us (0.73)
  starting transfers between devices: 48.2 us -> 27.1 us
  matrix products: 15.5 us -> 0 us
  local copies, waits for them, and re-layouts: 26.9 us -> 12 us
  other arithmetic: 14.3 us -> 3.8 us
  Pallas kernels: 0 us -> 9.87 us
  waiting for transfers between devices: 72.9 us -> 77.8 us
    ppermute x20 -> x19, starting transfers between devices: 48.2 us -> 27.1 us  [the longest x12 17.8 us: within(): return lax.ppermute(array, ('section', 'tp'), pairs)]
    dot_general x17 -> x0, matrix products: 15.5 us -> none  [the longest x12 11.8 us: dot(): return jnp.dot(a, b, preferred_element_type=F32)]
    dynamic_update_slice x14 -> x0, local copies, waits for them, and re-layouts: 10.7 us -> none  [gather(): lax.dynamic_update_slice_in_dim(whole, piece, lax.rem(tp_id - k + tp_coun...]
    pallas_call x0 -> x4, Pallas kernels: none -> 9.87 us  [call(): pl.pallas_call(kernel, out_shape=out_shape, in_specs=[SMEM] + [VMEM] * (l...]
    unnamed x67 -> x40, local copies, waits for them, and re-layouts: 2.78 us -> 9.36 us
    ppermute x20 -> x19, waiting for transfers between devices: 72.9 us -> 77.8 us  [the longest x12 37.8 us: within(): return lax.ppermute(array, ('section', 'tp'), pairs)]
    reduce_sum x7 -> x0, other arithmetic: 3.85 us -> none  [rms_rows(): jnp.mean(values * values, axis=-1, keepdims=True) + EPSILON]
    another operation x4, local copies, waits for them, and re-layouts: 3.12 us -> 0.06 us  [local_two(): ordered = jnp.stack([p[:latent_cols] for p in shares])]
  transfers between devices with their start and end apart: 20 -> 19, of which waited for: 6 -> 12; matrix products, arithmetic and copies ran while one was open for 29% -> 4% of each run, Pallas kernels for 0% -> 6%
where the time goes in v2:
time: 132 us
  waiting for transfers between devices  77.8 us (59%)
  starting transfers between devices  27.1 us (21%)
  local copies, waits for them, and re-layouts  12 us (9%)
  Pallas kernels  9.87 us (7%)
  other arithmetic  3.8 us (3%)
    ppermute x12, waiting for transfers between devices, within(): return lax.ppermute(array, ('section', 'tp'), pairs)  37.8 us
    ppermute x5, waiting for transfers between devices, onward(): return lax.ppermute(array, ('section', 'tp'), pairs)  25.6 us
    ppermute x12, starting transfers between devices, within(): return lax.ppermute(array, ('section', 'tp'), pairs)  17.8 us
    ppermute x2, waiting for transfers between devices, over_rep(): return lax.ppermute(array, 'rep', [(i, i ^ k) for i in range(4)])  14.3 us
    pallas_call x4, Pallas kernels, call(): pl.pallas_call(kernel, out_shape=out_shape, in_specs=[SMEM] + [VMEM] * (l...  9.87 us
    unnamed x40, local copies, waits for them, and re-layouts  9.36 us
    ppermute x5, starting transfers between devices, onward(): return lax.ppermute(array, ('section', 'tp'), pairs)  7.76 us
  transfers between devices with their start and end apart: 19, of which 12 were waited for; matrix products, arithmetic and copies ran while one was open for 4% of the time, Pallas kernels for 6%

profile of v2, /device:TPU:4, one launch (start us, length us, event | category | flops | bytes accessed | tf_op | source)
XLA Modules:
  0.0 131.5 jit_solution(13986332320480981514)
XLA Ops:
  0.6 0.9 dynamic-slice_bitcast_fusion
  1.7 3.7 %collective-permute-start.2 = (bf16[192,640]{1,0:T(8,128)(2,1)S(1)}, bf16[192,640]{1,0:T(8,128)(2,1)S(1)}, u32[]{:S(2)}, u32[]{:S(2)}) collective-permute-start(bf16[192,640]{1,0:T(8,128)(2,1)S(1)} %pad_select_fusion.own), channel_id=1, source_target_pairs={{0,12},{4,8},{8,4},{12,0},{16,28},{20,24},{24,20},{28,16},{1,13},{... | collective-permute-start | bytes 737288 | tf_op jit(solution)/shard_map/ppermute | solution.py:356
  5.3 0.8 collective-permute-start
  6.2 6.3 %collective-permute-done.2.three = bf16[192,640]{1,0:T(8,128)(2,1)S(1)} collective-permute-done((bf16[192,640]{1,0:T(8,128)(2,1)S(1)}, bf16[192,640]{1,0:T(8,128)(2,1)S(1)}, u32[]{:S(2)}, u32[]{:S(2)}) %collective-permute-start.2) | collective-permute-done | bytes 245792 | tf_op jit(solution)/shard_map/ppermute | solution.py:356
  12.5 13.8 %collective-permute-done.1.two = bf16[192,640]{1,0:T(8,128)(2,1)S(1)} collective-permute-done((bf16[192,640]{1,0:T(8,128)(2,1)S(1)}, bf16[192,640]{1,0:T(8,128)(2,1)S(1)}, u32[]{:S(2)}, u32[]{:S(2)}) %collective-permute-start.1) | collective-permute-done | bytes 245792 | tf_op jit(solution)/shard_map/ppermute | solution.py:356
  26.5 0.4 copy-done.13
  27.0 0.1 fusion.2
  27.2 1.6 %collective-permute-start.10 = (bf16[4,136,640]{2,1,0:T(8,128)(2,1)S(1)}, bf16[4,136,640]{2,1,0:T(8,128)(2,1)S(1)}, u32[]{:S(2)}, u32[]{:S(2)}) collective-permute-start(bf16[4,136,640]{2,1,0:T(8,128)(2,1)S(1)} %get-tuple-element.27.quarter0), channel_id=1, source_target_pairs={{0,2},{1,3},{2,0},{3,1},{4,6},{5,7},{6,4},{7,5},{8,10},{9,11},{10,... | collective-permute-start | bytes 2088968 | tf_op jit(solution)/shard_map/ppermute | solution.py:363
  28.7 0.9 copy-done.2
  29.6 14.3 %collective-permute-done.10.quarter2 = bf16[4,136,640]{2,1,0:T(8,128)(2,1)S(1)} collective-permute-done((bf16[4,136,640]{2,1,0:T(8,128)(2,1)S(1)}, bf16[4,136,640]{2,1,0:T(8,128)(2,1)S(1)}, u32[]{:S(2)}, u32[]{:S(2)}) %collective-permute-start.10) | collective-permute-done | bytes 696352 | tf_op jit(solution)/shard_map/ppermute | solution.py:363
  43.9 1.3 pad_maximum_fusion
  45.2 0.6 copy.18
  45.8 1.5 %copy.17 = bf16[1,2560,192]{2,1,0:T(8,128)(2,1)S(1)} copy(bf16[1,2560,192]{1,2,0:T(8,128)(2,1)} %param.10) | data formatting | bytes 1966080 | tf_op args[2]
  47.6 0.2 multiply_sine_fusion.1
  47.7 0.4 multiply_sine_fusion
  48.2 0.9 copy-done.9
  49.1 0.9 copy-done.12
  50.1 0.9 copy-done.14
  51.0 0.9 copy-done.16
  52.0 1.4 %shard_map.95.own = bf16[192,328]{1,0:T(8,128)(2,1)S(1)} custom-call(s32[3]{0:T(128)S(1)} %pad_add_fusion.ids, bf16[192,640]{1,0:T(8,128)(2,1)S(1)} %copy-done.9, bf16[192,640]{1,0:T(8,128)(2,1)S(1)} %copy-done.16, bf16[192,640]{1,0:T(8,128)(2,1)S(1)} %copy-done.14, bf16[192,640]{1,0:T(8,128)(2,1)S(1)} %copy-done.12, bf16[2560,192]{1,0:T(8,128)(2,1)S(1)} %bitcast.33, ...), custom_call_target="tpu_custom_call" | custom-call | flops 322437120 | bytes 2662412 | tf_op jit(solution)/shard_map/pallas_call | solution.py:176
  53.5 2.8 %collective-permute-start.4 = (bf16[192,328]{1,0:T(8,128)(2,1)S(1)}, bf16[192,328]{1,0:T(8,128)(2,1)S(1)}, u32[]{:S(2)}, u32[]{:S(2)}) collective-permute-start(bf16[192,328]{1,0:T(8,128)(2,1)S(1)} %shard_map.95.own), channel_id=1, source_target_pairs={{0,8},{4,12},{8,0},{12,4},{16,24},{20,28},{24,16},{28,20},{1,9},{5... | collective-permute-start | bytes 377864 | tf_op jit(solution)/shard_map/ppermute | solution.py:356
  56.3 1.5 %collective-permute-start.5 = (bf16[192,328]{1,0:T(8,128)(2,1)S(1)}, bf16[192,328]{1,0:T(8,128)(2,1)S(1)}, u32[]{:S(2)}, u32[]{:S(2)}) collective-permute-start(bf16[192,328]{1,0:T(8,128)(2,1)S(1)} %shard_map.95.own), channel_id=1, source_target_pairs={{0,12},{4,8},{8,4},{12,0},{16,28},{20,24},{24,20},{28,16},{1,13},{... | collective-permute-start | bytes 377864 | tf_op jit(solution)/shard_map/ppermute | solution.py:356
  57.8 4.6 %collective-permute-done.3.one = bf16[192,328]{1,0:T(8,128)(2,1)S(1)} collective-permute-done((bf16[192,328]{1,0:T(8,128)(2,1)S(1)}, bf16[192,328]{1,0:T(8,128)(2,1)S(1)}, u32[]{:S(2)}, u32[]{:S(2)}) %collective-permute-start.3) | collective-permute-done | bytes 125984 | tf_op jit(solution)/shard_map/ppermute | solution.py:356
  62.5 4.9 %collective-permute-done.4.two = bf16[192,328]{1,0:T(8,128)(2,1)S(1)} collective-permute-done((bf16[192,328]{1,0:T(8,128)(2,1)S(1)}, bf16[192,328]{1,0:T(8,128)(2,1)S(1)}, u32[]{:S(2)}, u32[]{:S(2)}) %collective-permute-start.4) | collective-permute-done | bytes 125984 | tf_op jit(solution)/shard_map/ppermute | solution.py:356
  67.5 1.0 copy-done.4
  68.5 1.0 copy-done.6
  69.5 3.6 %shard_map.96 = (bf16[56,2560]{1,0:T(8,128)(2,1)S(1)}, bf16[56,2560]{1,0:T(8,128)(2,1)S(1)}, bf16[56,2560]{1,0:T(8,128)(2,1)S(1)}, bf16[56,2560]{1,0:T(8,128)(2,1)S(1)}, bf16[48,544]{1,0:T(8,128)(2,1)S(1)}) custom-call(s32[3]{0:T(128)S(1)} %pad_add_fusion.ids, s32[8,1]{1,0:T(8,128)S(1)} %broadcast_add_fusion.ends, bf16[192,328]{1,0:T(8,128)(2,1)S(1)} %shard_map.95.own, ...), custom_call_target="tpu_custom_call" | custom-call | flops 893386752 | bytes 5427244 | tf_op jit(solution)/shard_map/pallas_call | solution.py:176
  73.1 1.5 %collective-permute-start.6 = (bf16[56,2560]{1,0:T(8,128)(2,1)S(1)}, bf16[56,2560]{1,0:T(8,128)(2,1)S(1)}, u32[]{:S(2)}, u32[]{:S(2)}) collective-permute-start(bf16[56,2560]{1,0:T(8,128)(2,1)S(1)} %get-tuple-element.14), channel_id=1, source_target_pairs={{0,28},{4,24},{8,20},{12,16},{16,0},{20,4},{24,8},{28,12},{1,29},{... | collective-permute-start | bytes 860168 | tf_op jit(solution)/shard_map/ppermute | solution.py:360
  74.6 2.3 %collective-permute-start.7 = (bf16[56,2560]{1,0:T(8,128)(2,1)S(1)}, bf16[56,2560]{1,0:T(8,128)(2,1)S(1)}, u32[]{:S(2)}, u32[]{:S(2)}) collective-permute-start(bf16[56,2560]{1,0:T(8,128)(2,1)S(1)} %get-tuple-element.15), channel_id=1, source_target_pairs={{0,24},{4,28},{8,16},{12,20},{16,0},{20,4},{24,8},{28,12},{1,25},{... | collective-permute-start | bytes 860168 | tf_op jit(solution)/shard_map/ppermute | solution.py:360
  76.9 3.3 %collective-permute-start.8 = (bf16[56,2560]{1,0:T(8,128)(2,1)S(1)}, bf16[56,2560]{1,0:T(8,128)(2,1)S(1)}, u32[]{:S(2)}, u32[]{:S(2)}) collective-permute-start(bf16[56,2560]{1,0:T(8,128)(2,1)S(1)} %get-tuple-element.16), channel_id=1, source_target_pairs={{0,20},{4,16},{8,28},{12,24},{16,0},{20,4},{24,8},{28,12},{1,21},{... | collective-permute-start | bytes 860168 | tf_op jit(solution)/shard_map/ppermute | solution.py:360
  80.3 0.6 collective-permute-start.9
  81.0 1.5 %slice_bitcast_fusion = (bf16[4,136,640]{2,1,0:T(8,128)(2,1)S(1)}, bf16[4,136,640]{2,1,0:T(8,128)(2,1)S(1)}) fusion(bf16[2,4,136,640]{3,2,1,0:T(8,128)(2,1)} %collective-permute-done.11), kind=kLoop, calls=%fused_computation.1 | loop fusion | bytes 2785280 | tf_op jit(solution)/shard_map/squeeze | solution.py:396
  82.5 3.4 %collective-permute-done.6.one = bf16[56,2560]{1,0:T(8,128)(2,1)S(1)} collective-permute-done((bf16[56,2560]{1,0:T(8,128)(2,1)S(1)}, bf16[56,2560]{1,0:T(8,128)(2,1)S(1)}, u32[]{:S(2)}, u32[]{:S(2)}) %collective-permute-start.6) | collective-permute-done | bytes 286752 | tf_op jit(solution)/shard_map/ppermute | solution.py:360
  85.8 22.3 %collective-permute-done.7.two = bf16[56,2560]{1,0:T(8,128)(2,1)S(1)} collective-permute-done((bf16[56,2560]{1,0:T(8,128)(2,1)S(1)}, bf16[56,2560]{1,0:T(8,128)(2,1)S(1)}, u32[]{:S(2)}, u32[]{:S(2)}) %collective-permute-start.7) | collective-permute-done | bytes 286752 | tf_op jit(solution)/shard_map/ppermute | solution.py:360
  108.1 2.5 %shard_map.97 = (bf16[56,544]{1,0:T(8,128)(2,1)S(1)}, bf16[8,640]{1,0:T(8,128)(2,1)S(1)}) custom-call(s32[3]{0:T(128)S(1)} %pad_add_fusion.ids, bf16[56,2560]{1,0:T(8,128)(2,1)S(1)} %collective-permute-done.6.one, bf16[56,2560]{1,0:T(8,128)(2,1)S(1)} %collective-permute-done.7.two, bf16[56,2560]{1,0:T(8,128)(2,1)S(1)} %collective-permute-done.8.three, ...), custom_call_target="tpu_custom_call" | custom-call | flops 133693440 | bytes 4921356 | tf_op jit(solution)/shard_map/pallas_call | solution.py:176
  110.7 3.3 %collective-permute-start.14 = (bf16[56,544]{1,0:T(8,128)(2,1)S(1)}, bf16[56,544]{1,0:T(8,128)(2,1)S(1)}, u32[]{:S(2)}, u32[]{:S(2)}) collective-permute-start(bf16[56,544]{1,0:T(8,128)(2,1)S(1)} %get-tuple-element.18.own), channel_id=1, source_target_pairs={{0,8},{4,12},{8,0},{12,4},{16,24},{20,28},{24,16},{28,20},{1,9},{5... | collective-permute-start | bytes 182792 | tf_op jit(solution)/shard_map/ppermute | solution.py:356
  114.0 1.0 collective-permute-start.15
  115.3 0.7 collective-permute-done.13.one
  115.9 3.2 %collective-permute-done.14.two = bf16[56,544]{1,0:T(8,128)(2,1)S(1)} collective-permute-done((bf16[56,544]{1,0:T(8,128)(2,1)S(1)}, bf16[56,544]{1,0:T(8,128)(2,1)S(1)}, u32[]{:S(2)}, u32[]{:S(2)}) %collective-permute-start.14) | collective-permute-done | bytes 60960 | tf_op jit(solution)/shard_map/ppermute | solution.py:356
  119.1 1.1 collective-permute-done.15.three
  120.3 2.4 %shard_map.98 = (bf16[8,640]{1,0:T(8,128)(2,1)S(1)}, bf16[8,640]{1,0:T(8,128)(2,1)S(1)}, bf16[8,640]{1,0:T(8,128)(2,1)S(1)}, bf16[8,640]{1,0:T(8,128)(2,1)S(1)}) custom-call(s32[3]{0:T(128)S(1)} %pad_add_fusion.ids, s32[8,1]{1,0:T(8,128)S(1)} %broadcast_add_fusion.ends, bf16[56,544]{1,0:T(8,128)(2,1)S(1)} %get-tuple-element.18.own, ...), custom_call_target="tpu_custom_call" | custom-call | flops 201326592 | bytes 4897836 | tf_op jit(solution)/shard_map/pallas_call | solution.py:176
  122.7 1.2 collective-permute-start.16
  123.9 1.6 %collective-permute-start.17 = (bf16[8,640]{1,0:T(8,128)(2,1)S(1)}, bf16[8,640]{1,0:T(8,128)(2,1)S(1)}, u32[]{:S(2)}, u32[]{:S(2)}) collective-permute-start(bf16[8,640]{1,0:T(8,128)(2,1)S(1)} %get-tuple-element.22), channel_id=1, source_target_pairs={{0,8},{4,12},{8,0},{12,4},{16,24},{20,28},{24,16},{28,20},{1,9},{5... | collective-permute-start | bytes 30728 | tf_op jit(solution)/shard_map/ppermute | solution.py:356
  125.4 1.6 %collective-permute-start.18 = (bf16[8,640]{1,0:T(8,128)(2,1)S(1)}, bf16[8,640]{1,0:T(8,128)(2,1)S(1)}, u32[]{:S(2)}, u32[]{:S(2)}) collective-permute-start(bf16[8,640]{1,0:T(8,128)(2,1)S(1)} %get-tuple-element.23), channel_id=1, source_target_pairs={{0,12},{4,8},{8,4},{12,0},{16,28},{20,24},{24,20},{28,16},{1,13},{... | collective-permute-start | bytes 30728 | tf_op jit(solution)/shard_map/ppermute | solution.py:356
  127.1 0.6 select_bitcast_fusion
  127.7 0.7 collective-permute-done.17
  128.4 2.5 %collective-permute-done.18 = bf16[8,640]{1,0:T(8,128)(2,1)S(1)} collective-permute-done((bf16[8,640]{1,0:T(8,128)(2,1)S(1)}, bf16[8,640]{1,0:T(8,128)(2,1)S(1)}, u32[]{:S(2)}, u32[]{:S(2)}) %collective-permute-start.18) | collective-permute-done | bytes 10272 | tf_op jit(solution)/shard_map/ppermute | solution.py:356
  130.9 0.6 fusion.1
  (58 shorter events, 1.2 us)
Async XLA Ops:
  1.7 24.8 %copy-start.8 = (bf16[192,640]{1,0:T(8,128)(2,1)}, bf16[192,640]{1,0:T(8,128)(2,1)S(1)}, u32[]{:S(2)}) copy-start(bf16[192,640]{1,0:T(8,128)(2,1)S(1)} %pad_select_fusion.own) | copy-start | bytes 737284
  1.7 10.8 %collective-permute-start.2 = (bf16[192,640]{1,0:T(8,128)(2,1)S(1)}, bf16[192,640]{1,0:T(8,128)(2,1)S(1)}, u32[]{:S(2)}, u32[]{:S(2)}) collective-permute-start(bf16[192,640]{1,0:T(8,128)(2,1)S(1)} %pad_select_fusion.own), channel_id=1, source_target_pairs={{0,12},{4,8},{8,4},{12,0},{16,28},{20,24},{24,20},{28,16},{1,13},{... | collective-permute-start | bytes 737288 | tf_op jit(solution)/shard_map/ppermute | solution.py:356
  5.3 20.9 %collective-permute-start.1 = (bf16[192,640]{1,0:T(8,128)(2,1)S(1)}, bf16[192,640]{1,0:T(8,128)(2,1)S(1)}, u32[]{:S(2)}, u32[]{:S(2)}) collective-permute-start(bf16[192,640]{1,0:T(8,128)(2,1)S(1)} %pad_select_fusion.own), channel_id=1, source_target_pairs={{0,8},{4,12},{8,0},{12,4},{16,24},{20,28},{24,16},{28,20},{1,9},{5... | collective-permute-start | bytes 737288 | tf_op jit(solution)/shard_map/ppermute | solution.py:356
  5.3 20.9 %collective-permute-start = (bf16[192,640]{1,0:T(8,128)(2,1)S(1)}, bf16[192,640]{1,0:T(8,128)(2,1)S(1)}, u32[]{:S(2)}, u32[]{:S(2)}) collective-permute-start(bf16[192,640]{1,0:T(8,128)(2,1)S(1)} %pad_select_fusion.own), channel_id=1, source_target_pairs={{0,4},{4,0},{8,12},{12,8},{16,20},{20,16},{24,28},{28,24},{1,5},{5... | collective-permute-start | bytes 737288 | tf_op jit(solution)/shard_map/ppermute | solution.py:356
  12.5 14.1 %copy-start.11 = (bf16[192,640]{1,0:T(8,128)(2,1)}, bf16[192,640]{1,0:T(8,128)(2,1)S(1)}, u32[]{:S(2)}) copy-start(bf16[192,640]{1,0:T(8,128)(2,1)S(1)} %collective-permute-done.2.three) | copy-start | bytes 737284
  26.2 0.7 copy-start.13
  26.3 0.8 copy-start.15
  27.2 16.7 %collective-permute-start.10 = (bf16[4,136,640]{2,1,0:T(8,128)(2,1)S(1)}, bf16[4,136,640]{2,1,0:T(8,128)(2,1)S(1)}, u32[]{:S(2)}, u32[]{:S(2)}) collective-permute-start(bf16[4,136,640]{2,1,0:T(8,128)(2,1)S(1)} %get-tuple-element.27.quarter0), channel_id=1, source_target_pairs={{0,2},{1,3},{2,0},{3,1},{4,6},{5,7},{6,4},{7,5},{8,10},{9,11},{10,... | collective-permute-start | bytes 2088968 | tf_op jit(solution)/shard_map/ppermute | solution.py:363
  28.7 0.9 copy-start.2
  43.9 1.3 copy-start.17
  45.2 35.7 %collective-permute-start.11 = (bf16[2,4,136,640]{3,2,1,0:T(8,128)(2,1)}, bf16[2,4,136,640]{3,2,1,0:T(8,128)(2,1)}, u32[]{:S(2)}, u32[]{:S(2)}) collective-permute-start(bf16[2,4,136,640]{3,2,1,0:T(8,128)(2,1)} %pad_maximum_fusion), channel_id=1, source_target_pairs={{0,1},{1,0},{2,3},{3,2},{4,5},{5,4},{6,7},{7,6},{8,9},{9,8},{10,11... | collective-permute-start | bytes 4177928 | tf_op jit(solution)/shard_map/ppermute | solution.py:363
  45.8 1.6 %copy-start.18 = (s32[8]{0:T(128)S(1)}, s32[8]{0:T(128)}, u32[]{:S(2)}) copy-start(s32[8]{0:T(128)} %param.9) | copy-start | bytes 100
  47.6 19.9 %copy-start.10 = (bf16[192,640]{1,0:T(8,128)(2,1)S(1)}, bf16[192,640]{1,0:T(8,128)(2,1)}, u32[]{:S(2)}) copy-start(bf16[192,640]{1,0:T(8,128)(2,1)} %share.1) | copy-start | bytes 737284
  48.2 0.9 copy-start.9
  49.1 0.9 copy-start.12
  50.1 0.9 copy-start.14
  51.0 0.9 copy-start.16
  51.9 15.5 %copy-start = (bf16[1,512,2560]{2,1,0:T(8,128)(2,1)S(1)}, bf16[1,512,2560]{2,1,0:T(8,128)(2,1)}, u32[]{:S(2)}) copy-start(bf16[1,512,2560]{2,1,0:T(8,128)(2,1)} %param.15) | copy-start | bytes 7864324
  51.9 15.5 %copy-start.1 = (bf16[1,768,640]{2,1,0:T(8,128)(2,1)S(1)}, bf16[1,768,640]{2,1,0:T(8,128)(2,1)}, u32[]{:S(2)}) copy-start(bf16[1,768,640]{2,1,0:T(8,128)(2,1)} %param.11) | copy-start | bytes 2949124
  53.4 9.1 %collective-permute-start.3 = (bf16[192,328]{1,0:T(8,128)(2,1)S(1)}, bf16[192,328]{1,0:T(8,128)(2,1)S(1)}, u32[]{:S(2)}, u32[]{:S(2)}) collective-permute-start(bf16[192,328]{1,0:T(8,128)(2,1)S(1)} %shard_map.95.own), channel_id=1, source_target_pairs={{0,4},{4,0},{8,12},{12,8},{16,20},{20,16},{24,28},{28,24},{1,5},{5... | collective-permute-start | bytes 377864 | tf_op jit(solution)/shard_map/ppermute | solution.py:356
  53.5 14.0 %collective-permute-start.4 = (bf16[192,328]{1,0:T(8,128)(2,1)S(1)}, bf16[192,328]{1,0:T(8,128)(2,1)S(1)}, u32[]{:S(2)}, u32[]{:S(2)}) collective-permute-start(bf16[192,328]{1,0:T(8,128)(2,1)S(1)} %shard_map.95.own), channel_id=1, source_target_pairs={{0,8},{4,12},{8,0},{12,4},{16,24},{20,28},{24,16},{28,20},{1,9},{5... | collective-permute-start | bytes 377864 | tf_op jit(solution)/shard_map/ppermute | solution.py:356
  56.3 11.1 %collective-permute-start.5 = (bf16[192,328]{1,0:T(8,128)(2,1)S(1)}, bf16[192,328]{1,0:T(8,128)(2,1)S(1)}, u32[]{:S(2)}, u32[]{:S(2)}) collective-permute-start(bf16[192,328]{1,0:T(8,128)(2,1)S(1)} %shard_map.95.own), channel_id=1, source_target_pairs={{0,12},{4,8},{8,4},{12,0},{16,28},{20,24},{24,20},{28,16},{1,13},{... | collective-permute-start | bytes 377864 | tf_op jit(solution)/shard_map/ppermute | solution.py:356
  67.4 1.0 copy-start.4
  68.5 1.0 copy-start.6
  73.1 12.7 %collective-permute-start.6 = (bf16[56,2560]{1,0:T(8,128)(2,1)S(1)}, bf16[56,2560]{1,0:T(8,128)(2,1)S(1)}, u32[]{:S(2)}, u32[]{:S(2)}) collective-permute-start(bf16[56,2560]{1,0:T(8,128)(2,1)S(1)} %get-tuple-element.14), channel_id=1, source_target_pairs={{0,28},{4,24},{8,20},{12,16},{16,0},{20,4},{24,8},{28,12},{1,29},{... | collective-permute-start | bytes 860168 | tf_op jit(solution)/shard_map/ppermute | solution.py:360
  74.6 33.5 %collective-permute-start.7 = (bf16[56,2560]{1,0:T(8,128)(2,1)S(1)}, bf16[56,2560]{1,0:T(8,128)(2,1)S(1)}, u32[]{:S(2)}, u32[]{:S(2)}) collective-permute-start(bf16[56,2560]{1,0:T(8,128)(2,1)S(1)} %get-tuple-element.15), channel_id=1, source_target_pairs={{0,24},{4,28},{8,16},{12,20},{16,0},{20,4},{24,8},{28,12},{1,25},{... | collective-permute-start | bytes 860168 | tf_op jit(solution)/shard_map/ppermute | solution.py:360
  76.9 31.2 %collective-permute-start.8 = (bf16[56,2560]{1,0:T(8,128)(2,1)S(1)}, bf16[56,2560]{1,0:T(8,128)(2,1)S(1)}, u32[]{:S(2)}, u32[]{:S(2)}) collective-permute-start(bf16[56,2560]{1,0:T(8,128)(2,1)S(1)} %get-tuple-element.16), channel_id=1, source_target_pairs={{0,20},{4,16},{8,28},{12,24},{16,0},{20,4},{24,8},{28,12},{1,21},{... | collective-permute-start | bytes 860168 | tf_op jit(solution)/shard_map/ppermute | solution.py:360
  80.3 27.8 %collective-permute-start.9 = (bf16[56,2560]{1,0:T(8,128)(2,1)S(1)}, bf16[56,2560]{1,0:T(8,128)(2,1)S(1)}, u32[]{:S(2)}, u32[]{:S(2)}) collective-permute-start(bf16[56,2560]{1,0:T(8,128)(2,1)S(1)} %get-tuple-element.17), channel_id=1, source_target_pairs={{0,16},{4,20},{8,24},{12,28},{16,0},{20,4},{24,8},{28,12},{1,17},{... | collective-permute-start | bytes 860168 | tf_op jit(solution)/shard_map/ppermute | solution.py:360
  80.9 27.2 %copy-start.3 = (bf16[4,136,640]{2,1,0:T(8,128)(2,1)S(1)}, bf16[4,136,640]{2,1,0:T(8,128)(2,1)}, u32[]{:S(2)}) copy-start(bf16[4,136,640]{2,1,0:T(8,128)(2,1)} %copy-done.2) | copy-start | bytes 2088964
  108.1 12.2 %copy-start.5 = (bf16[1,512,512]{2,1,0:T(8,128)(2,1)S(1)}, bf16[1,512,512]{2,1,0:T(8,128)(2,1)}, u32[]{:S(2)}) copy-start(bf16[1,512,512]{2,1,0:T(8,128)(2,1)} %param.13) | copy-start | bytes 1572868
  108.1 12.1 %copy-start.7 = (bf16[1,512,512]{2,1,0:T(8,128)(2,1)S(1)}, bf16[1,512,512]{2,1,0:T(8,128)(2,1)}, u32[]{:S(2)}) copy-start(bf16[1,512,512]{2,1,0:T(8,128)(2,1)} %param.14) | copy-start | bytes 1572868
  110.6 5.3 %collective-permute-start.13 = (bf16[56,544]{1,0:T(8,128)(2,1)S(1)}, bf16[56,544]{1,0:T(8,128)(2,1)S(1)}, u32[]{:S(2)}, u32[]{:S(2)}) collective-permute-start(bf16[56,544]{1,0:T(8,128)(2,1)S(1)} %get-tuple-element.18.own), channel_id=1, source_target_pairs={{0,4},{4,0},{8,12},{12,8},{16,20},{20,16},{24,28},{28,24},{1,5},{5... | collective-permute-start | bytes 182792 | tf_op jit(solution)/shard_map/ppermute | solution.py:356
  110.7 8.5 %collective-permute-start.14 = (bf16[56,544]{1,0:T(8,128)(2,1)S(1)}, bf16[56,544]{1,0:T(8,128)(2,1)S(1)}, u32[]{:S(2)}, u32[]{:S(2)}) collective-permute-start(bf16[56,544]{1,0:T(8,128)(2,1)S(1)} %get-tuple-element.18.own), channel_id=1, source_target_pairs={{0,8},{4,12},{8,0},{12,4},{16,24},{20,28},{24,16},{28,20},{1,9},{5... | collective-permute-start | bytes 182792 | tf_op jit(solution)/shard_map/ppermute | solution.py:356
  114.0 6.2 %collective-permute-start.15 = (bf16[56,544]{1,0:T(8,128)(2,1)S(1)}, bf16[56,544]{1,0:T(8,128)(2,1)S(1)}, u32[]{:S(2)}, u32[]{:S(2)}) collective-permute-start(bf16[56,544]{1,0:T(8,128)(2,1)S(1)} %get-tuple-element.18.own), channel_id=1, source_target_pairs={{0,12},{4,8},{8,4},{12,0},{16,28},{20,24},{24,20},{28,16},{1,13},{... | collective-permute-start | bytes 182792 | tf_op jit(solution)/shard_map/ppermute | solution.py:356
  115.2 12.6 %collective-permute-start.12 = (bf16[8,640]{1,0:T(8,128)(2,1)S(1)}, bf16[8,640]{1,0:T(8,128)(2,1)S(1)}, u32[]{:S(2)}, u32[]{:S(2)}) collective-permute-start(bf16[8,640]{1,0:T(8,128)(2,1)S(1)} %get-tuple-element.19), channel_id=1, source_target_pairs={{0,16},{4,20},{8,24},{12,28},{16,0},{20,4},{24,8},{28,12},{1,17},{... | collective-permute-start | bytes 30728 | tf_op jit(solution)/shard_map/ppermute | solution.py:360
  122.7 5.1 %collective-permute-start.16 = (bf16[8,640]{1,0:T(8,128)(2,1)S(1)}, bf16[8,640]{1,0:T(8,128)(2,1)S(1)}, u32[]{:S(2)}, u32[]{:S(2)}) collective-permute-start(bf16[8,640]{1,0:T(8,128)(2,1)S(1)} %get-tuple-element.21), channel_id=1, source_target_pairs={{0,4},{4,0},{8,12},{12,8},{16,20},{20,16},{24,28},{28,24},{1,5},{5... | collective-permute-start | bytes 30728 | tf_op jit(solution)/shard_map/ppermute | solution.py:356
  123.9 4.6 %collective-permute-start.17 = (bf16[8,640]{1,0:T(8,128)(2,1)S(1)}, bf16[8,640]{1,0:T(8,128)(2,1)S(1)}, u32[]{:S(2)}, u32[]{:S(2)}) collective-permute-start(bf16[8,640]{1,0:T(8,128)(2,1)S(1)} %get-tuple-element.22), channel_id=1, source_target_pairs={{0,8},{4,12},{8,0},{12,4},{16,24},{20,28},{24,16},{28,20},{1,9},{5... | collective-permute-start | bytes 30728 | tf_op jit(solution)/shard_map/ppermute | solution.py:356
  125.4 5.5 %collective-permute-start.18 = (bf16[8,640]{1,0:T(8,128)(2,1)S(1)}, bf16[8,640]{1,0:T(8,128)(2,1)S(1)}, u32[]{:S(2)}, u32[]{:S(2)}) collective-permute-start(bf16[8,640]{1,0:T(8,128)(2,1)S(1)} %get-tuple-element.23), channel_id=1, source_target_pairs={{0,12},{4,8},{8,4},{12,0},{16,28},{20,24},{24,20},{28,16},{1,13},{... | collective-permute-start | bytes 30728 | tf_op jit(solution)/shard_map/ppermute | solution.py:356

commit v3 on v2

--- a/solution.py
+++ b/solution.py
@@ -1,5 +1,6 @@
 import jax
 import jax.numpy as jnp
+import numpy as np
 from jax import lax
 from jax.experimental import pallas as pl
 from jax.experimental.pallas import tpu as pltpu
@@ -166,20 +167,21 @@
 
 ROW_WIDTH = LATENT + ROPE_DIM
 HEAD_WIDTH = NOPE_DIM + ROPE_DIM
+HALF = ROPE_DIM // 2
 SMEM = pl.BlockSpec(memory_space=pltpu.SMEM)
 VMEM = pl.BlockSpec(memory_space=pltpu.VMEM)
 
 
-def call(kernel, out_shape, args, scratch=(), flops=0):
+def call(kernel, out_shape, args, scratch=(), flops=0, scalars=0):
     many = isinstance(out_shape, list)
     moved = sum(a.size * a.dtype.itemsize for a in args)
     return pl.pallas_call(
         kernel,
         out_shape=out_shape,
-        in_specs=[SMEM] + [VMEM] * (len(args) - 1),
+        in_specs=[SMEM] * scalars + [VMEM] * (len(args) - scalars),
         out_specs=[VMEM] * len(out_shape) if many else VMEM,
         scratch_shapes=list(scratch),
-        compiler_params=pltpu.CompilerParams(vmem_limit_bytes=40 * 2**20),
+        compiler_params=pltpu.CompilerParams(vmem_limit_bytes=20 * 2**20),
         cost_estimate=pl.CostEstimate(flops=flops, bytes_accessed=moved, transcendentals=0),
     )(*args)
 
@@ -192,28 +194,61 @@
     return lax.rsqrt(jnp.mean(values * values, axis=-1, keepdims=True) + EPSILON)
 
 
-def turn(pair, cosine, sine):
-    half = pair.shape[1] // 2
-    a, b = pair[:, :half], pair[:, half:]
+def turn(pair, angles):
+    cosine, sine = angles[:, :HALF], angles[:, HALF:]
+    a, b = pair[:, :HALF], pair[:, HALF:]
     return jnp.concatenate([a * cosine - b * sine, a * sine + b * cosine], axis=1)
 
 
-def down_kernel(ids, own, one, two, three, w_down, w_latent, out):
-    tp = ids[1]
+def end_rows(sizes):
+    ends = [sizes[0] - 1]
+    for i in range(1, sizes.shape[0]):
+        ends.append(ends[-1] + sizes[i])
+    return ends
+
+
+def column(scalars):
+    rows = lax.broadcasted_iota(jnp.int32, (len(scalars), 1), 0)
+    out = jnp.zeros((len(scalars), 1), jnp.int32)
+    for i, value in enumerate(scalars):
+        out = jnp.where(rows == i, value, out)
+    return out
+
+
+def send_kernel(prompt, w_latent, out):
+    section, rep = lax.axis_index("section"), lax.axis_index("rep")
+    rows, width = prompt.shape
+    latent_cols = w_latent.shape[0]
+
+    @pl.when(section == 0)
+    def _():
+        out[...] = prompt[...]
+
+    @pl.when(section != 0)
+    def _():
+        quarter = w_latent[:, pl.ds(pl.multiple_of(rep * width, 128), width)]
+        rest = jnp.zeros((rows - latent_cols, width), BF16)
+        out[...] = jnp.concatenate([quarter, rest], axis=0)
+
+
+def down_kernel(own, one, two, three, w_down, w_latent, out, weights):
+    tp = lax.axis_index("tp")
     share = own.shape[1]
+    latent_cols = w_latent.shape[0]
     squares, down, latent = 0.0, 0.0, 0.0
     for k, ref in enumerate((own, one, two, three)):
-        rows = pl.ds(pl.multiple_of((tp ^ k) * share, share), share)
+        columns = pl.ds(pl.multiple_of((tp ^ k) * share, 128), share)
         piece = ref[...]
         wide = piece.astype(F32)
         squares = squares + jnp.sum(wide * wide, axis=1, keepdims=True)
-        down = down + dot(piece, w_down[rows, :])
-        latent = latent + dot(piece, w_latent[rows, :])
+        down = down + dot_t(piece, w_down[:, columns])
+        latent = latent + dot_t(piece, w_latent[:, columns])
+        weights[tp ^ k] = piece[:latent_cols]
     scale = lax.rsqrt(squares / (4 * share) + EPSILON)
     out[...] = jnp.concatenate([down * scale, latent * scale], axis=1).astype(BF16)
 
 
-def attend_rows(compressed, cache, seen, cosine, sine, w_query, w_keys, w_values):
+def attend_rows(compressed, cache, seen, angles, w_query, w_keys, w_values):
     queries = dot(compressed, w_query[...])
     plain, turned = cache[:, :LATENT], cache[:, LATENT:]
     keys = dot(plain, w_keys[...]).astype(BF16)
@@ -222,7 +257,7 @@
     for head in range(queries.shape[1] // HEAD_WIDTH):
         query = queries[:, head * HEAD_WIDTH : (head + 1) * HEAD_WIDTH]
         query = jnp.concatenate(
-            [query[:, :NOPE_DIM], turn(query[:, NOPE_DIM:], cosine, sine)], axis=1
+            [query[:, :NOPE_DIM], turn(query[:, NOPE_DIM:], angles)], axis=1
         ).astype(BF16)
         key = jnp.concatenate([keys[:, head * NOPE_DIM : (head + 1) * NOPE_DIM], turned], axis=1)
         scores = dot_t(query, key) * HEAD_WIDTH**-0.5
@@ -233,34 +268,32 @@
 
 
 def layer_kernel(
-    ids, ends, own, one, two, three, share, cosine, sine, w_query, w_keys, w_values, w_out,
+    sizes, own, one, two, three, share, angles, w_query, w_keys, w_values, w_out,
     out0, out1, out2, out3, own_cache, stack, total, cached,
 ):
-    tp = ids[1]
+    tp = lax.axis_index("tp")
     tokens, width = share.shape
     block = tokens // 4
     down_cols = w_query.shape[0] // 4
+    ends = column(end_rows(sizes))
     for k, ref in enumerate((own, one, two, three)):
-        stack[k] = ref[...]
-    pieces = [stack[tp ^ m].astype(F32) for m in range(4)]
+        stack[tp ^ k] = ref[...]
+    pieces = [stack[m].astype(F32) for m in range(4)]
     down = jnp.concatenate([p[:, :down_cols] for p in pieces], axis=1)
     latent = jnp.concatenate([p[:, down_cols:] for p in pieces], axis=1)
     compressed = (down * unit(down)).astype(BF16)
     plain = latent[:, :LATENT]
     cache = jnp.concatenate(
-        [plain * unit(plain), turn(latent[:, LATENT:], cosine[...], sine[...])], axis=1
+        [plain * unit(plain), turn(latent[:, LATENT:], angles[...])], axis=1
     ).astype(BF16)
     cached[...] = cache
     own_cache[...] = cached[pl.ds(pl.multiple_of(tp * block, block), block), :]
     seen = lax.broadcasted_iota(jnp.int32, (tokens, tokens), 0) >= lax.broadcasted_iota(
         jnp.int32, (tokens, tokens), 1
     )
-    mixed = attend_rows(
-        compressed, cache, seen, cosine[...], sine[...], w_query, w_keys, w_values
-    )
-    chosen = (
-        lax.broadcasted_iota(jnp.int32, (ends.shape[0], tokens), 1) == ends[...]
-    ).astype(BF16)
+    mixed = attend_rows(compressed, cache, seen, angles[...], w_query, w_keys, w_values)
+    chosen = lax.broadcasted_iota(jnp.int32, (ends.shape[0], tokens), 1) == ends
+    chosen = chosen.astype(BF16)
     rows = jnp.concatenate([mixed, dot(chosen, mixed).astype(BF16)], axis=0)
     total[...] = dot(rows, w_out[...])
     mine = pl.ds(pl.multiple_of(tp * width, 128), width)
@@ -273,32 +306,30 @@
 
 
 def latent_kernel(
-    ids, one, two, three, four, cosine, sine, quarter0, quarter1, quarter2, quarter3, w_down,
+    one, two, three, four, angles, quarter, near, far, w_down,
     out, own_ends, hidden,
 ):
-    tp, rep = ids[1], ids[2]
-    block = cosine.shape[0]
+    tp, rep = lax.axis_index("tp"), lax.axis_index("rep")
+    block = angles.shape[0] // 4
     width = own_ends.shape[1]
     rows = one[...].astype(F32) + two[...].astype(F32) + three[...].astype(F32) + four[...].astype(F32)
     narrow = rows.astype(BF16)
     rows = narrow.astype(F32)
     hidden[...] = rows
     scale = unit(rows)
-    count = w_down.shape[1]
-    parts = []
-    for source in range(4):
-        total = 0.0
-        for step, quarter in enumerate((quarter0, quarter1, quarter2, quarter3)):
-            columns = pl.ds(pl.multiple_of((rep ^ step) * width, 128), width)
-            piece = hidden[0:block, columns].astype(BF16)
-            total = total + dot_t(piece, quarter[source])
-        parts.append(total)
-    latent = jnp.concatenate(parts, axis=1) * scale[:block]
+    count = w_down.shape[0]
+    totals = [0.0] * 4
+    for step, weights in enumerate((quarter, near, far.at[0], far.at[1])):
+        columns = pl.ds(pl.multiple_of((rep ^ step) * width, 128), width)
+        piece = hidden[0:block, columns].astype(BF16)
+        totals = [total + dot_t(piece, weights[m]) for m, total in enumerate(totals)]
+    latent = jnp.concatenate(totals, axis=1) * scale[:block]
     plain = latent[:, :LATENT]
+    own_angles = angles[pl.ds(pl.multiple_of(tp * block, block), block), :]
     fresh = jnp.concatenate(
-        [plain * unit(plain), turn(latent[:, LATENT:], cosine[...], sine[...])], axis=1
-    )
-    down = dot(narrow[block:, :], w_down[...]) * scale[block:]
+        [plain * unit(plain), turn(latent[:, LATENT:], own_angles)], axis=1
+    )
+    down = dot_t(narrow[block:, :], w_down[...]) * scale[block:]
     down = jnp.concatenate([down, jnp.zeros((down.shape[0], ROW_WIDTH - count), F32)], axis=1)
     out[...] = jnp.concatenate([fresh, down], axis=0).astype(BF16)
     mine = pl.ds(pl.multiple_of(tp * width, 128), width)
@@ -306,24 +337,24 @@
 
 
 def ends_kernel(
-    ids, ends, own, one, two, three, cosine, sine, w_query, w_keys, w_values, w_out,
+    sizes, own, one, two, three, angles, w_query, w_keys, w_values, w_out,
     out0, out1, out2, out3, stack, total,
 ):
-    tp = ids[1]
-    count = ends.shape[0]
+    tp = lax.axis_index("tp")
+    ends = end_rows(sizes)
+    count = len(ends)
     block = own.shape[0] - count
     down_cols = w_query.shape[0] // 4
     width = out0.shape[1]
     for k, ref in enumerate((own, one, two, three)):
-        stack[k] = ref[...].astype(F32)
-    pieces = [stack[tp ^ m] for m in range(4)]
+        stack[tp ^ k] = ref[...].astype(F32)
+    pieces = [stack[m] for m in range(4)]
     cache = jnp.concatenate([p[:block] for p in pieces], axis=0).astype(BF16)
     down = jnp.concatenate([p[block:, :down_cols] for p in pieces], axis=1)
     compressed = (down * unit(down)).astype(BF16)
-    seen = lax.broadcasted_iota(jnp.int32, (count, 4 * block), 1) <= ends[...]
-    mixed = attend_rows(
-        compressed, cache, seen, cosine[...], sine[...], w_query, w_keys, w_values
-    )
+    end_angles = jnp.concatenate([angles[pl.ds(e, 1), :] for e in ends], axis=0)
+    seen = lax.broadcasted_iota(jnp.int32, (count, 4 * block), 1) <= column(ends)
+    mixed = attend_rows(compressed, cache, seen, end_angles, w_query, w_keys, w_values)
     total[...] = dot(mixed, w_out[...])
     for k, out in enumerate((out0, out1, out2, out3)):
         columns = pl.ds(pl.multiple_of((tp ^ k) * width, 128), width)
@@ -331,25 +362,17 @@
 
 
 def local_two(prompt, block_sizes, w_query_down, w_query, w_latent, w_keys, w_values, w_out):
-    section, tp, rep = (lax.axis_index(a) for a in ("section", "tp", "rep"))
-    ids = jnp.stack([section, tp, rep]).astype(jnp.int32)
+    section = lax.axis_index("section")
     tokens, share = prompt.shape
     block = tokens // 4
     count = block_sizes.shape[0]
-    w_down, w_up, w_lat = w_query_down[0], w_query[0], w_latent[0]
+    w_down, w_up, w_lat = w_query_down[0].T, w_query[0], w_latent[0].T
     w_key, w_value, w_final = w_keys[0], w_values[0], w_out[0]
-    down_cols, latent_cols = w_down.shape[1], w_lat.shape[1]
+    down_cols, latent_cols = w_down.shape[0], w_lat.shape[0]
     model = 4 * share
-    ends = (jnp.cumsum(block_sizes) - 1).astype(jnp.int32)[:, None]
-    frequency = 10000.0 ** (-2.0 * jnp.arange(ROPE_DIM // 2, dtype=F32) / ROPE_DIM)
-
-    def tables(positions):
-        angles = positions.astype(F32) * frequency[None, :]
-        return jnp.cos(angles), jnp.sin(angles)
-
-    cosine, sine = tables(jnp.arange(tokens)[:, None])
-    own_cosine, own_sine = tables(tp * block + jnp.arange(block)[:, None])
-    end_cosine, end_sine = tables(ends)
+    frequency = 10000.0 ** (-2.0 * np.arange(HALF, dtype=np.float32) / ROPE_DIM)
+    angles = np.arange(tokens, dtype=np.float32)[:, None] * frequency.astype(np.float32)[None, :]
+    angles = jnp.asarray(np.concatenate([np.cos(angles), np.sin(angles)], axis=1), F32)
 
     def within(array, k):
         pairs = [(s * 4 + i, s * 4 + (i ^ k)) for s in range(2) for i in range(4)]
@@ -362,45 +385,42 @@
     def over_rep(array, k):
         return lax.ppermute(array, "rep", [(i, i ^ k) for i in range(4)])
 
-    quarter = lax.dynamic_slice_in_dim(w_lat, rep * share, share, 0).T
-    quarter = jnp.pad(quarter, ((0, tokens - latent_cols), (0, 0)))
-    sent = jnp.where(section == 0, prompt, quarter)
+    sent = call(send_kernel, jax.ShapeDtypeStruct((tokens, share), BF16), [prompt, w_lat])
     shares = [sent] + [within(sent, k) for k in (1, 2, 3)]
-    parts = call(
+    parts, quarter = call(
         down_kernel,
-        jax.ShapeDtypeStruct((tokens, down_cols + latent_cols), BF16),
-        [ids, *shares, w_down, w_lat],
+        [
+            jax.ShapeDtypeStruct((tokens, down_cols + latent_cols), BF16),
+            jax.ShapeDtypeStruct((4, latent_cols, share), BF16),
+        ],
+        [*shares, w_down, w_lat],
         flops=2 * tokens * model * (down_cols + latent_cols),
     )
     pieces = [parts] + [within(parts, k) for k in (1, 2, 3)]
-
-    ordered = jnp.stack([p[:latent_cols] for p in shares])
-    ordered = jnp.stack([lax.dynamic_index_in_dim(ordered, tp ^ m, 0, False) for m in range(4)])
-    across = over_rep(ordered, 2)
-    both = jnp.stack([ordered, across])
+    near = over_rep(quarter, 1)
+    quarters = [quarter, near, over_rep(jnp.stack([quarter, near]), 2)]
 
     message = jax.ShapeDtypeStruct((block + count, model), BF16)
     *blocks, first_cache = call(
         layer_kernel,
         [message] * 4 + [jax.ShapeDtypeStruct((block, ROW_WIDTH), BF16)],
-        [ids, ends, *pieces, prompt, cosine, sine, w_up, w_key, w_value, w_final],
+        [block_sizes, *pieces, prompt, angles, w_up, w_key, w_value, w_final],
         [
             pltpu.VMEM((4, tokens, down_cols + latent_cols), BF16),
             pltpu.VMEM((tokens + count, model), F32),
             pltpu.VMEM((tokens, ROW_WIDTH), BF16),
         ],
         flops=2 * tokens * (w_up.size + w_key.size + w_value.size + w_final.size),
-    )
-    arrived = [onward(blocks[k], k) for k in (3, 2, 1, 0)]
-    near = over_rep(both, 1)
-    quarters = [both[0], near[0], both[1], near[1]]
+        scalars=1,
+    )
+    arrived = [onward(blocks[k], k) for k in (0, 3, 2, 1)]
     fresh, ends_share = call(
         latent_kernel,
         [
             jax.ShapeDtypeStruct((block + count, ROW_WIDTH), BF16),
             jax.ShapeDtypeStruct((count, share), BF16),
         ],
-        [ids, *arrived, own_cosine, own_sine, *quarters, w_down],
+        [*arrived, angles, *quarters, w_down],
         [pltpu.VMEM((block + count, model), F32)],
         flops=2 * block * model * ROW_WIDTH,
     )
@@ -409,12 +429,13 @@
     outs = call(
         ends_kernel,
         [jax.ShapeDtypeStruct((count, share), BF16)] * 4,
-        [ids, ends, *pieces, end_cosine, end_sine, w_up, w_key, w_value, w_final],
+        [block_sizes, *pieces, angles, w_up, w_key, w_value, w_final],
         [
             pltpu.VMEM((4, block + count, ROW_WIDTH), F32),
             pltpu.VMEM((count, model), F32),
         ],
         flops=2 * tokens * (w_key.size + w_value.size),
+        scalars=1,
     )
     total = ends_share.astype(F32) + outs[0].astype(F32)
     for k in (1, 2, 3):

time: 132 us -> 109 us (0.83)
  waiting for transfers between devices: 77.8 us -> 63.9 us
  local copies, waits for them, and re-layouts: 12 us -> 5.51 us
  other arithmetic: 3.8 us -> 1.4 us
  starting transfers between devices: 27.1 us -> 28.7 us
  Pallas kernels: 9.87 us -> 8.46 us
    ppermute x2, waiting for transfers between devices: 14.3 us -> 2.15 us  [over_rep(): return lax.ppermute(array, 'rep', [(i, i ^ k) for i in range(4)])]
    unnamed x40 -> x30, local copies, waits for them, and re-layouts: 9.36 us -> 5.51 us
    ppermute x12, waiting for transfers between devices: 37.8 us -> 34.9 us  [within(): return lax.ppermute(array, ('section', 'tp'), pairs)]
    ppermute x12, starting transfers between devices: 17.8 us -> 20.2 us  [within(): return lax.ppermute(array, ('section', 'tp'), pairs)]
    squeeze x1 -> x0, local copies, waits for them, and re-layouts: 1.5 us -> none  [local_two(): quarters = [both[0], near[0], both[1], near[1]]]
    another operation x5 -> x1, other arithmetic: 1.64 us -> 0.15 us  [local_two(): quarters = [quarter, near, over_rep(jnp.stack([quarter, near]), 2)]]
    pallas_call x4 -> x5, Pallas kernels: 9.87 us -> 8.46 us  [call(): pl.pallas_call(kernel, out_shape=out_shape, in_specs=[SMEM] * scalars + [...]
  transfers between devices with their start and end apart: 19 -> 19, of which waited for: 12 -> 11; matrix products, arithmetic and copies ran while one was open for 4% -> 1% of each run, Pallas kernels for 6% -> 5%
where the time goes in v3:
time: 109 us
  waiting for transfers between devices  63.9 us (59%)
  starting transfers between devices  28.7 us (26%)
  Pallas kernels  8.46 us (8%)
  local copies, waits for them, and re-layouts  5.51 us (5%)
  other arithmetic  1.4 us (1%)
    ppermute x12, waiting for transfers between devices, within(): return lax.ppermute(array, ('section', 'tp'), pairs)  34.9 us
    ppermute x5, waiting for transfers between devices, onward(): return lax.ppermute(array, ('section', 'tp'), pairs)  26.8 us
    ppermute x12, starting transfers between devices, within(): return lax.ppermute(array, ('section', 'tp'), pairs)  20.2 us
    pallas_call x5, Pallas kernels, call(): pl.pallas_call(kernel, out_shape=out_shape, in_specs=[SMEM] * scalars + [...  8.46 us
    ppermute x5, starting transfers between devices, onward(): return lax.ppermute(array, ('section', 'tp'), pairs)  6.82 us
    unnamed x30, local copies, waits for them, and re-layouts  5.51 us
  transfers between devices with their start and end apart: 19, of which 11 were waited for; matrix products, arithmetic and copies ran while one was open for 1% of the time, Pallas kernels for 5%

profile of v3, /device:TPU:4, one launch (start us, length us, event | category | flops | bytes accessed | tf_op | source)
XLA Modules:
  0.0 108.7 jit_solution(1513160386380485145)
XLA Ops:
  0.6 0.0 copy-start.4
  0.7 1.2 %copy-done.4 = bf16[1,2560,136]{1,2,0:T(8,128)(2,1)S(1)} copy-done((bf16[1,2560,136]{1,2,0:T(8,128)(2,1)S(1)}, bf16[1,2560,136]{1,2,0:T(8,128)(2,1)}, u32[]{:S(2)}) %copy-start.4) | copy-done | bytes 696344
  1.8 0.9 copy-done.9
  2.8 1.6 %collective-permute-start = (bf16[192,640]{1,0:T(8,128)(2,1)S(1)}, bf16[192,640]{1,0:T(8,128)(2,1)S(1)}, u32[]{:S(2)}, u32[]{:S(2)}) collective-permute-start(bf16[192,640]{1,0:T(8,128)(2,1)S(1)} %shard_map.104.own), channel_id=1, source_target_pairs={{0,4},{4,0},{8,12},{12,8},{16,20},{20,16},{24,28},{28,24},{1,5},{5... | collective-permute-start | bytes 737288 | tf_op jit(solution)/shard_map/ppermute | solution.py:379
  4.4 2.6 %collective-permute-start.1 = (bf16[192,640]{1,0:T(8,128)(2,1)S(1)}, bf16[192,640]{1,0:T(8,128)(2,1)S(1)}, u32[]{:S(2)}, u32[]{:S(2)}) collective-permute-start(bf16[192,640]{1,0:T(8,128)(2,1)S(1)} %shard_map.104.own), channel_id=1, source_target_pairs={{0,8},{4,12},{8,0},{12,4},{16,24},{20,28},{24,16},{28,20},{1,9},{5... | collective-permute-start | bytes 737288 | tf_op jit(solution)/shard_map/ppermute | solution.py:379
  7.0 0.2 collective-permute-start.2
  7.3 7.8 %collective-permute-done.one = bf16[192,640]{1,0:T(8,128)(2,1)S(1)} collective-permute-done((bf16[192,640]{1,0:T(8,128)(2,1)S(1)}, bf16[192,640]{1,0:T(8,128)(2,1)S(1)}, u32[]{:S(2)}, u32[]{:S(2)}) %collective-permute-start) | collective-permute-done | bytes 245792 | tf_op jit(solution)/shard_map/ppermute | solution.py:379
  15.1 9.7 %collective-permute-done.1.two = bf16[192,640]{1,0:T(8,128)(2,1)S(1)} collective-permute-done((bf16[192,640]{1,0:T(8,128)(2,1)S(1)}, bf16[192,640]{1,0:T(8,128)(2,1)S(1)}, u32[]{:S(2)}, u32[]{:S(2)}) %collective-permute-start.1) | collective-permute-done | bytes 245792 | tf_op jit(solution)/shard_map/ppermute | solution.py:379
  24.8 0.0 collective-permute-done.2.three
  24.8 1.1 %copy-done.5 = bf16[1,2560,136]{1,2,0:T(8,128)(2,1)S(1)} copy-done((bf16[1,2560,136]{1,2,0:T(8,128)(2,1)S(1)}, bf16[1,2560,136]{1,2,0:T(8,128)(2,1)}, u32[]{:S(2)}) %copy-start.5) | copy-done | bytes 696344
  25.9 0.9 shard_map.105
  26.8 0.1 collective-permute-start.10
  26.8 2.1 %collective-permute-done.10.near = bf16[4,136,640]{2,1,0:T(8,128)(2,1)S(1)} collective-permute-done((bf16[4,136,640]{2,1,0:T(8,128)(2,1)S(1)}, bf16[4,136,640]{2,1,0:T(8,128)(2,1)S(1)}, u32[]{:S(2)}, u32[]{:S(2)}) %collective-permute-start.10) | collective-permute-done | bytes 696352 | tf_op jit(solution)/shard_map/ppermute | solution.py:386
  29.0 0.1 pad_maximum_fusion
  29.1 1.6 %collective-permute-start.11 = (bf16[2,4,136,640]{3,2,1,0:T(8,128)(2,1)S(1)}, bf16[2,4,136,640]{3,2,1,0:T(8,128)(2,1)S(1)}, u32[]{:S(2)}, u32[]{:S(2)}) collective-permute-start(bf16[2,4,136,640]{3,2,1,0:T(8,128)(2,1)S(1)} %pad_maximum_fusion), channel_id=1, source_target_pairs={{0,2},{1,3},{2,0},{3,1},{4,6},{5,7},{6,4},{7,5},{8,10},{9,11},{10,... | collective-permute-start | bytes 4177928 | tf_op jit(solution)/shard_map/ppermute | solution.py:386
  30.7 4.4 %collective-permute-start.3 = (bf16[192,328]{1,0:T(8,128)(2,1)S(1)}, bf16[192,328]{1,0:T(8,128)(2,1)S(1)}, u32[]{:S(2)}, u32[]{:S(2)}) collective-permute-start(bf16[192,328]{1,0:T(8,128)(2,1)S(1)} %get-tuple-element.15.own), channel_id=1, source_target_pairs={{0,4},{4,0},{8,12},{12,8},{16,20},{20,16},{24,28},{28,24},{1,5},{5... | collective-permute-start | bytes 377864 | tf_op jit(solution)/shard_map/ppermute | solution.py:379
  35.1 1.0 collective-permute-start.4
  36.1 1.5 %collective-permute-start.5 = (bf16[192,328]{1,0:T(8,128)(2,1)S(1)}, bf16[192,328]{1,0:T(8,128)(2,1)S(1)}, u32[]{:S(2)}, u32[]{:S(2)}) collective-permute-start(bf16[192,328]{1,0:T(8,128)(2,1)S(1)} %get-tuple-element.15.own), channel_id=1, source_target_pairs={{0,12},{4,8},{8,4},{12,0},{16,28},{20,24},{24,20},{28,16},{1,13},{... | collective-permute-start | bytes 377864 | tf_op jit(solution)/shard_map/ppermute | solution.py:379
  37.6 3.4 %collective-permute-done.3.one = bf16[192,328]{1,0:T(8,128)(2,1)S(1)} collective-permute-done((bf16[192,328]{1,0:T(8,128)(2,1)S(1)}, bf16[192,328]{1,0:T(8,128)(2,1)S(1)}, u32[]{:S(2)}, u32[]{:S(2)}) %collective-permute-start.3) | collective-permute-done | bytes 125984 | tf_op jit(solution)/shard_map/ppermute | solution.py:379
  41.0 8.1 %collective-permute-done.4.two = bf16[192,328]{1,0:T(8,128)(2,1)S(1)} collective-permute-done((bf16[192,328]{1,0:T(8,128)(2,1)S(1)}, bf16[192,328]{1,0:T(8,128)(2,1)S(1)}, u32[]{:S(2)}, u32[]{:S(2)}) %collective-permute-start.4) | collective-permute-done | bytes 125984 | tf_op jit(solution)/shard_map/ppermute | solution.py:379
  49.1 0.0 collective-permute-done.5.three
  49.2 3.4 %shard_map.106 = (bf16[56,2560]{1,0:T(8,128)(2,1)S(1)}, bf16[56,2560]{1,0:T(8,128)(2,1)S(1)}, bf16[56,2560]{1,0:T(8,128)(2,1)S(1)}, bf16[56,2560]{1,0:T(8,128)(2,1)S(1)}, bf16[48,544]{1,0:T(8,128)(2,1)S(1)}) custom-call(s32[8]{0:T(128)S(1)} %copy-done.14, bf16[192,328]{1,0:T(8,128)(2,1)S(1)} %get-tuple-element.15.own, ...), custom_call_target="tpu_custom_call" | custom-call | flops 893386752 | bytes 5427232 | tf_op jit(solution)/shard_map/pallas_call | solution.py:178
  52.6 0.0 copy-start.12
  52.6 0.6 collective-permute-start.6
  53.2 1.5 %collective-permute-start.7 = (bf16[56,2560]{1,0:T(8,128)(2,1)S(1)}, bf16[56,2560]{1,0:T(8,128)(2,1)S(1)}, u32[]{:S(2)}, u32[]{:S(2)}) collective-permute-start(bf16[56,2560]{1,0:T(8,128)(2,1)S(1)} %get-tuple-element.18), channel_id=1, source_target_pairs={{0,28},{4,24},{8,20},{12,16},{16,0},{20,4},{24,8},{28,12},{1,29},{... | collective-permute-start | bytes 860168 | tf_op jit(solution)/shard_map/ppermute | solution.py:383
  54.7 2.1 %collective-permute-start.8 = (bf16[56,2560]{1,0:T(8,128)(2,1)S(1)}, bf16[56,2560]{1,0:T(8,128)(2,1)S(1)}, u32[]{:S(2)}, u32[]{:S(2)}) collective-permute-start(bf16[56,2560]{1,0:T(8,128)(2,1)S(1)} %get-tuple-element.19), channel_id=1, source_target_pairs={{0,24},{4,28},{8,16},{12,20},{16,0},{20,4},{24,8},{28,12},{1,25},{... | collective-permute-start | bytes 860168 | tf_op jit(solution)/shard_map/ppermute | solution.py:383
  56.8 2.6 %collective-permute-start.9 = (bf16[56,2560]{1,0:T(8,128)(2,1)S(1)}, bf16[56,2560]{1,0:T(8,128)(2,1)S(1)}, u32[]{:S(2)}, u32[]{:S(2)}) collective-permute-start(bf16[56,2560]{1,0:T(8,128)(2,1)S(1)} %get-tuple-element.20), channel_id=1, source_target_pairs={{0,20},{4,16},{8,28},{12,24},{16,0},{20,4},{24,8},{28,12},{1,21},{... | collective-permute-start | bytes 860168 | tf_op jit(solution)/shard_map/ppermute | solution.py:383
  59.4 11.7 %collective-permute-done.6.one = bf16[56,2560]{1,0:T(8,128)(2,1)S(1)} collective-permute-done((bf16[56,2560]{1,0:T(8,128)(2,1)S(1)}, bf16[56,2560]{1,0:T(8,128)(2,1)S(1)}, u32[]{:S(2)}, u32[]{:S(2)}) %collective-permute-start.6) | collective-permute-done | bytes 286752 | tf_op jit(solution)/shard_map/ppermute | solution.py:383
  71.1 15.1 %collective-permute-done.8.three = bf16[56,2560]{1,0:T(8,128)(2,1)S(1)} collective-permute-done((bf16[56,2560]{1,0:T(8,128)(2,1)S(1)}, bf16[56,2560]{1,0:T(8,128)(2,1)S(1)}, u32[]{:S(2)}, u32[]{:S(2)}) %collective-permute-start.8) | collective-permute-done | bytes 286752 | tf_op jit(solution)/shard_map/ppermute | solution.py:383
  86.2 1.7 %shard_map.107 = (bf16[56,544]{1,0:T(8,128)(2,1)S(1)}, bf16[8,640]{1,0:T(8,128)(2,1)S(1)}) custom-call(bf16[56,2560]{1,0:T(8,128)(2,1)S(1)} %collective-permute-done.6.one, bf16[56,2560]{1,0:T(8,128)(2,1)S(1)} %collective-permute-done.7.two, bf16[56,2560]{1,0:T(8,128)(2,1)S(1)} %collective-permute-done.8.three, ...), custom_call_target="tpu_custom_call" | custom-call | flops 133693440 | bytes 4939776 | tf_op jit(solution)/shard_map/pallas_call | solution.py:178
  88.0 0.1 collective-permute-start.13
  88.1 2.5 %collective-permute-start.14 = (bf16[56,544]{1,0:T(8,128)(2,1)S(1)}, bf16[56,544]{1,0:T(8,128)(2,1)S(1)}, u32[]{:S(2)}, u32[]{:S(2)}) collective-permute-start(bf16[56,544]{1,0:T(8,128)(2,1)S(1)} %get-tuple-element.22.own), channel_id=1, source_target_pairs={{0,8},{4,12},{8,0},{12,4},{16,24},{20,28},{24,16},{28,20},{1,9},{5... | collective-permute-start | bytes 182792 | tf_op jit(solution)/shard_map/ppermute | solution.py:379
  90.6 1.9 %collective-permute-start.15 = (bf16[56,544]{1,0:T(8,128)(2,1)S(1)}, bf16[56,544]{1,0:T(8,128)(2,1)S(1)}, u32[]{:S(2)}, u32[]{:S(2)}) collective-permute-start(bf16[56,544]{1,0:T(8,128)(2,1)S(1)} %get-tuple-element.22.own), channel_id=1, source_target_pairs={{0,12},{4,8},{8,4},{12,0},{16,28},{20,24},{24,20},{28,16},{1,13},{... | collective-permute-start | bytes 182792 | tf_op jit(solution)/shard_map/ppermute | solution.py:379
  92.5 0.0 collective-permute-start.12
  92.5 0.5 collective-permute-done.13.one
  93.0 3.8 %collective-permute-done.14.two = bf16[56,544]{1,0:T(8,128)(2,1)S(1)} collective-permute-done((bf16[56,544]{1,0:T(8,128)(2,1)S(1)}, bf16[56,544]{1,0:T(8,128)(2,1)S(1)}, u32[]{:S(2)}, u32[]{:S(2)}) %collective-permute-start.14) | collective-permute-done | bytes 60960 | tf_op jit(solution)/shard_map/ppermute | solution.py:379
  96.8 1.2 %copy-done.3 = bf16[1,768,640]{2,1,0:T(8,128)(2,1)S(1)} copy-done((bf16[1,768,640]{2,1,0:T(8,128)(2,1)S(1)}, bf16[1,768,640]{2,1,0:T(8,128)(2,1)}, u32[]{:S(2)}) %copy-start.3) | copy-done | bytes 983064
  98.0 1.0 copy-done.8
  99.1 2.4 %shard_map.108 = (bf16[8,640]{1,0:T(8,128)(2,1)S(1)}, bf16[8,640]{1,0:T(8,128)(2,1)S(1)}, bf16[8,640]{1,0:T(8,128)(2,1)S(1)}, bf16[8,640]{1,0:T(8,128)(2,1)S(1)}) custom-call(s32[8]{0:T(128)S(1)} %copy-done.14, bf16[56,544]{1,0:T(8,128)(2,1)S(1)} %get-tuple-element.22.own, bf16[56,544]{1,0:T(8,128)(2,1)S(1)} %collective-permute-done.13.one, ...), custom_call_target="tpu_custom_call" | custom-call | flops 201326592 | bytes 4921376 | tf_op jit(solution)/shard_map/pallas_call | solution.py:178
  101.5 2.0 %collective-permute-start.18 = (bf16[8,640]{1,0:T(8,128)(2,1)S(1)}, bf16[8,640]{1,0:T(8,128)(2,1)S(1)}, u32[]{:S(2)}, u32[]{:S(2)}) collective-permute-start(bf16[8,640]{1,0:T(8,128)(2,1)S(1)} %get-tuple-element.27), channel_id=1, source_target_pairs={{0,12},{4,8},{8,4},{12,0},{16,28},{20,24},{24,20},{28,16},{1,13},{... | collective-permute-start | bytes 30728 | tf_op jit(solution)/shard_map/ppermute | solution.py:379
  103.5 0.8 collective-permute-start.17
  104.3 1.6 %collective-permute-start.16 = (bf16[8,640]{1,0:T(8,128)(2,1)S(1)}, bf16[8,640]{1,0:T(8,128)(2,1)S(1)}, u32[]{:S(2)}, u32[]{:S(2)}) collective-permute-start(bf16[8,640]{1,0:T(8,128)(2,1)S(1)} %get-tuple-element.25), channel_id=1, source_target_pairs={{0,4},{4,0},{8,12},{12,8},{16,20},{20,16},{24,28},{28,24},{1,5},{5... | collective-permute-start | bytes 30728 | tf_op jit(solution)/shard_map/ppermute | solution.py:379
  105.9 0.6 select_bitcast_fusion
  106.6 0.0 collective-permute-done.12
  106.6 0.4 collective-permute-done.18
  107.0 1.1 %collective-permute-done.17 = bf16[8,640]{1,0:T(8,128)(2,1)S(1)} collective-permute-done((bf16[8,640]{1,0:T(8,128)(2,1)S(1)}, bf16[8,640]{1,0:T(8,128)(2,1)S(1)}, u32[]{:S(2)}, u32[]{:S(2)}) %collective-permute-start.17) | collective-permute-done | bytes 10272 | tf_op jit(solution)/shard_map/ppermute | solution.py:379
  108.1 0.0 collective-permute-done.16
  108.1 0.6 fusion.1
  (28 shorter events, 0.1 us)
Async XLA Ops:
  0.6 24.1 %copy-start.1 = (bf16[1,2560,192]{1,2,0:T(8,128)(2,1)S(1)}, bf16[1,2560,192]{1,2,0:T(8,128)(2,1)}, u32[]{:S(2)}) copy-start(bf16[1,2560,192]{1,2,0:T(8,128)(2,1)} %param.11) | copy-start | bytes 2949124
  0.6 1.2 %copy-start.4 = (bf16[1,2560,136]{1,2,0:T(8,128)(2,1)S(1)}, bf16[1,2560,136]{1,2,0:T(8,128)(2,1)}, u32[]{:S(2)}) copy-start(bf16[1,2560,136]{1,2,0:T(8,128)(2,1)} %param.13) | copy-start | bytes 2088964
  1.8 0.9 copy-start.9
  2.8 12.3 %collective-permute-start = (bf16[192,640]{1,0:T(8,128)(2,1)S(1)}, bf16[192,640]{1,0:T(8,128)(2,1)S(1)}, u32[]{:S(2)}, u32[]{:S(2)}) collective-permute-start(bf16[192,640]{1,0:T(8,128)(2,1)S(1)} %shard_map.104.own), channel_id=1, source_target_pairs={{0,4},{4,0},{8,12},{12,8},{16,20},{20,16},{24,28},{28,24},{1,5},{5... | collective-permute-start | bytes 737288 | tf_op jit(solution)/shard_map/ppermute | solution.py:379
  4.4 20.3 %collective-permute-start.1 = (bf16[192,640]{1,0:T(8,128)(2,1)S(1)}, bf16[192,640]{1,0:T(8,128)(2,1)S(1)}, u32[]{:S(2)}, u32[]{:S(2)}) collective-permute-start(bf16[192,640]{1,0:T(8,128)(2,1)S(1)} %shard_map.104.own), channel_id=1, source_target_pairs={{0,8},{4,12},{8,0},{12,4},{16,24},{20,28},{24,16},{28,20},{1,9},{5... | collective-permute-start | bytes 737288 | tf_op jit(solution)/shard_map/ppermute | solution.py:379
  7.0 17.7 %collective-permute-start.2 = (bf16[192,640]{1,0:T(8,128)(2,1)S(1)}, bf16[192,640]{1,0:T(8,128)(2,1)S(1)}, u32[]{:S(2)}, u32[]{:S(2)}) collective-permute-start(bf16[192,640]{1,0:T(8,128)(2,1)S(1)} %shard_map.104.own), channel_id=1, source_target_pairs={{0,12},{4,8},{8,4},{12,0},{16,28},{20,24},{24,20},{28,16},{1,13},{... | collective-permute-start | bytes 737288 | tf_op jit(solution)/shard_map/ppermute | solution.py:379
  24.8 1.1 %copy-start.5 = (bf16[1,2560,136]{1,2,0:T(8,128)(2,1)S(1)}, bf16[1,2560,136]{1,2,0:T(8,128)(2,1)}, u32[]{:S(2)}) copy-start(bf16[1,2560,136]{1,2,0:T(8,128)(2,1)} %param.13) | copy-start | bytes 2088964
  25.9 23.3 %copy-start.2 = (bf16[1,768,640]{2,1,0:T(8,128)(2,1)S(1)}, bf16[1,768,640]{2,1,0:T(8,128)(2,1)}, u32[]{:S(2)}) copy-start(bf16[1,768,640]{2,1,0:T(8,128)(2,1)} %param.12) | copy-start | bytes 2949124
  25.9 23.3 %copy-start.6 = (bf16[1,512,512]{2,1,0:T(8,128)(2,1)S(1)}, bf16[1,512,512]{2,1,0:T(8,128)(2,1)}, u32[]{:S(2)}) copy-start(bf16[1,512,512]{2,1,0:T(8,128)(2,1)} %param.14) | copy-start | bytes 1572868
  25.9 23.3 %copy-start.7 = (bf16[1,512,512]{2,1,0:T(8,128)(2,1)S(1)}, bf16[1,512,512]{2,1,0:T(8,128)(2,1)}, u32[]{:S(2)}) copy-start(bf16[1,512,512]{2,1,0:T(8,128)(2,1)} %param.15) | copy-start | bytes 1572868
  25.9 23.3 %copy-start.10 = (bf16[192,640]{1,0:T(8,128)(2,1)S(1)}, bf16[192,640]{1,0:T(8,128)(2,1)}, u32[]{:S(2)}) copy-start(bf16[192,640]{1,0:T(8,128)(2,1)} %share.1) | copy-start | bytes 737284
  26.8 2.2 %collective-permute-start.10 = (bf16[4,136,640]{2,1,0:T(8,128)(2,1)S(1)}, bf16[4,136,640]{2,1,0:T(8,128)(2,1)S(1)}, u32[]{:S(2)}, u32[]{:S(2)}) collective-permute-start(bf16[4,136,640]{2,1,0:T(8,128)(2,1)S(1)} %get-tuple-element.21.quarter), channel_id=1, source_target_pairs={{0,1},{1,0},{2,3},{3,2},{4,5},{5,4},{6,7},{7,6},{8,9},{9,8},{10,11... | collective-permute-start | bytes 2088968 | tf_op jit(solution)/shard_map/ppermute | solution.py:386
  29.0 20.2 %copy-start = (bf16[1,512,2560]{2,1,0:T(8,128)(2,1)S(1)}, bf16[1,512,2560]{2,1,0:T(8,128)(2,1)}, u32[]{:S(2)}) copy-start(bf16[1,512,2560]{2,1,0:T(8,128)(2,1)} %param.16) | copy-start | bytes 7864324
  29.0 20.2 %copy-start.11 = (f32[192,32]{1,0:T(8,128)S(1)}, f32[192,32]{1,0:T(8,128)}, u32[]{:S(2)}) copy-start(f32[192,32]{1,0:T(8,128)} %constant.10.clone.angles) | copy-start | bytes 73732
  29.0 20.2 %copy-start.14 = (s32[8]{0:T(128)S(1)}, s32[8]{0:T(128)}, u32[]{:S(2)}) copy-start(s32[8]{0:T(128)} %sizes.3) | copy-start | bytes 100
  29.1 57.1 %collective-permute-start.11 = (bf16[2,4,136,640]{3,2,1,0:T(8,128)(2,1)S(1)}, bf16[2,4,136,640]{3,2,1,0:T(8,128)(2,1)S(1)}, u32[]{:S(2)}, u32[]{:S(2)}) collective-permute-start(bf16[2,4,136,640]{3,2,1,0:T(8,128)(2,1)S(1)} %pad_maximum_fusion), channel_id=1, source_target_pairs={{0,2},{1,3},{2,0},{3,1},{4,6},{5,7},{6,4},{7,5},{8,10},{9,11},{10,... | collective-permute-start | bytes 4177928 | tf_op jit(solution)/shard_map/ppermute | solution.py:386
  30.7 10.3 %collective-permute-start.3 = (bf16[192,328]{1,0:T(8,128)(2,1)S(1)}, bf16[192,328]{1,0:T(8,128)(2,1)S(1)}, u32[]{:S(2)}, u32[]{:S(2)}) collective-permute-start(bf16[192,328]{1,0:T(8,128)(2,1)S(1)} %get-tuple-element.15.own), channel_id=1, source_target_pairs={{0,4},{4,0},{8,12},{12,8},{16,20},{20,16},{24,28},{28,24},{1,5},{5... | collective-permute-start | bytes 377864 | tf_op jit(solution)/shard_map/ppermute | solution.py:379
  35.1 14.0 %collective-permute-start.4 = (bf16[192,328]{1,0:T(8,128)(2,1)S(1)}, bf16[192,328]{1,0:T(8,128)(2,1)S(1)}, u32[]{:S(2)}, u32[]{:S(2)}) collective-permute-start(bf16[192,328]{1,0:T(8,128)(2,1)S(1)} %get-tuple-element.15.own), channel_id=1, source_target_pairs={{0,8},{4,12},{8,0},{12,4},{16,24},{20,28},{24,16},{28,20},{1,9},{5... | collective-permute-start | bytes 377864 | tf_op jit(solution)/shard_map/ppermute | solution.py:379
  36.1 13.0 %collective-permute-start.5 = (bf16[192,328]{1,0:T(8,128)(2,1)S(1)}, bf16[192,328]{1,0:T(8,128)(2,1)S(1)}, u32[]{:S(2)}, u32[]{:S(2)}) collective-permute-start(bf16[192,328]{1,0:T(8,128)(2,1)S(1)} %get-tuple-element.15.own), channel_id=1, source_target_pairs={{0,12},{4,8},{8,4},{12,0},{16,28},{20,24},{24,20},{28,16},{1,13},{... | collective-permute-start | bytes 377864 | tf_op jit(solution)/shard_map/ppermute | solution.py:379
  52.6 35.4 %copy-start.12 = (bf16[48,544]{1,0:T(8,128)(2,1)}, bf16[48,544]{1,0:T(8,128)(2,1)S(1)}, u32[]{:S(2)}) copy-start(bf16[48,544]{1,0:T(8,128)(2,1)S(1)} %get-tuple-element.16) | copy-start | bytes 156676
  52.6 18.5 %collective-permute-start.6 = (bf16[56,2560]{1,0:T(8,128)(2,1)S(1)}, bf16[56,2560]{1,0:T(8,128)(2,1)S(1)}, u32[]{:S(2)}, u32[]{:S(2)}) collective-permute-start(bf16[56,2560]{1,0:T(8,128)(2,1)S(1)} %get-tuple-element.17), channel_id=1, source_target_pairs={{0,16},{4,20},{8,24},{12,28},{16,0},{20,4},{24,8},{28,12},{1,17},{... | collective-permute-start | bytes 860168 | tf_op jit(solution)/shard_map/ppermute | solution.py:383
  53.2 17.9 %collective-permute-start.7 = (bf16[56,2560]{1,0:T(8,128)(2,1)S(1)}, bf16[56,2560]{1,0:T(8,128)(2,1)S(1)}, u32[]{:S(2)}, u32[]{:S(2)}) collective-permute-start(bf16[56,2560]{1,0:T(8,128)(2,1)S(1)} %get-tuple-element.18), channel_id=1, source_target_pairs={{0,28},{4,24},{8,20},{12,16},{16,0},{20,4},{24,8},{28,12},{1,29},{... | collective-permute-start | bytes 860168 | tf_op jit(solution)/shard_map/ppermute | solution.py:383
  54.7 31.5 %collective-permute-start.8 = (bf16[56,2560]{1,0:T(8,128)(2,1)S(1)}, bf16[56,2560]{1,0:T(8,128)(2,1)S(1)}, u32[]{:S(2)}, u32[]{:S(2)}) collective-permute-start(bf16[56,2560]{1,0:T(8,128)(2,1)S(1)} %get-tuple-element.19), channel_id=1, source_target_pairs={{0,24},{4,28},{8,16},{12,20},{16,0},{20,4},{24,8},{28,12},{1,25},{... | collective-permute-start | bytes 860168 | tf_op jit(solution)/shard_map/ppermute | solution.py:383
  56.8 29.4 %collective-permute-start.9 = (bf16[56,2560]{1,0:T(8,128)(2,1)S(1)}, bf16[56,2560]{1,0:T(8,128)(2,1)S(1)}, u32[]{:S(2)}, u32[]{:S(2)}) collective-permute-start(bf16[56,2560]{1,0:T(8,128)(2,1)S(1)} %get-tuple-element.20), channel_id=1, source_target_pairs={{0,20},{4,16},{8,28},{12,24},{16,0},{20,4},{24,8},{28,12},{1,21},{... | collective-permute-start | bytes 860168 | tf_op jit(solution)/shard_map/ppermute | solution.py:383
  88.0 5.0 %collective-permute-start.13 = (bf16[56,544]{1,0:T(8,128)(2,1)S(1)}, bf16[56,544]{1,0:T(8,128)(2,1)S(1)}, u32[]{:S(2)}, u32[]{:S(2)}) collective-permute-start(bf16[56,544]{1,0:T(8,128)(2,1)S(1)} %get-tuple-element.22.own), channel_id=1, source_target_pairs={{0,4},{4,0},{8,12},{12,8},{16,20},{20,16},{24,28},{28,24},{1,5},{5... | collective-permute-start | bytes 182792 | tf_op jit(solution)/shard_map/ppermute | solution.py:379
  88.1 8.7 %collective-permute-start.14 = (bf16[56,544]{1,0:T(8,128)(2,1)S(1)}, bf16[56,544]{1,0:T(8,128)(2,1)S(1)}, u32[]{:S(2)}, u32[]{:S(2)}) collective-permute-start(bf16[56,544]{1,0:T(8,128)(2,1)S(1)} %get-tuple-element.22.own), channel_id=1, source_target_pairs={{0,8},{4,12},{8,0},{12,4},{16,24},{20,28},{24,16},{28,20},{1,9},{5... | collective-permute-start | bytes 182792 | tf_op jit(solution)/shard_map/ppermute | solution.py:379
  90.6 6.2 %collective-permute-start.15 = (bf16[56,544]{1,0:T(8,128)(2,1)S(1)}, bf16[56,544]{1,0:T(8,128)(2,1)S(1)}, u32[]{:S(2)}, u32[]{:S(2)}) collective-permute-start(bf16[56,544]{1,0:T(8,128)(2,1)S(1)} %get-tuple-element.22.own), channel_id=1, source_target_pairs={{0,12},{4,8},{8,4},{12,0},{16,28},{20,24},{24,20},{28,16},{1,13},{... | collective-permute-start | bytes 182792 | tf_op jit(solution)/shard_map/ppermute | solution.py:379
  92.5 14.1 %collective-permute-start.12 = (bf16[8,640]{1,0:T(8,128)(2,1)S(1)}, bf16[8,640]{1,0:T(8,128)(2,1)S(1)}, u32[]{:S(2)}, u32[]{:S(2)}) collective-permute-start(bf16[8,640]{1,0:T(8,128)(2,1)S(1)} %get-tuple-element.23), channel_id=1, source_target_pairs={{0,16},{4,20},{8,24},{12,28},{16,0},{20,4},{24,8},{28,12},{1,17},{... | collective-permute-start | bytes 30728 | tf_op jit(solution)/shard_map/ppermute | solution.py:383
  96.8 1.2 %copy-start.3 = (bf16[1,768,640]{2,1,0:T(8,128)(2,1)S(1)}, bf16[1,768,640]{2,1,0:T(8,128)(2,1)}, u32[]{:S(2)}) copy-start(bf16[1,768,640]{2,1,0:T(8,128)(2,1)} %param.12) | copy-start | bytes 2949124
  98.0 1.0 copy-start.8
  99.1 6.8 %copy-start.13 = (bf16[48,544]{1,0:T(8,128)(2,1)S(1)}, bf16[48,544]{1,0:T(8,128)(2,1)}, u32[]{:S(2)}) copy-start(bf16[48,544]{1,0:T(8,128)(2,1)} %copy-done.12) | copy-start | bytes 156676
  101.5 5.5 %collective-permute-start.18 = (bf16[8,640]{1,0:T(8,128)(2,1)S(1)}, bf16[8,640]{1,0:T(8,128)(2,1)S(1)}, u32[]{:S(2)}, u32[]{:S(2)}) collective-permute-start(bf16[8,640]{1,0:T(8,128)(2,1)S(1)} %get-tuple-element.27), channel_id=1, source_target_pairs={{0,12},{4,8},{8,4},{12,0},{16,28},{20,24},{24,20},{28,16},{1,13},{... | collective-permute-start | bytes 30728 | tf_op jit(solution)/shard_map/ppermute | solution.py:379
  103.5 4.6 %collective-permute-start.17 = (bf16[8,640]{1,0:T(8,128)(2,1)S(1)}, bf16[8,640]{1,0:T(8,128)(2,1)S(1)}, u32[]{:S(2)}, u32[]{:S(2)}) collective-permute-start(bf16[8,640]{1,0:T(8,128)(2,1)S(1)} %get-tuple-element.26), channel_id=1, source_target_pairs={{0,8},{4,12},{8,0},{12,4},{16,24},{20,28},{24,16},{28,20},{1,9},{5... | collective-permute-start | bytes 30728 | tf_op jit(solution)/shard_map/ppermute | solution.py:379
  104.3 3.8 %collective-permute-start.16 = (bf16[8,640]{1,0:T(8,128)(2,1)S(1)}, bf16[8,640]{1,0:T(8,128)(2,1)S(1)}, u32[]{:S(2)}, u32[]{:S(2)}) collective-permute-start(bf16[8,640]{1,0:T(8,128)(2,1)S(1)} %get-tuple-element.25), channel_id=1, source_target_pairs={{0,4},{4,0},{8,12},{12,8},{16,20},{20,16},{24,28},{28,24},{1,5},{5... | collective-permute-start | bytes 30728 | tf_op jit(solution)/shard_map/ppermute | solution.py:379

commit v4 on v3

--- a/solution.py
+++ b/solution.py
@@ -170,18 +170,19 @@
 HALF = ROPE_DIM // 2
 SMEM = pl.BlockSpec(memory_space=pltpu.SMEM)
 VMEM = pl.BlockSpec(memory_space=pltpu.VMEM)
-
-
-def call(kernel, out_shape, args, scratch=(), flops=0, scalars=0):
+HBM = pl.BlockSpec(memory_space=pltpu.HBM)
+
+
+def call(kernel, out_shape, args, scratch=(), flops=0, scalars=0, left=0, space=VMEM, grant=8):
     many = isinstance(out_shape, list)
     moved = sum(a.size * a.dtype.itemsize for a in args)
     return pl.pallas_call(
         kernel,
         out_shape=out_shape,
-        in_specs=[SMEM] * scalars + [VMEM] * (len(args) - scalars),
-        out_specs=[VMEM] * len(out_shape) if many else VMEM,
+        in_specs=[SMEM] * scalars + [VMEM] * (len(args) - scalars - left) + [HBM] * left,
+        out_specs=[space] * len(out_shape) if many else space,
         scratch_shapes=list(scratch),
-        compiler_params=pltpu.CompilerParams(vmem_limit_bytes=20 * 2**20),
+        compiler_params=pltpu.CompilerParams(vmem_limit_bytes=grant * 2**20),
         cost_estimate=pl.CostEstimate(flops=flops, bytes_accessed=moved, transcendentals=0),
     )(*args)
 
@@ -215,44 +216,105 @@
     return out
 
 
-def send_kernel(prompt, w_latent, out):
+def send_kernel(prompt, w_latent, out, half, packed, sem):
     section, rep = lax.axis_index("section"), lax.axis_index("rep")
-    rows, width = prompt.shape
-    latent_cols = w_latent.shape[0]
+    width = out.shape[1]
+    cols = half.shape[0]
 
     @pl.when(section == 0)
     def _():
-        out[...] = prompt[...]
+        copy = pltpu.make_async_copy(prompt, packed, sem)
+        copy.start()
+        copy.wait()
+        copy = pltpu.make_async_copy(packed, out, sem)
+        copy.start()
+        copy.wait()
 
     @pl.when(section != 0)
     def _():
-        quarter = w_latent[:, pl.ds(pl.multiple_of(rep * width, 128), width)]
-        rest = jnp.zeros((rows - latent_cols, width), BF16)
-        out[...] = jnp.concatenate([quarter, rest], axis=0)
-
-
-def down_kernel(own, one, two, three, w_down, w_latent, out, weights):
-    tp = lax.axis_index("tp")
-    share = own.shape[1]
-    latent_cols = w_latent.shape[0]
-    squares, down, latent = 0.0, 0.0, 0.0
-    for k, ref in enumerate((own, one, two, three)):
-        columns = pl.ds(pl.multiple_of((tp ^ k) * share, 128), share)
-        piece = ref[...]
-        wide = piece.astype(F32)
-        squares = squares + jnp.sum(wide * wide, axis=1, keepdims=True)
-        down = down + dot_t(piece, w_down[:, columns])
-        latent = latent + dot_t(piece, w_latent[:, columns])
-        weights[tp ^ k] = piece[:latent_cols]
-    scale = lax.rsqrt(squares / (4 * share) + EPSILON)
-    out[...] = jnp.concatenate([down * scale, latent * scale], axis=1).astype(BF16)
+        columns = pl.ds(pl.multiple_of((rep & 1) * half.shape[1], 128), half.shape[1])
+        copy = pltpu.make_async_copy(w_latent.at[:, columns], half, sem)
+        copy.start()
+        copy.wait()
+        extra = half[:, width : width + 256].astype(F32)
+        rows = out.shape[0] - cols
+        left = cols - 2 * rows
+        tail = [extra[2 * rows :, :128], extra[2 * rows :, 128:], jnp.zeros((rows - 2 * left, 128), F32)]
+        extra = jnp.concatenate(
+            [extra[:rows], extra[rows : 2 * rows], jnp.concatenate(tail, axis=0)], axis=1
+        )
+        whole = jnp.concatenate([half[:, :width].astype(F32), extra], axis=0)
+        packed[...] = whole.astype(BF16)
+        copy = pltpu.make_async_copy(packed, out, sem)
+        copy.start()
+        copy.wait()
+
+
+def unpack_share(share, cols):
+    share = share.astype(F32)
+    rows = share.shape[0] - cols
+    left = cols - 2 * rows
+    extra, tail = share[cols:, :512], share[cols:, 512:]
+    tail = jnp.concatenate([tail[:left], tail[left : 2 * left]], axis=1)
+    extra = jnp.concatenate([extra[:, :256], extra[:, 256:], tail], axis=0)
+    return jnp.concatenate([share[:cols], extra], axis=1).astype(BF16)
+
+
+def down_kernel(own, one, two, three, w_down, w_latent, out):
+    section, tp, rep = (lax.axis_index(a) for a in ("section", "tp", "rep"))
+    tokens, share = own.shape
+    cols, model = w_latent.shape
+    third = tokens // 3
+
+    @pl.when(section == 0)
+    def _():
+        squares, down, latent = 0.0, 0.0, 0.0
+        for k, ref in enumerate((own, one, two, three)):
+            columns = pl.ds(pl.multiple_of((tp ^ k) * share, 128), share)
+            piece = ref[...]
+            wide = piece.astype(F32)
+            squares = squares + jnp.sum(wide * wide, axis=1, keepdims=True)
+            down = down + dot_t(piece, w_down[:, columns])
+            latent = latent + dot_t(piece, w_latent[:, columns])
+        scale = lax.rsqrt(squares / model + EPSILON)
+        parts = jnp.concatenate([down * scale, latent * scale], axis=1)
+        rest = parts[:, 256:]
+        rest = [rest[i * third : (i + 1) * third] for i in range(3)]
+        rest.append(jnp.zeros((third, 256 - 3 * rest[0].shape[1]), F32))
+        out[...] = jnp.concatenate([parts[:, :256], jnp.concatenate(rest, axis=1)], axis=0).astype(BF16)
+
+    @pl.when(section != 0)
+    def _():
+        first = (rep & 1) * (model // 2) + share + 256
+        mine = w_latent[:, pl.ds(pl.multiple_of(first, 128), 384)].astype(F32)
+        rest = mine[:, 256:]
+        high = cols // 2 + 4
+        lower = jnp.concatenate([rest[high:], jnp.zeros((2 * high - cols, 128), F32)], axis=0)
+        rest = jnp.concatenate([rest[:high], lower], axis=1)
+        blank = jnp.zeros((out.shape[0] - cols - high, 256), F32)
+        out[...] = jnp.concatenate([mine[:, :256], rest, blank], axis=0).astype(BF16)
+
+
+def unpack_rest(piece, cols):
+    piece = piece.astype(F32)
+    high = cols // 2 + 4
+    rest = piece[cols : cols + high]
+    rest = jnp.concatenate([rest[:, :128], rest[: cols - high, 128:]], axis=0)
+    return jnp.concatenate([piece[:cols], rest], axis=1).astype(BF16)
+
+
+def unpack_parts(piece, tokens, width):
+    piece = piece.astype(F32)
+    rest, size = piece[tokens:], width - 256
+    rest = jnp.concatenate([rest[:, i * size : (i + 1) * size] for i in range(3)], axis=0)
+    return jnp.concatenate([piece[:tokens], rest], axis=1)
 
 
 def attend_rows(compressed, cache, seen, angles, w_query, w_keys, w_values):
-    queries = dot(compressed, w_query[...])
     plain, turned = cache[:, :LATENT], cache[:, LATENT:]
     keys = dot(plain, w_keys[...]).astype(BF16)
     values = dot(plain, w_values[...]).astype(BF16)
+    queries = dot(compressed, w_query[...])
     mixed = []
     for head in range(queries.shape[1] // HEAD_WIDTH):
         query = queries[:, head * HEAD_WIDTH : (head + 1) * HEAD_WIDTH]
@@ -268,46 +330,56 @@
 
 
 def layer_kernel(
-    sizes, own, one, two, three, share, angles, w_query, w_keys, w_values, w_out,
-    out0, out1, out2, out3, own_cache, stack, total, cached,
+    sizes, own, one, two, three, share1, share2, share3, w_latent, prompt, angles,
+    w_query, w_keys, w_values, w_out, out0, out1, out2, out3, own_cache, half, stack, total, cached,
 ):
-    tp = lax.axis_index("tp")
-    tokens, width = share.shape
+    section, tp, rep = (lax.axis_index(a) for a in ("section", "tp", "rep"))
+    tokens, width = prompt.shape
     block = tokens // 4
+    cols, long = half.shape[1:]
     down_cols = w_query.shape[0] // 4
-    ends = column(end_rows(sizes))
-    for k, ref in enumerate((own, one, two, three)):
-        stack[tp ^ k] = ref[...]
-    pieces = [stack[m].astype(F32) for m in range(4)]
-    down = jnp.concatenate([p[:, :down_cols] for p in pieces], axis=1)
-    latent = jnp.concatenate([p[:, down_cols:] for p in pieces], axis=1)
-    compressed = (down * unit(down)).astype(BF16)
-    plain = latent[:, :LATENT]
-    cache = jnp.concatenate(
-        [plain * unit(plain), turn(latent[:, LATENT:], angles[...])], axis=1
-    ).astype(BF16)
-    cached[...] = cache
-    own_cache[...] = cached[pl.ds(pl.multiple_of(tp * block, block), block), :]
-    seen = lax.broadcasted_iota(jnp.int32, (tokens, tokens), 0) >= lax.broadcasted_iota(
-        jnp.int32, (tokens, tokens), 1
-    )
-    mixed = attend_rows(compressed, cache, seen, angles[...], w_query, w_keys, w_values)
-    chosen = lax.broadcasted_iota(jnp.int32, (ends.shape[0], tokens), 1) == ends
-    chosen = chosen.astype(BF16)
-    rows = jnp.concatenate([mixed, dot(chosen, mixed).astype(BF16)], axis=0)
-    total[...] = dot(rows, w_out[...])
-    mine = pl.ds(pl.multiple_of(tp * width, 128), width)
-    added = jnp.concatenate([share[...].astype(F32), dot(chosen, share[...])], axis=0)
-    total[:, mine] += added
-    last = total[tokens:, :]
-    for k, out in enumerate((out0, out1, out2, out3)):
-        part = total[pl.ds(pl.multiple_of((tp ^ k) * block, block), block), :]
-        out[...] = jnp.concatenate([part, last], axis=0).astype(BF16)
+
+    @pl.when(section != 0)
+    def _():
+        half[tp] = w_latent[:, pl.ds(pl.multiple_of((rep & 1) * long, 128), long)]
+        for k, weights, rest in ((1, share1, one), (2, share2, two), (3, share3, three)):
+            half[tp ^ k, :, : width + 256] = unpack_share(weights[...], cols)
+            half[tp ^ k, :, width + 256 :] = unpack_rest(rest[...], cols)
+
+    @pl.when(section == 0)
+    def _():
+        ends = column(end_rows(sizes))
+        for k, ref in enumerate((own, one, two, three)):
+            stack[tp ^ k] = ref[...]
+        pieces = [unpack_parts(stack[m], tokens, down_cols + cols) for m in range(4)]
+        down = jnp.concatenate([p[:, :down_cols] for p in pieces], axis=1)
+        latent = jnp.concatenate([p[:, down_cols:] for p in pieces], axis=1)
+        compressed = (down * unit(down)).astype(BF16)
+        plain = latent[:, :LATENT]
+        cache = jnp.concatenate(
+            [plain * unit(plain), turn(latent[:, LATENT:], angles[...])], axis=1
+        ).astype(BF16)
+        cached[...] = cache
+        own_cache[...] = cached[pl.ds(pl.multiple_of(tp * block, block), block), :]
+        seen = lax.broadcasted_iota(jnp.int32, (tokens, tokens), 0) >= lax.broadcasted_iota(
+            jnp.int32, (tokens, tokens), 1
+        )
+        mixed = attend_rows(compressed, cache, seen, angles[...], w_query, w_keys, w_values)
+        chosen = lax.broadcasted_iota(jnp.int32, (ends.shape[0], tokens), 1) == ends
+        chosen = chosen.astype(BF16)
+        rows = jnp.concatenate([mixed, dot(chosen, mixed).astype(BF16)], axis=0)
+        total[...] = dot(rows, w_out[...])
+        mine = pl.ds(pl.multiple_of(tp * width, 128), width)
+        added = jnp.concatenate([prompt[...].astype(F32), dot(chosen, prompt[...])], axis=0)
+        total[:, mine] += added
+        last = total[tokens:, :]
+        for k, out in enumerate((out0, out1, out2, out3)):
+            part = total[pl.ds(pl.multiple_of((tp ^ k) * block, block), block), :]
+            out[...] = jnp.concatenate([part, last], axis=0).astype(BF16)
 
 
 def latent_kernel(
-    one, two, three, four, angles, quarter, near, far, w_down,
-    out, own_ends, hidden,
+    one, two, three, four, angles, half, near, w_down, out, own_cache, own_ends, hidden
 ):
     tp, rep = lax.axis_index("tp"), lax.axis_index("rep")
     block = angles.shape[0] // 4
@@ -317,21 +389,24 @@
     rows = narrow.astype(F32)
     hidden[...] = rows
     scale = unit(rows)
-    count = w_down.shape[0]
     totals = [0.0] * 4
-    for step, weights in enumerate((quarter, near, far.at[0], far.at[1])):
-        columns = pl.ds(pl.multiple_of((rep ^ step) * width, 128), width)
+    for step, weights in enumerate((half, near)):
+        long = weights.shape[2]
+        columns = pl.ds(pl.multiple_of(((rep & 1) ^ step) * long, 128), long)
         piece = hidden[0:block, columns].astype(BF16)
         totals = [total + dot_t(piece, weights[m]) for m, total in enumerate(totals)]
     latent = jnp.concatenate(totals, axis=1) * scale[:block]
     plain = latent[:, :LATENT]
+    plain = plain * unit(plain)
     own_angles = angles[pl.ds(pl.multiple_of(tp * block, block), block), :]
-    fresh = jnp.concatenate(
-        [plain * unit(plain), turn(latent[:, LATENT:], own_angles)], axis=1
-    )
+    turned = turn(latent[:, LATENT:], own_angles)
+    own_cache[...] = jnp.concatenate([plain, turned], axis=1).astype(BF16)
     down = dot_t(narrow[block:, :], w_down[...]) * scale[block:]
-    down = jnp.concatenate([down, jnp.zeros((down.shape[0], ROW_WIDTH - count), F32)], axis=1)
-    out[...] = jnp.concatenate([fresh, down], axis=0).astype(BF16)
+    count = down.shape[0]
+    turned = [turned[i * count : (i + 1) * count] for i in range(block // count)]
+    last = jnp.concatenate([*turned, down], axis=1)
+    last = jnp.concatenate([last, jnp.zeros((count, LATENT - last.shape[1]), F32)], axis=1)
+    out[...] = jnp.concatenate([plain, last], axis=0).astype(BF16)
     mine = pl.ds(pl.multiple_of(tp * width, 128), width)
     own_ends[...] = hidden[block:, mine].astype(BF16)
 
@@ -344,13 +419,20 @@
     ends = end_rows(sizes)
     count = len(ends)
     block = own.shape[0] - count
+    steps = block // count
     down_cols = w_query.shape[0] // 4
     width = out0.shape[1]
     for k, ref in enumerate((own, one, two, three)):
         stack[tp ^ k] = ref[...].astype(F32)
     pieces = [stack[m] for m in range(4)]
-    cache = jnp.concatenate([p[:block] for p in pieces], axis=0).astype(BF16)
-    down = jnp.concatenate([p[block:, :down_cols] for p in pieces], axis=1)
+    plain = jnp.concatenate([p[:block] for p in pieces], axis=0)
+    last = [p[block:] for p in pieces]
+    turned = jnp.concatenate(
+        [p[:, i * ROPE_DIM : (i + 1) * ROPE_DIM] for p in last for i in range(steps)], axis=0
+    )
+    cache = jnp.concatenate([plain, turned], axis=1).astype(BF16)
+    first = steps * ROPE_DIM
+    down = jnp.concatenate([p[:, first : first + down_cols] for p in last], axis=1)
     compressed = (down * unit(down)).astype(BF16)
     end_angles = jnp.concatenate([angles[pl.ds(e, 1), :] for e in ends], axis=0)
     seen = lax.broadcasted_iota(jnp.int32, (count, 4 * block), 1) <= column(ends)
@@ -385,44 +467,59 @@
     def over_rep(array, k):
         return lax.ppermute(array, "rep", [(i, i ^ k) for i in range(4)])
 
-    sent = call(send_kernel, jax.ShapeDtypeStruct((tokens, share), BF16), [prompt, w_lat])
-    shares = [sent] + [within(sent, k) for k in (1, 2, 3)]
-    parts, quarter = call(
+    sent = call(
+        send_kernel,
+        jax.ShapeDtypeStruct((tokens, share), BF16),
+        [prompt, w_lat],
+        [
+            pltpu.VMEM((latent_cols, model // 2), BF16),
+            pltpu.VMEM((tokens, share), BF16),
+            pltpu.SemaphoreType.DMA,
+        ],
+        left=2,
+        space=HBM,
+        grant=57,
+        flops=2 * 10**10,
+    )
+    shares = [within(sent, k) for k in (1, 2, 3)]
+    parts = call(
         down_kernel,
+        jax.ShapeDtypeStruct((tokens + tokens // 3, 256), BF16),
+        [prompt, *shares, w_down, w_lat],
+        flops=2 * 10**10,
+    )
+    pieces = [parts] + [within(parts, k) for k in (1, 2, 3)]
+
+    message = jax.ShapeDtypeStruct((block + count, model), BF16)
+    *blocks, first_cache, half = call(
+        layer_kernel,
+        [message] * 4
+        + [
+            jax.ShapeDtypeStruct((block, ROW_WIDTH), BF16),
+            jax.ShapeDtypeStruct((4, latent_cols, model // 2), BF16),
+        ],
+        [block_sizes, *pieces, *shares, w_lat, prompt, angles, w_up, w_key, w_value, w_final],
         [
-            jax.ShapeDtypeStruct((tokens, down_cols + latent_cols), BF16),
-            jax.ShapeDtypeStruct((4, latent_cols, share), BF16),
-        ],
-        [*shares, w_down, w_lat],
-        flops=2 * tokens * model * (down_cols + latent_cols),
-    )
-    pieces = [parts] + [within(parts, k) for k in (1, 2, 3)]
-    near = over_rep(quarter, 1)
-    quarters = [quarter, near, over_rep(jnp.stack([quarter, near]), 2)]
-
-    message = jax.ShapeDtypeStruct((block + count, model), BF16)
-    *blocks, first_cache = call(
-        layer_kernel,
-        [message] * 4 + [jax.ShapeDtypeStruct((block, ROW_WIDTH), BF16)],
-        [block_sizes, *pieces, prompt, angles, w_up, w_key, w_value, w_final],
-        [
-            pltpu.VMEM((4, tokens, down_cols + latent_cols), BF16),
+            pltpu.VMEM((4, *parts.shape), BF16),
             pltpu.VMEM((tokens + count, model), F32),
             pltpu.VMEM((tokens, ROW_WIDTH), BF16),
         ],
         flops=2 * tokens * (w_up.size + w_key.size + w_value.size + w_final.size),
         scalars=1,
-    )
-    arrived = [onward(blocks[k], k) for k in (0, 3, 2, 1)]
-    fresh, ends_share = call(
+        grant=16,
+    )
+    arrived = [onward(blocks[k], k) for k in (3, 2, 1, 0)]
+    near = over_rep(half, 1)
+    fresh, last_cache, ends_share = call(
         latent_kernel,
         [
-            jax.ShapeDtypeStruct((block + count, ROW_WIDTH), BF16),
+            jax.ShapeDtypeStruct((block + count, LATENT), BF16),
+            jax.ShapeDtypeStruct((block, ROW_WIDTH), BF16),
             jax.ShapeDtypeStruct((count, share), BF16),
         ],
-        [*arrived, angles, *quarters, w_down],
+        [*arrived, angles, half, near, w_down],
         [pltpu.VMEM((block + count, model), F32)],
-        flops=2 * block * model * ROW_WIDTH,
+        flops=2 * 10**11,
     )
     pieces = [fresh] + [within(fresh, k) for k in (1, 2, 3)]
     first_ends = onward(ends_share, 0)
@@ -431,7 +528,7 @@
         [jax.ShapeDtypeStruct((count, share), BF16)] * 4,
         [block_sizes, *pieces, angles, w_up, w_key, w_value, w_final],
         [
-            pltpu.VMEM((4, block + count, ROW_WIDTH), F32),
+            pltpu.VMEM((4, block + count, LATENT), F32),
             pltpu.VMEM((count, model), F32),
         ],
         flops=2 * tokens * (w_key.size + w_value.size),
@@ -441,7 +538,7 @@
     for k in (1, 2, 3):
         total = total + within(outs[k], k).astype(F32)
     own_ends = jnp.where(section == 0, first_ends, total.astype(BF16))
-    own_cache = jnp.where(section == 0, first_cache, fresh[:block])
+    own_cache = jnp.where(section == 0, first_cache, last_cache)
     return (own_cache[None], own_ends[None])
 
 

time: 109 us -> 101 us (0.927)
  local copies, waits for them, and re-layouts: 5.51 us -> 1.81 us
  waiting for transfers between devices: 63.9 us -> 61.2 us
  Pallas kernels: 8.46 us -> 6.83 us
    unnamed x30 -> x28, local copies, waits for them, and re-layouts: 5.51 us -> 1.81 us
    ppermute x12, waiting for transfers between devices: 34.9 us -> 32.7 us  [within(): return lax.ppermute(array, ('section', 'tp'), pairs)]
    ppermute x2 -> x1, waiting for transfers between devices: 2.15 us -> 0.01 us  [over_rep(): return lax.ppermute(array, 'rep', [(i, i ^ k) for i in range(4)])]
    ppermute x5, starting transfers between devices: 6.82 us -> 8.65 us  [onward(): return lax.ppermute(array, ('section', 'tp'), pairs)]
    ppermute x5, waiting for transfers between devices: 26.8 us -> 28.5 us  [onward(): return lax.ppermute(array, ('section', 'tp'), pairs)]
    pallas_call x5, Pallas kernels: 8.46 us -> 6.83 us  [call(): pl.pallas_call(kernel, out_shape=out_shape, in_specs=[SMEM] * scalars + [...]
    ppermute x2 -> x1, starting transfers between devices: 1.63 us -> 0.07 us  [over_rep(): return lax.ppermute(array, 'rep', [(i, i ^ k) for i in range(4)])]
  transfers between devices with their start and end apart: 19 -> 18, of which waited for: 11 -> 11; matrix products, arithmetic and copies ran while one was open for 1% -> 1% of each run, Pallas kernels for 5% -> 3%
where the time goes in v4:
time: 101 us
  waiting for transfers between devices  61.2 us (61%)
  starting transfers between devices  29 us (29%)
  Pallas kernels  6.83 us (7%)
  local copies, waits for them, and re-layouts  1.81 us (2%)
  other arithmetic  1.25 us (1%)
    ppermute x12, waiting for transfers between devices, within(): return lax.ppermute(array, ('section', 'tp'), pairs)  32.7 us
    ppermute x5, waiting for transfers between devices, onward(): return lax.ppermute(array, ('section', 'tp'), pairs)  28.5 us
    ppermute x12, starting transfers between devices, within(): return lax.ppermute(array, ('section', 'tp'), pairs)  20.3 us
    ppermute x5, starting transfers between devices, onward(): return lax.ppermute(array, ('section', 'tp'), pairs)  8.65 us
    pallas_call x5, Pallas kernels, call(): pl.pallas_call(kernel, out_shape=out_shape, in_specs=[SMEM] * scalars + [...  6.83 us
  transfers between devices with their start and end apart: 18, of which 11 were waited for; matrix products, arithmetic and copies ran while one was open for 1% of the time, Pallas kernels for 3%

profile of v4, /device:TPU:4, one launch (start us, length us, event | category | flops | bytes accessed | tf_op | source)
XLA Modules:
  0.0 101.0 jit_solution(12003106493956675752)
XLA Ops:
  0.7 1.8 %shard_map.104 = bf16[192,640]{1,0:T(8,128)(2,1)} custom-call(bf16[192,640]{1,0:T(8,128)(2,1)} %prompt.3, bf16[136,2560]{1,0:T(8,128)(2,1)} %bitcast.22), custom_call_target="tpu_custom_call" | custom-call | flops 20000000000 | bytes 942080 | tf_op jit(solution)/shard_map/pallas_call | solution.py:179
  2.5 1.6 %collective-permute-start = (bf16[192,640]{1,0:T(8,128)(2,1)}, bf16[192,640]{1,0:T(8,128)(2,1)S(1)}, u32[]{:S(2)}, u32[]{:S(2)}) collective-permute-start(bf16[192,640]{1,0:T(8,128)(2,1)} %shard_map.104), channel_id=1, source_target_pairs={{0,4},{4,0},{8,12},{12,8},{16,20},{20,16},{24,28},{28,24},{1,5},{5... | collective-permute-start | bytes 737288 | tf_op jit(solution)/shard_map/ppermute | solution.py:461
  4.1 2.6 %collective-permute-start.1 = (bf16[192,640]{1,0:T(8,128)(2,1)}, bf16[192,640]{1,0:T(8,128)(2,1)S(1)}, u32[]{:S(2)}, u32[]{:S(2)}) collective-permute-start(bf16[192,640]{1,0:T(8,128)(2,1)} %shard_map.104), channel_id=1, source_target_pairs={{0,8},{4,12},{8,0},{12,4},{16,24},{20,28},{24,16},{28,20},{1,9},{5... | collective-permute-start | bytes 737288 | tf_op jit(solution)/shard_map/ppermute | solution.py:461
  6.7 0.2 collective-permute-start.2
  7.0 8.0 %collective-permute-done.one.share1 = bf16[192,640]{1,0:T(8,128)(2,1)S(1)} collective-permute-done((bf16[192,640]{1,0:T(8,128)(2,1)}, bf16[192,640]{1,0:T(8,128)(2,1)S(1)}, u32[]{:S(2)}, u32[]{:S(2)}) %collective-permute-start) | collective-permute-done | bytes 245792 | tf_op jit(solution)/shard_map/ppermute | solution.py:461
  15.0 9.7 %collective-permute-done.1.two.share2 = bf16[192,640]{1,0:T(8,128)(2,1)S(1)} collective-permute-done((bf16[192,640]{1,0:T(8,128)(2,1)}, bf16[192,640]{1,0:T(8,128)(2,1)S(1)}, u32[]{:S(2)}, u32[]{:S(2)}) %collective-permute-start.1) | collective-permute-done | bytes 245792 | tf_op jit(solution)/shard_map/ppermute | solution.py:461
  24.7 0.0 collective-permute-done.2.three.share3
  24.7 0.0 copy-start
  24.7 0.0 copy-start.2
  24.7 0.0 copy-start.4
  24.7 0.0 copy-start.6
  24.7 0.0 copy-start.9
  24.8 0.0 copy-start.11
  24.8 4.5 %collective-permute-start.3 = (bf16[256,256]{1,0:T(8,128)(2,1)S(1)}, bf16[256,256]{1,0:T(8,128)(2,1)S(1)}, u32[]{:S(2)}, u32[]{:S(2)}) collective-permute-start(bf16[256,256]{1,0:T(8,128)(2,1)S(1)} %shard_map.105.own), channel_id=1, source_target_pairs={{0,4},{4,0},{8,12},{12,8},{16,20},{20,16},{24,28},{28,24},{1,5},{5... | collective-permute-start | bytes 393224 | tf_op jit(solution)/shard_map/ppermute | solution.py:461
  29.3 1.1 %collective-permute-start.4 = (bf16[256,256]{1,0:T(8,128)(2,1)S(1)}, bf16[256,256]{1,0:T(8,128)(2,1)S(1)}, u32[]{:S(2)}, u32[]{:S(2)}) collective-permute-start(bf16[256,256]{1,0:T(8,128)(2,1)S(1)} %shard_map.105.own), channel_id=1, source_target_pairs={{0,8},{4,12},{8,0},{12,4},{16,24},{20,28},{24,16},{28,20},{1,9},{5... | collective-permute-start | bytes 393224 | tf_op jit(solution)/shard_map/ppermute | solution.py:461
  30.4 1.4 %collective-permute-start.5 = (bf16[256,256]{1,0:T(8,128)(2,1)S(1)}, bf16[256,256]{1,0:T(8,128)(2,1)S(1)}, u32[]{:S(2)}, u32[]{:S(2)}) collective-permute-start(bf16[256,256]{1,0:T(8,128)(2,1)S(1)} %shard_map.105.own), channel_id=1, source_target_pairs={{0,12},{4,8},{8,4},{12,0},{16,28},{20,24},{24,20},{28,16},{1,13},{... | collective-permute-start | bytes 393224 | tf_op jit(solution)/shard_map/ppermute | solution.py:461
  31.7 1.7 %collective-permute-done.3.one = bf16[256,256]{1,0:T(8,128)(2,1)S(1)} collective-permute-done((bf16[256,256]{1,0:T(8,128)(2,1)S(1)}, bf16[256,256]{1,0:T(8,128)(2,1)S(1)}, u32[]{:S(2)}, u32[]{:S(2)}) %collective-permute-start.3) | collective-permute-done | bytes 131104 | tf_op jit(solution)/shard_map/ppermute | solution.py:461
  33.5 7.6 %collective-permute-done.4.two = bf16[256,256]{1,0:T(8,128)(2,1)S(1)} collective-permute-done((bf16[256,256]{1,0:T(8,128)(2,1)S(1)}, bf16[256,256]{1,0:T(8,128)(2,1)S(1)}, u32[]{:S(2)}, u32[]{:S(2)}) %collective-permute-start.4) | collective-permute-done | bytes 131104 | tf_op jit(solution)/shard_map/ppermute | solution.py:461
  41.1 0.7 shard_map.106
  41.8 0.1 collective-permute-start.10
  41.9 4.3 %collective-permute-start.6 = (bf16[56,2560]{1,0:T(8,128)(2,1)S(1)}, bf16[56,2560]{1,0:T(8,128)(2,1)S(1)}, u32[]{:S(2)}, u32[]{:S(2)}) collective-permute-start(bf16[56,2560]{1,0:T(8,128)(2,1)S(1)} %get-tuple-element.16), channel_id=1, source_target_pairs={{0,28},{4,24},{8,20},{12,16},{16,0},{20,4},{24,8},{28,12},{1,29},{... | collective-permute-start | bytes 860168 | tf_op jit(solution)/shard_map/ppermute | solution.py:465
  46.2 0.1 collective-permute-start.7
  46.3 4.2 %collective-permute-start.8 = (bf16[56,2560]{1,0:T(8,128)(2,1)S(1)}, bf16[56,2560]{1,0:T(8,128)(2,1)S(1)}, u32[]{:S(2)}, u32[]{:S(2)}) collective-permute-start(bf16[56,2560]{1,0:T(8,128)(2,1)S(1)} %get-tuple-element.18), channel_id=1, source_target_pairs={{0,20},{4,16},{8,28},{12,24},{16,0},{20,4},{24,8},{28,12},{1,21},{... | collective-permute-start | bytes 860168 | tf_op jit(solution)/shard_map/ppermute | solution.py:465
  50.5 0.0 collective-permute-start.9
  50.5 4.9 %collective-permute-done.6.one = bf16[56,2560]{1,0:T(8,128)(2,1)S(1)} collective-permute-done((bf16[56,2560]{1,0:T(8,128)(2,1)S(1)}, bf16[56,2560]{1,0:T(8,128)(2,1)S(1)}, u32[]{:S(2)}, u32[]{:S(2)}) %collective-permute-start.6) | collective-permute-done | bytes 286752 | tf_op jit(solution)/shard_map/ppermute | solution.py:465
  55.4 23.7 %collective-permute-done.7.two = bf16[56,2560]{1,0:T(8,128)(2,1)S(1)} collective-permute-done((bf16[56,2560]{1,0:T(8,128)(2,1)S(1)}, bf16[56,2560]{1,0:T(8,128)(2,1)S(1)}, u32[]{:S(2)}, u32[]{:S(2)}) %collective-permute-start.7) | collective-permute-done | bytes 286752 | tf_op jit(solution)/shard_map/ppermute | solution.py:465
  79.1 0.0 collective-permute-done.9.four
  79.1 0.0 copy-start.3
  79.1 0.0 copy-start.5
  79.1 0.0 copy-start.7
  79.1 0.0 copy-start.12
  79.1 1.6 %shard_map.107 = (bf16[56,512]{1,0:T(8,128)(2,1)S(1)}, bf16[48,544]{1,0:T(8,128)(2,1)S(1)}, bf16[8,640]{1,0:T(8,128)(2,1)S(1)}) custom-call(bf16[56,2560]{1,0:T(8,128)(2,1)S(1)} %collective-permute-done.6.one, bf16[56,2560]{1,0:T(8,128)(2,1)S(1)} %collective-permute-done.7.two, bf16[56,2560]{1,0:T(8,128)(2,1)S(1)} %collective-permute-done.8.three, ...), custom_call_target="tpu_custom_call" | custom-call | flops 199999995904 | bytes 4939776 | tf_op jit(solution)/shard_map/pallas_call | solution.py:179
  80.8 0.1 collective-permute-start.12
  80.8 2.4 %collective-permute-start.13 = (bf16[56,512]{1,0:T(8,128)(2,1)S(1)}, bf16[56,512]{1,0:T(8,128)(2,1)S(1)}, u32[]{:S(2)}, u32[]{:S(2)}) collective-permute-start(bf16[56,512]{1,0:T(8,128)(2,1)S(1)} %get-tuple-element.23.own), channel_id=1, source_target_pairs={{0,8},{4,12},{8,0},{12,4},{16,24},{20,28},{24,16},{28,20},{1,9},{5... | collective-permute-start | bytes 172040 | tf_op jit(solution)/shard_map/ppermute | solution.py:461
  83.2 2.0 %collective-permute-start.14 = (bf16[56,512]{1,0:T(8,128)(2,1)S(1)}, bf16[56,512]{1,0:T(8,128)(2,1)S(1)}, u32[]{:S(2)}, u32[]{:S(2)}) collective-permute-start(bf16[56,512]{1,0:T(8,128)(2,1)S(1)} %get-tuple-element.23.own), channel_id=1, source_target_pairs={{0,12},{4,8},{8,4},{12,0},{16,28},{20,24},{24,20},{28,16},{1,13},{... | collective-permute-start | bytes 172040 | tf_op jit(solution)/shard_map/ppermute | solution.py:461
  85.2 0.6 collective-permute-done.12.one
  85.8 2.4 %collective-permute-done.13.two = bf16[56,512]{1,0:T(8,128)(2,1)S(1)} collective-permute-done((bf16[56,512]{1,0:T(8,128)(2,1)S(1)}, bf16[56,512]{1,0:T(8,128)(2,1)S(1)}, u32[]{:S(2)}, u32[]{:S(2)}) %collective-permute-start.13) | collective-permute-done | bytes 57376 | tf_op jit(solution)/shard_map/ppermute | solution.py:461
  88.2 1.1 %collective-permute-done.14.three = bf16[56,512]{1,0:T(8,128)(2,1)S(1)} collective-permute-done((bf16[56,512]{1,0:T(8,128)(2,1)S(1)}, bf16[56,512]{1,0:T(8,128)(2,1)S(1)}, u32[]{:S(2)}, u32[]{:S(2)}) %collective-permute-start.14) | collective-permute-done | bytes 57376 | tf_op jit(solution)/shard_map/ppermute | solution.py:461
  89.3 0.0 copy-start.1
  89.3 1.7 %copy-done.1 = bf16[1,512,2560]{2,1,0:T(8,128)(2,1)S(1)} copy-done((bf16[1,512,2560]{2,1,0:T(8,128)(2,1)S(1)}, bf16[1,512,2560]{2,1,0:T(8,128)(2,1)}, u32[]{:S(2)}) %copy-start.1) | copy-done | bytes 2621464
  91.1 2.6 %shard_map.108 = (bf16[8,640]{1,0:T(8,128)(2,1)S(1)}, bf16[8,640]{1,0:T(8,128)(2,1)S(1)}, bf16[8,640]{1,0:T(8,128)(2,1)S(1)}, bf16[8,640]{1,0:T(8,128)(2,1)S(1)}) custom-call(s32[8]{0:T(128)S(1)} %copy-done.12, bf16[56,512]{1,0:T(8,128)(2,1)S(1)} %get-tuple-element.23.own, bf16[56,512]{1,0:T(8,128)(2,1)S(1)} %collective-permute-done.12.one, ...), custom_call_target="tpu_custom_call" | custom-call | flops 201326592 | bytes 4907040 | tf_op jit(solution)/shard_map/pallas_call | solution.py:179
  93.7 2.1 %collective-permute-start.17 = (bf16[8,640]{1,0:T(8,128)(2,1)S(1)}, bf16[8,640]{1,0:T(8,128)(2,1)S(1)}, u32[]{:S(2)}, u32[]{:S(2)}) collective-permute-start(bf16[8,640]{1,0:T(8,128)(2,1)S(1)} %get-tuple-element.27), channel_id=1, source_target_pairs={{0,12},{4,8},{8,4},{12,0},{16,28},{20,24},{24,20},{28,16},{1,13},{... | collective-permute-start | bytes 30728 | tf_op jit(solution)/shard_map/ppermute | solution.py:461
  95.8 0.2 collective-permute-start.16
  95.9 2.2 %collective-permute-start.15 = (bf16[8,640]{1,0:T(8,128)(2,1)S(1)}, bf16[8,640]{1,0:T(8,128)(2,1)S(1)}, u32[]{:S(2)}, u32[]{:S(2)}) collective-permute-start(bf16[8,640]{1,0:T(8,128)(2,1)S(1)} %get-tuple-element.25), channel_id=1, source_target_pairs={{0,4},{4,0},{8,12},{12,8},{16,20},{20,16},{24,28},{28,24},{1,5},{5... | collective-permute-start | bytes 30728 | tf_op jit(solution)/shard_map/ppermute | solution.py:461
  98.2 0.6 select_bitcast_fusion
  98.8 0.4 collective-permute-done.17
  99.2 1.1 %collective-permute-done.16 = bf16[8,640]{1,0:T(8,128)(2,1)S(1)} collective-permute-done((bf16[8,640]{1,0:T(8,128)(2,1)S(1)}, bf16[8,640]{1,0:T(8,128)(2,1)S(1)}, u32[]{:S(2)}, u32[]{:S(2)}) %collective-permute-start.16) | collective-permute-done | bytes 10272 | tf_op jit(solution)/shard_map/ppermute | solution.py:461
  100.3 0.6 fusion.1
  (23 shorter events, 0.1 us)
Async XLA Ops:
  0.6 24.0 %copy-start.8 = (bf16[1,2560,136]{1,2,0:T(8,128)(2,1)S(1)}, bf16[1,2560,136]{1,2,0:T(8,128)(2,1)}, u32[]{:S(2)}) copy-start(bf16[1,2560,136]{1,2,0:T(8,128)(2,1)} %param.13) | copy-start | bytes 2088964
  0.6 24.0 %copy-start.10 = (bf16[192,640]{1,0:T(8,128)(2,1)S(1)}, bf16[192,640]{1,0:T(8,128)(2,1)}, u32[]{:S(2)}) copy-start(bf16[192,640]{1,0:T(8,128)(2,1)} %prompt.3) | copy-start | bytes 737284
  0.6 24.0 %copy-start.13 = (bf16[1,2560,192]{1,2,0:T(8,128)(2,1)S(1)}, bf16[1,2560,192]{1,2,0:T(8,128)(2,1)}, u32[]{:S(2)}) copy-start(bf16[1,2560,192]{1,2,0:T(8,128)(2,1)} %param.11) | copy-start | bytes 2949124
  2.5 12.5 %collective-permute-start = (bf16[192,640]{1,0:T(8,128)(2,1)}, bf16[192,640]{1,0:T(8,128)(2,1)S(1)}, u32[]{:S(2)}, u32[]{:S(2)}) collective-permute-start(bf16[192,640]{1,0:T(8,128)(2,1)} %shard_map.104), channel_id=1, source_target_pairs={{0,4},{4,0},{8,12},{12,8},{16,20},{20,16},{24,28},{28,24},{1,5},{5... | collective-permute-start | bytes 737288 | tf_op jit(solution)/shard_map/ppermute | solution.py:461
  4.1 20.5 %collective-permute-start.1 = (bf16[192,640]{1,0:T(8,128)(2,1)}, bf16[192,640]{1,0:T(8,128)(2,1)S(1)}, u32[]{:S(2)}, u32[]{:S(2)}) collective-permute-start(bf16[192,640]{1,0:T(8,128)(2,1)} %shard_map.104), channel_id=1, source_target_pairs={{0,8},{4,12},{8,0},{12,4},{16,24},{20,28},{24,16},{28,20},{1,9},{5... | collective-permute-start | bytes 737288 | tf_op jit(solution)/shard_map/ppermute | solution.py:461
  6.7 17.9 %collective-permute-start.2 = (bf16[192,640]{1,0:T(8,128)(2,1)}, bf16[192,640]{1,0:T(8,128)(2,1)S(1)}, u32[]{:S(2)}, u32[]{:S(2)}) collective-permute-start(bf16[192,640]{1,0:T(8,128)(2,1)} %shard_map.104), channel_id=1, source_target_pairs={{0,12},{4,8},{8,4},{12,0},{16,28},{20,24},{24,20},{28,16},{1,13},{... | collective-permute-start | bytes 737288 | tf_op jit(solution)/shard_map/ppermute | solution.py:461
  24.7 16.4 %copy-start = (bf16[1,512,2560]{2,1,0:T(8,128)(2,1)S(1)}, bf16[1,512,2560]{2,1,0:T(8,128)(2,1)}, u32[]{:S(2)}) copy-start(bf16[1,512,2560]{2,1,0:T(8,128)(2,1)} %param.16) | copy-start | bytes 7864324
  24.7 16.4 %copy-start.2 = (bf16[1,768,640]{2,1,0:T(8,128)(2,1)S(1)}, bf16[1,768,640]{2,1,0:T(8,128)(2,1)}, u32[]{:S(2)}) copy-start(bf16[1,768,640]{2,1,0:T(8,128)(2,1)} %param.12) | copy-start | bytes 2949124
  24.7 16.4 %copy-start.4 = (bf16[1,512,512]{2,1,0:T(8,128)(2,1)S(1)}, bf16[1,512,512]{2,1,0:T(8,128)(2,1)}, u32[]{:S(2)}) copy-start(bf16[1,512,512]{2,1,0:T(8,128)(2,1)} %param.14) | copy-start | bytes 1572868
  24.7 16.4 %copy-start.6 = (bf16[1,512,512]{2,1,0:T(8,128)(2,1)S(1)}, bf16[1,512,512]{2,1,0:T(8,128)(2,1)}, u32[]{:S(2)}) copy-start(bf16[1,512,512]{2,1,0:T(8,128)(2,1)} %param.15) | copy-start | bytes 1572868
  24.7 16.4 %copy-start.9 = (f32[192,32]{1,0:T(8,128)S(1)}, f32[192,32]{1,0:T(8,128)}, u32[]{:S(2)}) copy-start(f32[192,32]{1,0:T(8,128)} %constant.10.clone.angles) | copy-start | bytes 73732
  24.8 16.4 %copy-start.11 = (s32[8]{0:T(128)S(1)}, s32[8]{0:T(128)}, u32[]{:S(2)}) copy-start(s32[8]{0:T(128)} %sizes.3) | copy-start | bytes 100
  24.8 8.7 %collective-permute-start.3 = (bf16[256,256]{1,0:T(8,128)(2,1)S(1)}, bf16[256,256]{1,0:T(8,128)(2,1)S(1)}, u32[]{:S(2)}, u32[]{:S(2)}) collective-permute-start(bf16[256,256]{1,0:T(8,128)(2,1)S(1)} %shard_map.105.own), channel_id=1, source_target_pairs={{0,4},{4,0},{8,12},{12,8},{16,20},{20,16},{24,28},{28,24},{1,5},{5... | collective-permute-start | bytes 393224 | tf_op jit(solution)/shard_map/ppermute | solution.py:461
  29.3 11.8 %collective-permute-start.4 = (bf16[256,256]{1,0:T(8,128)(2,1)S(1)}, bf16[256,256]{1,0:T(8,128)(2,1)S(1)}, u32[]{:S(2)}, u32[]{:S(2)}) collective-permute-start(bf16[256,256]{1,0:T(8,128)(2,1)S(1)} %shard_map.105.own), channel_id=1, source_target_pairs={{0,8},{4,12},{8,0},{12,4},{16,24},{20,28},{24,16},{28,20},{1,9},{5... | collective-permute-start | bytes 393224 | tf_op jit(solution)/shard_map/ppermute | solution.py:461
  30.4 10.7 %collective-permute-start.5 = (bf16[256,256]{1,0:T(8,128)(2,1)S(1)}, bf16[256,256]{1,0:T(8,128)(2,1)S(1)}, u32[]{:S(2)}, u32[]{:S(2)}) collective-permute-start(bf16[256,256]{1,0:T(8,128)(2,1)S(1)} %shard_map.105.own), channel_id=1, source_target_pairs={{0,12},{4,8},{8,4},{12,0},{16,28},{20,24},{24,20},{28,16},{1,13},{... | collective-permute-start | bytes 393224 | tf_op jit(solution)/shard_map/ppermute | solution.py:461
  41.8 37.3 %collective-permute-start.10 = (bf16[4,136,1280]{2,1,0:T(8,128)(2,1)S(1)}, bf16[4,136,1280]{2,1,0:T(8,128)(2,1)S(1)}, u32[]{:S(2)}, u32[]{:S(2)}) collective-permute-start(bf16[4,136,1280]{2,1,0:T(8,128)(2,1)S(1)} %get-tuple-element.20.half), channel_id=1, source_target_pairs={{0,1},{1,0},{2,3},{3,2},{4,5},{5,4},{6,7},{7,6},{8,9},{9,8},{10,11... | collective-permute-start | bytes 4177928 | tf_op jit(solution)/shard_map/ppermute | solution.py:468
  41.9 13.5 %collective-permute-start.6 = (bf16[56,2560]{1,0:T(8,128)(2,1)S(1)}, bf16[56,2560]{1,0:T(8,128)(2,1)S(1)}, u32[]{:S(2)}, u32[]{:S(2)}) collective-permute-start(bf16[56,2560]{1,0:T(8,128)(2,1)S(1)} %get-tuple-element.16), channel_id=1, source_target_pairs={{0,28},{4,24},{8,20},{12,16},{16,0},{20,4},{24,8},{28,12},{1,29},{... | collective-permute-start | bytes 860168 | tf_op jit(solution)/shard_map/ppermute | solution.py:465
  46.2 32.9 %collective-permute-start.7 = (bf16[56,2560]{1,0:T(8,128)(2,1)S(1)}, bf16[56,2560]{1,0:T(8,128)(2,1)S(1)}, u32[]{:S(2)}, u32[]{:S(2)}) collective-permute-start(bf16[56,2560]{1,0:T(8,128)(2,1)S(1)} %get-tuple-element.17), channel_id=1, source_target_pairs={{0,24},{4,28},{8,16},{12,20},{16,0},{20,4},{24,8},{28,12},{1,25},{... | collective-permute-start | bytes 860168 | tf_op jit(solution)/shard_map/ppermute | solution.py:465
  46.3 32.8 %collective-permute-start.8 = (bf16[56,2560]{1,0:T(8,128)(2,1)S(1)}, bf16[56,2560]{1,0:T(8,128)(2,1)S(1)}, u32[]{:S(2)}, u32[]{:S(2)}) collective-permute-start(bf16[56,2560]{1,0:T(8,128)(2,1)S(1)} %get-tuple-element.18), channel_id=1, source_target_pairs={{0,20},{4,16},{8,28},{12,24},{16,0},{20,4},{24,8},{28,12},{1,21},{... | collective-permute-start | bytes 860168 | tf_op jit(solution)/shard_map/ppermute | solution.py:465
  50.5 28.6 %collective-permute-start.9 = (bf16[56,2560]{1,0:T(8,128)(2,1)S(1)}, bf16[56,2560]{1,0:T(8,128)(2,1)S(1)}, u32[]{:S(2)}, u32[]{:S(2)}) collective-permute-start(bf16[56,2560]{1,0:T(8,128)(2,1)S(1)} %get-tuple-element.19), channel_id=1, source_target_pairs={{0,16},{4,20},{8,24},{12,28},{16,0},{20,4},{24,8},{28,12},{1,17},{... | collective-permute-start | bytes 860168 | tf_op jit(solution)/shard_map/ppermute | solution.py:465
  79.1 10.2 %copy-start.3 = (bf16[1,768,640]{2,1,0:T(8,128)(2,1)S(1)}, bf16[1,768,640]{2,1,0:T(8,128)(2,1)}, u32[]{:S(2)}) copy-start(bf16[1,768,640]{2,1,0:T(8,128)(2,1)} %param.12) | copy-start | bytes 2949124
  79.1 10.2 %copy-start.5 = (bf16[1,512,512]{2,1,0:T(8,128)(2,1)S(1)}, bf16[1,512,512]{2,1,0:T(8,128)(2,1)}, u32[]{:S(2)}) copy-start(bf16[1,512,512]{2,1,0:T(8,128)(2,1)} %param.14) | copy-start | bytes 1572868
  79.1 10.2 %copy-start.7 = (bf16[1,512,512]{2,1,0:T(8,128)(2,1)S(1)}, bf16[1,512,512]{2,1,0:T(8,128)(2,1)}, u32[]{:S(2)}) copy-start(bf16[1,512,512]{2,1,0:T(8,128)(2,1)} %param.15) | copy-start | bytes 1572868
  79.1 10.2 %copy-start.12 = (s32[8]{0:T(128)S(1)}, s32[8]{0:T(128)}, u32[]{:S(2)}) copy-start(s32[8]{0:T(128)} %sizes.3) | copy-start | bytes 100
  80.8 5.0 %collective-permute-start.12 = (bf16[56,512]{1,0:T(8,128)(2,1)S(1)}, bf16[56,512]{1,0:T(8,128)(2,1)S(1)}, u32[]{:S(2)}, u32[]{:S(2)}) collective-permute-start(bf16[56,512]{1,0:T(8,128)(2,1)S(1)} %get-tuple-element.23.own), channel_id=1, source_target_pairs={{0,4},{4,0},{8,12},{12,8},{16,20},{20,16},{24,28},{28,24},{1,5},{5... | collective-permute-start | bytes 172040 | tf_op jit(solution)/shard_map/ppermute | solution.py:461
  80.8 7.4 %collective-permute-start.13 = (bf16[56,512]{1,0:T(8,128)(2,1)S(1)}, bf16[56,512]{1,0:T(8,128)(2,1)S(1)}, u32[]{:S(2)}, u32[]{:S(2)}) collective-permute-start(bf16[56,512]{1,0:T(8,128)(2,1)S(1)} %get-tuple-element.23.own), channel_id=1, source_target_pairs={{0,8},{4,12},{8,0},{12,4},{16,24},{20,28},{24,16},{28,20},{1,9},{5... | collective-permute-start | bytes 172040 | tf_op jit(solution)/shard_map/ppermute | solution.py:461
  83.2 6.1 %collective-permute-start.14 = (bf16[56,512]{1,0:T(8,128)(2,1)S(1)}, bf16[56,512]{1,0:T(8,128)(2,1)S(1)}, u32[]{:S(2)}, u32[]{:S(2)}) collective-permute-start(bf16[56,512]{1,0:T(8,128)(2,1)S(1)} %get-tuple-element.23.own), channel_id=1, source_target_pairs={{0,12},{4,8},{8,4},{12,0},{16,28},{20,24},{24,20},{28,16},{1,13},{... | collective-permute-start | bytes 172040 | tf_op jit(solution)/shard_map/ppermute | solution.py:461
  85.2 13.6 %collective-permute-start.11 = (bf16[8,640]{1,0:T(8,128)(2,1)S(1)}, bf16[8,640]{1,0:T(8,128)(2,1)S(1)}, u32[]{:S(2)}, u32[]{:S(2)}) collective-permute-start(bf16[8,640]{1,0:T(8,128)(2,1)S(1)} %get-tuple-element.22), channel_id=1, source_target_pairs={{0,16},{4,20},{8,24},{12,28},{16,0},{20,4},{24,8},{28,12},{1,17},{... | collective-permute-start | bytes 30728 | tf_op jit(solution)/shard_map/ppermute | solution.py:465
  89.3 1.7 %copy-start.1 = (bf16[1,512,2560]{2,1,0:T(8,128)(2,1)S(1)}, bf16[1,512,2560]{2,1,0:T(8,128)(2,1)}, u32[]{:S(2)}) copy-start(bf16[1,512,2560]{2,1,0:T(8,128)(2,1)} %param.16) | copy-start | bytes 7864324
  93.7 5.5 %collective-permute-start.17 = (bf16[8,640]{1,0:T(8,128)(2,1)S(1)}, bf16[8,640]{1,0:T(8,128)(2,1)S(1)}, u32[]{:S(2)}, u32[]{:S(2)}) collective-permute-start(bf16[8,640]{1,0:T(8,128)(2,1)S(1)} %get-tuple-element.27), channel_id=1, source_target_pairs={{0,12},{4,8},{8,4},{12,0},{16,28},{20,24},{24,20},{28,16},{1,13},{... | collective-permute-start | bytes 30728 | tf_op jit(solution)/shard_map/ppermute | solution.py:461
  95.8 4.6 %collective-permute-start.16 = (bf16[8,640]{1,0:T(8,128)(2,1)S(1)}, bf16[8,640]{1,0:T(8,128)(2,1)S(1)}, u32[]{:S(2)}, u32[]{:S(2)}) collective-permute-start(bf16[8,640]{1,0:T(8,128)(2,1)S(1)} %get-tuple-element.26), channel_id=1, source_target_pairs={{0,8},{4,12},{8,0},{12,4},{16,24},{20,28},{24,16},{28,20},{1,9},{5... | collective-permute-start | bytes 30728 | tf_op jit(solution)/shard_map/ppermute | solution.py:461
  95.9 4.4 %collective-permute-start.15 = (bf16[8,640]{1,0:T(8,128)(2,1)S(1)}, bf16[8,640]{1,0:T(8,128)(2,1)S(1)}, u32[]{:S(2)}, u32[]{:S(2)}) collective-permute-start(bf16[8,640]{1,0:T(8,128)(2,1)S(1)} %get-tuple-element.25), channel_id=1, source_target_pairs={{0,4},{4,0},{8,12},{12,8},{16,20},{20,16},{24,28},{28,24},{1,5},{5... | collective-permute-start | bytes 30728 | tf_op jit(solution)/shard_map/ppermute | solution.py:461

commit v5 on v4

--- a/solution.py
+++ b/solution.py
@@ -216,51 +216,39 @@
     return out
 
 
-def send_kernel(prompt, w_latent, out, half, packed, sem):
+def send_kernel(prompt, w_latent, out, other, half, packed, sems):
     section, rep = lax.axis_index("section"), lax.axis_index("rep")
-    width = out.shape[1]
-    cols = half.shape[0]
+    rows, width = out.shape
+    cols, long = half.shape
 
     @pl.when(section == 0)
     def _():
-        copy = pltpu.make_async_copy(prompt, packed, sem)
+        copy = pltpu.make_async_copy(prompt, packed.at[0], sems.at[0])
         copy.start()
         copy.wait()
-        copy = pltpu.make_async_copy(packed, out, sem)
+        packed[1] = packed[0]
+
+    @pl.when(section != 0)
+    def _():
+        columns = pl.ds(pl.multiple_of((rep & 1) * long, 128), long)
+        copy = pltpu.make_async_copy(w_latent.at[:, columns], half, sems.at[0])
         copy.start()
         copy.wait()
-
-    @pl.when(section != 0)
-    def _():
-        columns = pl.ds(pl.multiple_of((rep & 1) * half.shape[1], 128), half.shape[1])
-        copy = pltpu.make_async_copy(w_latent.at[:, columns], half, sem)
+        rest = jnp.zeros((rows - cols, width), F32)
+        for i in range(2):
+            piece = half[:, i * width : (i + 1) * width].astype(F32)
+            packed[i] = jnp.concatenate([piece, rest], axis=0).astype(BF16)
+
+    copies = [
+        pltpu.make_async_copy(packed.at[i], ref, sems.at[i]) for i, ref in enumerate((out, other))
+    ]
+    for copy in copies:
         copy.start()
+    for copy in copies:
         copy.wait()
-        extra = half[:, width : width + 256].astype(F32)
-        rows = out.shape[0] - cols
-        left = cols - 2 * rows
-        tail = [extra[2 * rows :, :128], extra[2 * rows :, 128:], jnp.zeros((rows - 2 * left, 128), F32)]
-        extra = jnp.concatenate(
-            [extra[:rows], extra[rows : 2 * rows], jnp.concatenate(tail, axis=0)], axis=1
-        )
-        whole = jnp.concatenate([half[:, :width].astype(F32), extra], axis=0)
-        packed[...] = whole.astype(BF16)
-        copy = pltpu.make_async_copy(packed, out, sem)
-        copy.start()
-        copy.wait()
-
-
-def unpack_share(share, cols):
-    share = share.astype(F32)
-    rows = share.shape[0] - cols
-    left = cols - 2 * rows
-    extra, tail = share[cols:, :512], share[cols:, 512:]
-    tail = jnp.concatenate([tail[:left], tail[left : 2 * left]], axis=1)
-    extra = jnp.concatenate([extra[:, :256], extra[:, 256:], tail], axis=0)
-    return jnp.concatenate([share[:cols], extra], axis=1).astype(BF16)
-
-
-def down_kernel(own, one, two, three, w_down, w_latent, out):
+
+
+def down_kernel(own, two, three, one, w_down, w_latent, out):
     section, tp, rep = (lax.axis_index(a) for a in ("section", "tp", "rep"))
     tokens, share = own.shape
     cols, model = w_latent.shape
@@ -285,7 +273,7 @@
 
     @pl.when(section != 0)
     def _():
-        first = (rep & 1) * (model // 2) + share + 256
+        first = ((rep & 1) + 1) * (model // 2) - 384
         mine = w_latent[:, pl.ds(pl.multiple_of(first, 128), 384)].astype(F32)
         rest = mine[:, 256:]
         high = cols // 2 + 4
@@ -330,21 +318,23 @@
 
 
 def layer_kernel(
-    sizes, own, one, two, three, share1, share2, share3, w_latent, prompt, angles,
-    w_query, w_keys, w_values, w_out, out0, out1, out2, out3, own_cache, half, stack, total, cached,
+    sizes, own, one, two, three, share1, share3, w_latent, prompt, angles,
+    w_query, w_keys, w_values, w_out, out0, out1, out2, out3, own_cache, passed, rest, stack, total, cached,
 ):
     section, tp, rep = (lax.axis_index(a) for a in ("section", "tp", "rep"))
     tokens, width = prompt.shape
     block = tokens // 4
-    cols, long = half.shape[1:]
+    cols, early = passed.shape[1:]
     down_cols = w_query.shape[0] // 4
 
     @pl.when(section != 0)
     def _():
-        half[tp] = w_latent[:, pl.ds(pl.multiple_of((rep & 1) * long, 128), long)]
-        for k, weights, rest in ((1, share1, one), (2, share2, two), (3, share3, three)):
-            half[tp ^ k, :, : width + 256] = unpack_share(weights[...], cols)
-            half[tp ^ k, :, width + 256 :] = unpack_rest(rest[...], cols)
+        first = (rep & 1) * (early + rest.shape[2])
+        passed[0] = w_latent[:, pl.ds(pl.multiple_of(first, 128), early)]
+        passed[1, :, :width] = share3[:cols, :]
+        passed[1, :, width:] = share1[:cols, : early - width]
+        rest[0] = unpack_rest(two[...], cols)
+        rest[1] = unpack_rest(three[...], cols)
 
     @pl.when(section == 0)
     def _():
@@ -379,23 +369,37 @@
 
 
 def latent_kernel(
-    one, two, three, four, angles, half, near, w_down, out, own_cache, own_ends, hidden
+    one, two, three, four, angles, w_latent, share3, share1, near3, near1, passed, near_two, near_three,
+    rest, near_rest, w_down, out, own_cache, own_ends, hidden, parts,
 ):
     tp, rep = lax.axis_index("tp"), lax.axis_index("rep")
     block = angles.shape[0] // 4
     width = own_ends.shape[1]
+    cols, model = w_latent.shape
+    early = passed.shape[2]
     rows = one[...].astype(F32) + two[...].astype(F32) + three[...].astype(F32) + four[...].astype(F32)
     narrow = rows.astype(BF16)
     rows = narrow.astype(F32)
     hidden[...] = rows
     scale = unit(rows)
-    totals = [0.0] * 4
-    for step, weights in enumerate((half, near)):
-        long = weights.shape[2]
-        columns = pl.ds(pl.multiple_of(((rep & 1) ^ step) * long, 128), long)
-        piece = hidden[0:block, columns].astype(BF16)
-        totals = [total + dot_t(piece, weights[m]) for m, total in enumerate(totals)]
-    latent = jnp.concatenate(totals, axis=1) * scale[:block]
+    parts[tp] = dot_t(narrow[:block], w_latent[...])
+    sums = [0.0, 0.0, 0.0]
+    for core, (lower, upper, from_two, from_three, late) in enumerate(
+        ((share3, share1, passed.at[0], passed.at[1], rest), (near3, near1, near_two, near_three, near_rest))
+    ):
+        first = ((rep & 1) ^ core) * (model // 2)
+
+        def piece(start, size):
+            columns = pl.ds(pl.multiple_of(first + start, 128), size)
+            return hidden[0:block, columns].astype(BF16)
+
+        sums[0] += dot_t(piece(0, width), lower[:cols, :]) + dot_t(piece(width, width), upper[:cols, :])
+        head, tail = piece(0, early), piece(early, model // 2 - early)
+        sums[1] += dot_t(head, from_two[...]) + dot_t(tail, late[0])
+        sums[2] += dot_t(head, from_three[...]) + dot_t(tail, late[1])
+    for k, value in enumerate(sums):
+        parts[tp ^ (k + 1)] = value
+    latent = jnp.concatenate([parts[m] for m in range(4)], axis=1) * scale[:block]
     plain = latent[:, :LATENT]
     plain = plain * unit(plain)
     own_angles = angles[pl.ds(pl.multiple_of(tp * block, block), block), :]
@@ -456,49 +460,57 @@
     angles = np.arange(tokens, dtype=np.float32)[:, None] * frequency.astype(np.float32)[None, :]
     angles = jnp.asarray(np.concatenate([np.cos(angles), np.sin(angles)], axis=1), F32)
 
+    def route(array, *ways):
+        pairs = [
+            (s * 4 + i, way[0] * 4 + (i ^ way[1])) for s, way in enumerate(ways) if way for i in range(4)
+        ]
+        return lax.ppermute(array, ("section", "tp"), pairs)
+
     def within(array, k):
-        pairs = [(s * 4 + i, s * 4 + (i ^ k)) for s in range(2) for i in range(4)]
-        return lax.ppermute(array, ("section", "tp"), pairs)
+        return route(array, (0, k), (1, k))
 
     def onward(array, k):
-        pairs = [(i, 4 + (i ^ k)) for i in range(4)] + [(4 + i, i) for i in range(4)]
-        return lax.ppermute(array, ("section", "tp"), pairs)
+        return route(array, (1, k), (0, 0))
 
     def over_rep(array, k):
         return lax.ppermute(array, "rep", [(i, i ^ k) for i in range(4)])
 
     sent = call(
         send_kernel,
-        jax.ShapeDtypeStruct((tokens, share), BF16),
+        [jax.ShapeDtypeStruct((tokens, share), BF16)] * 2,
         [prompt, w_lat],
         [
             pltpu.VMEM((latent_cols, model // 2), BF16),
-            pltpu.VMEM((tokens, share), BF16),
-            pltpu.SemaphoreType.DMA,
+            pltpu.VMEM((2, tokens, share), BF16),
+            pltpu.SemaphoreType.DMA((2,)),
         ],
         left=2,
         space=HBM,
         grant=57,
         flops=2 * 10**10,
     )
-    shares = [within(sent, k) for k in (1, 2, 3)]
+    two = route(prompt, (1, 0), (0, 2))
+    three = route(sent[0], (0, 3), (1, 1))
+    one = route(sent[1], (0, 1), (1, 1))
     parts = call(
         down_kernel,
         jax.ShapeDtypeStruct((tokens + tokens // 3, 256), BF16),
-        [prompt, *shares, w_down, w_lat],
+        [prompt, two, three, one, w_down, w_lat],
         flops=2 * 10**10,
     )
     pieces = [parts] + [within(parts, k) for k in (1, 2, 3)]
+    near = [over_rep(three, 1), over_rep(one, 1)]
 
     message = jax.ShapeDtypeStruct((block + count, model), BF16)
-    *blocks, first_cache, half = call(
+    *blocks, first_cache, passed, rest = call(
         layer_kernel,
         [message] * 4
         + [
             jax.ShapeDtypeStruct((block, ROW_WIDTH), BF16),
-            jax.ShapeDtypeStruct((4, latent_cols, model // 2), BF16),
+            jax.ShapeDtypeStruct((2, latent_cols, model // 2 - 384), BF16),
+            jax.ShapeDtypeStruct((2, latent_cols, 384), BF16),
         ],
-        [block_sizes, *pieces, *shares, w_lat, prompt, angles, w_up, w_key, w_value, w_final],
+        [block_sizes, *pieces, one, three, w_lat, prompt, angles, w_up, w_key, w_value, w_final],
         [
             pltpu.VMEM((4, *parts.shape), BF16),
             pltpu.VMEM((tokens + count, model), F32),
@@ -509,7 +521,8 @@
         grant=16,
     )
     arrived = [onward(blocks[k], k) for k in (3, 2, 1, 0)]
-    near = over_rep(half, 1)
+    passed = route(passed, None, (1, 2))
+    near += [passed, over_rep(passed[0], 1), over_rep(passed[1], 1), rest, over_rep(rest, 1)]
     fresh, last_cache, ends_share = call(
         latent_kernel,
         [
@@ -517,8 +530,8 @@
             jax.ShapeDtypeStruct((block, ROW_WIDTH), BF16),
             jax.ShapeDtypeStruct((count, share), BF16),
         ],
-        [*arrived, angles, half, near, w_down],
-        [pltpu.VMEM((block + count, model), F32)],
+        [*arrived, angles, w_lat, three, one, *near, w_down],
+        [pltpu.VMEM((block + count, model), F32), pltpu.VMEM((4, block, latent_cols), F32)],
         flops=2 * 10**11,
     )
     pieces = [fresh] + [within(fresh, k) for k in (1, 2, 3)]

time: 101 us -> 94.6 us (0.937)
  waiting for transfers between devices: 61.2 us -> 55.3 us
  starting transfers between devices: 29 us -> 27.4 us
    ppermute x17 -> x18, waiting for transfers between devices: 61.2 us -> 53.9 us  [route(): return lax.ppermute(array, ('section', 'tp'), pairs)]
    ppermute x17 -> x18, starting transfers between devices: 28.9 us -> 26.3 us  [route(): return lax.ppermute(array, ('section', 'tp'), pairs)]
    ppermute x1 -> x5, waiting for transfers between devices: 0.01 us -> 1.42 us  [over_rep(): return lax.ppermute(array, 'rep', [(i, i ^ k) for i in range(4)])]
    ppermute x1 -> x5, starting transfers between devices: 0.07 us -> 1.08 us  [over_rep(): return lax.ppermute(array, 'rep', [(i, i ^ k) for i in range(4)])]
  transfers between devices with their start and end apart: 18 -> 23, of which waited for: 11 -> 12; matrix products, arithmetic and copies ran while one was open for 1% -> 1% of each run, Pallas kernels for 3% -> 5%
where the time goes in v5:
time: 94.6 us; the launch traced here: 94.4 us
  waiting for transfers between devices  55.3 us (58%)
  starting transfers between devices  27.4 us (29%)
  Pallas kernels  7.15 us (8%)
  local copies, waits for them, and re-layouts  2.35 us (2%)
  other arithmetic  1.25 us (1%)
    ppermute x18, waiting for transfers between devices, route(): return lax.ppermute(array, ('section', 'tp'), pairs)  53.9 us
    ppermute x18, starting transfers between devices, route(): return lax.ppermute(array, ('section', 'tp'), pairs)  26.3 us
    pallas_call x5, Pallas kernels, call(): pl.pallas_call(kernel, out_shape=out_shape, in_specs=[SMEM] * scalars + [...  7.15 us
    unnamed x28, local copies, waits for them, and re-layouts  2.31 us
  transfers between devices with their start and end apart: 23, of which 12 were waited for; matrix products, arithmetic and copies ran while one was open for 1% of the time, Pallas kernels for 5%

profile of v5, /device:TPU:4, one launch (start us, length us, event | category | flops | bytes accessed | tf_op | source)
XLA Modules:
  0.0 94.4 jit_solution(3533756693412120763)
XLA Ops:
  0.6 2.6 %collective-permute-start = (bf16[192,640]{1,0:T(8,128)(2,1)}, bf16[192,640]{1,0:T(8,128)(2,1)S(1)}, u32[]{:S(2)}, u32[]{:S(2)}) collective-permute-start(bf16[192,640]{1,0:T(8,128)(2,1)} %prompt.3), channel_id=1, source_target_pairs={{0,16},{4,20},{8,24},{12,28},{16,8},{20,12},{24,0},{28,4},{1,17},{... | collective-permute-start | bytes 737288 | tf_op jit(solution)/shard_map/ppermute | solution.py:467
  3.2 2.0 %shard_map.104 = (bf16[192,640]{1,0:T(8,128)(2,1)}, bf16[192,640]{1,0:T(8,128)(2,1)}) custom-call(bf16[192,640]{1,0:T(8,128)(2,1)} %prompt.3, bf16[136,2560]{1,0:T(8,128)(2,1)} %bitcast.26), custom_call_target="tpu_custom_call" | custom-call | flops 20000000000 | bytes 942080 | tf_op jit(solution)/shard_map/pallas_call | solution.py:179
  5.2 1.6 %collective-permute-start.1 = (bf16[192,640]{1,0:T(8,128)(2,1)}, bf16[192,640]{1,0:T(8,128)(2,1)S(1)}, u32[]{:S(2)}, u32[]{:S(2)}) collective-permute-start(bf16[192,640]{1,0:T(8,128)(2,1)} %get-tuple-element.18), channel_id=1, source_target_pairs={{0,12},{4,8},{8,4},{12,0},{16,20},{20,16},{24,28},{28,24},{1,13},{... | collective-permute-start | bytes 737288 | tf_op jit(solution)/shard_map/ppermute | solution.py:467
  6.8 0.4 collective-permute-start.2
  7.3 2.7 %collective-permute-done.two = bf16[192,640]{1,0:T(8,128)(2,1)S(1)} collective-permute-done((bf16[192,640]{1,0:T(8,128)(2,1)}, bf16[192,640]{1,0:T(8,128)(2,1)S(1)}, u32[]{:S(2)}, u32[]{:S(2)}) %collective-permute-start) | collective-permute-done | bytes 245792 | tf_op jit(solution)/shard_map/ppermute | solution.py:467
  9.9 8.6 %collective-permute-done.1.three.share3 = bf16[192,640]{1,0:T(8,128)(2,1)S(1)} collective-permute-done((bf16[192,640]{1,0:T(8,128)(2,1)}, bf16[192,640]{1,0:T(8,128)(2,1)S(1)}, u32[]{:S(2)}, u32[]{:S(2)}) %collective-permute-start.1) | collective-permute-done | bytes 245792 | tf_op jit(solution)/shard_map/ppermute | solution.py:467
  18.5 3.8 %collective-permute-done.2.one.share1 = bf16[192,640]{1,0:T(8,128)(2,1)S(1)} collective-permute-done((bf16[192,640]{1,0:T(8,128)(2,1)}, bf16[192,640]{1,0:T(8,128)(2,1)S(1)}, u32[]{:S(2)}, u32[]{:S(2)}) %collective-permute-start.2) | collective-permute-done | bytes 245792 | tf_op jit(solution)/shard_map/ppermute | solution.py:467
  22.3 0.0 copy-start
  22.3 0.0 copy-start.2
  22.3 0.0 copy-start.4
  22.3 0.0 copy-start.6
  22.4 0.0 copy-start.9
  22.4 0.0 copy-start.11
  22.4 0.1 collective-permute-start.3
  22.5 3.0 %collective-permute-start.4 = (bf16[256,256]{1,0:T(8,128)(2,1)S(1)}, bf16[256,256]{1,0:T(8,128)(2,1)S(1)}, u32[]{:S(2)}, u32[]{:S(2)}) collective-permute-start(bf16[256,256]{1,0:T(8,128)(2,1)S(1)} %shard_map.105.own), channel_id=1, source_target_pairs={{0,8},{4,12},{8,0},{12,4},{16,24},{20,28},{24,16},{28,20},{1,9},{5... | collective-permute-start | bytes 393224 | tf_op jit(solution)/shard_map/ppermute | solution.py:467
  25.5 1.4 %collective-permute-start.5 = (bf16[256,256]{1,0:T(8,128)(2,1)S(1)}, bf16[256,256]{1,0:T(8,128)(2,1)S(1)}, u32[]{:S(2)}, u32[]{:S(2)}) collective-permute-start(bf16[256,256]{1,0:T(8,128)(2,1)S(1)} %shard_map.105.own), channel_id=1, source_target_pairs={{0,12},{4,8},{8,4},{12,0},{16,28},{20,24},{24,20},{28,16},{1,13},{... | collective-permute-start | bytes 393224 | tf_op jit(solution)/shard_map/ppermute | solution.py:467
  26.9 1.7 %collective-permute-done.3.one = bf16[256,256]{1,0:T(8,128)(2,1)S(1)} collective-permute-done((bf16[256,256]{1,0:T(8,128)(2,1)S(1)}, bf16[256,256]{1,0:T(8,128)(2,1)S(1)}, u32[]{:S(2)}, u32[]{:S(2)}) %collective-permute-start.3) | collective-permute-done | bytes 131104 | tf_op jit(solution)/shard_map/ppermute | solution.py:467
  28.5 6.1 %collective-permute-done.4.two = bf16[256,256]{1,0:T(8,128)(2,1)S(1)} collective-permute-done((bf16[256,256]{1,0:T(8,128)(2,1)S(1)}, bf16[256,256]{1,0:T(8,128)(2,1)S(1)}, u32[]{:S(2)}, u32[]{:S(2)}) %collective-permute-start.4) | collective-permute-done | bytes 131104 | tf_op jit(solution)/shard_map/ppermute | solution.py:467
  34.7 0.6 shard_map.106
  35.3 4.8 %collective-permute-start.12 = (bf16[2,136,896]{2,1,0:T(8,128)(2,1)S(1)}, bf16[2,136,896]{2,1,0:T(8,128)(2,1)S(1)}, u32[]{:S(2)}, u32[]{:S(2)}) collective-permute-start(bf16[2,136,896]{2,1,0:T(8,128)(2,1)S(1)} %get-tuple-element.25), channel_id=1, source_target_pairs={{16,24},{20,28},{24,16},{28,20},{17,25},{21,29},{25,17},{29,21},{1... | collective-permute-start | bytes 1462280 | tf_op jit(solution)/shard_map/ppermute | solution.py:467
  40.1 0.1 collective-permute-start.10
  40.2 0.5 collective-permute-start.11
  40.7 2.8 %collective-permute-start.7 = (bf16[56,2560]{1,0:T(8,128)(2,1)S(1)}, bf16[56,2560]{1,0:T(8,128)(2,1)S(1)}, u32[]{:S(2)}, u32[]{:S(2)}) collective-permute-start(bf16[56,2560]{1,0:T(8,128)(2,1)S(1)} %get-tuple-element.22), channel_id=1, source_target_pairs={{0,24},{4,28},{8,16},{12,20},{16,0},{20,4},{24,8},{28,12},{1,25},{... | collective-permute-start | bytes 860168 | tf_op jit(solution)/shard_map/ppermute | solution.py:467
  43.6 0.0 collective-permute-start.8
  43.6 0.6 collective-permute-start.9
  44.2 15.8 %collective-permute-done.12.passed = bf16[2,136,896]{2,1,0:T(8,128)(2,1)S(1)} collective-permute-done((bf16[2,136,896]{2,1,0:T(8,128)(2,1)S(1)}, bf16[2,136,896]{2,1,0:T(8,128)(2,1)S(1)}, u32[]{:S(2)}, u32[]{:S(2)}) %collective-permute-start.12) | collective-permute-done | bytes 487456 | tf_op jit(solution)/shard_map/ppermute | solution.py:467
  60.1 1.4 %collective-permute-done.15.near_rest = bf16[2,136,384]{2,1,0:T(8,128)(2,1)S(1)} collective-permute-done((bf16[2,136,384]{2,1,0:T(8,128)(2,1)S(1)}, bf16[2,136,384]{2,1,0:T(8,128)(2,1)S(1)}, u32[]{:S(2)}, u32[]{:S(2)}) %collective-permute-start.15) | collective-permute-done | bytes 208928 | tf_op jit(solution)/shard_map/ppermute | solution.py:476
  61.5 0.1 collective-permute-start.13
  61.6 0.4 collective-permute-start.14
  62.0 9.7 %collective-permute-done.7.two = bf16[56,2560]{1,0:T(8,128)(2,1)S(1)} collective-permute-done((bf16[56,2560]{1,0:T(8,128)(2,1)S(1)}, bf16[56,2560]{1,0:T(8,128)(2,1)S(1)}, u32[]{:S(2)}, u32[]{:S(2)}) %collective-permute-start.7) | collective-permute-done | bytes 286752 | tf_op jit(solution)/shard_map/ppermute | solution.py:467
  71.7 0.0 copy-start.1
  71.7 0.0 copy-start.5
  71.8 0.0 copy-start.12
  71.8 1.6 %shard_map.107 = (bf16[56,512]{1,0:T(8,128)(2,1)S(1)}, bf16[48,544]{1,0:T(8,128)(2,1)S(1)}, bf16[8,640]{1,0:T(8,128)(2,1)S(1)}) custom-call(bf16[56,2560]{1,0:T(8,128)(2,1)S(1)} %collective-permute-done.6.one, bf16[56,2560]{1,0:T(8,128)(2,1)S(1)} %collective-permute-done.7.two, bf16[56,2560]{1,0:T(8,128)(2,1)S(1)} %collective-permute-done.8.three, ...), custom_call_target="tpu_custom_call" | custom-call | flops 199999995904 | bytes 5226496 | tf_op jit(solution)/shard_map/pallas_call | solution.py:179
  73.4 0.1 collective-permute-start.17
  73.5 1.0 %collective-permute-start.18 = (bf16[56,512]{1,0:T(8,128)(2,1)S(1)}, bf16[56,512]{1,0:T(8,128)(2,1)S(1)}, u32[]{:S(2)}, u32[]{:S(2)}) collective-permute-start(bf16[56,512]{1,0:T(8,128)(2,1)S(1)} %get-tuple-element.29.own), channel_id=1, source_target_pairs={{0,8},{4,12},{8,0},{12,4},{16,24},{20,28},{24,16},{28,20},{1,9},{5... | collective-permute-start | bytes 172040 | tf_op jit(solution)/shard_map/ppermute | solution.py:467
  74.4 3.4 %collective-permute-start.19 = (bf16[56,512]{1,0:T(8,128)(2,1)S(1)}, bf16[56,512]{1,0:T(8,128)(2,1)}, u32[]{:S(2)}, u32[]{:S(2)}) collective-permute-start(bf16[56,512]{1,0:T(8,128)(2,1)S(1)} %get-tuple-element.29.own), channel_id=1, source_target_pairs={{0,12},{4,8},{8,4},{12,0},{16,28},{20,24},{24,20},{28,16},{1,13},{... | collective-permute-start | bytes 172040 | tf_op jit(solution)/shard_map/ppermute | solution.py:467
  77.8 1.5 %collective-permute-done.18.two = bf16[56,512]{1,0:T(8,128)(2,1)S(1)} collective-permute-done((bf16[56,512]{1,0:T(8,128)(2,1)S(1)}, bf16[56,512]{1,0:T(8,128)(2,1)S(1)}, u32[]{:S(2)}, u32[]{:S(2)}) %collective-permute-start.18) | collective-permute-done | bytes 57376 | tf_op jit(solution)/shard_map/ppermute | solution.py:467
  79.3 1.5 %collective-permute-done.19.three = bf16[56,512]{1,0:T(8,128)(2,1)} collective-permute-done((bf16[56,512]{1,0:T(8,128)(2,1)S(1)}, bf16[56,512]{1,0:T(8,128)(2,1)}, u32[]{:S(2)}, u32[]{:S(2)}) %collective-permute-start.19) | collective-permute-done | bytes 57376 | tf_op jit(solution)/shard_map/ppermute | solution.py:467
  80.8 1.2 %copy-done.3 = bf16[1,768,640]{2,1,0:T(8,128)(2,1)S(1)} copy-done((bf16[1,768,640]{2,1,0:T(8,128)(2,1)S(1)}, bf16[1,768,640]{2,1,0:T(8,128)(2,1)}, u32[]{:S(2)}) %copy-start.3) | copy-done | bytes 983064
  82.0 1.0 %copy-done.7 = bf16[1,512,512]{2,1,0:T(8,128)(2,1)S(1)} copy-done((bf16[1,512,512]{2,1,0:T(8,128)(2,1)S(1)}, bf16[1,512,512]{2,1,0:T(8,128)(2,1)}, u32[]{:S(2)}) %copy-start.7) | copy-done | bytes 524312
  83.1 2.9 %shard_map.108 = (bf16[8,640]{1,0:T(8,128)(2,1)S(1)}, bf16[8,640]{1,0:T(8,128)(2,1)S(1)}, bf16[8,640]{1,0:T(8,128)(2,1)S(1)}, bf16[8,640]{1,0:T(8,128)(2,1)S(1)}) custom-call(s32[8]{0:T(128)S(1)} %copy-done.12, bf16[56,512]{1,0:T(8,128)(2,1)S(1)} %get-tuple-element.29.own, bf16[56,512]{1,0:T(8,128)(2,1)S(1)} %collective-permute-done.17.one, ...), custom_call_target="tpu_custom_call" | custom-call | flops 201326592 | bytes 4907040 | tf_op jit(solution)/shard_map/pallas_call | solution.py:179
  86.0 3.2 %collective-permute-start.22 = (bf16[8,640]{1,0:T(8,128)(2,1)S(1)}, bf16[8,640]{1,0:T(8,128)(2,1)S(1)}, u32[]{:S(2)}, u32[]{:S(2)}) collective-permute-start(bf16[8,640]{1,0:T(8,128)(2,1)S(1)} %get-tuple-element.33), channel_id=1, source_target_pairs={{0,12},{4,8},{8,4},{12,0},{16,28},{20,24},{24,20},{28,16},{1,13},{... | collective-permute-start | bytes 30728 | tf_op jit(solution)/shard_map/ppermute | solution.py:467
  89.2 1.3 %collective-permute-start.20 = (bf16[8,640]{1,0:T(8,128)(2,1)S(1)}, bf16[8,640]{1,0:T(8,128)(2,1)S(1)}, u32[]{:S(2)}, u32[]{:S(2)}) collective-permute-start(bf16[8,640]{1,0:T(8,128)(2,1)S(1)} %get-tuple-element.31), channel_id=1, source_target_pairs={{0,4},{4,0},{8,12},{12,8},{16,20},{20,16},{24,28},{28,24},{1,5},{5... | collective-permute-start | bytes 30728 | tf_op jit(solution)/shard_map/ppermute | solution.py:467
  90.4 0.6 select_bitcast_fusion
  91.1 0.4 collective-permute-done.22
  91.5 2.2 %collective-permute-done.21 = bf16[8,640]{1,0:T(8,128)(2,1)S(1)} collective-permute-done((bf16[8,640]{1,0:T(8,128)(2,1)S(1)}, bf16[8,640]{1,0:T(8,128)(2,1)S(1)}, u32[]{:S(2)}, u32[]{:S(2)}) %collective-permute-start.21) | collective-permute-done | bytes 10272 | tf_op jit(solution)/shard_map/ppermute | solution.py:467
  93.7 0.6 fusion.1
  (34 shorter events, 0.1 us)
Async XLA Ops:
  0.6 9.3 %collective-permute-start = (bf16[192,640]{1,0:T(8,128)(2,1)}, bf16[192,640]{1,0:T(8,128)(2,1)S(1)}, u32[]{:S(2)}, u32[]{:S(2)}) collective-permute-start(bf16[192,640]{1,0:T(8,128)(2,1)} %prompt.3), channel_id=1, source_target_pairs={{0,16},{4,20},{8,24},{12,28},{16,8},{20,12},{24,0},{28,4},{1,17},{... | collective-permute-start | bytes 737288 | tf_op jit(solution)/shard_map/ppermute | solution.py:467
  3.2 19.1 %copy-start.8 = (bf16[1,2560,136]{1,2,0:T(8,128)(2,1)S(1)}, bf16[1,2560,136]{1,2,0:T(8,128)(2,1)}, u32[]{:S(2)}) copy-start(bf16[1,2560,136]{1,2,0:T(8,128)(2,1)} %param.13) | copy-start | bytes 2088964
  3.2 19.1 %copy-start.10 = (bf16[192,640]{1,0:T(8,128)(2,1)S(1)}, bf16[192,640]{1,0:T(8,128)(2,1)}, u32[]{:S(2)}) copy-start(bf16[192,640]{1,0:T(8,128)(2,1)} %prompt.3) | copy-start | bytes 737284
  3.2 19.1 %copy-start.13 = (bf16[1,2560,192]{1,2,0:T(8,128)(2,1)S(1)}, bf16[1,2560,192]{1,2,0:T(8,128)(2,1)}, u32[]{:S(2)}) copy-start(bf16[1,2560,192]{1,2,0:T(8,128)(2,1)} %param.11) | copy-start | bytes 2949124
  5.2 13.3 %collective-permute-start.1 = (bf16[192,640]{1,0:T(8,128)(2,1)}, bf16[192,640]{1,0:T(8,128)(2,1)S(1)}, u32[]{:S(2)}, u32[]{:S(2)}) collective-permute-start(bf16[192,640]{1,0:T(8,128)(2,1)} %get-tuple-element.18), channel_id=1, source_target_pairs={{0,12},{4,8},{8,4},{12,0},{16,20},{20,16},{24,28},{28,24},{1,13},{... | collective-permute-start | bytes 737288 | tf_op jit(solution)/shard_map/ppermute | solution.py:467
  6.8 15.5 %collective-permute-start.2 = (bf16[192,640]{1,0:T(8,128)(2,1)}, bf16[192,640]{1,0:T(8,128)(2,1)S(1)}, u32[]{:S(2)}, u32[]{:S(2)}) collective-permute-start(bf16[192,640]{1,0:T(8,128)(2,1)} %get-tuple-element.19), channel_id=1, source_target_pairs={{0,4},{4,0},{8,12},{12,8},{16,20},{20,16},{24,28},{28,24},{1,5},{5... | collective-permute-start | bytes 737288 | tf_op jit(solution)/shard_map/ppermute | solution.py:467
  22.3 12.3 %copy-start = (bf16[1,512,2560]{2,1,0:T(8,128)(2,1)S(1)}, bf16[1,512,2560]{2,1,0:T(8,128)(2,1)}, u32[]{:S(2)}) copy-start(bf16[1,512,2560]{2,1,0:T(8,128)(2,1)} %param.16) | copy-start | bytes 7864324
  22.3 12.3 %copy-start.2 = (bf16[1,768,640]{2,1,0:T(8,128)(2,1)S(1)}, bf16[1,768,640]{2,1,0:T(8,128)(2,1)}, u32[]{:S(2)}) copy-start(bf16[1,768,640]{2,1,0:T(8,128)(2,1)} %param.12) | copy-start | bytes 2949124
  22.3 12.3 %copy-start.4 = (bf16[1,512,512]{2,1,0:T(8,128)(2,1)S(1)}, bf16[1,512,512]{2,1,0:T(8,128)(2,1)}, u32[]{:S(2)}) copy-start(bf16[1,512,512]{2,1,0:T(8,128)(2,1)} %param.14) | copy-start | bytes 1572868
  22.3 12.3 %copy-start.6 = (bf16[1,512,512]{2,1,0:T(8,128)(2,1)S(1)}, bf16[1,512,512]{2,1,0:T(8,128)(2,1)}, u32[]{:S(2)}) copy-start(bf16[1,512,512]{2,1,0:T(8,128)(2,1)} %param.15) | copy-start | bytes 1572868
  22.4 12.3 %copy-start.9 = (f32[192,32]{1,0:T(8,128)S(1)}, f32[192,32]{1,0:T(8,128)}, u32[]{:S(2)}) copy-start(f32[192,32]{1,0:T(8,128)} %constant.10.clone.angles) | copy-start | bytes 73732
  22.4 12.3 %copy-start.11 = (s32[8]{0:T(128)S(1)}, s32[8]{0:T(128)}, u32[]{:S(2)}) copy-start(s32[8]{0:T(128)} %sizes.3) | copy-start | bytes 100
  22.4 6.1 %collective-permute-start.3 = (bf16[256,256]{1,0:T(8,128)(2,1)S(1)}, bf16[256,256]{1,0:T(8,128)(2,1)S(1)}, u32[]{:S(2)}, u32[]{:S(2)}) collective-permute-start(bf16[256,256]{1,0:T(8,128)(2,1)S(1)} %shard_map.105.own), channel_id=1, source_target_pairs={{0,4},{4,0},{8,12},{12,8},{16,20},{20,16},{24,28},{28,24},{1,5},{5... | collective-permute-start | bytes 393224 | tf_op jit(solution)/shard_map/ppermute | solution.py:467
  22.5 12.1 %collective-permute-start.4 = (bf16[256,256]{1,0:T(8,128)(2,1)S(1)}, bf16[256,256]{1,0:T(8,128)(2,1)S(1)}, u32[]{:S(2)}, u32[]{:S(2)}) collective-permute-start(bf16[256,256]{1,0:T(8,128)(2,1)S(1)} %shard_map.105.own), channel_id=1, source_target_pairs={{0,8},{4,12},{8,0},{12,4},{16,24},{20,28},{24,16},{28,20},{1,9},{5... | collective-permute-start | bytes 393224 | tf_op jit(solution)/shard_map/ppermute | solution.py:467
  25.5 9.1 %collective-permute-start.5 = (bf16[256,256]{1,0:T(8,128)(2,1)S(1)}, bf16[256,256]{1,0:T(8,128)(2,1)S(1)}, u32[]{:S(2)}, u32[]{:S(2)}) collective-permute-start(bf16[256,256]{1,0:T(8,128)(2,1)S(1)} %shard_map.105.own), channel_id=1, source_target_pairs={{0,12},{4,8},{8,4},{12,0},{16,28},{20,24},{24,20},{28,16},{1,13},{... | collective-permute-start | bytes 393224 | tf_op jit(solution)/shard_map/ppermute | solution.py:467
  35.3 24.7 %collective-permute-start.12 = (bf16[2,136,896]{2,1,0:T(8,128)(2,1)S(1)}, bf16[2,136,896]{2,1,0:T(8,128)(2,1)S(1)}, u32[]{:S(2)}, u32[]{:S(2)}) collective-permute-start(bf16[2,136,896]{2,1,0:T(8,128)(2,1)S(1)} %get-tuple-element.25), channel_id=1, source_target_pairs={{16,24},{20,28},{24,16},{28,20},{17,25},{21,29},{25,17},{29,21},{1... | collective-permute-start | bytes 1462280 | tf_op jit(solution)/shard_map/ppermute | solution.py:467
  40.1 3.4 %collective-permute-start.10 = (bf16[192,640]{1,0:T(8,128)(2,1)S(1)}, bf16[192,640]{1,0:T(8,128)(2,1)S(1)}, u32[]{:S(2)}, u32[]{:S(2)}) collective-permute-start(bf16[192,640]{1,0:T(8,128)(2,1)S(1)} %collective-permute-done.1.three.share3), channel_id=1, source_target_pairs={{0,1},{1,0},{2,3},{3,2},{4,5},{5,4},{6,7},{7,6},{8,9},{9,8},{10,11... | collective-permute-start | bytes 737288 | tf_op jit(solution)/shard_map/ppermute | solution.py:476
  40.2 3.4 %collective-permute-start.11 = (bf16[192,640]{1,0:T(8,128)(2,1)S(1)}, bf16[192,640]{1,0:T(8,128)(2,1)S(1)}, u32[]{:S(2)}, u32[]{:S(2)}) collective-permute-start(bf16[192,640]{1,0:T(8,128)(2,1)S(1)} %collective-permute-done.2.one.share1), channel_id=1, source_target_pairs={{0,1},{1,0},{2,3},{3,2},{4,5},{5,4},{6,7},{7,6},{8,9},{9,8},{10,11... | collective-permute-start | bytes 737288 | tf_op jit(solution)/shard_map/ppermute | solution.py:476
  40.7 20.9 %collective-permute-start.6 = (bf16[56,2560]{1,0:T(8,128)(2,1)S(1)}, bf16[56,2560]{1,0:T(8,128)(2,1)S(1)}, u32[]{:S(2)}, u32[]{:S(2)}) collective-permute-start(bf16[56,2560]{1,0:T(8,128)(2,1)S(1)} %get-tuple-element.21), channel_id=1, source_target_pairs={{0,28},{4,24},{8,20},{12,16},{16,0},{20,4},{24,8},{28,12},{1,29},{... | collective-permute-start | bytes 860168 | tf_op jit(solution)/shard_map/ppermute | solution.py:467
  40.7 31.0 %collective-permute-start.7 = (bf16[56,2560]{1,0:T(8,128)(2,1)S(1)}, bf16[56,2560]{1,0:T(8,128)(2,1)S(1)}, u32[]{:S(2)}, u32[]{:S(2)}) collective-permute-start(bf16[56,2560]{1,0:T(8,128)(2,1)S(1)} %get-tuple-element.22), channel_id=1, source_target_pairs={{0,24},{4,28},{8,16},{12,20},{16,0},{20,4},{24,8},{28,12},{1,25},{... | collective-permute-start | bytes 860168 | tf_op jit(solution)/shard_map/ppermute | solution.py:467
  43.6 28.1 %collective-permute-start.8 = (bf16[56,2560]{1,0:T(8,128)(2,1)S(1)}, bf16[56,2560]{1,0:T(8,128)(2,1)S(1)}, u32[]{:S(2)}, u32[]{:S(2)}) collective-permute-start(bf16[56,2560]{1,0:T(8,128)(2,1)S(1)} %get-tuple-element.23), channel_id=1, source_target_pairs={{0,20},{4,16},{8,28},{12,24},{16,0},{20,4},{24,8},{28,12},{1,21},{... | collective-permute-start | bytes 860168 | tf_op jit(solution)/shard_map/ppermute | solution.py:467
  43.6 28.1 %collective-permute-start.9 = (bf16[56,2560]{1,0:T(8,128)(2,1)S(1)}, bf16[56,2560]{1,0:T(8,128)(2,1)S(1)}, u32[]{:S(2)}, u32[]{:S(2)}) collective-permute-start(bf16[56,2560]{1,0:T(8,128)(2,1)S(1)} %get-tuple-element.24), channel_id=1, source_target_pairs={{0,16},{4,20},{8,24},{12,28},{16,0},{20,4},{24,8},{28,12},{1,17},{... | collective-permute-start | bytes 860168 | tf_op jit(solution)/shard_map/ppermute | solution.py:467
  60.0 1.5 %collective-permute-start.15 = (bf16[2,136,384]{2,1,0:T(8,128)(2,1)S(1)}, bf16[2,136,384]{2,1,0:T(8,128)(2,1)S(1)}, u32[]{:S(2)}, u32[]{:S(2)}) collective-permute-start(bf16[2,136,384]{2,1,0:T(8,128)(2,1)S(1)} %get-tuple-element.26.rest), channel_id=1, source_target_pairs={{0,1},{1,0},{2,3},{3,2},{4,5},{5,4},{6,7},{7,6},{8,9},{9,8},{10,11... | collective-permute-start | bytes 626696 | tf_op jit(solution)/shard_map/ppermute | solution.py:476
  61.5 10.2 %collective-permute-start.13 = (bf16[136,896]{1,0:T(8,128)(2,1)S(1)}, bf16[136,896]{1,0:T(8,128)(2,1)S(1)}, u32[]{:S(2)}, u32[]{:S(2)}) collective-permute-start(bf16[136,896]{1,0:T(8,128)(2,1)S(1)} %get-tuple-element.35), channel_id=1, source_target_pairs={{0,1},{1,0},{2,3},{3,2},{4,5},{5,4},{6,7},{7,6},{8,9},{9,8},{10,11... | collective-permute-start | bytes 731144 | tf_op jit(solution)/shard_map/ppermute | solution.py:476
  61.6 10.1 %collective-permute-start.14 = (bf16[136,896]{1,0:T(8,128)(2,1)S(1)}, bf16[136,896]{1,0:T(8,128)(2,1)S(1)}, u32[]{:S(2)}, u32[]{:S(2)}) collective-permute-start(bf16[136,896]{1,0:T(8,128)(2,1)S(1)} %get-tuple-element.34), channel_id=1, source_target_pairs={{0,1},{1,0},{2,3},{3,2},{4,5},{5,4},{6,7},{7,6},{8,9},{9,8},{10,11... | collective-permute-start | bytes 731144 | tf_op jit(solution)/shard_map/ppermute | solution.py:476
  71.7 9.1 %copy-start.1 = (bf16[1,512,2560]{2,1,0:T(8,128)(2,1)S(1)}, bf16[1,512,2560]{2,1,0:T(8,128)(2,1)}, u32[]{:S(2)}) copy-start(bf16[1,512,2560]{2,1,0:T(8,128)(2,1)} %param.16) | copy-start | bytes 7864324
  71.7 9.1 %copy-start.5 = (bf16[1,512,512]{2,1,0:T(8,128)(2,1)S(1)}, bf16[1,512,512]{2,1,0:T(8,128)(2,1)}, u32[]{:S(2)}) copy-start(bf16[1,512,512]{2,1,0:T(8,128)(2,1)} %param.14) | copy-start | bytes 1572868
  71.8 9.1 %copy-start.12 = (s32[8]{0:T(128)S(1)}, s32[8]{0:T(128)}, u32[]{:S(2)}) copy-start(s32[8]{0:T(128)} %sizes.3) | copy-start | bytes 100
  73.4 4.4 %collective-permute-start.17 = (bf16[56,512]{1,0:T(8,128)(2,1)S(1)}, bf16[56,512]{1,0:T(8,128)(2,1)S(1)}, u32[]{:S(2)}, u32[]{:S(2)}) collective-permute-start(bf16[56,512]{1,0:T(8,128)(2,1)S(1)} %get-tuple-element.29.own), channel_id=1, source_target_pairs={{0,4},{4,0},{8,12},{12,8},{16,20},{20,16},{24,28},{28,24},{1,5},{5... | collective-permute-start | bytes 172040 | tf_op jit(solution)/shard_map/ppermute | solution.py:467
  73.5 5.9 %collective-permute-start.18 = (bf16[56,512]{1,0:T(8,128)(2,1)S(1)}, bf16[56,512]{1,0:T(8,128)(2,1)S(1)}, u32[]{:S(2)}, u32[]{:S(2)}) collective-permute-start(bf16[56,512]{1,0:T(8,128)(2,1)S(1)} %get-tuple-element.29.own), channel_id=1, source_target_pairs={{0,8},{4,12},{8,0},{12,4},{16,24},{20,28},{24,16},{28,20},{1,9},{5... | collective-permute-start | bytes 172040 | tf_op jit(solution)/shard_map/ppermute | solution.py:467
  74.4 6.4 %collective-permute-start.19 = (bf16[56,512]{1,0:T(8,128)(2,1)S(1)}, bf16[56,512]{1,0:T(8,128)(2,1)}, u32[]{:S(2)}, u32[]{:S(2)}) collective-permute-start(bf16[56,512]{1,0:T(8,128)(2,1)S(1)} %get-tuple-element.29.own), channel_id=1, source_target_pairs={{0,12},{4,8},{8,4},{12,0},{16,28},{20,24},{24,20},{28,16},{1,13},{... | collective-permute-start | bytes 172040 | tf_op jit(solution)/shard_map/ppermute | solution.py:467
  77.8 13.3 %collective-permute-start.16 = (bf16[8,640]{1,0:T(8,128)(2,1)S(1)}, bf16[8,640]{1,0:T(8,128)(2,1)S(1)}, u32[]{:S(2)}, u32[]{:S(2)}) collective-permute-start(bf16[8,640]{1,0:T(8,128)(2,1)S(1)} %get-tuple-element.28), channel_id=1, source_target_pairs={{0,16},{4,20},{8,24},{12,28},{16,0},{20,4},{24,8},{28,12},{1,17},{... | collective-permute-start | bytes 30728 | tf_op jit(solution)/shard_map/ppermute | solution.py:467
  80.8 1.2 %copy-start.3 = (bf16[1,768,640]{2,1,0:T(8,128)(2,1)S(1)}, bf16[1,768,640]{2,1,0:T(8,128)(2,1)}, u32[]{:S(2)}) copy-start(bf16[1,768,640]{2,1,0:T(8,128)(2,1)} %param.12) | copy-start | bytes 2949124
  82.0 1.0 %copy-start.7 = (bf16[1,512,512]{2,1,0:T(8,128)(2,1)S(1)}, bf16[1,512,512]{2,1,0:T(8,128)(2,1)}, u32[]{:S(2)}) copy-start(bf16[1,512,512]{2,1,0:T(8,128)(2,1)} %param.15) | copy-start | bytes 1572868
  86.0 5.5 %collective-permute-start.22 = (bf16[8,640]{1,0:T(8,128)(2,1)S(1)}, bf16[8,640]{1,0:T(8,128)(2,1)S(1)}, u32[]{:S(2)}, u32[]{:S(2)}) collective-permute-start(bf16[8,640]{1,0:T(8,128)(2,1)S(1)} %get-tuple-element.33), channel_id=1, source_target_pairs={{0,12},{4,8},{8,4},{12,0},{16,28},{20,24},{24,20},{28,16},{1,13},{... | collective-permute-start | bytes 30728 | tf_op jit(solution)/shard_map/ppermute | solution.py:467
  89.2 4.6 %collective-permute-start.21 = (bf16[8,640]{1,0:T(8,128)(2,1)S(1)}, bf16[8,640]{1,0:T(8,128)(2,1)S(1)}, u32[]{:S(2)}, u32[]{:S(2)}) collective-permute-start(bf16[8,640]{1,0:T(8,128)(2,1)S(1)} %get-tuple-element.32), channel_id=1, source_target_pairs={{0,8},{4,12},{8,0},{12,4},{16,24},{20,28},{24,16},{28,20},{1,9},{5... | collective-permute-start | bytes 30728 | tf_op jit(solution)/shard_map/ppermute | solution.py:467
  89.2 4.6 %collective-permute-start.20 = (bf16[8,640]{1,0:T(8,128)(2,1)S(1)}, bf16[8,640]{1,0:T(8,128)(2,1)S(1)}, u32[]{:S(2)}, u32[]{:S(2)}) collective-permute-start(bf16[8,640]{1,0:T(8,128)(2,1)S(1)} %get-tuple-element.31), channel_id=1, source_target_pairs={{0,4},{4,0},{8,12},{12,8},{16,20},{20,16},{24,28},{28,24},{1,5},{5... | collective-permute-start | bytes 30728 | tf_op jit(solution)/shard_map/ppermute | solution.py:467

commit v6 on v5

--- a/solution.py
+++ b/solution.py
@@ -216,36 +216,46 @@
     return out
 
 
-def send_kernel(prompt, w_latent, out, other, half, packed, sems):
+def send_kernel(prompt, w_latent, out, half, packed, sem):
     section, rep = lax.axis_index("section"), lax.axis_index("rep")
     rows, width = out.shape
     cols, long = half.shape
 
     @pl.when(section == 0)
     def _():
-        copy = pltpu.make_async_copy(prompt, packed.at[0], sems.at[0])
+        copy = pltpu.make_async_copy(prompt, packed, sem)
         copy.start()
         copy.wait()
-        packed[1] = packed[0]
 
     @pl.when(section != 0)
     def _():
         columns = pl.ds(pl.multiple_of((rep & 1) * long, 128), long)
-        copy = pltpu.make_async_copy(w_latent.at[:, columns], half, sems.at[0])
+        copy = pltpu.make_async_copy(w_latent.at[:, columns], half, sem)
         copy.start()
         copy.wait()
-        rest = jnp.zeros((rows - cols, width), F32)
-        for i in range(2):
-            piece = half[:, i * width : (i + 1) * width].astype(F32)
-            packed[i] = jnp.concatenate([piece, rest], axis=0).astype(BF16)
-
-    copies = [
-        pltpu.make_async_copy(packed.at[i], ref, sems.at[i]) for i, ref in enumerate((out, other))
-    ]
-    for copy in copies:
-        copy.start()
-    for copy in copies:
-        copy.wait()
+        extra = half[:, width : width + 256].astype(F32)
+        free = rows - cols
+        left = cols - 2 * free
+        tail = [extra[2 * free :, :128], extra[2 * free :, 128:], jnp.zeros((free - 2 * left, 128), F32)]
+        extra = jnp.concatenate(
+            [extra[:free], extra[free : 2 * free], jnp.concatenate(tail, axis=0)], axis=1
+        )
+        whole = jnp.concatenate([half[:, :width].astype(F32), extra], axis=0)
+        packed[...] = whole.astype(BF16)
+
+    copy = pltpu.make_async_copy(packed, out, sem)
+    copy.start()
+    copy.wait()
+
+
+def unpack_share(share, cols):
+    share = share.astype(F32)
+    free = share.shape[0] - cols
+    left = cols - 2 * free
+    extra, tail = share[cols:, :512], share[cols:, 512:]
+    tail = jnp.concatenate([tail[:left], tail[left : 2 * left]], axis=1)
+    extra = jnp.concatenate([extra[:, :256], extra[:, 256:], tail], axis=0)
+    return jnp.concatenate([share[:cols], extra], axis=1).astype(BF16)
 
 
 def down_kernel(own, two, three, one, w_down, w_latent, out):
@@ -318,7 +328,7 @@
 
 
 def layer_kernel(
-    sizes, own, one, two, three, share1, share3, w_latent, prompt, angles,
+    sizes, own, one, two, three, share1, w_latent, prompt, angles,
     w_query, w_keys, w_values, w_out, out0, out1, out2, out3, own_cache, passed, rest, stack, total, cached,
 ):
     section, tp, rep = (lax.axis_index(a) for a in ("section", "tp", "rep"))
@@ -331,10 +341,9 @@
     def _():
         first = (rep & 1) * (early + rest.shape[2])
         passed[0] = w_latent[:, pl.ds(pl.multiple_of(first, 128), early)]
-        passed[1, :, :width] = share3[:cols, :]
-        passed[1, :, width:] = share1[:cols, : early - width]
-        rest[0] = unpack_rest(two[...], cols)
-        rest[1] = unpack_rest(three[...], cols)
+        passed[1] = unpack_share(share1[...], cols)
+        for k, ref in enumerate((one, two, three)):
+            rest[k] = unpack_rest(ref[...], cols)
 
     @pl.when(section == 0)
     def _():
@@ -369,14 +378,14 @@
 
 
 def latent_kernel(
-    one, two, three, four, angles, w_latent, share3, share1, near3, near1, passed, near_two, near_three,
-    rest, near_rest, w_down, out, own_cache, own_ends, hidden, parts,
+    one, two, three, four, angles, w_latent, first1, first2, first3, rest,
+    near1, near2, near3, near_rest, w_down, out, own_cache, own_ends, hidden, parts,
 ):
     tp, rep = lax.axis_index("tp"), lax.axis_index("rep")
     block = angles.shape[0] // 4
     width = own_ends.shape[1]
-    cols, model = w_latent.shape
-    early = passed.shape[2]
+    model = w_latent.shape[1]
+    early = first1.shape[1]
     rows = one[...].astype(F32) + two[...].astype(F32) + three[...].astype(F32) + four[...].astype(F32)
     narrow = rows.astype(BF16)
     rows = narrow.astype(F32)
@@ -384,19 +393,18 @@
     scale = unit(rows)
     parts[tp] = dot_t(narrow[:block], w_latent[...])
     sums = [0.0, 0.0, 0.0]
-    for core, (lower, upper, from_two, from_three, late) in enumerate(
-        ((share3, share1, passed.at[0], passed.at[1], rest), (near3, near1, near_two, near_three, near_rest))
+    for core, weights in enumerate(
+        (
+            (first1, first2, first3, rest),
+            (near1, near2, near3, near_rest),
+        )
     ):
         first = ((rep & 1) ^ core) * (model // 2)
-
-        def piece(start, size):
-            columns = pl.ds(pl.multiple_of(first + start, 128), size)
-            return hidden[0:block, columns].astype(BF16)
-
-        sums[0] += dot_t(piece(0, width), lower[:cols, :]) + dot_t(piece(width, width), upper[:cols, :])
-        head, tail = piece(0, early), piece(early, model // 2 - early)
-        sums[1] += dot_t(head, from_two[...]) + dot_t(tail, late[0])
-        sums[2] += dot_t(head, from_three[...]) + dot_t(tail, late[1])
+        head = hidden[0:block, pl.ds(pl.multiple_of(first, 128), early)].astype(BF16)
+        late = pl.ds(pl.multiple_of(first + early, 128), model // 2 - early)
+        tail = hidden[0:block, late].astype(BF16)
+        for k in range(3):
+            sums[k] += dot_t(head, weights[k][...]) + dot_t(tail, weights[3][k])
     for k, value in enumerate(sums):
         parts[tp ^ (k + 1)] = value
     latent = jnp.concatenate([parts[m] for m in range(4)], axis=1) * scale[:block]
@@ -477,12 +485,12 @@
 
     sent = call(
         send_kernel,
-        [jax.ShapeDtypeStruct((tokens, share), BF16)] * 2,
+        jax.ShapeDtypeStruct((tokens, share), BF16),
         [prompt, w_lat],
         [
             pltpu.VMEM((latent_cols, model // 2), BF16),
-            pltpu.VMEM((2, tokens, share), BF16),
-            pltpu.SemaphoreType.DMA((2,)),
+            pltpu.VMEM((tokens, share), BF16),
+            pltpu.SemaphoreType.DMA,
         ],
         left=2,
         space=HBM,
@@ -490,8 +498,8 @@
         flops=2 * 10**10,
     )
     two = route(prompt, (1, 0), (0, 2))
-    three = route(sent[0], (0, 3), (1, 1))
-    one = route(sent[1], (0, 1), (1, 1))
+    three = route(prompt, (0, 3), (1, 1))
+    one = route(sent, (0, 1), (1, 1))
     parts = call(
         down_kernel,
         jax.ShapeDtypeStruct((tokens + tokens // 3, 256), BF16),
@@ -499,7 +507,6 @@
         flops=2 * 10**10,
     )
     pieces = [parts] + [within(parts, k) for k in (1, 2, 3)]
-    near = [over_rep(three, 1), over_rep(one, 1)]
 
     message = jax.ShapeDtypeStruct((block + count, model), BF16)
     *blocks, first_cache, passed, rest = call(
@@ -508,9 +515,9 @@
         + [
             jax.ShapeDtypeStruct((block, ROW_WIDTH), BF16),
             jax.ShapeDtypeStruct((2, latent_cols, model // 2 - 384), BF16),
-            jax.ShapeDtypeStruct((2, latent_cols, 384), BF16),
+            jax.ShapeDtypeStruct((3, latent_cols, 384), BF16),
         ],
-        [block_sizes, *pieces, one, three, w_lat, prompt, angles, w_up, w_key, w_value, w_final],
+        [block_sizes, *pieces, one, w_lat, prompt, angles, w_up, w_key, w_value, w_final],
         [
             pltpu.VMEM((4, *parts.shape), BF16),
             pltpu.VMEM((tokens + count, model), F32),
@@ -521,8 +528,10 @@
         grant=16,
     )
     arrived = [onward(blocks[k], k) for k in (3, 2, 1, 0)]
-    passed = route(passed, None, (1, 2))
-    near += [passed, over_rep(passed[0], 1), over_rep(passed[1], 1), rest, over_rep(rest, 1)]
+    relayed = route(passed, None, (1, 2))
+    relayed, late, first = lax.optimization_barrier((relayed, rest, passed[1]))
+    weights = [first, relayed[0], relayed[1], late]
+    weights += [over_rep(w, 1) for w in weights]
     fresh, last_cache, ends_share = call(
         latent_kernel,
         [
@@ -530,7 +539,7 @@
             jax.ShapeDtypeStruct((block, ROW_WIDTH), BF16),
             jax.ShapeDtypeStruct((count, share), BF16),
         ],
-        [*arrived, angles, w_lat, three, one, *near, w_down],
+        [*arrived, angles, w_lat, *weights, w_down],
         [pltpu.VMEM((block + count, model), F32), pltpu.VMEM((4, block, latent_cols), F32)],
         flops=2 * 10**11,
     )

time: 94.6 us -> 92.5 us (0.978)
  waiting for transfers between devices: 55.3 us -> 53.2 us
    ppermute x18, waiting for transfers between devices: 53.9 us -> 51.9 us  [route(): return lax.ppermute(array, ('section', 'tp'), pairs)]
  transfers between devices with their start and end apart: 23 -> 22, of which waited for: 12 -> 13; matrix products, arithmetic and copies ran while one was open for 1% -> 1% of each run, Pallas kernels for 5% -> 5%
where the time goes in v6:
time: 92.5 us; the launch traced here: 92.2 us
  waiting for transfers between devices  53.2 us (58%)
  starting transfers between devices  27.5 us (30%)
  Pallas kernels  7.05 us (8%)
  local copies, waits for them, and re-layouts  2.36 us (3%)
  other arithmetic  1.25 us (1%)
    ppermute x18, waiting for transfers between devices, route(): return lax.ppermute(array, ('section', 'tp'), pairs)  51.9 us
    ppermute x18, starting transfers between devices, route(): return lax.ppermute(array, ('section', 'tp'), pairs)  26.4 us
    pallas_call x5, Pallas kernels, call(): pl.pallas_call(kernel, out_shape=out_shape, in_specs=[SMEM] * scalars + [...  7.05 us
    unnamed x28, local copies, waits for them, and re-layouts  2.3 us
  transfers between devices with their start and end apart: 22, of which 13 were waited for; matrix products, arithmetic and copies ran while one was open for 1% of the time, Pallas kernels for 5%

profile of v6, /device:TPU:4, one launch (start us, length us, event | category | flops | bytes accessed | tf_op | source)
XLA Modules:
  0.0 92.2 jit_solution(17618023974173170829)
XLA Ops:
  0.6 2.6 %collective-permute-start = (bf16[192,640]{1,0:T(8,128)(2,1)}, bf16[192,640]{1,0:T(8,128)(2,1)S(1)}, u32[]{:S(2)}, u32[]{:S(2)}) collective-permute-start(bf16[192,640]{1,0:T(8,128)(2,1)} %prompt.3), channel_id=1, source_target_pairs={{0,16},{4,20},{8,24},{12,28},{16,8},{20,12},{24,0},{28,4},{1,17},{... | collective-permute-start | bytes 737288 | tf_op jit(solution)/shard_map/ppermute | solution.py:475
  3.2 1.6 %collective-permute-start.1 = (bf16[192,640]{1,0:T(8,128)(2,1)}, bf16[192,640]{1,0:T(8,128)(2,1)S(1)}, u32[]{:S(2)}, u32[]{:S(2)}) collective-permute-start(bf16[192,640]{1,0:T(8,128)(2,1)} %prompt.3), channel_id=1, source_target_pairs={{0,12},{4,8},{8,4},{12,0},{16,20},{20,16},{24,28},{28,24},{1,13},{... | collective-permute-start | bytes 737288 | tf_op jit(solution)/shard_map/ppermute | solution.py:475
  4.8 1.8 %shard_map.104 = bf16[192,640]{1,0:T(8,128)(2,1)} custom-call(bf16[192,640]{1,0:T(8,128)(2,1)} %prompt.3, bf16[136,2560]{1,0:T(8,128)(2,1)} %bitcast.28), custom_call_target="tpu_custom_call" | custom-call | flops 20000000000 | bytes 942080 | tf_op jit(solution)/shard_map/pallas_call | solution.py:179
  6.6 0.5 collective-permute-start.2
  7.2 2.8 %collective-permute-done.two = bf16[192,640]{1,0:T(8,128)(2,1)S(1)} collective-permute-done((bf16[192,640]{1,0:T(8,128)(2,1)}, bf16[192,640]{1,0:T(8,128)(2,1)S(1)}, u32[]{:S(2)}, u32[]{:S(2)}) %collective-permute-start) | collective-permute-done | bytes 245792 | tf_op jit(solution)/shard_map/ppermute | solution.py:475
  9.9 6.5 %collective-permute-done.1.three = bf16[192,640]{1,0:T(8,128)(2,1)S(1)} collective-permute-done((bf16[192,640]{1,0:T(8,128)(2,1)}, bf16[192,640]{1,0:T(8,128)(2,1)S(1)}, u32[]{:S(2)}, u32[]{:S(2)}) %collective-permute-start.1) | collective-permute-done | bytes 245792 | tf_op jit(solution)/shard_map/ppermute | solution.py:475
  16.5 3.8 %collective-permute-done.2.one.share1 = bf16[192,640]{1,0:T(8,128)(2,1)S(1)} collective-permute-done((bf16[192,640]{1,0:T(8,128)(2,1)}, bf16[192,640]{1,0:T(8,128)(2,1)S(1)}, u32[]{:S(2)}, u32[]{:S(2)}) %collective-permute-start.2) | collective-permute-done | bytes 245792 | tf_op jit(solution)/shard_map/ppermute | solution.py:475
  20.3 0.0 copy-start
  20.3 0.0 copy-start.2
  20.3 0.0 copy-start.4
  20.3 0.0 copy-start.6
  20.3 0.0 copy-start.9
  20.3 0.0 copy-start.11
  20.4 1.5 %collective-permute-start.3 = (bf16[256,256]{1,0:T(8,128)(2,1)S(1)}, bf16[256,256]{1,0:T(8,128)(2,1)S(1)}, u32[]{:S(2)}, u32[]{:S(2)}) collective-permute-start(bf16[256,256]{1,0:T(8,128)(2,1)S(1)} %shard_map.105.own), channel_id=1, source_target_pairs={{0,4},{4,0},{8,12},{12,8},{16,20},{20,16},{24,28},{28,24},{1,5},{5... | collective-permute-start | bytes 393224 | tf_op jit(solution)/shard_map/ppermute | solution.py:475
  21.9 1.7 %collective-permute-start.4 = (bf16[256,256]{1,0:T(8,128)(2,1)S(1)}, bf16[256,256]{1,0:T(8,128)(2,1)S(1)}, u32[]{:S(2)}, u32[]{:S(2)}) collective-permute-start(bf16[256,256]{1,0:T(8,128)(2,1)S(1)} %shard_map.105.own), channel_id=1, source_target_pairs={{0,8},{4,12},{8,0},{12,4},{16,24},{20,28},{24,16},{28,20},{1,9},{5... | collective-permute-start | bytes 393224 | tf_op jit(solution)/shard_map/ppermute | solution.py:475
  23.6 1.3 %collective-permute-start.5 = (bf16[256,256]{1,0:T(8,128)(2,1)S(1)}, bf16[256,256]{1,0:T(8,128)(2,1)S(1)}, u32[]{:S(2)}, u32[]{:S(2)}) collective-permute-start(bf16[256,256]{1,0:T(8,128)(2,1)S(1)} %shard_map.105.own), channel_id=1, source_target_pairs={{0,12},{4,8},{8,4},{12,0},{16,28},{20,24},{24,20},{28,16},{1,13},{... | collective-permute-start | bytes 393224 | tf_op jit(solution)/shard_map/ppermute | solution.py:475
  24.8 1.5 %collective-permute-done.3.one = bf16[256,256]{1,0:T(8,128)(2,1)S(1)} collective-permute-done((bf16[256,256]{1,0:T(8,128)(2,1)S(1)}, bf16[256,256]{1,0:T(8,128)(2,1)S(1)}, u32[]{:S(2)}, u32[]{:S(2)}) %collective-permute-start.3) | collective-permute-done | bytes 131104 | tf_op jit(solution)/shard_map/ppermute | solution.py:475
  26.3 7.1 %collective-permute-done.4.two = bf16[256,256]{1,0:T(8,128)(2,1)S(1)} collective-permute-done((bf16[256,256]{1,0:T(8,128)(2,1)S(1)}, bf16[256,256]{1,0:T(8,128)(2,1)S(1)}, u32[]{:S(2)}, u32[]{:S(2)}) %collective-permute-start.4) | collective-permute-done | bytes 131104 | tf_op jit(solution)/shard_map/ppermute | solution.py:475
  33.5 0.6 shard_map.106
  34.2 4.3 %collective-permute-start.10 = (bf16[2,136,896]{2,1,0:T(8,128)(2,1)S(1)}, bf16[2,136,896]{2,1,0:T(8,128)(2,1)S(1)}, u32[]{:S(2)}, u32[]{:S(2)}) collective-permute-start(bf16[2,136,896]{2,1,0:T(8,128)(2,1)S(1)} %get-tuple-element.24), channel_id=1, source_target_pairs={{16,24},{20,28},{24,16},{28,20},{17,25},{21,29},{25,17},{29,21},{1... | collective-permute-start | bytes 1462280 | tf_op jit(solution)/shard_map/ppermute | solution.py:475
  38.4 0.1 collective-permute-start.6
  38.5 3.8 %collective-permute-start.7 = (bf16[56,2560]{1,0:T(8,128)(2,1)S(1)}, bf16[56,2560]{1,0:T(8,128)(2,1)S(1)}, u32[]{:S(2)}, u32[]{:S(2)}) collective-permute-start(bf16[56,2560]{1,0:T(8,128)(2,1)S(1)} %get-tuple-element.21), channel_id=1, source_target_pairs={{0,24},{4,28},{8,16},{12,20},{16,0},{20,4},{24,8},{28,12},{1,25},{... | collective-permute-start | bytes 860168 | tf_op jit(solution)/shard_map/ppermute | solution.py:475
  42.3 0.0 collective-permute-start.8
  42.4 0.2 collective-permute-start.9
  42.6 16.3 %collective-permute-done.10 = bf16[2,136,896]{2,1,0:T(8,128)(2,1)S(1)} collective-permute-done((bf16[2,136,896]{2,1,0:T(8,128)(2,1)S(1)}, bf16[2,136,896]{2,1,0:T(8,128)(2,1)S(1)}, u32[]{:S(2)}, u32[]{:S(2)}) %collective-permute-start.10) | collective-permute-done | bytes 487456 | tf_op jit(solution)/shard_map/ppermute | solution.py:475
  58.9 0.0 collective-permute-start.14
  58.9 0.6 collective-permute-start.11
  59.5 8.3 %collective-permute-done.7.two = bf16[56,2560]{1,0:T(8,128)(2,1)S(1)} collective-permute-done((bf16[56,2560]{1,0:T(8,128)(2,1)S(1)}, bf16[56,2560]{1,0:T(8,128)(2,1)S(1)}, u32[]{:S(2)}, u32[]{:S(2)}) %collective-permute-start.7) | collective-permute-done | bytes 286752 | tf_op jit(solution)/shard_map/ppermute | solution.py:475
  67.8 0.5 collective-permute-start.13
  68.3 1.0 %collective-permute-done.12.near2 = bf16[136,896]{1,0:T(8,128)(2,1)S(1)} collective-permute-done((bf16[136,896]{1,0:T(8,128)(2,1)S(1)}, bf16[136,896]{1,0:T(8,128)(2,1)S(1)}, u32[]{:S(2)}, u32[]{:S(2)}) %collective-permute-start.12) | collective-permute-done | bytes 243744 | tf_op jit(solution)/shard_map/ppermute | solution.py:484
  69.3 0.3 collective-permute-done.13.near3
  69.6 1.6 %shard_map.107 = (bf16[56,512]{1,0:T(8,128)(2,1)S(1)}, bf16[48,544]{1,0:T(8,128)(2,1)S(1)}, bf16[8,640]{1,0:T(8,128)(2,1)S(1)}) custom-call(bf16[56,2560]{1,0:T(8,128)(2,1)S(1)} %collective-permute-done.6.one, bf16[56,2560]{1,0:T(8,128)(2,1)S(1)} %collective-permute-done.7.two, bf16[56,2560]{1,0:T(8,128)(2,1)S(1)} %collective-permute-done.8.three, ...), custom_call_target="tpu_custom_call" | custom-call | flops 199999995904 | bytes 4939776 | tf_op jit(solution)/shard_map/pallas_call | solution.py:179
  71.3 0.1 collective-permute-start.16
  71.3 1.3 %collective-permute-start.17 = (bf16[56,512]{1,0:T(8,128)(2,1)S(1)}, bf16[56,512]{1,0:T(8,128)(2,1)S(1)}, u32[]{:S(2)}, u32[]{:S(2)}) collective-permute-start(bf16[56,512]{1,0:T(8,128)(2,1)S(1)} %get-tuple-element.31.own), channel_id=1, source_target_pairs={{0,8},{4,12},{8,0},{12,4},{16,24},{20,28},{24,16},{28,20},{1,9},{5... | collective-permute-start | bytes 172040 | tf_op jit(solution)/shard_map/ppermute | solution.py:475
  72.6 3.1 %collective-permute-start.18 = (bf16[56,512]{1,0:T(8,128)(2,1)S(1)}, bf16[56,512]{1,0:T(8,128)(2,1)}, u32[]{:S(2)}, u32[]{:S(2)}) collective-permute-start(bf16[56,512]{1,0:T(8,128)(2,1)S(1)} %get-tuple-element.31.own), channel_id=1, source_target_pairs={{0,12},{4,8},{8,4},{12,0},{16,28},{20,24},{24,20},{28,16},{1,13},{... | collective-permute-start | bytes 172040 | tf_op jit(solution)/shard_map/ppermute | solution.py:475
  75.7 0.6 collective-permute-done.16.one
  76.3 3.0 %collective-permute-done.17.two = bf16[56,512]{1,0:T(8,128)(2,1)S(1)} collective-permute-done((bf16[56,512]{1,0:T(8,128)(2,1)S(1)}, bf16[56,512]{1,0:T(8,128)(2,1)S(1)}, u32[]{:S(2)}, u32[]{:S(2)}) %collective-permute-start.17) | collective-permute-done | bytes 57376 | tf_op jit(solution)/shard_map/ppermute | solution.py:475
  79.4 0.0 copy-start.3
  79.4 1.2 %copy-done.3 = bf16[1,768,640]{2,1,0:T(8,128)(2,1)S(1)} copy-done((bf16[1,768,640]{2,1,0:T(8,128)(2,1)S(1)}, bf16[1,768,640]{2,1,0:T(8,128)(2,1)}, u32[]{:S(2)}) %copy-start.3) | copy-done | bytes 983064
  80.6 1.0 %copy-done.7 = bf16[1,512,512]{2,1,0:T(8,128)(2,1)S(1)} copy-done((bf16[1,512,512]{2,1,0:T(8,128)(2,1)S(1)}, bf16[1,512,512]{2,1,0:T(8,128)(2,1)}, u32[]{:S(2)}) %copy-start.7) | copy-done | bytes 524312
  81.6 2.9 %shard_map.108 = (bf16[8,640]{1,0:T(8,128)(2,1)S(1)}, bf16[8,640]{1,0:T(8,128)(2,1)S(1)}, bf16[8,640]{1,0:T(8,128)(2,1)S(1)}, bf16[8,640]{1,0:T(8,128)(2,1)S(1)}) custom-call(s32[8]{0:T(128)S(1)} %copy-done.12, bf16[56,512]{1,0:T(8,128)(2,1)S(1)} %get-tuple-element.31.own, bf16[56,512]{1,0:T(8,128)(2,1)S(1)} %collective-permute-done.16.one, ...), custom_call_target="tpu_custom_call" | custom-call | flops 201326592 | bytes 4907040 | tf_op jit(solution)/shard_map/pallas_call | solution.py:179
  84.6 2.5 %collective-permute-start.21 = (bf16[8,640]{1,0:T(8,128)(2,1)S(1)}, bf16[8,640]{1,0:T(8,128)(2,1)S(1)}, u32[]{:S(2)}, u32[]{:S(2)}) collective-permute-start(bf16[8,640]{1,0:T(8,128)(2,1)S(1)} %get-tuple-element.35), channel_id=1, source_target_pairs={{0,12},{4,8},{8,4},{12,0},{16,28},{20,24},{24,20},{28,16},{1,13},{... | collective-permute-start | bytes 30728 | tf_op jit(solution)/shard_map/ppermute | solution.py:475
  87.0 0.3 collective-permute-start.20
  87.4 1.6 %collective-permute-start.19 = (bf16[8,640]{1,0:T(8,128)(2,1)S(1)}, bf16[8,640]{1,0:T(8,128)(2,1)S(1)}, u32[]{:S(2)}, u32[]{:S(2)}) collective-permute-start(bf16[8,640]{1,0:T(8,128)(2,1)S(1)} %get-tuple-element.33), channel_id=1, source_target_pairs={{0,4},{4,0},{8,12},{12,8},{16,20},{20,16},{24,28},{28,24},{1,5},{5... | collective-permute-start | bytes 30728 | tf_op jit(solution)/shard_map/ppermute | solution.py:475
  89.0 0.6 select_bitcast_fusion
  89.6 0.5 collective-permute-done.21
  90.2 1.4 %collective-permute-done.20 = bf16[8,640]{1,0:T(8,128)(2,1)S(1)} collective-permute-done((bf16[8,640]{1,0:T(8,128)(2,1)S(1)}, bf16[8,640]{1,0:T(8,128)(2,1)S(1)}, u32[]{:S(2)}, u32[]{:S(2)}) %collective-permute-start.20) | collective-permute-done | bytes 10272 | tf_op jit(solution)/shard_map/ppermute | solution.py:475
  91.6 0.6 fusion.1
  (33 shorter events, 0.2 us)
Async XLA Ops:
  0.6 9.3 %collective-permute-start = (bf16[192,640]{1,0:T(8,128)(2,1)}, bf16[192,640]{1,0:T(8,128)(2,1)S(1)}, u32[]{:S(2)}, u32[]{:S(2)}) collective-permute-start(bf16[192,640]{1,0:T(8,128)(2,1)} %prompt.3), channel_id=1, source_target_pairs={{0,16},{4,20},{8,24},{12,28},{16,8},{20,12},{24,0},{28,4},{1,17},{... | collective-permute-start | bytes 737288 | tf_op jit(solution)/shard_map/ppermute | solution.py:475
  3.2 13.2 %collective-permute-start.1 = (bf16[192,640]{1,0:T(8,128)(2,1)}, bf16[192,640]{1,0:T(8,128)(2,1)S(1)}, u32[]{:S(2)}, u32[]{:S(2)}) collective-permute-start(bf16[192,640]{1,0:T(8,128)(2,1)} %prompt.3), channel_id=1, source_target_pairs={{0,12},{4,8},{8,4},{12,0},{16,20},{20,16},{24,28},{28,24},{1,13},{... | collective-permute-start | bytes 737288 | tf_op jit(solution)/shard_map/ppermute | solution.py:475
  4.8 15.5 %copy-start.8 = (bf16[1,2560,136]{1,2,0:T(8,128)(2,1)S(1)}, bf16[1,2560,136]{1,2,0:T(8,128)(2,1)}, u32[]{:S(2)}) copy-start(bf16[1,2560,136]{1,2,0:T(8,128)(2,1)} %param.13) | copy-start | bytes 2088964
  4.8 15.5 %copy-start.10 = (bf16[192,640]{1,0:T(8,128)(2,1)S(1)}, bf16[192,640]{1,0:T(8,128)(2,1)}, u32[]{:S(2)}) copy-start(bf16[192,640]{1,0:T(8,128)(2,1)} %prompt.3) | copy-start | bytes 737284
  4.8 15.5 %copy-start.13 = (bf16[1,2560,192]{1,2,0:T(8,128)(2,1)S(1)}, bf16[1,2560,192]{1,2,0:T(8,128)(2,1)}, u32[]{:S(2)}) copy-start(bf16[1,2560,192]{1,2,0:T(8,128)(2,1)} %param.11) | copy-start | bytes 2949124
  6.6 13.6 %collective-permute-start.2 = (bf16[192,640]{1,0:T(8,128)(2,1)}, bf16[192,640]{1,0:T(8,128)(2,1)S(1)}, u32[]{:S(2)}, u32[]{:S(2)}) collective-permute-start(bf16[192,640]{1,0:T(8,128)(2,1)} %shard_map.104), channel_id=1, source_target_pairs={{0,4},{4,0},{8,12},{12,8},{16,20},{20,16},{24,28},{28,24},{1,5},{5... | collective-permute-start | bytes 737288 | tf_op jit(solution)/shard_map/ppermute | solution.py:475
  20.3 13.2 %copy-start = (bf16[1,512,2560]{2,1,0:T(8,128)(2,1)S(1)}, bf16[1,512,2560]{2,1,0:T(8,128)(2,1)}, u32[]{:S(2)}) copy-start(bf16[1,512,2560]{2,1,0:T(8,128)(2,1)} %param.16) | copy-start | bytes 7864324
  20.3 13.2 %copy-start.2 = (bf16[1,768,640]{2,1,0:T(8,128)(2,1)S(1)}, bf16[1,768,640]{2,1,0:T(8,128)(2,1)}, u32[]{:S(2)}) copy-start(bf16[1,768,640]{2,1,0:T(8,128)(2,1)} %param.12) | copy-start | bytes 2949124
  20.3 13.2 %copy-start.4 = (bf16[1,512,512]{2,1,0:T(8,128)(2,1)S(1)}, bf16[1,512,512]{2,1,0:T(8,128)(2,1)}, u32[]{:S(2)}) copy-start(bf16[1,512,512]{2,1,0:T(8,128)(2,1)} %param.14) | copy-start | bytes 1572868
  20.3 13.2 %copy-start.6 = (bf16[1,512,512]{2,1,0:T(8,128)(2,1)S(1)}, bf16[1,512,512]{2,1,0:T(8,128)(2,1)}, u32[]{:S(2)}) copy-start(bf16[1,512,512]{2,1,0:T(8,128)(2,1)} %param.15) | copy-start | bytes 1572868
  20.3 13.2 %copy-start.9 = (f32[192,32]{1,0:T(8,128)S(1)}, f32[192,32]{1,0:T(8,128)}, u32[]{:S(2)}) copy-start(f32[192,32]{1,0:T(8,128)} %constant.10.clone.angles) | copy-start | bytes 73732
  20.3 13.2 %copy-start.11 = (s32[8]{0:T(128)S(1)}, s32[8]{0:T(128)}, u32[]{:S(2)}) copy-start(s32[8]{0:T(128)} %sizes.3) | copy-start | bytes 100
  20.4 5.9 %collective-permute-start.3 = (bf16[256,256]{1,0:T(8,128)(2,1)S(1)}, bf16[256,256]{1,0:T(8,128)(2,1)S(1)}, u32[]{:S(2)}, u32[]{:S(2)}) collective-permute-start(bf16[256,256]{1,0:T(8,128)(2,1)S(1)} %shard_map.105.own), channel_id=1, source_target_pairs={{0,4},{4,0},{8,12},{12,8},{16,20},{20,16},{24,28},{28,24},{1,5},{5... | collective-permute-start | bytes 393224 | tf_op jit(solution)/shard_map/ppermute | solution.py:475
  21.9 11.6 %collective-permute-start.4 = (bf16[256,256]{1,0:T(8,128)(2,1)S(1)}, bf16[256,256]{1,0:T(8,128)(2,1)S(1)}, u32[]{:S(2)}, u32[]{:S(2)}) collective-permute-start(bf16[256,256]{1,0:T(8,128)(2,1)S(1)} %shard_map.105.own), channel_id=1, source_target_pairs={{0,8},{4,12},{8,0},{12,4},{16,24},{20,28},{24,16},{28,20},{1,9},{5... | collective-permute-start | bytes 393224 | tf_op jit(solution)/shard_map/ppermute | solution.py:475
  23.6 9.9 %collective-permute-start.5 = (bf16[256,256]{1,0:T(8,128)(2,1)S(1)}, bf16[256,256]{1,0:T(8,128)(2,1)S(1)}, u32[]{:S(2)}, u32[]{:S(2)}) collective-permute-start(bf16[256,256]{1,0:T(8,128)(2,1)S(1)} %shard_map.105.own), channel_id=1, source_target_pairs={{0,12},{4,8},{8,4},{12,0},{16,28},{20,24},{24,20},{28,16},{1,13},{... | collective-permute-start | bytes 393224 | tf_op jit(solution)/shard_map/ppermute | solution.py:475
  34.2 24.7 %collective-permute-start.10 = (bf16[2,136,896]{2,1,0:T(8,128)(2,1)S(1)}, bf16[2,136,896]{2,1,0:T(8,128)(2,1)S(1)}, u32[]{:S(2)}, u32[]{:S(2)}) collective-permute-start(bf16[2,136,896]{2,1,0:T(8,128)(2,1)S(1)} %get-tuple-element.24), channel_id=1, source_target_pairs={{16,24},{20,28},{24,16},{28,20},{17,25},{21,29},{25,17},{29,21},{1... | collective-permute-start | bytes 1462280 | tf_op jit(solution)/shard_map/ppermute | solution.py:475
  38.4 20.5 %collective-permute-start.6 = (bf16[56,2560]{1,0:T(8,128)(2,1)S(1)}, bf16[56,2560]{1,0:T(8,128)(2,1)S(1)}, u32[]{:S(2)}, u32[]{:S(2)}) collective-permute-start(bf16[56,2560]{1,0:T(8,128)(2,1)S(1)} %get-tuple-element.20), channel_id=1, source_target_pairs={{0,28},{4,24},{8,20},{12,16},{16,0},{20,4},{24,8},{28,12},{1,29},{... | collective-permute-start | bytes 860168 | tf_op jit(solution)/shard_map/ppermute | solution.py:475
  38.5 29.3 %collective-permute-start.7 = (bf16[56,2560]{1,0:T(8,128)(2,1)S(1)}, bf16[56,2560]{1,0:T(8,128)(2,1)S(1)}, u32[]{:S(2)}, u32[]{:S(2)}) collective-permute-start(bf16[56,2560]{1,0:T(8,128)(2,1)S(1)} %get-tuple-element.21), channel_id=1, source_target_pairs={{0,24},{4,28},{8,16},{12,20},{16,0},{20,4},{24,8},{28,12},{1,25},{... | collective-permute-start | bytes 860168 | tf_op jit(solution)/shard_map/ppermute | solution.py:475
  42.3 25.4 %collective-permute-start.8 = (bf16[56,2560]{1,0:T(8,128)(2,1)S(1)}, bf16[56,2560]{1,0:T(8,128)(2,1)S(1)}, u32[]{:S(2)}, u32[]{:S(2)}) collective-permute-start(bf16[56,2560]{1,0:T(8,128)(2,1)S(1)} %get-tuple-element.22), channel_id=1, source_target_pairs={{0,20},{4,16},{8,28},{12,24},{16,0},{20,4},{24,8},{28,12},{1,21},{... | collective-permute-start | bytes 860168 | tf_op jit(solution)/shard_map/ppermute | solution.py:475
  42.4 25.9 %collective-permute-start.9 = (bf16[56,2560]{1,0:T(8,128)(2,1)S(1)}, bf16[56,2560]{1,0:T(8,128)(2,1)S(1)}, u32[]{:S(2)}, u32[]{:S(2)}) collective-permute-start(bf16[56,2560]{1,0:T(8,128)(2,1)S(1)} %get-tuple-element.23), channel_id=1, source_target_pairs={{0,16},{4,20},{8,24},{12,28},{16,0},{20,4},{24,8},{28,12},{1,17},{... | collective-permute-start | bytes 860168 | tf_op jit(solution)/shard_map/ppermute | solution.py:475
  58.9 10.7 %collective-permute-start.14 = (bf16[3,136,384]{2,1,0:T(8,128)(2,1)S(1)}, bf16[3,136,384]{2,1,0:T(8,128)(2,1)S(1)}, u32[]{:S(2)}, u32[]{:S(2)}) collective-permute-start(bf16[3,136,384]{2,1,0:T(8,128)(2,1)S(1)} %get-tuple-element.28.rest), channel_id=1, source_target_pairs={{0,1},{1,0},{2,3},{3,2},{4,5},{5,4},{6,7},{7,6},{8,9},{9,8},{10,11... | collective-permute-start | bytes 940040 | tf_op jit(solution)/shard_map/ppermute | solution.py:484
  58.9 9.3 %collective-permute-start.11 = (bf16[136,896]{1,0:T(8,128)(2,1)S(1)}, bf16[136,896]{1,0:T(8,128)(2,1)S(1)}, u32[]{:S(2)}, u32[]{:S(2)}) collective-permute-start(bf16[136,896]{1,0:T(8,128)(2,1)S(1)} %slice_bitcast_fusion.2.first1), channel_id=1, source_target_pairs={{0,1},{1,0},{2,3},{3,2},{4,5},{5,4},{6,7},{7,6},{8,9},{9,8},{10,11... | collective-permute-start | bytes 731144 | tf_op jit(solution)/shard_map/ppermute | solution.py:484
  67.8 1.5 %collective-permute-start.12 = (bf16[136,896]{1,0:T(8,128)(2,1)S(1)}, bf16[136,896]{1,0:T(8,128)(2,1)S(1)}, u32[]{:S(2)}, u32[]{:S(2)}) collective-permute-start(bf16[136,896]{1,0:T(8,128)(2,1)S(1)} %get-tuple-element.37.first2), channel_id=1, source_target_pairs={{0,1},{1,0},{2,3},{3,2},{4,5},{5,4},{6,7},{7,6},{8,9},{9,8},{10,11... | collective-permute-start | bytes 731144 | tf_op jit(solution)/shard_map/ppermute | solution.py:484
  67.8 1.9 %collective-permute-start.13 = (bf16[136,896]{1,0:T(8,128)(2,1)S(1)}, bf16[136,896]{1,0:T(8,128)(2,1)S(1)}, u32[]{:S(2)}, u32[]{:S(2)}) collective-permute-start(bf16[136,896]{1,0:T(8,128)(2,1)S(1)} %get-tuple-element.36.first3), channel_id=1, source_target_pairs={{0,1},{1,0},{2,3},{3,2},{4,5},{5,4},{6,7},{7,6},{8,9},{9,8},{10,11... | collective-permute-start | bytes 731144 | tf_op jit(solution)/shard_map/ppermute | solution.py:484
  69.6 9.7 %copy-start.1 = (bf16[1,512,2560]{2,1,0:T(8,128)(2,1)S(1)}, bf16[1,512,2560]{2,1,0:T(8,128)(2,1)}, u32[]{:S(2)}) copy-start(bf16[1,512,2560]{2,1,0:T(8,128)(2,1)} %param.16) | copy-start | bytes 7864324
  69.6 9.7 %copy-start.5 = (bf16[1,512,512]{2,1,0:T(8,128)(2,1)S(1)}, bf16[1,512,512]{2,1,0:T(8,128)(2,1)}, u32[]{:S(2)}) copy-start(bf16[1,512,512]{2,1,0:T(8,128)(2,1)} %param.14) | copy-start | bytes 1572868
  69.6 9.7 %copy-start.12 = (s32[8]{0:T(128)S(1)}, s32[8]{0:T(128)}, u32[]{:S(2)}) copy-start(s32[8]{0:T(128)} %sizes.3) | copy-start | bytes 100
  71.3 5.1 %collective-permute-start.16 = (bf16[56,512]{1,0:T(8,128)(2,1)S(1)}, bf16[56,512]{1,0:T(8,128)(2,1)S(1)}, u32[]{:S(2)}, u32[]{:S(2)}) collective-permute-start(bf16[56,512]{1,0:T(8,128)(2,1)S(1)} %get-tuple-element.31.own), channel_id=1, source_target_pairs={{0,4},{4,0},{8,12},{12,8},{16,20},{20,16},{24,28},{28,24},{1,5},{5... | collective-permute-start | bytes 172040 | tf_op jit(solution)/shard_map/ppermute | solution.py:475
  71.3 8.0 %collective-permute-start.17 = (bf16[56,512]{1,0:T(8,128)(2,1)S(1)}, bf16[56,512]{1,0:T(8,128)(2,1)S(1)}, u32[]{:S(2)}, u32[]{:S(2)}) collective-permute-start(bf16[56,512]{1,0:T(8,128)(2,1)S(1)} %get-tuple-element.31.own), channel_id=1, source_target_pairs={{0,8},{4,12},{8,0},{12,4},{16,24},{20,28},{24,16},{28,20},{1,9},{5... | collective-permute-start | bytes 172040 | tf_op jit(solution)/shard_map/ppermute | solution.py:475
  72.6 6.8 %collective-permute-start.18 = (bf16[56,512]{1,0:T(8,128)(2,1)S(1)}, bf16[56,512]{1,0:T(8,128)(2,1)}, u32[]{:S(2)}, u32[]{:S(2)}) collective-permute-start(bf16[56,512]{1,0:T(8,128)(2,1)S(1)} %get-tuple-element.31.own), channel_id=1, source_target_pairs={{0,12},{4,8},{8,4},{12,0},{16,28},{20,24},{24,20},{28,16},{1,13},{... | collective-permute-start | bytes 172040 | tf_op jit(solution)/shard_map/ppermute | solution.py:475
  75.7 13.9 %collective-permute-start.15 = (bf16[8,640]{1,0:T(8,128)(2,1)S(1)}, bf16[8,640]{1,0:T(8,128)(2,1)S(1)}, u32[]{:S(2)}, u32[]{:S(2)}) collective-permute-start(bf16[8,640]{1,0:T(8,128)(2,1)S(1)} %get-tuple-element.30), channel_id=1, source_target_pairs={{0,16},{4,20},{8,24},{12,28},{16,0},{20,4},{24,8},{28,12},{1,17},{... | collective-permute-start | bytes 30728 | tf_op jit(solution)/shard_map/ppermute | solution.py:475
  79.4 1.2 %copy-start.3 = (bf16[1,768,640]{2,1,0:T(8,128)(2,1)S(1)}, bf16[1,768,640]{2,1,0:T(8,128)(2,1)}, u32[]{:S(2)}) copy-start(bf16[1,768,640]{2,1,0:T(8,128)(2,1)} %param.12) | copy-start | bytes 2949124
  80.6 1.0 %copy-start.7 = (bf16[1,512,512]{2,1,0:T(8,128)(2,1)S(1)}, bf16[1,512,512]{2,1,0:T(8,128)(2,1)}, u32[]{:S(2)}) copy-start(bf16[1,512,512]{2,1,0:T(8,128)(2,1)} %param.15) | copy-start | bytes 1572868
  84.6 5.6 %collective-permute-start.21 = (bf16[8,640]{1,0:T(8,128)(2,1)S(1)}, bf16[8,640]{1,0:T(8,128)(2,1)S(1)}, u32[]{:S(2)}, u32[]{:S(2)}) collective-permute-start(bf16[8,640]{1,0:T(8,128)(2,1)S(1)} %get-tuple-element.35), channel_id=1, source_target_pairs={{0,12},{4,8},{8,4},{12,0},{16,28},{20,24},{24,20},{28,16},{1,13},{... | collective-permute-start | bytes 30728 | tf_op jit(solution)/shard_map/ppermute | solution.py:475
  87.0 4.6 %collective-permute-start.20 = (bf16[8,640]{1,0:T(8,128)(2,1)S(1)}, bf16[8,640]{1,0:T(8,128)(2,1)S(1)}, u32[]{:S(2)}, u32[]{:S(2)}) collective-permute-start(bf16[8,640]{1,0:T(8,128)(2,1)S(1)} %get-tuple-element.34), channel_id=1, source_target_pairs={{0,8},{4,12},{8,0},{12,4},{16,24},{20,28},{24,16},{28,20},{1,9},{5... | collective-permute-start | bytes 30728 | tf_op jit(solution)/shard_map/ppermute | solution.py:475
  87.4 4.3 %collective-permute-start.19 = (bf16[8,640]{1,0:T(8,128)(2,1)S(1)}, bf16[8,640]{1,0:T(8,128)(2,1)S(1)}, u32[]{:S(2)}, u32[]{:S(2)}) collective-permute-start(bf16[8,640]{1,0:T(8,128)(2,1)S(1)} %get-tuple-element.33), channel_id=1, source_target_pairs={{0,4},{4,0},{8,12},{12,8},{16,20},{20,16},{24,28},{28,24},{1,5},{5... | collective-permute-start | bytes 30728 | tf_op jit(solution)/shard_map/ppermute | solution.py:475

commit v7 on v6

--- a/solution.py
+++ b/solution.py
@@ -258,7 +258,7 @@
     return jnp.concatenate([share[:cols], extra], axis=1).astype(BF16)
 
 
-def down_kernel(own, two, three, one, w_down, w_latent, out):
+def down_kernel(own, three, two, one, w_down, w_latent, out):
     section, tp, rep = (lax.axis_index(a) for a in ("section", "tp", "rep"))
     tokens, share = own.shape
     cols, model = w_latent.shape
@@ -503,7 +503,7 @@
     parts = call(
         down_kernel,
         jax.ShapeDtypeStruct((tokens + tokens // 3, 256), BF16),
-        [prompt, two, three, one, w_down, w_lat],
+        [prompt, three, two, one, w_down, w_lat],
         flops=2 * 10**10,
     )
     pieces = [parts] + [within(parts, k) for k in (1, 2, 3)]

time: 92.5 us -> 91.3 us (0.987)
  waiting for transfers between devices: 53.2 us -> 52 us
  transfers between devices with their start and end apart: 22 -> 22, of which waited for: 13 -> 15; matrix products, arithmetic and copies ran while one was open for 1% -> 1% of each run, Pallas kernels for 5% -> 5%
where the time goes in v7:
time: 91.3 us; the launch traced here: 90.7 us
  waiting for transfers between devices  52 us (57%)
  starting transfers between devices  27.2 us (30%)
  Pallas kernels  7.05 us (8%)
  local copies, waits for them, and re-layouts  2.36 us (3%)
  other arithmetic  1.25 us (1%)
    ppermute x18, waiting for transfers between devices, route(): return lax.ppermute(array, ('section', 'tp'), pairs)  51.3 us
    ppermute x18, starting transfers between devices, route(): return lax.ppermute(array, ('section', 'tp'), pairs)  26.1 us
    pallas_call x5, Pallas kernels, call(): pl.pallas_call(kernel, out_shape=out_shape, in_specs=[SMEM] * scalars + [...  7.05 us
    unnamed x28, local copies, waits for them, and re-layouts  2.3 us
  transfers between devices with their start and end apart: 22, of which 15 were waited for; matrix products, arithmetic and copies ran while one was open for 1% of the time, Pallas kernels for 5%

profile of v7, /device:TPU:4, one launch (start us, length us, event | category | flops | bytes accessed | tf_op | source)
XLA Modules:
  0.0 90.7 jit_solution(3406484533787022213)
XLA Ops:
  0.6 1.6 %collective-permute-start = (bf16[192,640]{1,0:T(8,128)(2,1)}, bf16[192,640]{1,0:T(8,128)(2,1)S(1)}, u32[]{:S(2)}, u32[]{:S(2)}) collective-permute-start(bf16[192,640]{1,0:T(8,128)(2,1)} %prompt.3), channel_id=1, source_target_pairs={{0,12},{4,8},{8,4},{12,0},{16,20},{20,16},{24,28},{28,24},{1,13},{... | collective-permute-start | bytes 737288 | tf_op jit(solution)/shard_map/ppermute | solution.py:475
  2.3 1.4 %collective-permute-start.1 = (bf16[192,640]{1,0:T(8,128)(2,1)}, bf16[192,640]{1,0:T(8,128)(2,1)S(1)}, u32[]{:S(2)}, u32[]{:S(2)}) collective-permute-start(bf16[192,640]{1,0:T(8,128)(2,1)} %prompt.3), channel_id=1, source_target_pairs={{0,16},{4,20},{8,24},{12,28},{16,8},{20,12},{24,0},{28,4},{1,17},{... | collective-permute-start | bytes 737288 | tf_op jit(solution)/shard_map/ppermute | solution.py:475
  3.7 1.8 %shard_map.104 = bf16[192,640]{1,0:T(8,128)(2,1)} custom-call(bf16[192,640]{1,0:T(8,128)(2,1)} %prompt.3, bf16[136,2560]{1,0:T(8,128)(2,1)} %bitcast.28), custom_call_target="tpu_custom_call" | custom-call | flops 20000000000 | bytes 942080 | tf_op jit(solution)/shard_map/pallas_call | solution.py:179
  5.5 1.3 %collective-permute-start.2 = (bf16[192,640]{1,0:T(8,128)(2,1)}, bf16[192,640]{1,0:T(8,128)(2,1)S(1)}, u32[]{:S(2)}, u32[]{:S(2)}) collective-permute-start(bf16[192,640]{1,0:T(8,128)(2,1)} %shard_map.104), channel_id=1, source_target_pairs={{0,4},{4,0},{8,12},{12,8},{16,20},{20,16},{24,28},{28,24},{1,5},{5... | collective-permute-start | bytes 737288 | tf_op jit(solution)/shard_map/ppermute | solution.py:475
  6.8 5.9 %collective-permute-done.three = bf16[192,640]{1,0:T(8,128)(2,1)S(1)} collective-permute-done((bf16[192,640]{1,0:T(8,128)(2,1)}, bf16[192,640]{1,0:T(8,128)(2,1)S(1)}, u32[]{:S(2)}, u32[]{:S(2)}) %collective-permute-start) | collective-permute-done | bytes 245792 | tf_op jit(solution)/shard_map/ppermute | solution.py:475
  12.7 1.5 %collective-permute-done.1.two = bf16[192,640]{1,0:T(8,128)(2,1)S(1)} collective-permute-done((bf16[192,640]{1,0:T(8,128)(2,1)}, bf16[192,640]{1,0:T(8,128)(2,1)S(1)}, u32[]{:S(2)}, u32[]{:S(2)}) %collective-permute-start.1) | collective-permute-done | bytes 245792 | tf_op jit(solution)/shard_map/ppermute | solution.py:475
  14.3 4.9 %collective-permute-done.2.one.share1 = bf16[192,640]{1,0:T(8,128)(2,1)S(1)} collective-permute-done((bf16[192,640]{1,0:T(8,128)(2,1)}, bf16[192,640]{1,0:T(8,128)(2,1)S(1)}, u32[]{:S(2)}, u32[]{:S(2)}) %collective-permute-start.2) | collective-permute-done | bytes 245792 | tf_op jit(solution)/shard_map/ppermute | solution.py:475
  19.1 0.0 copy-start
  19.2 0.0 copy-start.2
  19.2 0.0 copy-start.4
  19.2 0.0 copy-start.6
  19.2 0.0 copy-start.9
  19.2 0.0 copy-start.11
  19.3 1.7 %collective-permute-start.3 = (bf16[256,256]{1,0:T(8,128)(2,1)S(1)}, bf16[256,256]{1,0:T(8,128)(2,1)S(1)}, u32[]{:S(2)}, u32[]{:S(2)}) collective-permute-start(bf16[256,256]{1,0:T(8,128)(2,1)S(1)} %shard_map.105.own), channel_id=1, source_target_pairs={{0,4},{4,0},{8,12},{12,8},{16,20},{20,16},{24,28},{28,24},{1,5},{5... | collective-permute-start | bytes 393224 | tf_op jit(solution)/shard_map/ppermute | solution.py:475
  20.9 2.5 %collective-permute-start.4 = (bf16[256,256]{1,0:T(8,128)(2,1)S(1)}, bf16[256,256]{1,0:T(8,128)(2,1)S(1)}, u32[]{:S(2)}, u32[]{:S(2)}) collective-permute-start(bf16[256,256]{1,0:T(8,128)(2,1)S(1)} %shard_map.105.own), channel_id=1, source_target_pairs={{0,8},{4,12},{8,0},{12,4},{16,24},{20,28},{24,16},{28,20},{1,9},{5... | collective-permute-start | bytes 393224 | tf_op jit(solution)/shard_map/ppermute | solution.py:475
  23.5 0.2 collective-permute-start.5
  23.7 2.0 %collective-permute-done.3.one = bf16[256,256]{1,0:T(8,128)(2,1)S(1)} collective-permute-done((bf16[256,256]{1,0:T(8,128)(2,1)S(1)}, bf16[256,256]{1,0:T(8,128)(2,1)S(1)}, u32[]{:S(2)}, u32[]{:S(2)}) %collective-permute-start.3) | collective-permute-done | bytes 131104 | tf_op jit(solution)/shard_map/ppermute | solution.py:475
  25.7 7.3 %collective-permute-done.4.two = bf16[256,256]{1,0:T(8,128)(2,1)S(1)} collective-permute-done((bf16[256,256]{1,0:T(8,128)(2,1)S(1)}, bf16[256,256]{1,0:T(8,128)(2,1)S(1)}, u32[]{:S(2)}, u32[]{:S(2)}) %collective-permute-start.4) | collective-permute-done | bytes 131104 | tf_op jit(solution)/shard_map/ppermute | solution.py:475
  33.1 0.6 shard_map.106
  33.7 4.9 %collective-permute-start.10 = (bf16[2,136,896]{2,1,0:T(8,128)(2,1)S(1)}, bf16[2,136,896]{2,1,0:T(8,128)(2,1)S(1)}, u32[]{:S(2)}, u32[]{:S(2)}) collective-permute-start(bf16[2,136,896]{2,1,0:T(8,128)(2,1)S(1)} %get-tuple-element.24), channel_id=1, source_target_pairs={{16,24},{20,28},{24,16},{28,20},{17,25},{21,29},{25,17},{29,21},{1... | collective-permute-start | bytes 1462280 | tf_op jit(solution)/shard_map/ppermute | solution.py:475
  38.6 0.1 collective-permute-start.6
  38.6 2.8 %collective-permute-start.7 = (bf16[56,2560]{1,0:T(8,128)(2,1)S(1)}, bf16[56,2560]{1,0:T(8,128)(2,1)S(1)}, u32[]{:S(2)}, u32[]{:S(2)}) collective-permute-start(bf16[56,2560]{1,0:T(8,128)(2,1)S(1)} %get-tuple-element.21), channel_id=1, source_target_pairs={{0,24},{4,28},{8,16},{12,20},{16,0},{20,4},{24,8},{28,12},{1,25},{... | collective-permute-start | bytes 860168 | tf_op jit(solution)/shard_map/ppermute | solution.py:475
  41.5 0.0 collective-permute-start.8
  41.5 0.7 collective-permute-start.9
  42.2 16.2 %collective-permute-done.10 = bf16[2,136,896]{2,1,0:T(8,128)(2,1)S(1)} collective-permute-done((bf16[2,136,896]{2,1,0:T(8,128)(2,1)S(1)}, bf16[2,136,896]{2,1,0:T(8,128)(2,1)S(1)}, u32[]{:S(2)}, u32[]{:S(2)}) %collective-permute-start.10) | collective-permute-done | bytes 487456 | tf_op jit(solution)/shard_map/ppermute | solution.py:475
  58.5 0.6 collective-permute-start.11
  59.1 6.0 %collective-permute-done.7.two = bf16[56,2560]{1,0:T(8,128)(2,1)S(1)} collective-permute-done((bf16[56,2560]{1,0:T(8,128)(2,1)S(1)}, bf16[56,2560]{1,0:T(8,128)(2,1)S(1)}, u32[]{:S(2)}, u32[]{:S(2)}) %collective-permute-start.7) | collective-permute-done | bytes 286752 | tf_op jit(solution)/shard_map/ppermute | solution.py:475
  65.1 0.5 collective-permute-start.13
  65.6 0.7 collective-permute-done.9.four
  66.3 0.3 collective-permute-done.12.near2
  66.6 0.3 collective-permute-done.13.near3
  67.0 1.6 %shard_map.107 = (bf16[56,512]{1,0:T(8,128)(2,1)S(1)}, bf16[48,544]{1,0:T(8,128)(2,1)S(1)}, bf16[8,640]{1,0:T(8,128)(2,1)S(1)}) custom-call(bf16[56,2560]{1,0:T(8,128)(2,1)S(1)} %collective-permute-done.6.one, bf16[56,2560]{1,0:T(8,128)(2,1)S(1)} %collective-permute-done.7.two, bf16[56,2560]{1,0:T(8,128)(2,1)S(1)} %collective-permute-done.8.three, ...), custom_call_target="tpu_custom_call" | custom-call | flops 199999995904 | bytes 4939776 | tf_op jit(solution)/shard_map/pallas_call | solution.py:179
  68.6 0.1 collective-permute-start.16
  68.7 3.9 %collective-permute-start.17 = (bf16[56,512]{1,0:T(8,128)(2,1)S(1)}, bf16[56,512]{1,0:T(8,128)(2,1)S(1)}, u32[]{:S(2)}, u32[]{:S(2)}) collective-permute-start(bf16[56,512]{1,0:T(8,128)(2,1)S(1)} %get-tuple-element.31.own), channel_id=1, source_target_pairs={{0,8},{4,12},{8,0},{12,4},{16,24},{20,28},{24,16},{28,20},{1,9},{5... | collective-permute-start | bytes 172040 | tf_op jit(solution)/shard_map/ppermute | solution.py:475
  72.6 0.4 collective-permute-start.18
  73.0 3.2 %collective-permute-done.17.two = bf16[56,512]{1,0:T(8,128)(2,1)S(1)} collective-permute-done((bf16[56,512]{1,0:T(8,128)(2,1)S(1)}, bf16[56,512]{1,0:T(8,128)(2,1)S(1)}, u32[]{:S(2)}, u32[]{:S(2)}) %collective-permute-start.17) | collective-permute-done | bytes 57376 | tf_op jit(solution)/shard_map/ppermute | solution.py:475
  76.2 2.5 %collective-permute-done.18.three = bf16[56,512]{1,0:T(8,128)(2,1)} collective-permute-done((bf16[56,512]{1,0:T(8,128)(2,1)S(1)}, bf16[56,512]{1,0:T(8,128)(2,1)}, u32[]{:S(2)}, u32[]{:S(2)}) %collective-permute-start.18) | collective-permute-done | bytes 57376 | tf_op jit(solution)/shard_map/ppermute | solution.py:475
  78.7 0.0 copy-start.3
  78.7 1.2 %copy-done.3 = bf16[1,768,640]{2,1,0:T(8,128)(2,1)S(1)} copy-done((bf16[1,768,640]{2,1,0:T(8,128)(2,1)S(1)}, bf16[1,768,640]{2,1,0:T(8,128)(2,1)}, u32[]{:S(2)}) %copy-start.3) | copy-done | bytes 983064
  79.9 1.0 %copy-done.7 = bf16[1,512,512]{2,1,0:T(8,128)(2,1)S(1)} copy-done((bf16[1,512,512]{2,1,0:T(8,128)(2,1)S(1)}, bf16[1,512,512]{2,1,0:T(8,128)(2,1)}, u32[]{:S(2)}) %copy-start.7) | copy-done | bytes 524312
  81.0 2.9 %shard_map.108 = (bf16[8,640]{1,0:T(8,128)(2,1)S(1)}, bf16[8,640]{1,0:T(8,128)(2,1)S(1)}, bf16[8,640]{1,0:T(8,128)(2,1)S(1)}, bf16[8,640]{1,0:T(8,128)(2,1)S(1)}) custom-call(s32[8]{0:T(128)S(1)} %copy-done.12, bf16[56,512]{1,0:T(8,128)(2,1)S(1)} %get-tuple-element.31.own, bf16[56,512]{1,0:T(8,128)(2,1)S(1)} %collective-permute-done.16.one, ...), custom_call_target="tpu_custom_call" | custom-call | flops 201326592 | bytes 4907040 | tf_op jit(solution)/shard_map/pallas_call | solution.py:179
  83.9 1.5 %collective-permute-start.21 = (bf16[8,640]{1,0:T(8,128)(2,1)S(1)}, bf16[8,640]{1,0:T(8,128)(2,1)S(1)}, u32[]{:S(2)}, u32[]{:S(2)}) collective-permute-start(bf16[8,640]{1,0:T(8,128)(2,1)S(1)} %get-tuple-element.35), channel_id=1, source_target_pairs={{0,12},{4,8},{8,4},{12,0},{16,28},{20,24},{24,20},{28,16},{1,13},{... | collective-permute-start | bytes 30728 | tf_op jit(solution)/shard_map/ppermute | solution.py:475
  85.4 3.0 %collective-permute-start.19 = (bf16[8,640]{1,0:T(8,128)(2,1)S(1)}, bf16[8,640]{1,0:T(8,128)(2,1)S(1)}, u32[]{:S(2)}, u32[]{:S(2)}) collective-permute-start(bf16[8,640]{1,0:T(8,128)(2,1)S(1)} %get-tuple-element.33), channel_id=1, source_target_pairs={{0,4},{4,0},{8,12},{12,8},{16,20},{20,16},{24,28},{28,24},{1,5},{5... | collective-permute-start | bytes 30728 | tf_op jit(solution)/shard_map/ppermute | solution.py:475
  88.3 0.6 select_bitcast_fusion
  89.0 0.4 collective-permute-done.21
  89.4 0.5 collective-permute-done.20
  89.9 0.1 collective-permute-done.19
  90.0 0.6 fusion.1
  (33 shorter events, 0.2 us)
Async XLA Ops:
  0.6 12.1 %collective-permute-start = (bf16[192,640]{1,0:T(8,128)(2,1)}, bf16[192,640]{1,0:T(8,128)(2,1)S(1)}, u32[]{:S(2)}, u32[]{:S(2)}) collective-permute-start(bf16[192,640]{1,0:T(8,128)(2,1)} %prompt.3), channel_id=1, source_target_pairs={{0,12},{4,8},{8,4},{12,0},{16,20},{20,16},{24,28},{28,24},{1,13},{... | collective-permute-start | bytes 737288 | tf_op jit(solution)/shard_map/ppermute | solution.py:475
  2.3 12.0 %collective-permute-start.1 = (bf16[192,640]{1,0:T(8,128)(2,1)}, bf16[192,640]{1,0:T(8,128)(2,1)S(1)}, u32[]{:S(2)}, u32[]{:S(2)}) collective-permute-start(bf16[192,640]{1,0:T(8,128)(2,1)} %prompt.3), channel_id=1, source_target_pairs={{0,16},{4,20},{8,24},{12,28},{16,8},{20,12},{24,0},{28,4},{1,17},{... | collective-permute-start | bytes 737288 | tf_op jit(solution)/shard_map/ppermute | solution.py:475
  3.7 15.5 %copy-start.8 = (bf16[1,2560,136]{1,2,0:T(8,128)(2,1)S(1)}, bf16[1,2560,136]{1,2,0:T(8,128)(2,1)}, u32[]{:S(2)}) copy-start(bf16[1,2560,136]{1,2,0:T(8,128)(2,1)} %param.13) | copy-start | bytes 2088964
  3.7 15.5 %copy-start.10 = (bf16[192,640]{1,0:T(8,128)(2,1)S(1)}, bf16[192,640]{1,0:T(8,128)(2,1)}, u32[]{:S(2)}) copy-start(bf16[192,640]{1,0:T(8,128)(2,1)} %prompt.3) | copy-start | bytes 737284
  3.7 15.5 %copy-start.13 = (bf16[1,2560,192]{1,2,0:T(8,128)(2,1)S(1)}, bf16[1,2560,192]{1,2,0:T(8,128)(2,1)}, u32[]{:S(2)}) copy-start(bf16[1,2560,192]{1,2,0:T(8,128)(2,1)} %param.11) | copy-start | bytes 2949124
  5.5 13.6 %collective-permute-start.2 = (bf16[192,640]{1,0:T(8,128)(2,1)}, bf16[192,640]{1,0:T(8,128)(2,1)S(1)}, u32[]{:S(2)}, u32[]{:S(2)}) collective-permute-start(bf16[192,640]{1,0:T(8,128)(2,1)} %shard_map.104), channel_id=1, source_target_pairs={{0,4},{4,0},{8,12},{12,8},{16,20},{20,16},{24,28},{28,24},{1,5},{5... | collective-permute-start | bytes 737288 | tf_op jit(solution)/shard_map/ppermute | solution.py:475
  19.1 13.9 %copy-start = (bf16[1,512,2560]{2,1,0:T(8,128)(2,1)S(1)}, bf16[1,512,2560]{2,1,0:T(8,128)(2,1)}, u32[]{:S(2)}) copy-start(bf16[1,512,2560]{2,1,0:T(8,128)(2,1)} %param.16) | copy-start | bytes 7864324
  19.2 13.9 %copy-start.2 = (bf16[1,768,640]{2,1,0:T(8,128)(2,1)S(1)}, bf16[1,768,640]{2,1,0:T(8,128)(2,1)}, u32[]{:S(2)}) copy-start(bf16[1,768,640]{2,1,0:T(8,128)(2,1)} %param.12) | copy-start | bytes 2949124
  19.2 13.9 %copy-start.4 = (bf16[1,512,512]{2,1,0:T(8,128)(2,1)S(1)}, bf16[1,512,512]{2,1,0:T(8,128)(2,1)}, u32[]{:S(2)}) copy-start(bf16[1,512,512]{2,1,0:T(8,128)(2,1)} %param.14) | copy-start | bytes 1572868
  19.2 13.9 %copy-start.6 = (bf16[1,512,512]{2,1,0:T(8,128)(2,1)S(1)}, bf16[1,512,512]{2,1,0:T(8,128)(2,1)}, u32[]{:S(2)}) copy-start(bf16[1,512,512]{2,1,0:T(8,128)(2,1)} %param.15) | copy-start | bytes 1572868
  19.2 13.9 %copy-start.9 = (f32[192,32]{1,0:T(8,128)S(1)}, f32[192,32]{1,0:T(8,128)}, u32[]{:S(2)}) copy-start(f32[192,32]{1,0:T(8,128)} %constant.10.clone.angles) | copy-start | bytes 73732
  19.2 13.9 %copy-start.11 = (s32[8]{0:T(128)S(1)}, s32[8]{0:T(128)}, u32[]{:S(2)}) copy-start(s32[8]{0:T(128)} %sizes.3) | copy-start | bytes 100
  19.3 6.5 %collective-permute-start.3 = (bf16[256,256]{1,0:T(8,128)(2,1)S(1)}, bf16[256,256]{1,0:T(8,128)(2,1)S(1)}, u32[]{:S(2)}, u32[]{:S(2)}) collective-permute-start(bf16[256,256]{1,0:T(8,128)(2,1)S(1)} %shard_map.105.own), channel_id=1, source_target_pairs={{0,4},{4,0},{8,12},{12,8},{16,20},{20,16},{24,28},{28,24},{1,5},{5... | collective-permute-start | bytes 393224 | tf_op jit(solution)/shard_map/ppermute | solution.py:475
  20.9 12.1 %collective-permute-start.4 = (bf16[256,256]{1,0:T(8,128)(2,1)S(1)}, bf16[256,256]{1,0:T(8,128)(2,1)S(1)}, u32[]{:S(2)}, u32[]{:S(2)}) collective-permute-start(bf16[256,256]{1,0:T(8,128)(2,1)S(1)} %shard_map.105.own), channel_id=1, source_target_pairs={{0,8},{4,12},{8,0},{12,4},{16,24},{20,28},{24,16},{28,20},{1,9},{5... | collective-permute-start | bytes 393224 | tf_op jit(solution)/shard_map/ppermute | solution.py:475
  23.5 9.5 %collective-permute-start.5 = (bf16[256,256]{1,0:T(8,128)(2,1)S(1)}, bf16[256,256]{1,0:T(8,128)(2,1)S(1)}, u32[]{:S(2)}, u32[]{:S(2)}) collective-permute-start(bf16[256,256]{1,0:T(8,128)(2,1)S(1)} %shard_map.105.own), channel_id=1, source_target_pairs={{0,12},{4,8},{8,4},{12,0},{16,28},{20,24},{24,20},{28,16},{1,13},{... | collective-permute-start | bytes 393224 | tf_op jit(solution)/shard_map/ppermute | solution.py:475
  33.7 24.7 %collective-permute-start.10 = (bf16[2,136,896]{2,1,0:T(8,128)(2,1)S(1)}, bf16[2,136,896]{2,1,0:T(8,128)(2,1)S(1)}, u32[]{:S(2)}, u32[]{:S(2)}) collective-permute-start(bf16[2,136,896]{2,1,0:T(8,128)(2,1)S(1)} %get-tuple-element.24), channel_id=1, source_target_pairs={{16,24},{20,28},{24,16},{28,20},{17,25},{21,29},{25,17},{29,21},{1... | collective-permute-start | bytes 1462280 | tf_op jit(solution)/shard_map/ppermute | solution.py:475
  38.6 19.9 %collective-permute-start.6 = (bf16[56,2560]{1,0:T(8,128)(2,1)S(1)}, bf16[56,2560]{1,0:T(8,128)(2,1)S(1)}, u32[]{:S(2)}, u32[]{:S(2)}) collective-permute-start(bf16[56,2560]{1,0:T(8,128)(2,1)S(1)} %get-tuple-element.20), channel_id=1, source_target_pairs={{0,28},{4,24},{8,20},{12,16},{16,0},{20,4},{24,8},{28,12},{1,29},{... | collective-permute-start | bytes 860168 | tf_op jit(solution)/shard_map/ppermute | solution.py:475
  38.6 26.5 %collective-permute-start.7 = (bf16[56,2560]{1,0:T(8,128)(2,1)S(1)}, bf16[56,2560]{1,0:T(8,128)(2,1)S(1)}, u32[]{:S(2)}, u32[]{:S(2)}) collective-permute-start(bf16[56,2560]{1,0:T(8,128)(2,1)S(1)} %get-tuple-element.21), channel_id=1, source_target_pairs={{0,24},{4,28},{8,16},{12,20},{16,0},{20,4},{24,8},{28,12},{1,25},{... | collective-permute-start | bytes 860168 | tf_op jit(solution)/shard_map/ppermute | solution.py:475
  41.5 23.6 %collective-permute-start.8 = (bf16[56,2560]{1,0:T(8,128)(2,1)S(1)}, bf16[56,2560]{1,0:T(8,128)(2,1)S(1)}, u32[]{:S(2)}, u32[]{:S(2)}) collective-permute-start(bf16[56,2560]{1,0:T(8,128)(2,1)S(1)} %get-tuple-element.22), channel_id=1, source_target_pairs={{0,20},{4,16},{8,28},{12,24},{16,0},{20,4},{24,8},{28,12},{1,21},{... | collective-permute-start | bytes 860168 | tf_op jit(solution)/shard_map/ppermute | solution.py:475
  41.5 24.8 %collective-permute-start.9 = (bf16[56,2560]{1,0:T(8,128)(2,1)S(1)}, bf16[56,2560]{1,0:T(8,128)(2,1)S(1)}, u32[]{:S(2)}, u32[]{:S(2)}) collective-permute-start(bf16[56,2560]{1,0:T(8,128)(2,1)S(1)} %get-tuple-element.23), channel_id=1, source_target_pairs={{0,16},{4,20},{8,24},{12,28},{16,0},{20,4},{24,8},{28,12},{1,17},{... | collective-permute-start | bytes 860168 | tf_op jit(solution)/shard_map/ppermute | solution.py:475
  58.5 8.5 %collective-permute-start.14 = (bf16[3,136,384]{2,1,0:T(8,128)(2,1)S(1)}, bf16[3,136,384]{2,1,0:T(8,128)(2,1)S(1)}, u32[]{:S(2)}, u32[]{:S(2)}) collective-permute-start(bf16[3,136,384]{2,1,0:T(8,128)(2,1)S(1)} %get-tuple-element.28.rest), channel_id=1, source_target_pairs={{0,1},{1,0},{2,3},{3,2},{4,5},{5,4},{6,7},{7,6},{8,9},{9,8},{10,11... | collective-permute-start | bytes 940040 | tf_op jit(solution)/shard_map/ppermute | solution.py:484
  58.5 7.8 %collective-permute-start.11 = (bf16[136,896]{1,0:T(8,128)(2,1)S(1)}, bf16[136,896]{1,0:T(8,128)(2,1)S(1)}, u32[]{:S(2)}, u32[]{:S(2)}) collective-permute-start(bf16[136,896]{1,0:T(8,128)(2,1)S(1)} %slice_bitcast_fusion.2.first1), channel_id=1, source_target_pairs={{0,1},{1,0},{2,3},{3,2},{4,5},{5,4},{6,7},{7,6},{8,9},{9,8},{10,11... | collective-permute-start | bytes 731144 | tf_op jit(solution)/shard_map/ppermute | solution.py:484
  65.1 1.5 %collective-permute-start.12 = (bf16[136,896]{1,0:T(8,128)(2,1)S(1)}, bf16[136,896]{1,0:T(8,128)(2,1)S(1)}, u32[]{:S(2)}, u32[]{:S(2)}) collective-permute-start(bf16[136,896]{1,0:T(8,128)(2,1)S(1)} %get-tuple-element.37.first2), channel_id=1, source_target_pairs={{0,1},{1,0},{2,3},{3,2},{4,5},{5,4},{6,7},{7,6},{8,9},{9,8},{10,11... | collective-permute-start | bytes 731144 | tf_op jit(solution)/shard_map/ppermute | solution.py:484
  65.1 1.9 %collective-permute-start.13 = (bf16[136,896]{1,0:T(8,128)(2,1)S(1)}, bf16[136,896]{1,0:T(8,128)(2,1)S(1)}, u32[]{:S(2)}, u32[]{:S(2)}) collective-permute-start(bf16[136,896]{1,0:T(8,128)(2,1)S(1)} %get-tuple-element.36.first3), channel_id=1, source_target_pairs={{0,1},{1,0},{2,3},{3,2},{4,5},{5,4},{6,7},{7,6},{8,9},{9,8},{10,11... | collective-permute-start | bytes 731144 | tf_op jit(solution)/shard_map/ppermute | solution.py:484
  67.0 11.7 %copy-start.1 = (bf16[1,512,2560]{2,1,0:T(8,128)(2,1)S(1)}, bf16[1,512,2560]{2,1,0:T(8,128)(2,1)}, u32[]{:S(2)}) copy-start(bf16[1,512,2560]{2,1,0:T(8,128)(2,1)} %param.16) | copy-start | bytes 7864324
  67.0 11.7 %copy-start.5 = (bf16[1,512,512]{2,1,0:T(8,128)(2,1)S(1)}, bf16[1,512,512]{2,1,0:T(8,128)(2,1)}, u32[]{:S(2)}) copy-start(bf16[1,512,512]{2,1,0:T(8,128)(2,1)} %param.14) | copy-start | bytes 1572868
  67.0 11.7 %copy-start.12 = (s32[8]{0:T(128)S(1)}, s32[8]{0:T(128)}, u32[]{:S(2)}) copy-start(s32[8]{0:T(128)} %sizes.3) | copy-start | bytes 100
  68.6 4.4 %collective-permute-start.16 = (bf16[56,512]{1,0:T(8,128)(2,1)S(1)}, bf16[56,512]{1,0:T(8,128)(2,1)S(1)}, u32[]{:S(2)}, u32[]{:S(2)}) collective-permute-start(bf16[56,512]{1,0:T(8,128)(2,1)S(1)} %get-tuple-element.31.own), channel_id=1, source_target_pairs={{0,4},{4,0},{8,12},{12,8},{16,20},{20,16},{24,28},{28,24},{1,5},{5... | collective-permute-start | bytes 172040 | tf_op jit(solution)/shard_map/ppermute | solution.py:475
  68.7 7.6 %collective-permute-start.17 = (bf16[56,512]{1,0:T(8,128)(2,1)S(1)}, bf16[56,512]{1,0:T(8,128)(2,1)S(1)}, u32[]{:S(2)}, u32[]{:S(2)}) collective-permute-start(bf16[56,512]{1,0:T(8,128)(2,1)S(1)} %get-tuple-element.31.own), channel_id=1, source_target_pairs={{0,8},{4,12},{8,0},{12,4},{16,24},{20,28},{24,16},{28,20},{1,9},{5... | collective-permute-start | bytes 172040 | tf_op jit(solution)/shard_map/ppermute | solution.py:475
  72.6 6.1 %collective-permute-start.18 = (bf16[56,512]{1,0:T(8,128)(2,1)S(1)}, bf16[56,512]{1,0:T(8,128)(2,1)}, u32[]{:S(2)}, u32[]{:S(2)}) collective-permute-start(bf16[56,512]{1,0:T(8,128)(2,1)S(1)} %get-tuple-element.31.own), channel_id=1, source_target_pairs={{0,12},{4,8},{8,4},{12,0},{16,28},{20,24},{24,20},{28,16},{1,13},{... | collective-permute-start | bytes 172040 | tf_op jit(solution)/shard_map/ppermute | solution.py:475
  73.0 15.9 %collective-permute-start.15 = (bf16[8,640]{1,0:T(8,128)(2,1)S(1)}, bf16[8,640]{1,0:T(8,128)(2,1)S(1)}, u32[]{:S(2)}, u32[]{:S(2)}) collective-permute-start(bf16[8,640]{1,0:T(8,128)(2,1)S(1)} %get-tuple-element.30), channel_id=1, source_target_pairs={{0,16},{4,20},{8,24},{12,28},{16,0},{20,4},{24,8},{28,12},{1,17},{... | collective-permute-start | bytes 30728 | tf_op jit(solution)/shard_map/ppermute | solution.py:475
  78.7 1.2 %copy-start.3 = (bf16[1,768,640]{2,1,0:T(8,128)(2,1)S(1)}, bf16[1,768,640]{2,1,0:T(8,128)(2,1)}, u32[]{:S(2)}) copy-start(bf16[1,768,640]{2,1,0:T(8,128)(2,1)} %param.12) | copy-start | bytes 2949124
  79.9 1.0 %copy-start.7 = (bf16[1,512,512]{2,1,0:T(8,128)(2,1)S(1)}, bf16[1,512,512]{2,1,0:T(8,128)(2,1)}, u32[]{:S(2)}) copy-start(bf16[1,512,512]{2,1,0:T(8,128)(2,1)} %param.15) | copy-start | bytes 1572868
  83.9 5.5 %collective-permute-start.21 = (bf16[8,640]{1,0:T(8,128)(2,1)S(1)}, bf16[8,640]{1,0:T(8,128)(2,1)S(1)}, u32[]{:S(2)}, u32[]{:S(2)}) collective-permute-start(bf16[8,640]{1,0:T(8,128)(2,1)S(1)} %get-tuple-element.35), channel_id=1, source_target_pairs={{0,12},{4,8},{8,4},{12,0},{16,28},{20,24},{24,20},{28,16},{1,13},{... | collective-permute-start | bytes 30728 | tf_op jit(solution)/shard_map/ppermute | solution.py:475
  85.4 4.6 %collective-permute-start.20 = (bf16[8,640]{1,0:T(8,128)(2,1)S(1)}, bf16[8,640]{1,0:T(8,128)(2,1)S(1)}, u32[]{:S(2)}, u32[]{:S(2)}) collective-permute-start(bf16[8,640]{1,0:T(8,128)(2,1)S(1)} %get-tuple-element.34), channel_id=1, source_target_pairs={{0,8},{4,12},{8,0},{12,4},{16,24},{20,28},{24,16},{28,20},{1,9},{5... | collective-permute-start | bytes 30728 | tf_op jit(solution)/shard_map/ppermute | solution.py:475
  85.4 4.7 %collective-permute-start.19 = (bf16[8,640]{1,0:T(8,128)(2,1)S(1)}, bf16[8,640]{1,0:T(8,128)(2,1)S(1)}, u32[]{:S(2)}, u32[]{:S(2)}) collective-permute-start(bf16[8,640]{1,0:T(8,128)(2,1)S(1)} %get-tuple-element.33), channel_id=1, source_target_pairs={{0,4},{4,0},{8,12},{12,8},{16,20},{20,16},{24,28},{28,24},{1,5},{5... | collective-permute-start | bytes 30728 | tf_op jit(solution)/shard_map/ppermute | solution.py:475

commit v8 on v7

--- a/solution.py
+++ b/solution.py
@@ -424,8 +424,7 @@
 
 
 def ends_kernel(
-    sizes, own, one, two, three, angles, w_query, w_keys, w_values, w_out,
-    out0, out1, out2, out3, stack, total,
+    sizes, own, three, two, one, angles, w_query, w_keys, w_values, out, stack
 ):
     tp = lax.axis_index("tp")
     ends = end_rows(sizes)
@@ -433,7 +432,6 @@
     block = own.shape[0] - count
     steps = block // count
     down_cols = w_query.shape[0] // 4
-    width = out0.shape[1]
     for k, ref in enumerate((own, one, two, three)):
         stack[tp ^ k] = ref[...].astype(F32)
     pieces = [stack[m] for m in range(4)]
@@ -448,8 +446,13 @@
     compressed = (down * unit(down)).astype(BF16)
     end_angles = jnp.concatenate([angles[pl.ds(e, 1), :] for e in ends], axis=0)
     seen = lax.broadcasted_iota(jnp.int32, (count, 4 * block), 1) <= column(ends)
-    mixed = attend_rows(compressed, cache, seen, end_angles, w_query, w_keys, w_values)
-    total[...] = dot(mixed, w_out[...])
+    out[...] = attend_rows(compressed, cache, seen, end_angles, w_query, w_keys, w_values)
+
+
+def final_kernel(mixed, w_out, out0, out1, out2, out3, total):
+    tp = lax.axis_index("tp")
+    width = out0.shape[1]
+    total[...] = dot(mixed[...], w_out[...])
     for k, out in enumerate((out0, out1, out2, out3)):
         columns = pl.ds(pl.multiple_of((tp ^ k) * width, 128), width)
         out[...] = total[:, columns].astype(BF16)
@@ -527,7 +530,7 @@
         scalars=1,
         grant=16,
     )
-    arrived = [onward(blocks[k], k) for k in (3, 2, 1, 0)]
+    arrived = [onward(blocks[k], k) for k in (2, 1, 3, 0)]
     relayed = route(passed, None, (1, 2))
     relayed, late, first = lax.optimization_barrier((relayed, rest, passed[1]))
     weights = [first, relayed[0], relayed[1], late]
@@ -543,18 +546,22 @@
         [pltpu.VMEM((block + count, model), F32), pltpu.VMEM((4, block, latent_cols), F32)],
         flops=2 * 10**11,
     )
-    pieces = [fresh] + [within(fresh, k) for k in (1, 2, 3)]
+    pieces = [fresh] + [within(fresh, k) for k in (3, 2, 1)]
     first_ends = onward(ends_share, 0)
+    mixed = call(
+        ends_kernel,
+        jax.ShapeDtypeStruct((count, w_final.shape[0]), BF16),
+        [block_sizes, *pieces, angles, w_up, w_key, w_value],
+        [pltpu.VMEM((4, block + count, LATENT), F32)],
+        flops=2 * 10**10,
+        scalars=1,
+    )
     outs = call(
-        ends_kernel,
+        final_kernel,
         [jax.ShapeDtypeStruct((count, share), BF16)] * 4,
-        [block_sizes, *pieces, angles, w_up, w_key, w_value, w_final],
-        [
-            pltpu.VMEM((4, block + count, LATENT), F32),
-            pltpu.VMEM((count, model), F32),
-        ],
-        flops=2 * tokens * (w_key.size + w_value.size),
-        scalars=1,
+        [mixed, w_final],
+        [pltpu.VMEM((count, model), F32)],
+        flops=10**8,
     )
     total = ends_share.astype(F32) + outs[0].astype(F32)
     for k in (1, 2, 3):

time: 91.3 us -> 85.7 us (0.939)
  waiting for transfers between devices: 52 us -> 48 us
  local copies, waits for them, and re-layouts: 2.36 us -> 0.14 us
  starting transfers between devices: 27.2 us -> 28.5 us
    ppermute x18, waiting for transfers between devices: 51.3 us -> 48 us  [route(): return lax.ppermute(array, ('section', 'tp'), pairs)]
    unnamed x28, local copies, waits for them, and re-layouts: 2.3 us -> 0.08 us
    ppermute x18, starting transfers between devices: 26.1 us -> 27.9 us  [route(): return lax.ppermute(array, ('section', 'tp'), pairs)]
    pallas_call x5 -> x6, Pallas kernels: 7.05 us -> 6.82 us  [call(): pl.pallas_call(kernel, out_shape=out_shape, in_specs=[SMEM] * scalars + [...]
  transfers between devices with their start and end apart: 22 -> 22, of which waited for: 15 -> 12; matrix products, arithmetic and copies ran while one was open for 1% -> 1% of each run, Pallas kernels for 5% -> 5%
where the time goes in v8:
time: 85.7 us; the launch traced here: 85.6 us
  waiting for transfers between devices  48 us (56%)
  starting transfers between devices  28.5 us (33%)
  Pallas kernels  6.82 us (8%)
  other arithmetic  1.25 us (1%)
    ppermute x18, waiting for transfers between devices, route(): return lax.ppermute(array, ('section', 'tp'), pairs)  48 us
    ppermute x18, starting transfers between devices, route(): return lax.ppermute(array, ('section', 'tp'), pairs)  27.9 us
    pallas_call x6, Pallas kernels, call(): pl.pallas_call(kernel, out_shape=out_shape, in_specs=[SMEM] * scalars + [...  6.82 us
  transfers between devices with their start and end apart: 22, of which 12 were waited for; matrix products, arithmetic and copies ran while one was open for 1% of the time, Pallas kernels for 5%

profile of v8, /device:TPU:4, one launch (start us, length us, event | category | flops | bytes accessed | tf_op | source)
XLA Modules:
  0.0 85.6 jit_solution(3843621628731176822)
XLA Ops:
  0.6 1.6 %collective-permute-start = (bf16[192,640]{1,0:T(8,128)(2,1)}, bf16[192,640]{1,0:T(8,128)(2,1)S(1)}, u32[]{:S(2)}, u32[]{:S(2)}) collective-permute-start(bf16[192,640]{1,0:T(8,128)(2,1)} %prompt.3), channel_id=1, source_target_pairs={{0,12},{4,8},{8,4},{12,0},{16,20},{20,16},{24,28},{28,24},{1,13},{... | collective-permute-start | bytes 737288 | tf_op jit(solution)/shard_map/ppermute | solution.py:478
  2.3 1.4 %collective-permute-start.1 = (bf16[192,640]{1,0:T(8,128)(2,1)}, bf16[192,640]{1,0:T(8,128)(2,1)S(1)}, u32[]{:S(2)}, u32[]{:S(2)}) collective-permute-start(bf16[192,640]{1,0:T(8,128)(2,1)} %prompt.3), channel_id=1, source_target_pairs={{0,16},{4,20},{8,24},{12,28},{16,8},{20,12},{24,0},{28,4},{1,17},{... | collective-permute-start | bytes 737288 | tf_op jit(solution)/shard_map/ppermute | solution.py:478
  3.7 1.8 %shard_map.104 = bf16[192,640]{1,0:T(8,128)(2,1)} custom-call(bf16[192,640]{1,0:T(8,128)(2,1)} %prompt.3, bf16[136,2560]{1,0:T(8,128)(2,1)} %bitcast.24), custom_call_target="tpu_custom_call" | custom-call | flops 20000000000 | bytes 942080 | tf_op jit(solution)/shard_map/pallas_call | solution.py:179
  5.5 1.3 %collective-permute-start.2 = (bf16[192,640]{1,0:T(8,128)(2,1)}, bf16[192,640]{1,0:T(8,128)(2,1)S(1)}, u32[]{:S(2)}, u32[]{:S(2)}) collective-permute-start(bf16[192,640]{1,0:T(8,128)(2,1)} %shard_map.104), channel_id=1, source_target_pairs={{0,4},{4,0},{8,12},{12,8},{16,20},{20,16},{24,28},{28,24},{1,5},{5... | collective-permute-start | bytes 737288 | tf_op jit(solution)/shard_map/ppermute | solution.py:478
  6.8 5.9 %collective-permute-done.three = bf16[192,640]{1,0:T(8,128)(2,1)S(1)} collective-permute-done((bf16[192,640]{1,0:T(8,128)(2,1)}, bf16[192,640]{1,0:T(8,128)(2,1)S(1)}, u32[]{:S(2)}, u32[]{:S(2)}) %collective-permute-start) | collective-permute-done | bytes 245792 | tf_op jit(solution)/shard_map/ppermute | solution.py:478
  12.7 1.5 %collective-permute-done.1.two = bf16[192,640]{1,0:T(8,128)(2,1)S(1)} collective-permute-done((bf16[192,640]{1,0:T(8,128)(2,1)}, bf16[192,640]{1,0:T(8,128)(2,1)S(1)}, u32[]{:S(2)}, u32[]{:S(2)}) %collective-permute-start.1) | collective-permute-done | bytes 245792 | tf_op jit(solution)/shard_map/ppermute | solution.py:478
  14.3 4.9 %collective-permute-done.2.one.share1 = bf16[192,640]{1,0:T(8,128)(2,1)S(1)} collective-permute-done((bf16[192,640]{1,0:T(8,128)(2,1)}, bf16[192,640]{1,0:T(8,128)(2,1)S(1)}, u32[]{:S(2)}, u32[]{:S(2)}) %collective-permute-start.2) | collective-permute-done | bytes 245792 | tf_op jit(solution)/shard_map/ppermute | solution.py:478
  19.1 0.0 copy-start
  19.2 0.0 copy-start.2
  19.2 0.0 copy-start.5
  19.2 0.0 copy-start.7
  19.2 0.0 copy-start.10
  19.2 0.0 copy-start.11
  19.3 1.7 %collective-permute-start.3 = (bf16[256,256]{1,0:T(8,128)(2,1)S(1)}, bf16[256,256]{1,0:T(8,128)(2,1)S(1)}, u32[]{:S(2)}, u32[]{:S(2)}) collective-permute-start(bf16[256,256]{1,0:T(8,128)(2,1)S(1)} %shard_map.105.own), channel_id=1, source_target_pairs={{0,4},{4,0},{8,12},{12,8},{16,20},{20,16},{24,28},{28,24},{1,5},{5... | collective-permute-start | bytes 393224 | tf_op jit(solution)/shard_map/ppermute | solution.py:478
  20.9 2.5 %collective-permute-start.4 = (bf16[256,256]{1,0:T(8,128)(2,1)S(1)}, bf16[256,256]{1,0:T(8,128)(2,1)S(1)}, u32[]{:S(2)}, u32[]{:S(2)}) collective-permute-start(bf16[256,256]{1,0:T(8,128)(2,1)S(1)} %shard_map.105.own), channel_id=1, source_target_pairs={{0,8},{4,12},{8,0},{12,4},{16,24},{20,28},{24,16},{28,20},{1,9},{5... | collective-permute-start | bytes 393224 | tf_op jit(solution)/shard_map/ppermute | solution.py:478
  23.5 0.2 collective-permute-start.5
  23.7 2.0 %collective-permute-done.3.one = bf16[256,256]{1,0:T(8,128)(2,1)S(1)} collective-permute-done((bf16[256,256]{1,0:T(8,128)(2,1)S(1)}, bf16[256,256]{1,0:T(8,128)(2,1)S(1)}, u32[]{:S(2)}, u32[]{:S(2)}) %collective-permute-start.3) | collective-permute-done | bytes 131104 | tf_op jit(solution)/shard_map/ppermute | solution.py:478
  25.7 7.3 %collective-permute-done.4.two = bf16[256,256]{1,0:T(8,128)(2,1)S(1)} collective-permute-done((bf16[256,256]{1,0:T(8,128)(2,1)S(1)}, bf16[256,256]{1,0:T(8,128)(2,1)S(1)}, u32[]{:S(2)}, u32[]{:S(2)}) %collective-permute-start.4) | collective-permute-done | bytes 131104 | tf_op jit(solution)/shard_map/ppermute | solution.py:478
  33.0 0.0 collective-permute-done.5.three
  33.1 0.6 shard_map.106
  33.7 4.9 %collective-permute-start.10 = (bf16[2,136,896]{2,1,0:T(8,128)(2,1)S(1)}, bf16[2,136,896]{2,1,0:T(8,128)(2,1)S(1)}, u32[]{:S(2)}, u32[]{:S(2)}) collective-permute-start(bf16[2,136,896]{2,1,0:T(8,128)(2,1)S(1)} %get-tuple-element.24), channel_id=1, source_target_pairs={{16,24},{20,28},{24,16},{28,20},{17,25},{21,29},{25,17},{29,21},{1... | collective-permute-start | bytes 1462280 | tf_op jit(solution)/shard_map/ppermute | solution.py:478
  38.6 0.1 collective-permute-start.6
  38.6 1.5 %collective-permute-start.7 = (bf16[56,2560]{1,0:T(8,128)(2,1)S(1)}, bf16[56,2560]{1,0:T(8,128)(2,1)S(1)}, u32[]{:S(2)}, u32[]{:S(2)}) collective-permute-start(bf16[56,2560]{1,0:T(8,128)(2,1)S(1)} %get-tuple-element.21), channel_id=1, source_target_pairs={{0,20},{4,16},{8,28},{12,24},{16,0},{20,4},{24,8},{28,12},{1,21},{... | collective-permute-start | bytes 860168 | tf_op jit(solution)/shard_map/ppermute | solution.py:478
  40.1 0.1 collective-permute-start.8
  40.3 3.8 %collective-permute-start.9 = (bf16[56,2560]{1,0:T(8,128)(2,1)S(1)}, bf16[56,2560]{1,0:T(8,128)(2,1)S(1)}, u32[]{:S(2)}, u32[]{:S(2)}) collective-permute-start(bf16[56,2560]{1,0:T(8,128)(2,1)S(1)} %get-tuple-element.23), channel_id=1, source_target_pairs={{0,16},{4,20},{8,24},{12,28},{16,0},{20,4},{24,8},{28,12},{1,17},{... | collective-permute-start | bytes 860168 | tf_op jit(solution)/shard_map/ppermute | solution.py:478
  44.1 14.4 %collective-permute-done.10 = bf16[2,136,896]{2,1,0:T(8,128)(2,1)S(1)} collective-permute-done((bf16[2,136,896]{2,1,0:T(8,128)(2,1)S(1)}, bf16[2,136,896]{2,1,0:T(8,128)(2,1)S(1)}, u32[]{:S(2)}, u32[]{:S(2)}) %collective-permute-start.10) | collective-permute-done | bytes 487456 | tf_op jit(solution)/shard_map/ppermute | solution.py:478
  58.5 0.7 collective-permute-done.6.one
  59.2 0.5 collective-permute-start.12
  59.7 0.1 collective-permute-start.13
  59.8 4.9 %collective-permute-done.9.four = bf16[56,2560]{1,0:T(8,128)(2,1)S(1)} collective-permute-done((bf16[56,2560]{1,0:T(8,128)(2,1)S(1)}, bf16[56,2560]{1,0:T(8,128)(2,1)S(1)}, u32[]{:S(2)}, u32[]{:S(2)}) %collective-permute-start.9) | collective-permute-done | bytes 286752 | tf_op jit(solution)/shard_map/ppermute | solution.py:478
  64.8 0.0 copy-start.3
  64.8 0.0 copy-start.6
  64.8 0.0 copy-start.8
  64.8 0.0 copy-start.12
  64.8 1.6 %shard_map.107 = (bf16[56,512]{1,0:T(8,128)(2,1)S(1)}, bf16[48,544]{1,0:T(8,128)(2,1)S(1)}, bf16[8,640]{1,0:T(8,128)(2,1)S(1)}) custom-call(bf16[56,2560]{1,0:T(8,128)(2,1)S(1)} %collective-permute-done.6.one, bf16[56,2560]{1,0:T(8,128)(2,1)S(1)} %collective-permute-done.7.two, bf16[56,2560]{1,0:T(8,128)(2,1)S(1)} %collective-permute-done.8.three, ...), custom_call_target="tpu_custom_call" | custom-call | flops 199999995904 | bytes 4939776 | tf_op jit(solution)/shard_map/pallas_call | solution.py:179
  66.4 2.3 %collective-permute-start.16 = (bf16[56,512]{1,0:T(8,128)(2,1)S(1)}, bf16[56,512]{1,0:T(8,128)(2,1)S(1)}, u32[]{:S(2)}, u32[]{:S(2)}) collective-permute-start(bf16[56,512]{1,0:T(8,128)(2,1)S(1)} %get-tuple-element.31.own), channel_id=1, source_target_pairs={{0,12},{4,8},{8,4},{12,0},{16,28},{20,24},{24,20},{28,16},{1,13},{... | collective-permute-start | bytes 172040 | tf_op jit(solution)/shard_map/ppermute | solution.py:478
  68.7 1.1 %collective-permute-start.17 = (bf16[56,512]{1,0:T(8,128)(2,1)S(1)}, bf16[56,512]{1,0:T(8,128)(2,1)S(1)}, u32[]{:S(2)}, u32[]{:S(2)}) collective-permute-start(bf16[56,512]{1,0:T(8,128)(2,1)S(1)} %get-tuple-element.31.own), channel_id=1, source_target_pairs={{0,8},{4,12},{8,0},{12,4},{16,24},{20,28},{24,16},{28,20},{1,9},{5... | collective-permute-start | bytes 172040 | tf_op jit(solution)/shard_map/ppermute | solution.py:478
  69.8 1.1 %collective-permute-start.18 = (bf16[56,512]{1,0:T(8,128)(2,1)S(1)}, bf16[56,512]{1,0:T(8,128)(2,1)S(1)}, u32[]{:S(2)}, u32[]{:S(2)}) collective-permute-start(bf16[56,512]{1,0:T(8,128)(2,1)S(1)} %get-tuple-element.31.own), channel_id=1, source_target_pairs={{0,4},{4,0},{8,12},{12,8},{16,20},{20,16},{24,28},{28,24},{1,5},{5... | collective-permute-start | bytes 172040 | tf_op jit(solution)/shard_map/ppermute | solution.py:478
  70.9 1.7 %collective-permute-done.16.three = bf16[56,512]{1,0:T(8,128)(2,1)S(1)} collective-permute-done((bf16[56,512]{1,0:T(8,128)(2,1)S(1)}, bf16[56,512]{1,0:T(8,128)(2,1)S(1)}, u32[]{:S(2)}, u32[]{:S(2)}) %collective-permute-start.16) | collective-permute-done | bytes 57376 | tf_op jit(solution)/shard_map/ppermute | solution.py:478
  72.6 2.8 %collective-permute-done.17.two = bf16[56,512]{1,0:T(8,128)(2,1)S(1)} collective-permute-done((bf16[56,512]{1,0:T(8,128)(2,1)S(1)}, bf16[56,512]{1,0:T(8,128)(2,1)S(1)}, u32[]{:S(2)}, u32[]{:S(2)}) %collective-permute-start.17) | collective-permute-done | bytes 57376 | tf_op jit(solution)/shard_map/ppermute | solution.py:478
  75.4 2.2 %shard_map.108.mixed = bf16[8,512]{1,0:T(8,128)(2,1)S(1)} custom-call(s32[8]{0:T(128)S(1)} %copy-done.12, bf16[56,512]{1,0:T(8,128)(2,1)S(1)} %get-tuple-element.31.own, bf16[56,512]{1,0:T(8,128)(2,1)S(1)} %collective-permute-done.16.three, bf16[56,512]{1,0:T(8,128)(2,1)S(1)} %collective-permute-done.17.two, ...), custom_call_target="tpu_custom_call" | custom-call | flops 20000000000 | bytes 2285600 | tf_op jit(solution)/shard_map/pallas_call | solution.py:179
  77.6 0.5 shard_map.109
  78.1 2.2 %collective-permute-start.21 = (bf16[8,640]{1,0:T(8,128)(2,1)S(1)}, bf16[8,640]{1,0:T(8,128)(2,1)S(1)}, u32[]{:S(2)}, u32[]{:S(2)}) collective-permute-start(bf16[8,640]{1,0:T(8,128)(2,1)S(1)} %get-tuple-element.35), channel_id=1, source_target_pairs={{0,12},{4,8},{8,4},{12,0},{16,28},{20,24},{24,20},{28,16},{1,13},{... | collective-permute-start | bytes 30728 | tf_op jit(solution)/shard_map/ppermute | solution.py:478
  80.4 2.2 %collective-permute-start.19 = (bf16[8,640]{1,0:T(8,128)(2,1)S(1)}, bf16[8,640]{1,0:T(8,128)(2,1)S(1)}, u32[]{:S(2)}, u32[]{:S(2)}) collective-permute-start(bf16[8,640]{1,0:T(8,128)(2,1)S(1)} %get-tuple-element.33), channel_id=1, source_target_pairs={{0,4},{4,0},{8,12},{12,8},{16,20},{20,16},{24,28},{28,24},{1,5},{5... | collective-permute-start | bytes 30728 | tf_op jit(solution)/shard_map/ppermute | solution.py:478
  82.6 0.6 select_bitcast_fusion
  83.2 0.4 collective-permute-done.21
  83.6 1.3 %collective-permute-done.20 = bf16[8,640]{1,0:T(8,128)(2,1)S(1)} collective-permute-done((bf16[8,640]{1,0:T(8,128)(2,1)S(1)}, bf16[8,640]{1,0:T(8,128)(2,1)S(1)}, u32[]{:S(2)}, u32[]{:S(2)}) %collective-permute-start.20) | collective-permute-done | bytes 10272 | tf_op jit(solution)/shard_map/ppermute | solution.py:478
  85.0 0.6 fusion.1
  (34 shorter events, 0.2 us)
Async XLA Ops:
  0.6 12.1 %collective-permute-start = (bf16[192,640]{1,0:T(8,128)(2,1)}, bf16[192,640]{1,0:T(8,128)(2,1)S(1)}, u32[]{:S(2)}, u32[]{:S(2)}) collective-permute-start(bf16[192,640]{1,0:T(8,128)(2,1)} %prompt.3), channel_id=1, source_target_pairs={{0,12},{4,8},{8,4},{12,0},{16,20},{20,16},{24,28},{28,24},{1,13},{... | collective-permute-start | bytes 737288 | tf_op jit(solution)/shard_map/ppermute | solution.py:478
  2.3 12.0 %collective-permute-start.1 = (bf16[192,640]{1,0:T(8,128)(2,1)}, bf16[192,640]{1,0:T(8,128)(2,1)S(1)}, u32[]{:S(2)}, u32[]{:S(2)}) collective-permute-start(bf16[192,640]{1,0:T(8,128)(2,1)} %prompt.3), channel_id=1, source_target_pairs={{0,16},{4,20},{8,24},{12,28},{16,8},{20,12},{24,0},{28,4},{1,17},{... | collective-permute-start | bytes 737288 | tf_op jit(solution)/shard_map/ppermute | solution.py:478
  3.7 15.5 %copy-start.4 = (bf16[1,2560,136]{1,2,0:T(8,128)(2,1)S(1)}, bf16[1,2560,136]{1,2,0:T(8,128)(2,1)}, u32[]{:S(2)}) copy-start(bf16[1,2560,136]{1,2,0:T(8,128)(2,1)} %param.13) | copy-start | bytes 2088964
  3.7 15.5 %copy-start.9 = (bf16[192,640]{1,0:T(8,128)(2,1)S(1)}, bf16[192,640]{1,0:T(8,128)(2,1)}, u32[]{:S(2)}) copy-start(bf16[192,640]{1,0:T(8,128)(2,1)} %prompt.3) | copy-start | bytes 737284
  3.7 15.5 %copy-start.13 = (bf16[1,2560,192]{1,2,0:T(8,128)(2,1)S(1)}, bf16[1,2560,192]{1,2,0:T(8,128)(2,1)}, u32[]{:S(2)}) copy-start(bf16[1,2560,192]{1,2,0:T(8,128)(2,1)} %param.11) | copy-start | bytes 2949124
  5.5 13.6 %collective-permute-start.2 = (bf16[192,640]{1,0:T(8,128)(2,1)}, bf16[192,640]{1,0:T(8,128)(2,1)S(1)}, u32[]{:S(2)}, u32[]{:S(2)}) collective-permute-start(bf16[192,640]{1,0:T(8,128)(2,1)} %shard_map.104), channel_id=1, source_target_pairs={{0,4},{4,0},{8,12},{12,8},{16,20},{20,16},{24,28},{28,24},{1,5},{5... | collective-permute-start | bytes 737288 | tf_op jit(solution)/shard_map/ppermute | solution.py:478
  19.1 13.9 %copy-start = (bf16[1,512,2560]{2,1,0:T(8,128)(2,1)S(1)}, bf16[1,512,2560]{2,1,0:T(8,128)(2,1)}, u32[]{:S(2)}) copy-start(bf16[1,512,2560]{2,1,0:T(8,128)(2,1)} %param.16) | copy-start | bytes 7864324
  19.2 13.9 %copy-start.2 = (bf16[1,768,640]{2,1,0:T(8,128)(2,1)S(1)}, bf16[1,768,640]{2,1,0:T(8,128)(2,1)}, u32[]{:S(2)}) copy-start(bf16[1,768,640]{2,1,0:T(8,128)(2,1)} %param.12) | copy-start | bytes 2949124
  19.2 13.9 %copy-start.5 = (bf16[1,512,512]{2,1,0:T(8,128)(2,1)S(1)}, bf16[1,512,512]{2,1,0:T(8,128)(2,1)}, u32[]{:S(2)}) copy-start(bf16[1,512,512]{2,1,0:T(8,128)(2,1)} %param.14) | copy-start | bytes 1572868
  19.2 13.9 %copy-start.7 = (bf16[1,512,512]{2,1,0:T(8,128)(2,1)S(1)}, bf16[1,512,512]{2,1,0:T(8,128)(2,1)}, u32[]{:S(2)}) copy-start(bf16[1,512,512]{2,1,0:T(8,128)(2,1)} %param.15) | copy-start | bytes 1572868
  19.2 13.9 %copy-start.10 = (f32[192,32]{1,0:T(8,128)S(1)}, f32[192,32]{1,0:T(8,128)}, u32[]{:S(2)}) copy-start(f32[192,32]{1,0:T(8,128)} %constant.10.clone.angles) | copy-start | bytes 73732
  19.2 13.9 %copy-start.11 = (s32[8]{0:T(128)S(1)}, s32[8]{0:T(128)}, u32[]{:S(2)}) copy-start(s32[8]{0:T(128)} %sizes.3) | copy-start | bytes 100
  19.3 6.5 %collective-permute-start.3 = (bf16[256,256]{1,0:T(8,128)(2,1)S(1)}, bf16[256,256]{1,0:T(8,128)(2,1)S(1)}, u32[]{:S(2)}, u32[]{:S(2)}) collective-permute-start(bf16[256,256]{1,0:T(8,128)(2,1)S(1)} %shard_map.105.own), channel_id=1, source_target_pairs={{0,4},{4,0},{8,12},{12,8},{16,20},{20,16},{24,28},{28,24},{1,5},{5... | collective-permute-start | bytes 393224 | tf_op jit(solution)/shard_map/ppermute | solution.py:478
  20.9 12.1 %collective-permute-start.4 = (bf16[256,256]{1,0:T(8,128)(2,1)S(1)}, bf16[256,256]{1,0:T(8,128)(2,1)S(1)}, u32[]{:S(2)}, u32[]{:S(2)}) collective-permute-start(bf16[256,256]{1,0:T(8,128)(2,1)S(1)} %shard_map.105.own), channel_id=1, source_target_pairs={{0,8},{4,12},{8,0},{12,4},{16,24},{20,28},{24,16},{28,20},{1,9},{5... | collective-permute-start | bytes 393224 | tf_op jit(solution)/shard_map/ppermute | solution.py:478
  23.5 9.5 %collective-permute-start.5 = (bf16[256,256]{1,0:T(8,128)(2,1)S(1)}, bf16[256,256]{1,0:T(8,128)(2,1)S(1)}, u32[]{:S(2)}, u32[]{:S(2)}) collective-permute-start(bf16[256,256]{1,0:T(8,128)(2,1)S(1)} %shard_map.105.own), channel_id=1, source_target_pairs={{0,12},{4,8},{8,4},{12,0},{16,28},{20,24},{24,20},{28,16},{1,13},{... | collective-permute-start | bytes 393224 | tf_op jit(solution)/shard_map/ppermute | solution.py:478
  33.7 24.7 %collective-permute-start.10 = (bf16[2,136,896]{2,1,0:T(8,128)(2,1)S(1)}, bf16[2,136,896]{2,1,0:T(8,128)(2,1)S(1)}, u32[]{:S(2)}, u32[]{:S(2)}) collective-permute-start(bf16[2,136,896]{2,1,0:T(8,128)(2,1)S(1)} %get-tuple-element.24), channel_id=1, source_target_pairs={{16,24},{20,28},{24,16},{28,20},{17,25},{21,29},{25,17},{29,21},{1... | collective-permute-start | bytes 1462280 | tf_op jit(solution)/shard_map/ppermute | solution.py:478
  38.6 20.6 %collective-permute-start.6 = (bf16[56,2560]{1,0:T(8,128)(2,1)S(1)}, bf16[56,2560]{1,0:T(8,128)(2,1)S(1)}, u32[]{:S(2)}, u32[]{:S(2)}) collective-permute-start(bf16[56,2560]{1,0:T(8,128)(2,1)S(1)} %get-tuple-element.20), channel_id=1, source_target_pairs={{0,24},{4,28},{8,16},{12,20},{16,0},{20,4},{24,8},{28,12},{1,25},{... | collective-permute-start | bytes 860168 | tf_op jit(solution)/shard_map/ppermute | solution.py:478
  38.6 20.6 %collective-permute-start.7 = (bf16[56,2560]{1,0:T(8,128)(2,1)S(1)}, bf16[56,2560]{1,0:T(8,128)(2,1)S(1)}, u32[]{:S(2)}, u32[]{:S(2)}) collective-permute-start(bf16[56,2560]{1,0:T(8,128)(2,1)S(1)} %get-tuple-element.21), channel_id=1, source_target_pairs={{0,20},{4,16},{8,28},{12,24},{16,0},{20,4},{24,8},{28,12},{1,21},{... | collective-permute-start | bytes 860168 | tf_op jit(solution)/shard_map/ppermute | solution.py:478
  40.1 19.6 %collective-permute-start.8 = (bf16[56,2560]{1,0:T(8,128)(2,1)S(1)}, bf16[56,2560]{1,0:T(8,128)(2,1)S(1)}, u32[]{:S(2)}, u32[]{:S(2)}) collective-permute-start(bf16[56,2560]{1,0:T(8,128)(2,1)S(1)} %get-tuple-element.22), channel_id=1, source_target_pairs={{0,28},{4,24},{8,20},{12,16},{16,0},{20,4},{24,8},{28,12},{1,29},{... | collective-permute-start | bytes 860168 | tf_op jit(solution)/shard_map/ppermute | solution.py:478
  40.3 24.5 %collective-permute-start.9 = (bf16[56,2560]{1,0:T(8,128)(2,1)S(1)}, bf16[56,2560]{1,0:T(8,128)(2,1)S(1)}, u32[]{:S(2)}, u32[]{:S(2)}) collective-permute-start(bf16[56,2560]{1,0:T(8,128)(2,1)S(1)} %get-tuple-element.23), channel_id=1, source_target_pairs={{0,16},{4,20},{8,24},{12,28},{16,0},{20,4},{24,8},{28,12},{1,17},{... | collective-permute-start | bytes 860168 | tf_op jit(solution)/shard_map/ppermute | solution.py:478
  58.5 6.3 %collective-permute-start.14 = (bf16[3,136,384]{2,1,0:T(8,128)(2,1)S(1)}, bf16[3,136,384]{2,1,0:T(8,128)(2,1)S(1)}, u32[]{:S(2)}, u32[]{:S(2)}) collective-permute-start(bf16[3,136,384]{2,1,0:T(8,128)(2,1)S(1)} %get-tuple-element.28.rest), channel_id=1, source_target_pairs={{0,1},{1,0},{2,3},{3,2},{4,5},{5,4},{6,7},{7,6},{8,9},{9,8},{10,11... | collective-permute-start | bytes 940040 | tf_op jit(solution)/shard_map/ppermute | solution.py:487
  59.2 5.5 %collective-permute-start.11 = (bf16[136,896]{1,0:T(8,128)(2,1)S(1)}, bf16[136,896]{1,0:T(8,128)(2,1)S(1)}, u32[]{:S(2)}, u32[]{:S(2)}) collective-permute-start(bf16[136,896]{1,0:T(8,128)(2,1)S(1)} %slice_bitcast_fusion.2.first1), channel_id=1, source_target_pairs={{0,1},{1,0},{2,3},{3,2},{4,5},{5,4},{6,7},{7,6},{8,9},{9,8},{10,11... | collective-permute-start | bytes 731144 | tf_op jit(solution)/shard_map/ppermute | solution.py:487
  59.2 5.5 %collective-permute-start.12 = (bf16[136,896]{1,0:T(8,128)(2,1)S(1)}, bf16[136,896]{1,0:T(8,128)(2,1)S(1)}, u32[]{:S(2)}, u32[]{:S(2)}) collective-permute-start(bf16[136,896]{1,0:T(8,128)(2,1)S(1)} %get-tuple-element.37.first2), channel_id=1, source_target_pairs={{0,1},{1,0},{2,3},{3,2},{4,5},{5,4},{6,7},{7,6},{8,9},{9,8},{10,11... | collective-permute-start | bytes 731144 | tf_op jit(solution)/shard_map/ppermute | solution.py:487
  59.7 5.0 %collective-permute-start.13 = (bf16[136,896]{1,0:T(8,128)(2,1)S(1)}, bf16[136,896]{1,0:T(8,128)(2,1)S(1)}, u32[]{:S(2)}, u32[]{:S(2)}) collective-permute-start(bf16[136,896]{1,0:T(8,128)(2,1)S(1)} %get-tuple-element.36.first3), channel_id=1, source_target_pairs={{0,1},{1,0},{2,3},{3,2},{4,5},{5,4},{6,7},{7,6},{8,9},{9,8},{10,11... | collective-permute-start | bytes 731144 | tf_op jit(solution)/shard_map/ppermute | solution.py:487
  64.8 10.7 %copy-start.3 = (bf16[1,768,640]{2,1,0:T(8,128)(2,1)S(1)}, bf16[1,768,640]{2,1,0:T(8,128)(2,1)}, u32[]{:S(2)}) copy-start(bf16[1,768,640]{2,1,0:T(8,128)(2,1)} %param.12) | copy-start | bytes 2949124
  64.8 10.6 %copy-start.6 = (bf16[1,512,512]{2,1,0:T(8,128)(2,1)S(1)}, bf16[1,512,512]{2,1,0:T(8,128)(2,1)}, u32[]{:S(2)}) copy-start(bf16[1,512,512]{2,1,0:T(8,128)(2,1)} %param.14) | copy-start | bytes 1572868
  64.8 10.6 %copy-start.8 = (bf16[1,512,512]{2,1,0:T(8,128)(2,1)S(1)}, bf16[1,512,512]{2,1,0:T(8,128)(2,1)}, u32[]{:S(2)}) copy-start(bf16[1,512,512]{2,1,0:T(8,128)(2,1)} %param.15) | copy-start | bytes 1572868
  64.8 10.6 %copy-start.12 = (s32[8]{0:T(128)S(1)}, s32[8]{0:T(128)}, u32[]{:S(2)}) copy-start(s32[8]{0:T(128)} %sizes.3) | copy-start | bytes 100
  66.4 6.2 %collective-permute-start.16 = (bf16[56,512]{1,0:T(8,128)(2,1)S(1)}, bf16[56,512]{1,0:T(8,128)(2,1)S(1)}, u32[]{:S(2)}, u32[]{:S(2)}) collective-permute-start(bf16[56,512]{1,0:T(8,128)(2,1)S(1)} %get-tuple-element.31.own), channel_id=1, source_target_pairs={{0,12},{4,8},{8,4},{12,0},{16,28},{20,24},{24,20},{28,16},{1,13},{... | collective-permute-start | bytes 172040 | tf_op jit(solution)/shard_map/ppermute | solution.py:478
  68.7 6.7 %collective-permute-start.17 = (bf16[56,512]{1,0:T(8,128)(2,1)S(1)}, bf16[56,512]{1,0:T(8,128)(2,1)S(1)}, u32[]{:S(2)}, u32[]{:S(2)}) collective-permute-start(bf16[56,512]{1,0:T(8,128)(2,1)S(1)} %get-tuple-element.31.own), channel_id=1, source_target_pairs={{0,8},{4,12},{8,0},{12,4},{16,24},{20,28},{24,16},{28,20},{1,9},{5... | collective-permute-start | bytes 172040 | tf_op jit(solution)/shard_map/ppermute | solution.py:478
  69.8 5.6 %collective-permute-start.18 = (bf16[56,512]{1,0:T(8,128)(2,1)S(1)}, bf16[56,512]{1,0:T(8,128)(2,1)S(1)}, u32[]{:S(2)}, u32[]{:S(2)}) collective-permute-start(bf16[56,512]{1,0:T(8,128)(2,1)S(1)} %get-tuple-element.31.own), channel_id=1, source_target_pairs={{0,4},{4,0},{8,12},{12,8},{16,20},{20,16},{24,28},{28,24},{1,5},{5... | collective-permute-start | bytes 172040 | tf_op jit(solution)/shard_map/ppermute | solution.py:478
  70.9 6.7 %copy-start.1 = (bf16[1,512,2560]{2,1,0:T(8,128)(2,1)S(1)}, bf16[1,512,2560]{2,1,0:T(8,128)(2,1)}, u32[]{:S(2)}) copy-start(bf16[1,512,2560]{2,1,0:T(8,128)(2,1)} %param.16) | copy-start | bytes 7864324
  70.9 12.3 %collective-permute-start.15 = (bf16[8,640]{1,0:T(8,128)(2,1)S(1)}, bf16[8,640]{1,0:T(8,128)(2,1)S(1)}, u32[]{:S(2)}, u32[]{:S(2)}) collective-permute-start(bf16[8,640]{1,0:T(8,128)(2,1)S(1)} %get-tuple-element.30), channel_id=1, source_target_pairs={{0,16},{4,20},{8,24},{12,28},{16,0},{20,4},{24,8},{28,12},{1,17},{... | collective-permute-start | bytes 30728 | tf_op jit(solution)/shard_map/ppermute | solution.py:478
  78.1 5.5 %collective-permute-start.21 = (bf16[8,640]{1,0:T(8,128)(2,1)S(1)}, bf16[8,640]{1,0:T(8,128)(2,1)S(1)}, u32[]{:S(2)}, u32[]{:S(2)}) collective-permute-start(bf16[8,640]{1,0:T(8,128)(2,1)S(1)} %get-tuple-element.35), channel_id=1, source_target_pairs={{0,12},{4,8},{8,4},{12,0},{16,28},{20,24},{24,20},{28,16},{1,13},{... | collective-permute-start | bytes 30728 | tf_op jit(solution)/shard_map/ppermute | solution.py:478
  80.4 4.6 %collective-permute-start.20 = (bf16[8,640]{1,0:T(8,128)(2,1)S(1)}, bf16[8,640]{1,0:T(8,128)(2,1)S(1)}, u32[]{:S(2)}, u32[]{:S(2)}) collective-permute-start(bf16[8,640]{1,0:T(8,128)(2,1)S(1)} %get-tuple-element.34), channel_id=1, source_target_pairs={{0,8},{4,12},{8,0},{12,4},{16,24},{20,28},{24,16},{28,20},{1,9},{5... | collective-permute-start | bytes 30728 | tf_op jit(solution)/shard_map/ppermute | solution.py:478
  80.4 4.6 %collective-permute-start.19 = (bf16[8,640]{1,0:T(8,128)(2,1)S(1)}, bf16[8,640]{1,0:T(8,128)(2,1)S(1)}, u32[]{:S(2)}, u32[]{:S(2)}) collective-permute-start(bf16[8,640]{1,0:T(8,128)(2,1)S(1)} %get-tuple-element.33), channel_id=1, source_target_pairs={{0,4},{4,0},{8,12},{12,8},{16,20},{20,16},{24,28},{28,24},{1,5},{5... | collective-permute-start | bytes 30728 | tf_op jit(solution)/shard_map/ppermute | solution.py:478

commit v9 on v8

--- a/solution.py
+++ b/solution.py
@@ -170,17 +170,16 @@
 HALF = ROPE_DIM // 2
 SMEM = pl.BlockSpec(memory_space=pltpu.SMEM)
 VMEM = pl.BlockSpec(memory_space=pltpu.VMEM)
-HBM = pl.BlockSpec(memory_space=pltpu.HBM)
-
-
-def call(kernel, out_shape, args, scratch=(), flops=0, scalars=0, left=0, space=VMEM, grant=8):
+
+
+def call(kernel, out_shape, args, scratch=(), flops=0, scalars=0, grant=8):
     many = isinstance(out_shape, list)
     moved = sum(a.size * a.dtype.itemsize for a in args)
     return pl.pallas_call(
         kernel,
         out_shape=out_shape,
-        in_specs=[SMEM] * scalars + [VMEM] * (len(args) - scalars - left) + [HBM] * left,
-        out_specs=[space] * len(out_shape) if many else space,
+        in_specs=[SMEM] * scalars + [VMEM] * (len(args) - scalars),
+        out_specs=[VMEM] * len(out_shape) if many else VMEM,
         scratch_shapes=list(scratch),
         compiler_params=pltpu.CompilerParams(vmem_limit_bytes=grant * 2**20),
         cost_estimate=pl.CostEstimate(flops=flops, bytes_accessed=moved, transcendentals=0),
@@ -216,36 +215,27 @@
     return out
 
 
-def send_kernel(prompt, w_latent, out, half, packed, sem):
+def send_kernel(prompt, w_latent, out):
     section, rep = lax.axis_index("section"), lax.axis_index("rep")
     rows, width = out.shape
-    cols, long = half.shape
+    cols, model = w_latent.shape
 
     @pl.when(section == 0)
     def _():
-        copy = pltpu.make_async_copy(prompt, packed, sem)
-        copy.start()
-        copy.wait()
+        out[...] = prompt[...]
 
     @pl.when(section != 0)
     def _():
-        columns = pl.ds(pl.multiple_of((rep & 1) * long, 128), long)
-        copy = pltpu.make_async_copy(w_latent.at[:, columns], half, sem)
-        copy.start()
-        copy.wait()
-        extra = half[:, width : width + 256].astype(F32)
+        first = (rep & 1) * (model // 2)
+        half = w_latent[:, pl.ds(pl.multiple_of(first, 128), width + 256)].astype(F32)
+        extra = half[:, width:]
         free = rows - cols
         left = cols - 2 * free
         tail = [extra[2 * free :, :128], extra[2 * free :, 128:], jnp.zeros((free - 2 * left, 128), F32)]
         extra = jnp.concatenate(
             [extra[:free], extra[free : 2 * free], jnp.concatenate(tail, axis=0)], axis=1
         )
-        whole = jnp.concatenate([half[:, :width].astype(F32), extra], axis=0)
-        packed[...] = whole.astype(BF16)
-
-    copy = pltpu.make_async_copy(packed, out, sem)
-    copy.start()
-    copy.wait()
+        out[...] = jnp.concatenate([half[:, :width], extra], axis=0).astype(BF16)
 
 
 def unpack_share(share, cols):
@@ -472,10 +462,14 @@
     angles = jnp.asarray(np.concatenate([np.cos(angles), np.sin(angles)], axis=1), F32)
 
     def route(array, *ways):
-        pairs = [
-            (s * 4 + i, way[0] * 4 + (i ^ way[1])) for s, way in enumerate(ways) if way for i in range(4)
-        ]
-        return lax.ppermute(array, ("section", "tp"), pairs)
+        pairs = []
+        for s, way in enumerate(ways):
+            if way:
+                to, k, r = (*way, 0)[:3]
+                pairs += [
+                    ((s * 4 + i) * 4 + j, (to * 4 + (i ^ k)) * 4 + (j ^ r)) for i in range(4) for j in range(4)
+                ]
+        return lax.ppermute(array, ("section", "tp", "rep"), pairs)
 
     def within(array, k):
         return route(array, (0, k), (1, k))
@@ -490,18 +484,11 @@
         send_kernel,
         jax.ShapeDtypeStruct((tokens, share), BF16),
         [prompt, w_lat],
-        [
-            pltpu.VMEM((latent_cols, model // 2), BF16),
-            pltpu.VMEM((tokens, share), BF16),
-            pltpu.SemaphoreType.DMA,
-        ],
-        left=2,
-        space=HBM,
-        grant=57,
+        grant=8,
         flops=2 * 10**10,
     )
     two = route(prompt, (1, 0), (0, 2))
-    three = route(prompt, (0, 3), (1, 1))
+    three = route(prompt, (0, 3), (1, 0, 1))
     one = route(sent, (0, 1), (1, 1))
     parts = call(
         down_kernel,

time: 85.7 us -> 84.6 us (0.987)
  local copies, waits for them, and re-layouts: 0.14 us -> 2.18 us
  Pallas kernels: 6.82 us -> 5.01 us
  waiting for transfers between devices: 48 us -> 46.2 us
    unnamed x28 -> x32, local copies, waits for them, and re-layouts: 0.08 us -> 2.12 us
    pallas_call x6, Pallas kernels: 6.82 us -> 5.01 us  [call(): pl.pallas_call(kernel, out_shape=out_shape, in_specs=[SMEM] * scalars + [...]
    ppermute x18, waiting for transfers between devices: 48 us -> 46.2 us  [route(): return lax.ppermute(array, ('section', 'tp', 'rep'), pairs)]
  transfers between devices with their start and end apart: 22 -> 22, of which waited for: 12 -> 11; matrix products, arithmetic and copies ran while one was open for 1% -> 1% of each run, Pallas kernels for 5% -> 3%
where the time goes in v9:
time: 84.6 us; the launch traced here: 84 us
  waiting for transfers between devices  46.2 us (55%)
  starting transfers between devices  28.5 us (34%)
  Pallas kernels  5.01 us (6%)
  local copies, waits for them, and re-layouts  2.18 us (3%)
  other arithmetic  1.25 us (1%)
  between operations  0.87 us (1%)
    ppermute x18, waiting for transfers between devices, route(): return lax.ppermute(array, ('section', 'tp', 'rep'), pairs)  46.2 us
    ppermute x18, starting transfers between devices, route(): return lax.ppermute(array, ('section', 'tp', 'rep'), pairs)  28 us
    pallas_call x6, Pallas kernels, call(): pl.pallas_call(kernel, out_shape=out_shape, in_specs=[SMEM] * scalars + [...  5.01 us
    unnamed x32, local copies, waits for them, and re-layouts  2.12 us
  transfers between devices with their start and end apart: 22, of which 11 were waited for; matrix products, arithmetic and copies ran while one was open for 1% of the time, Pallas kernels for 3%

profile of v9, /device:TPU:4, one launch (start us, length us, event | category | flops | bytes accessed | tf_op | source)
XLA Modules:
  0.0 84.0 jit_solution(16195606195506959923)
XLA Ops:
  0.6 0.1 collective-permute-start
  0.7 3.0 %collective-permute-start.1 = (bf16[192,640]{1,0:T(8,128)(2,1)}, bf16[192,640]{1,0:T(8,128)(2,1)S(1)}, u32[]{:S(2)}, u32[]{:S(2)}) collective-permute-start(bf16[192,640]{1,0:T(8,128)(2,1)} %prompt.3), channel_id=1, source_target_pairs={{0,16},{1,17},{2,18},{3,19},{4,20},{5,21},{6,22},{7,23},{8,24},{9,... | collective-permute-start | bytes 737288 | tf_op jit(solution)/shard_map/ppermute | solution.py:472
  3.7 1.1 %copy-done.4 = bf16[1,2560,136]{1,2,0:T(8,128)(2,1)S(1)} copy-done((bf16[1,2560,136]{1,2,0:T(8,128)(2,1)S(1)}, bf16[1,2560,136]{1,2,0:T(8,128)(2,1)}, u32[]{:S(2)}) %copy-start.4) | copy-done | bytes 696344
  4.8 0.9 %copy-done.10 = bf16[192,640]{1,0:T(8,128)(2,1)S(1)} copy-done((bf16[192,640]{1,0:T(8,128)(2,1)S(1)}, bf16[192,640]{1,0:T(8,128)(2,1)}, u32[]{:S(2)}) %copy-start.10) | copy-done | bytes 245784
  5.8 1.3 %collective-permute-start.2 = (bf16[192,640]{1,0:T(8,128)(2,1)S(1)}, bf16[192,640]{1,0:T(8,128)(2,1)S(1)}, u32[]{:S(2)}, u32[]{:S(2)}) collective-permute-start(bf16[192,640]{1,0:T(8,128)(2,1)S(1)} %shard_map.104), channel_id=1, source_target_pairs={{0,4},{1,5},{2,6},{3,7},{4,0},{5,1},{6,2},{7,3},{8,12},{9,13},{10,... | collective-permute-start | bytes 737288 | tf_op jit(solution)/shard_map/ppermute | solution.py:472
  7.0 0.0 collective-permute-done.three
  7.0 3.7 %collective-permute-done.1.two = bf16[192,640]{1,0:T(8,128)(2,1)S(1)} collective-permute-done((bf16[192,640]{1,0:T(8,128)(2,1)}, bf16[192,640]{1,0:T(8,128)(2,1)S(1)}, u32[]{:S(2)}, u32[]{:S(2)}) %collective-permute-start.1) | collective-permute-done | bytes 245792 | tf_op jit(solution)/shard_map/ppermute | solution.py:472
  10.7 8.5 %collective-permute-done.2.one.share1 = bf16[192,640]{1,0:T(8,128)(2,1)S(1)} collective-permute-done((bf16[192,640]{1,0:T(8,128)(2,1)S(1)}, bf16[192,640]{1,0:T(8,128)(2,1)S(1)}, u32[]{:S(2)}, u32[]{:S(2)}) %collective-permute-start.2) | collective-permute-done | bytes 245792 | tf_op jit(solution)/shard_map/ppermute | solution.py:472
  19.2 0.0 copy-start.6
  19.2 0.0 copy-start.8
  19.3 0.0 copy-start.11
  19.3 0.0 copy-start.12
  19.3 0.0 copy-start.13
  19.3 0.1 collective-permute-start.3
  19.4 2.7 %collective-permute-start.4 = (bf16[256,256]{1,0:T(8,128)(2,1)S(1)}, bf16[256,256]{1,0:T(8,128)(2,1)S(1)}, u32[]{:S(2)}, u32[]{:S(2)}) collective-permute-start(bf16[256,256]{1,0:T(8,128)(2,1)S(1)} %shard_map.105.own), channel_id=1, source_target_pairs={{0,8},{1,9},{2,10},{3,11},{4,12},{5,13},{6,14},{7,15},{8,0},{9,1},... | collective-permute-start | bytes 393224 | tf_op jit(solution)/shard_map/ppermute | solution.py:472
  22.1 1.7 %collective-permute-start.5 = (bf16[256,256]{1,0:T(8,128)(2,1)S(1)}, bf16[256,256]{1,0:T(8,128)(2,1)S(1)}, u32[]{:S(2)}, u32[]{:S(2)}) collective-permute-start(bf16[256,256]{1,0:T(8,128)(2,1)S(1)} %shard_map.105.own), channel_id=1, source_target_pairs={{0,12},{1,13},{2,14},{3,15},{4,8},{5,9},{6,10},{7,11},{8,4},{9,5},... | collective-permute-start | bytes 393224 | tf_op jit(solution)/shard_map/ppermute | solution.py:472
  23.8 0.9 %collective-permute-done.3.one = bf16[256,256]{1,0:T(8,128)(2,1)S(1)} collective-permute-done((bf16[256,256]{1,0:T(8,128)(2,1)S(1)}, bf16[256,256]{1,0:T(8,128)(2,1)S(1)}, u32[]{:S(2)}, u32[]{:S(2)}) %collective-permute-start.3) | collective-permute-done | bytes 131104 | tf_op jit(solution)/shard_map/ppermute | solution.py:472
  24.7 6.7 %collective-permute-done.4.two = bf16[256,256]{1,0:T(8,128)(2,1)S(1)} collective-permute-done((bf16[256,256]{1,0:T(8,128)(2,1)S(1)}, bf16[256,256]{1,0:T(8,128)(2,1)S(1)}, u32[]{:S(2)}, u32[]{:S(2)}) %collective-permute-start.4) | collective-permute-done | bytes 131104 | tf_op jit(solution)/shard_map/ppermute | solution.py:472
  31.4 0.0 collective-permute-done.5.three
  31.5 0.6 shard_map.106
  32.1 4.9 %collective-permute-start.10 = (bf16[2,136,896]{2,1,0:T(8,128)(2,1)S(1)}, bf16[2,136,896]{2,1,0:T(8,128)(2,1)S(1)}, u32[]{:S(2)}, u32[]{:S(2)}) collective-permute-start(bf16[2,136,896]{2,1,0:T(8,128)(2,1)S(1)} %get-tuple-element.24), channel_id=1, source_target_pairs={{16,24},{17,25},{18,26},{19,27},{20,28},{21,29},{22,30},{23,31},{2... | collective-permute-start | bytes 1462280 | tf_op jit(solution)/shard_map/ppermute | solution.py:472
  37.0 0.1 collective-permute-start.6
  37.1 1.5 %collective-permute-start.7 = (bf16[56,2560]{1,0:T(8,128)(2,1)S(1)}, bf16[56,2560]{1,0:T(8,128)(2,1)S(1)}, u32[]{:S(2)}, u32[]{:S(2)}) collective-permute-start(bf16[56,2560]{1,0:T(8,128)(2,1)S(1)} %get-tuple-element.21), channel_id=1, source_target_pairs={{0,20},{1,21},{2,22},{3,23},{4,16},{5,17},{6,18},{7,19},{8,28},{9,... | collective-permute-start | bytes 860168 | tf_op jit(solution)/shard_map/ppermute | solution.py:472
  38.5 2.4 %collective-permute-start.8 = (bf16[56,2560]{1,0:T(8,128)(2,1)S(1)}, bf16[56,2560]{1,0:T(8,128)(2,1)S(1)}, u32[]{:S(2)}, u32[]{:S(2)}) collective-permute-start(bf16[56,2560]{1,0:T(8,128)(2,1)S(1)} %get-tuple-element.22), channel_id=1, source_target_pairs={{0,28},{1,29},{2,30},{3,31},{4,24},{5,25},{6,26},{7,27},{8,20},{9,... | collective-permute-start | bytes 860168 | tf_op jit(solution)/shard_map/ppermute | solution.py:472
  40.9 1.6 %collective-permute-start.9 = (bf16[56,2560]{1,0:T(8,128)(2,1)S(1)}, bf16[56,2560]{1,0:T(8,128)(2,1)S(1)}, u32[]{:S(2)}, u32[]{:S(2)}) collective-permute-start(bf16[56,2560]{1,0:T(8,128)(2,1)S(1)} %get-tuple-element.23), channel_id=1, source_target_pairs={{0,16},{1,17},{2,18},{3,19},{4,20},{5,21},{6,22},{7,23},{8,24},{9,... | collective-permute-start | bytes 860168 | tf_op jit(solution)/shard_map/ppermute | solution.py:472
  42.5 14.4 %collective-permute-done.10 = bf16[2,136,896]{2,1,0:T(8,128)(2,1)S(1)} collective-permute-done((bf16[2,136,896]{2,1,0:T(8,128)(2,1)S(1)}, bf16[2,136,896]{2,1,0:T(8,128)(2,1)S(1)}, u32[]{:S(2)}, u32[]{:S(2)}) %collective-permute-start.10) | collective-permute-done | bytes 487456 | tf_op jit(solution)/shard_map/ppermute | solution.py:472
  57.0 0.6 collective-permute-done.6.one
  57.6 0.5 collective-permute-start.12
  58.1 0.1 collective-permute-start.13
  58.2 5.3 %collective-permute-done.9.four = bf16[56,2560]{1,0:T(8,128)(2,1)S(1)} collective-permute-done((bf16[56,2560]{1,0:T(8,128)(2,1)S(1)}, bf16[56,2560]{1,0:T(8,128)(2,1)S(1)}, u32[]{:S(2)}, u32[]{:S(2)}) %collective-permute-start.9) | collective-permute-done | bytes 286752 | tf_op jit(solution)/shard_map/ppermute | solution.py:472
  63.5 0.0 copy-start.3
  63.5 0.0 copy-start.7
  63.6 0.0 copy-start.9
  63.6 0.0 copy-start.14
  63.6 1.6 %shard_map.107 = (bf16[56,512]{1,0:T(8,128)(2,1)S(1)}, bf16[48,544]{1,0:T(8,128)(2,1)S(1)}, bf16[8,640]{1,0:T(8,128)(2,1)S(1)}) custom-call(bf16[56,2560]{1,0:T(8,128)(2,1)S(1)} %collective-permute-done.6.one, bf16[56,2560]{1,0:T(8,128)(2,1)S(1)} %collective-permute-done.7.two, bf16[56,2560]{1,0:T(8,128)(2,1)S(1)} %collective-permute-done.8.three, ...), custom_call_target="tpu_custom_call" | custom-call | flops 199999995904 | bytes 4939776 | tf_op jit(solution)/shard_map/pallas_call | solution.py:178
  65.2 2.0 %collective-permute-start.16 = (bf16[56,512]{1,0:T(8,128)(2,1)S(1)}, bf16[56,512]{1,0:T(8,128)(2,1)S(1)}, u32[]{:S(2)}, u32[]{:S(2)}) collective-permute-start(bf16[56,512]{1,0:T(8,128)(2,1)S(1)} %get-tuple-element.31.own), channel_id=1, source_target_pairs={{0,12},{1,13},{2,14},{3,15},{4,8},{5,9},{6,10},{7,11},{8,4},{9,5},... | collective-permute-start | bytes 172040 | tf_op jit(solution)/shard_map/ppermute | solution.py:472
  67.2 0.8 collective-permute-start.17
  68.0 1.6 %collective-permute-start.18 = (bf16[56,512]{1,0:T(8,128)(2,1)S(1)}, bf16[56,512]{1,0:T(8,128)(2,1)S(1)}, u32[]{:S(2)}, u32[]{:S(2)}) collective-permute-start(bf16[56,512]{1,0:T(8,128)(2,1)S(1)} %get-tuple-element.31.own), channel_id=1, source_target_pairs={{0,4},{1,5},{2,6},{3,7},{4,0},{5,1},{6,2},{7,3},{8,12},{9,13},{10,... | collective-permute-start | bytes 172040 | tf_op jit(solution)/shard_map/ppermute | solution.py:472
  69.6 1.9 %collective-permute-done.16.three = bf16[56,512]{1,0:T(8,128)(2,1)S(1)} collective-permute-done((bf16[56,512]{1,0:T(8,128)(2,1)S(1)}, bf16[56,512]{1,0:T(8,128)(2,1)S(1)}, u32[]{:S(2)}, u32[]{:S(2)}) %collective-permute-start.16) | collective-permute-done | bytes 57376 | tf_op jit(solution)/shard_map/ppermute | solution.py:472
  71.5 2.3 %collective-permute-done.17.two = bf16[56,512]{1,0:T(8,128)(2,1)S(1)} collective-permute-done((bf16[56,512]{1,0:T(8,128)(2,1)S(1)}, bf16[56,512]{1,0:T(8,128)(2,1)S(1)}, u32[]{:S(2)}, u32[]{:S(2)}) %collective-permute-start.17) | collective-permute-done | bytes 57376 | tf_op jit(solution)/shard_map/ppermute | solution.py:472
  73.9 2.2 %shard_map.108.mixed = bf16[8,512]{1,0:T(8,128)(2,1)S(1)} custom-call(s32[8]{0:T(128)S(1)} %copy-done.14, bf16[56,512]{1,0:T(8,128)(2,1)S(1)} %get-tuple-element.31.own, bf16[56,512]{1,0:T(8,128)(2,1)S(1)} %collective-permute-done.16.three, bf16[56,512]{1,0:T(8,128)(2,1)S(1)} %collective-permute-done.17.two, ...), custom_call_target="tpu_custom_call" | custom-call | flops 20000000000 | bytes 2285600 | tf_op jit(solution)/shard_map/pallas_call | solution.py:178
  76.0 0.5 shard_map.109
  76.6 2.3 %collective-permute-start.21 = (bf16[8,640]{1,0:T(8,128)(2,1)S(1)}, bf16[8,640]{1,0:T(8,128)(2,1)S(1)}, u32[]{:S(2)}, u32[]{:S(2)}) collective-permute-start(bf16[8,640]{1,0:T(8,128)(2,1)S(1)} %get-tuple-element.35), channel_id=1, source_target_pairs={{0,12},{1,13},{2,14},{3,15},{4,8},{5,9},{6,10},{7,11},{8,4},{9,5},... | collective-permute-start | bytes 30728 | tf_op jit(solution)/shard_map/ppermute | solution.py:472
  78.9 2.1 %collective-permute-start.19 = (bf16[8,640]{1,0:T(8,128)(2,1)S(1)}, bf16[8,640]{1,0:T(8,128)(2,1)S(1)}, u32[]{:S(2)}, u32[]{:S(2)}) collective-permute-start(bf16[8,640]{1,0:T(8,128)(2,1)S(1)} %get-tuple-element.33), channel_id=1, source_target_pairs={{0,4},{1,5},{2,6},{3,7},{4,0},{5,1},{6,2},{7,3},{8,12},{9,13},{10,... | collective-permute-start | bytes 30728 | tf_op jit(solution)/shard_map/ppermute | solution.py:472
  81.0 0.6 select_bitcast_fusion
  81.6 0.4 collective-permute-done.21
  82.1 1.4 %collective-permute-done.20 = bf16[8,640]{1,0:T(8,128)(2,1)S(1)} collective-permute-done((bf16[8,640]{1,0:T(8,128)(2,1)S(1)}, bf16[8,640]{1,0:T(8,128)(2,1)S(1)}, u32[]{:S(2)}, u32[]{:S(2)}) %collective-permute-start.20) | collective-permute-done | bytes 10272 | tf_op jit(solution)/shard_map/ppermute | solution.py:472
  83.4 0.6 fusion.1
  (38 shorter events, 0.2 us)
Async XLA Ops:
  0.6 6.4 %collective-permute-start = (bf16[192,640]{1,0:T(8,128)(2,1)}, bf16[192,640]{1,0:T(8,128)(2,1)S(1)}, u32[]{:S(2)}, u32[]{:S(2)}) collective-permute-start(bf16[192,640]{1,0:T(8,128)(2,1)} %prompt.3), channel_id=1, source_target_pairs={{0,12},{1,13},{2,14},{3,15},{4,8},{5,9},{6,10},{7,11},{8,4},{9,5},... | collective-permute-start | bytes 737288 | tf_op jit(solution)/shard_map/ppermute | solution.py:472
  0.7 10.0 %collective-permute-start.1 = (bf16[192,640]{1,0:T(8,128)(2,1)}, bf16[192,640]{1,0:T(8,128)(2,1)S(1)}, u32[]{:S(2)}, u32[]{:S(2)}) collective-permute-start(bf16[192,640]{1,0:T(8,128)(2,1)} %prompt.3), channel_id=1, source_target_pairs={{0,16},{1,17},{2,18},{3,19},{4,20},{5,21},{6,22},{7,23},{8,24},{9,... | collective-permute-start | bytes 737288 | tf_op jit(solution)/shard_map/ppermute | solution.py:472
  3.7 1.1 %copy-start.4 = (bf16[1,2560,136]{1,2,0:T(8,128)(2,1)S(1)}, bf16[1,2560,136]{1,2,0:T(8,128)(2,1)}, u32[]{:S(2)}) copy-start(bf16[1,2560,136]{1,2,0:T(8,128)(2,1)} %param.13) | copy-start | bytes 2088964
  4.8 0.9 %copy-start.10 = (bf16[192,640]{1,0:T(8,128)(2,1)S(1)}, bf16[192,640]{1,0:T(8,128)(2,1)}, u32[]{:S(2)}) copy-start(bf16[192,640]{1,0:T(8,128)(2,1)} %prompt.3) | copy-start | bytes 737284
  5.7 13.5 %copy-start.15 = (bf16[1,2560,192]{1,2,0:T(8,128)(2,1)S(1)}, bf16[1,2560,192]{1,2,0:T(8,128)(2,1)}, u32[]{:S(2)}) copy-start(bf16[1,2560,192]{1,2,0:T(8,128)(2,1)} %param.11) | copy-start | bytes 2949124
  5.8 13.5 %collective-permute-start.2 = (bf16[192,640]{1,0:T(8,128)(2,1)S(1)}, bf16[192,640]{1,0:T(8,128)(2,1)S(1)}, u32[]{:S(2)}, u32[]{:S(2)}) collective-permute-start(bf16[192,640]{1,0:T(8,128)(2,1)S(1)} %shard_map.104), channel_id=1, source_target_pairs={{0,4},{1,5},{2,6},{3,7},{4,0},{5,1},{6,2},{7,3},{8,12},{9,13},{10,... | collective-permute-start | bytes 737288 | tf_op jit(solution)/shard_map/ppermute | solution.py:472
  19.2 12.2 %copy-start = (bf16[1,512,2560]{2,1,0:T(8,128)(2,1)S(1)}, bf16[1,512,2560]{2,1,0:T(8,128)(2,1)}, u32[]{:S(2)}) copy-start(bf16[1,512,2560]{2,1,0:T(8,128)(2,1)} %param.16) | copy-start | bytes 7864324
  19.2 12.2 %copy-start.2 = (bf16[1,768,640]{2,1,0:T(8,128)(2,1)S(1)}, bf16[1,768,640]{2,1,0:T(8,128)(2,1)}, u32[]{:S(2)}) copy-start(bf16[1,768,640]{2,1,0:T(8,128)(2,1)} %param.12) | copy-start | bytes 2949124
  19.2 12.2 %copy-start.5 = (bf16[1,2560,136]{1,2,0:T(8,128)(2,1)S(1)}, bf16[1,2560,136]{1,2,0:T(8,128)(2,1)}, u32[]{:S(2)}) copy-start(bf16[1,2560,136]{1,2,0:T(8,128)(2,1)} %param.13) | copy-start | bytes 2088964
  19.2 12.2 %copy-start.6 = (bf16[1,512,512]{2,1,0:T(8,128)(2,1)S(1)}, bf16[1,512,512]{2,1,0:T(8,128)(2,1)}, u32[]{:S(2)}) copy-start(bf16[1,512,512]{2,1,0:T(8,128)(2,1)} %param.14) | copy-start | bytes 1572868
  19.2 12.2 %copy-start.8 = (bf16[1,512,512]{2,1,0:T(8,128)(2,1)S(1)}, bf16[1,512,512]{2,1,0:T(8,128)(2,1)}, u32[]{:S(2)}) copy-start(bf16[1,512,512]{2,1,0:T(8,128)(2,1)} %param.15) | copy-start | bytes 1572868
  19.3 12.2 %copy-start.11 = (bf16[192,640]{1,0:T(8,128)(2,1)S(1)}, bf16[192,640]{1,0:T(8,128)(2,1)}, u32[]{:S(2)}) copy-start(bf16[192,640]{1,0:T(8,128)(2,1)} %prompt.3) | copy-start | bytes 737284
  19.3 12.2 %copy-start.12 = (f32[192,32]{1,0:T(8,128)S(1)}, f32[192,32]{1,0:T(8,128)}, u32[]{:S(2)}) copy-start(f32[192,32]{1,0:T(8,128)} %constant.10.clone.angles) | copy-start | bytes 73732
  19.3 12.2 %copy-start.13 = (s32[8]{0:T(128)S(1)}, s32[8]{0:T(128)}, u32[]{:S(2)}) copy-start(s32[8]{0:T(128)} %sizes.3) | copy-start | bytes 100
  19.3 5.4 %collective-permute-start.3 = (bf16[256,256]{1,0:T(8,128)(2,1)S(1)}, bf16[256,256]{1,0:T(8,128)(2,1)S(1)}, u32[]{:S(2)}, u32[]{:S(2)}) collective-permute-start(bf16[256,256]{1,0:T(8,128)(2,1)S(1)} %shard_map.105.own), channel_id=1, source_target_pairs={{0,4},{1,5},{2,6},{3,7},{4,0},{5,1},{6,2},{7,3},{8,12},{9,13},{10,... | collective-permute-start | bytes 393224 | tf_op jit(solution)/shard_map/ppermute | solution.py:472
  19.4 12.0 %collective-permute-start.4 = (bf16[256,256]{1,0:T(8,128)(2,1)S(1)}, bf16[256,256]{1,0:T(8,128)(2,1)S(1)}, u32[]{:S(2)}, u32[]{:S(2)}) collective-permute-start(bf16[256,256]{1,0:T(8,128)(2,1)S(1)} %shard_map.105.own), channel_id=1, source_target_pairs={{0,8},{1,9},{2,10},{3,11},{4,12},{5,13},{6,14},{7,15},{8,0},{9,1},... | collective-permute-start | bytes 393224 | tf_op jit(solution)/shard_map/ppermute | solution.py:472
  22.1 9.3 %collective-permute-start.5 = (bf16[256,256]{1,0:T(8,128)(2,1)S(1)}, bf16[256,256]{1,0:T(8,128)(2,1)S(1)}, u32[]{:S(2)}, u32[]{:S(2)}) collective-permute-start(bf16[256,256]{1,0:T(8,128)(2,1)S(1)} %shard_map.105.own), channel_id=1, source_target_pairs={{0,12},{1,13},{2,14},{3,15},{4,8},{5,9},{6,10},{7,11},{8,4},{9,5},... | collective-permute-start | bytes 393224 | tf_op jit(solution)/shard_map/ppermute | solution.py:472
  32.1 24.8 %collective-permute-start.10 = (bf16[2,136,896]{2,1,0:T(8,128)(2,1)S(1)}, bf16[2,136,896]{2,1,0:T(8,128)(2,1)S(1)}, u32[]{:S(2)}, u32[]{:S(2)}) collective-permute-start(bf16[2,136,896]{2,1,0:T(8,128)(2,1)S(1)} %get-tuple-element.24), channel_id=1, source_target_pairs={{16,24},{17,25},{18,26},{19,27},{20,28},{21,29},{22,30},{23,31},{2... | collective-permute-start | bytes 1462280 | tf_op jit(solution)/shard_map/ppermute | solution.py:472
  37.0 20.6 %collective-permute-start.6 = (bf16[56,2560]{1,0:T(8,128)(2,1)S(1)}, bf16[56,2560]{1,0:T(8,128)(2,1)S(1)}, u32[]{:S(2)}, u32[]{:S(2)}) collective-permute-start(bf16[56,2560]{1,0:T(8,128)(2,1)S(1)} %get-tuple-element.20), channel_id=1, source_target_pairs={{0,24},{1,25},{2,26},{3,27},{4,28},{5,29},{6,30},{7,31},{8,16},{9,... | collective-permute-start | bytes 860168 | tf_op jit(solution)/shard_map/ppermute | solution.py:472
  37.1 20.6 %collective-permute-start.7 = (bf16[56,2560]{1,0:T(8,128)(2,1)S(1)}, bf16[56,2560]{1,0:T(8,128)(2,1)S(1)}, u32[]{:S(2)}, u32[]{:S(2)}) collective-permute-start(bf16[56,2560]{1,0:T(8,128)(2,1)S(1)} %get-tuple-element.21), channel_id=1, source_target_pairs={{0,20},{1,21},{2,22},{3,23},{4,16},{5,17},{6,18},{7,19},{8,28},{9,... | collective-permute-start | bytes 860168 | tf_op jit(solution)/shard_map/ppermute | solution.py:472
  38.5 19.6 %collective-permute-start.8 = (bf16[56,2560]{1,0:T(8,128)(2,1)S(1)}, bf16[56,2560]{1,0:T(8,128)(2,1)S(1)}, u32[]{:S(2)}, u32[]{:S(2)}) collective-permute-start(bf16[56,2560]{1,0:T(8,128)(2,1)S(1)} %get-tuple-element.22), channel_id=1, source_target_pairs={{0,28},{1,29},{2,30},{3,31},{4,24},{5,25},{6,26},{7,27},{8,20},{9,... | collective-permute-start | bytes 860168 | tf_op jit(solution)/shard_map/ppermute | solution.py:472
  40.9 22.6 %collective-permute-start.9 = (bf16[56,2560]{1,0:T(8,128)(2,1)S(1)}, bf16[56,2560]{1,0:T(8,128)(2,1)S(1)}, u32[]{:S(2)}, u32[]{:S(2)}) collective-permute-start(bf16[56,2560]{1,0:T(8,128)(2,1)S(1)} %get-tuple-element.23), channel_id=1, source_target_pairs={{0,16},{1,17},{2,18},{3,19},{4,20},{5,21},{6,22},{7,23},{8,24},{9,... | collective-permute-start | bytes 860168 | tf_op jit(solution)/shard_map/ppermute | solution.py:472
  56.9 6.6 %collective-permute-start.14 = (bf16[3,136,384]{2,1,0:T(8,128)(2,1)S(1)}, bf16[3,136,384]{2,1,0:T(8,128)(2,1)S(1)}, u32[]{:S(2)}, u32[]{:S(2)}) collective-permute-start(bf16[3,136,384]{2,1,0:T(8,128)(2,1)S(1)} %get-tuple-element.28.rest), channel_id=1, source_target_pairs={{0,1},{1,0},{2,3},{3,2},{4,5},{5,4},{6,7},{7,6},{8,9},{9,8},{10,11... | collective-permute-start | bytes 940040 | tf_op jit(solution)/shard_map/ppermute | solution.py:481
  57.6 5.9 %collective-permute-start.11 = (bf16[136,896]{1,0:T(8,128)(2,1)S(1)}, bf16[136,896]{1,0:T(8,128)(2,1)S(1)}, u32[]{:S(2)}, u32[]{:S(2)}) collective-permute-start(bf16[136,896]{1,0:T(8,128)(2,1)S(1)} %slice_bitcast_fusion.2.first1), channel_id=1, source_target_pairs={{0,1},{1,0},{2,3},{3,2},{4,5},{5,4},{6,7},{7,6},{8,9},{9,8},{10,11... | collective-permute-start | bytes 731144 | tf_op jit(solution)/shard_map/ppermute | solution.py:481
  57.6 5.9 %collective-permute-start.12 = (bf16[136,896]{1,0:T(8,128)(2,1)S(1)}, bf16[136,896]{1,0:T(8,128)(2,1)S(1)}, u32[]{:S(2)}, u32[]{:S(2)}) collective-permute-start(bf16[136,896]{1,0:T(8,128)(2,1)S(1)} %get-tuple-element.37.first2), channel_id=1, source_target_pairs={{0,1},{1,0},{2,3},{3,2},{4,5},{5,4},{6,7},{7,6},{8,9},{9,8},{10,11... | collective-permute-start | bytes 731144 | tf_op jit(solution)/shard_map/ppermute | solution.py:481
  58.1 5.4 %collective-permute-start.13 = (bf16[136,896]{1,0:T(8,128)(2,1)S(1)}, bf16[136,896]{1,0:T(8,128)(2,1)S(1)}, u32[]{:S(2)}, u32[]{:S(2)}) collective-permute-start(bf16[136,896]{1,0:T(8,128)(2,1)S(1)} %get-tuple-element.36.first3), channel_id=1, source_target_pairs={{0,1},{1,0},{2,3},{3,2},{4,5},{5,4},{6,7},{7,6},{8,9},{9,8},{10,11... | collective-permute-start | bytes 731144 | tf_op jit(solution)/shard_map/ppermute | solution.py:481
  63.5 10.3 %copy-start.3 = (bf16[1,768,640]{2,1,0:T(8,128)(2,1)S(1)}, bf16[1,768,640]{2,1,0:T(8,128)(2,1)}, u32[]{:S(2)}) copy-start(bf16[1,768,640]{2,1,0:T(8,128)(2,1)} %param.12) | copy-start | bytes 2949124
  63.5 10.3 %copy-start.7 = (bf16[1,512,512]{2,1,0:T(8,128)(2,1)S(1)}, bf16[1,512,512]{2,1,0:T(8,128)(2,1)}, u32[]{:S(2)}) copy-start(bf16[1,512,512]{2,1,0:T(8,128)(2,1)} %param.14) | copy-start | bytes 1572868
  63.6 10.3 %copy-start.9 = (bf16[1,512,512]{2,1,0:T(8,128)(2,1)S(1)}, bf16[1,512,512]{2,1,0:T(8,128)(2,1)}, u32[]{:S(2)}) copy-start(bf16[1,512,512]{2,1,0:T(8,128)(2,1)} %param.15) | copy-start | bytes 1572868
  63.6 10.3 %copy-start.14 = (s32[8]{0:T(128)S(1)}, s32[8]{0:T(128)}, u32[]{:S(2)}) copy-start(s32[8]{0:T(128)} %sizes.3) | copy-start | bytes 100
  65.2 6.3 %collective-permute-start.16 = (bf16[56,512]{1,0:T(8,128)(2,1)S(1)}, bf16[56,512]{1,0:T(8,128)(2,1)S(1)}, u32[]{:S(2)}, u32[]{:S(2)}) collective-permute-start(bf16[56,512]{1,0:T(8,128)(2,1)S(1)} %get-tuple-element.31.own), channel_id=1, source_target_pairs={{0,12},{1,13},{2,14},{3,15},{4,8},{5,9},{6,10},{7,11},{8,4},{9,5},... | collective-permute-start | bytes 172040 | tf_op jit(solution)/shard_map/ppermute | solution.py:472
  67.2 6.7 %collective-permute-start.17 = (bf16[56,512]{1,0:T(8,128)(2,1)S(1)}, bf16[56,512]{1,0:T(8,128)(2,1)S(1)}, u32[]{:S(2)}, u32[]{:S(2)}) collective-permute-start(bf16[56,512]{1,0:T(8,128)(2,1)S(1)} %get-tuple-element.31.own), channel_id=1, source_target_pairs={{0,8},{1,9},{2,10},{3,11},{4,12},{5,13},{6,14},{7,15},{8,0},{9,1},... | collective-permute-start | bytes 172040 | tf_op jit(solution)/shard_map/ppermute | solution.py:472
  68.0 5.8 %collective-permute-start.18 = (bf16[56,512]{1,0:T(8,128)(2,1)S(1)}, bf16[56,512]{1,0:T(8,128)(2,1)S(1)}, u32[]{:S(2)}, u32[]{:S(2)}) collective-permute-start(bf16[56,512]{1,0:T(8,128)(2,1)S(1)} %get-tuple-element.31.own), channel_id=1, source_target_pairs={{0,4},{1,5},{2,6},{3,7},{4,0},{5,1},{6,2},{7,3},{8,12},{9,13},{10,... | collective-permute-start | bytes 172040 | tf_op jit(solution)/shard_map/ppermute | solution.py:472
  69.6 6.4 %copy-start.1 = (bf16[1,512,2560]{2,1,0:T(8,128)(2,1)S(1)}, bf16[1,512,2560]{2,1,0:T(8,128)(2,1)}, u32[]{:S(2)}) copy-start(bf16[1,512,2560]{2,1,0:T(8,128)(2,1)} %param.16) | copy-start | bytes 7864324
  69.6 12.0 %collective-permute-start.15 = (bf16[8,640]{1,0:T(8,128)(2,1)S(1)}, bf16[8,640]{1,0:T(8,128)(2,1)S(1)}, u32[]{:S(2)}, u32[]{:S(2)}) collective-permute-start(bf16[8,640]{1,0:T(8,128)(2,1)S(1)} %get-tuple-element.30), channel_id=1, source_target_pairs={{0,16},{1,17},{2,18},{3,19},{4,20},{5,21},{6,22},{7,23},{8,24},{9,... | collective-permute-start | bytes 30728 | tf_op jit(solution)/shard_map/ppermute | solution.py:472
  76.6 5.5 %collective-permute-start.21 = (bf16[8,640]{1,0:T(8,128)(2,1)S(1)}, bf16[8,640]{1,0:T(8,128)(2,1)S(1)}, u32[]{:S(2)}, u32[]{:S(2)}) collective-permute-start(bf16[8,640]{1,0:T(8,128)(2,1)S(1)} %get-tuple-element.35), channel_id=1, source_target_pairs={{0,12},{1,13},{2,14},{3,15},{4,8},{5,9},{6,10},{7,11},{8,4},{9,5},... | collective-permute-start | bytes 30728 | tf_op jit(solution)/shard_map/ppermute | solution.py:472
  78.9 4.6 %collective-permute-start.20 = (bf16[8,640]{1,0:T(8,128)(2,1)S(1)}, bf16[8,640]{1,0:T(8,128)(2,1)S(1)}, u32[]{:S(2)}, u32[]{:S(2)}) collective-permute-start(bf16[8,640]{1,0:T(8,128)(2,1)S(1)} %get-tuple-element.34), channel_id=1, source_target_pairs={{0,8},{1,9},{2,10},{3,11},{4,12},{5,13},{6,14},{7,15},{8,0},{9,1},... | collective-permute-start | bytes 30728 | tf_op jit(solution)/shard_map/ppermute | solution.py:472
  78.9 4.6 %collective-permute-start.19 = (bf16[8,640]{1,0:T(8,128)(2,1)S(1)}, bf16[8,640]{1,0:T(8,128)(2,1)S(1)}, u32[]{:S(2)}, u32[]{:S(2)}) collective-permute-start(bf16[8,640]{1,0:T(8,128)(2,1)S(1)} %get-tuple-element.33), channel_id=1, source_target_pairs={{0,4},{1,5},{2,6},{3,7},{4,0},{5,1},{6,2},{7,3},{8,12},{9,13},{10,... | collective-permute-start | bytes 30728 | tf_op jit(solution)/shard_map/ppermute | solution.py:472

commit v10 on v9

--- a/solution.py
+++ b/solution.py
@@ -318,7 +318,7 @@
 
 
 def layer_kernel(
-    sizes, own, one, two, three, share1, w_latent, prompt, angles,
+    sizes, own, two, one, three, share1, w_latent, prompt, angles,
     w_query, w_keys, w_values, w_out, out0, out1, out2, out3, own_cache, passed, rest, stack, total, cached,
 ):
     section, tp, rep = (lax.axis_index(a) for a in ("section", "tp", "rep"))
@@ -487,8 +487,8 @@
         grant=8,
         flops=2 * 10**10,
     )
-    two = route(prompt, (1, 0), (0, 2))
-    three = route(prompt, (0, 3), (1, 0, 1))
+    two = route(prompt, (0, 2), (1, 0, 1))
+    three = route(prompt, (1, 0), (0, 3))
     one = route(sent, (0, 1), (1, 1))
     parts = call(
         down_kernel,
@@ -507,7 +507,7 @@
             jax.ShapeDtypeStruct((2, latent_cols, model // 2 - 384), BF16),
             jax.ShapeDtypeStruct((3, latent_cols, 384), BF16),
         ],
-        [block_sizes, *pieces, one, w_lat, prompt, angles, w_up, w_key, w_value, w_final],
+        [block_sizes, pieces[0], pieces[2], pieces[1], pieces[3], one, w_lat, prompt, angles, w_up, w_key, w_value, w_final],
         [
             pltpu.VMEM((4, *parts.shape), BF16),
             pltpu.VMEM((tokens + count, model), F32),

time: 84.6 us -> 83.5 us (0.987)
  starting transfers between devices: 28.5 us -> 27.5 us
    ppermute x18, starting transfers between devices: 28 us -> 26.6 us  [route(): return lax.ppermute(array, ('section', 'tp', 'rep'), pairs)]
where the time goes in v10:
time: 83.5 us; the launch traced here: 83.2 us
  waiting for transfers between devices  46.3 us (55%)
  starting transfers between devices  27.5 us (33%)
  Pallas kernels  5.01 us (6%)
  local copies, waits for them, and re-layouts  2.18 us (3%)
  other arithmetic  1.25 us (1%)
  between operations  0.86 us (1%)
    ppermute x18, waiting for transfers between devices, route(): return lax.ppermute(array, ('section', 'tp', 'rep'), pairs)  46.3 us
    ppermute x18, starting transfers between devices, route(): return lax.ppermute(array, ('section', 'tp', 'rep'), pairs)  26.6 us
    pallas_call x6, Pallas kernels, call(): pl.pallas_call(kernel, out_shape=out_shape, in_specs=[SMEM] * scalars + [...  5.01 us
    unnamed x32, local copies, waits for them, and re-layouts  2.12 us
  transfers between devices with their start and end apart: 22, of which 11 were waited for; matrix products, arithmetic and copies ran while one was open for 1% of the time, Pallas kernels for 3%

profile of v10, /device:TPU:4, one launch (start us, length us, event | category | flops | bytes accessed | tf_op | source)
XLA Modules:
  0.0 83.2 jit_solution(12374264952739328962)
XLA Ops:
  0.6 3.6 %collective-permute-start = (bf16[192,640]{1,0:T(8,128)(2,1)}, bf16[192,640]{1,0:T(8,128)(2,1)S(1)}, u32[]{:S(2)}, u32[]{:S(2)}) collective-permute-start(bf16[192,640]{1,0:T(8,128)(2,1)} %prompt.3), channel_id=1, source_target_pairs={{0,16},{1,17},{2,18},{3,19},{4,20},{5,21},{6,22},{7,23},{8,24},{9,... | collective-permute-start | bytes 737288 | tf_op jit(solution)/shard_map/ppermute | solution.py:472
  4.2 1.1 %copy-done.4 = bf16[1,2560,136]{1,2,0:T(8,128)(2,1)S(1)} copy-done((bf16[1,2560,136]{1,2,0:T(8,128)(2,1)S(1)}, bf16[1,2560,136]{1,2,0:T(8,128)(2,1)}, u32[]{:S(2)}) %copy-start.4) | copy-done | bytes 696344
  5.3 0.9 %copy-done.10 = bf16[192,640]{1,0:T(8,128)(2,1)S(1)} copy-done((bf16[192,640]{1,0:T(8,128)(2,1)S(1)}, bf16[192,640]{1,0:T(8,128)(2,1)}, u32[]{:S(2)}) %copy-start.10) | copy-done | bytes 245784
  6.3 0.1 collective-permute-start.2
  6.4 4.6 %collective-permute-done.three = bf16[192,640]{1,0:T(8,128)(2,1)S(1)} collective-permute-done((bf16[192,640]{1,0:T(8,128)(2,1)}, bf16[192,640]{1,0:T(8,128)(2,1)S(1)}, u32[]{:S(2)}, u32[]{:S(2)}) %collective-permute-start) | collective-permute-done | bytes 245792 | tf_op jit(solution)/shard_map/ppermute | solution.py:472
  10.9 0.0 collective-permute-done.1.two
  11.0 4.9 %collective-permute-done.2.one.share1 = bf16[192,640]{1,0:T(8,128)(2,1)S(1)} collective-permute-done((bf16[192,640]{1,0:T(8,128)(2,1)S(1)}, bf16[192,640]{1,0:T(8,128)(2,1)S(1)}, u32[]{:S(2)}, u32[]{:S(2)}) %collective-permute-start.2) | collective-permute-done | bytes 245792 | tf_op jit(solution)/shard_map/ppermute | solution.py:472
  15.8 0.0 copy-start.6
  15.8 0.0 copy-start.8
  15.9 0.0 copy-start.11
  15.9 0.0 copy-start.12
  15.9 0.0 copy-start.13
  15.9 1.6 %collective-permute-start.3 = (bf16[256,256]{1,0:T(8,128)(2,1)S(1)}, bf16[256,256]{1,0:T(8,128)(2,1)S(1)}, u32[]{:S(2)}, u32[]{:S(2)}) collective-permute-start(bf16[256,256]{1,0:T(8,128)(2,1)S(1)} %shard_map.105.own), channel_id=1, source_target_pairs={{0,8},{1,9},{2,10},{3,11},{4,12},{5,13},{6,14},{7,15},{8,0},{9,1},... | collective-permute-start | bytes 393224 | tf_op jit(solution)/shard_map/ppermute | solution.py:472
  17.6 2.5 %collective-permute-start.4 = (bf16[256,256]{1,0:T(8,128)(2,1)S(1)}, bf16[256,256]{1,0:T(8,128)(2,1)S(1)}, u32[]{:S(2)}, u32[]{:S(2)}) collective-permute-start(bf16[256,256]{1,0:T(8,128)(2,1)S(1)} %shard_map.105.own), channel_id=1, source_target_pairs={{0,4},{1,5},{2,6},{3,7},{4,0},{5,1},{6,2},{7,3},{8,12},{9,13},{10,... | collective-permute-start | bytes 393224 | tf_op jit(solution)/shard_map/ppermute | solution.py:472
  20.0 0.3 collective-permute-start.5
  20.4 6.8 %collective-permute-done.3.two = bf16[256,256]{1,0:T(8,128)(2,1)S(1)} collective-permute-done((bf16[256,256]{1,0:T(8,128)(2,1)S(1)}, bf16[256,256]{1,0:T(8,128)(2,1)S(1)}, u32[]{:S(2)}, u32[]{:S(2)}) %collective-permute-start.3) | collective-permute-done | bytes 131104 | tf_op jit(solution)/shard_map/ppermute | solution.py:472
  27.2 0.0 collective-permute-done.4.one
  27.2 1.8 %collective-permute-done.5.three = bf16[256,256]{1,0:T(8,128)(2,1)S(1)} collective-permute-done((bf16[256,256]{1,0:T(8,128)(2,1)S(1)}, bf16[256,256]{1,0:T(8,128)(2,1)S(1)}, u32[]{:S(2)}, u32[]{:S(2)}) %collective-permute-start.5) | collective-permute-done | bytes 131104 | tf_op jit(solution)/shard_map/ppermute | solution.py:472
  29.0 0.6 shard_map.106
  29.7 5.3 %collective-permute-start.10 = (bf16[2,136,896]{2,1,0:T(8,128)(2,1)S(1)}, bf16[2,136,896]{2,1,0:T(8,128)(2,1)S(1)}, u32[]{:S(2)}, u32[]{:S(2)}) collective-permute-start(bf16[2,136,896]{2,1,0:T(8,128)(2,1)S(1)} %get-tuple-element.24), channel_id=1, source_target_pairs={{16,24},{17,25},{18,26},{19,27},{20,28},{21,29},{22,30},{23,31},{2... | collective-permute-start | bytes 1462280 | tf_op jit(solution)/shard_map/ppermute | solution.py:472
  35.0 0.5 collective-permute-start.6
  35.5 1.0 %collective-permute-start.7 = (bf16[56,2560]{1,0:T(8,128)(2,1)S(1)}, bf16[56,2560]{1,0:T(8,128)(2,1)S(1)}, u32[]{:S(2)}, u32[]{:S(2)}) collective-permute-start(bf16[56,2560]{1,0:T(8,128)(2,1)S(1)} %get-tuple-element.21), channel_id=1, source_target_pairs={{0,20},{1,21},{2,22},{3,23},{4,16},{5,17},{6,18},{7,19},{8,28},{9,... | collective-permute-start | bytes 860168 | tf_op jit(solution)/shard_map/ppermute | solution.py:472
  36.6 2.7 %collective-permute-start.8 = (bf16[56,2560]{1,0:T(8,128)(2,1)S(1)}, bf16[56,2560]{1,0:T(8,128)(2,1)S(1)}, u32[]{:S(2)}, u32[]{:S(2)}) collective-permute-start(bf16[56,2560]{1,0:T(8,128)(2,1)S(1)} %get-tuple-element.22), channel_id=1, source_target_pairs={{0,28},{1,29},{2,30},{3,31},{4,24},{5,25},{6,26},{7,27},{8,20},{9,... | collective-permute-start | bytes 860168 | tf_op jit(solution)/shard_map/ppermute | solution.py:472
  39.3 0.1 collective-permute-start.9
  39.4 17.4 %collective-permute-done.10 = bf16[2,136,896]{2,1,0:T(8,128)(2,1)S(1)} collective-permute-done((bf16[2,136,896]{2,1,0:T(8,128)(2,1)S(1)}, bf16[2,136,896]{2,1,0:T(8,128)(2,1)S(1)}, u32[]{:S(2)}, u32[]{:S(2)}) %collective-permute-start.10) | collective-permute-done | bytes 487456 | tf_op jit(solution)/shard_map/ppermute | solution.py:472
  56.8 0.6 collective-permute-start.11
  57.4 0.1 collective-permute-start.12
  57.5 0.2 collective-permute-done.8.three
  57.7 0.2 collective-permute-start.13
  57.9 5.0 %collective-permute-done.9.four = bf16[56,2560]{1,0:T(8,128)(2,1)S(1)} collective-permute-done((bf16[56,2560]{1,0:T(8,128)(2,1)S(1)}, bf16[56,2560]{1,0:T(8,128)(2,1)S(1)}, u32[]{:S(2)}, u32[]{:S(2)}) %collective-permute-start.9) | collective-permute-done | bytes 286752 | tf_op jit(solution)/shard_map/ppermute | solution.py:472
  63.0 0.0 copy-start.3
  63.0 0.0 copy-start.7
  63.0 0.0 copy-start.9
  63.0 0.0 copy-start.14
  63.0 1.6 %shard_map.107 = (bf16[56,512]{1,0:T(8,128)(2,1)S(1)}, bf16[48,544]{1,0:T(8,128)(2,1)S(1)}, bf16[8,640]{1,0:T(8,128)(2,1)S(1)}) custom-call(bf16[56,2560]{1,0:T(8,128)(2,1)S(1)} %collective-permute-done.6.one, bf16[56,2560]{1,0:T(8,128)(2,1)S(1)} %collective-permute-done.7.two, bf16[56,2560]{1,0:T(8,128)(2,1)S(1)} %collective-permute-done.8.three, ...), custom_call_target="tpu_custom_call" | custom-call | flops 199999995904 | bytes 4939776 | tf_op jit(solution)/shard_map/pallas_call | solution.py:178
  64.7 1.5 %collective-permute-start.16 = (bf16[56,512]{1,0:T(8,128)(2,1)S(1)}, bf16[56,512]{1,0:T(8,128)(2,1)S(1)}, u32[]{:S(2)}, u32[]{:S(2)}) collective-permute-start(bf16[56,512]{1,0:T(8,128)(2,1)S(1)} %get-tuple-element.31.own), channel_id=1, source_target_pairs={{0,12},{1,13},{2,14},{3,15},{4,8},{5,9},{6,10},{7,11},{8,4},{9,5},... | collective-permute-start | bytes 172040 | tf_op jit(solution)/shard_map/ppermute | solution.py:472
  66.2 0.8 collective-permute-start.17
  66.9 2.1 %collective-permute-start.18 = (bf16[56,512]{1,0:T(8,128)(2,1)S(1)}, bf16[56,512]{1,0:T(8,128)(2,1)S(1)}, u32[]{:S(2)}, u32[]{:S(2)}) collective-permute-start(bf16[56,512]{1,0:T(8,128)(2,1)S(1)} %get-tuple-element.31.own), channel_id=1, source_target_pairs={{0,4},{1,5},{2,6},{3,7},{4,0},{5,1},{6,2},{7,3},{8,12},{9,13},{10,... | collective-permute-start | bytes 172040 | tf_op jit(solution)/shard_map/ppermute | solution.py:472
  69.1 2.2 %collective-permute-done.16.three = bf16[56,512]{1,0:T(8,128)(2,1)S(1)} collective-permute-done((bf16[56,512]{1,0:T(8,128)(2,1)S(1)}, bf16[56,512]{1,0:T(8,128)(2,1)S(1)}, u32[]{:S(2)}, u32[]{:S(2)}) %collective-permute-start.16) | collective-permute-done | bytes 57376 | tf_op jit(solution)/shard_map/ppermute | solution.py:472
  71.3 1.5 %collective-permute-done.17.two = bf16[56,512]{1,0:T(8,128)(2,1)S(1)} collective-permute-done((bf16[56,512]{1,0:T(8,128)(2,1)S(1)}, bf16[56,512]{1,0:T(8,128)(2,1)S(1)}, u32[]{:S(2)}, u32[]{:S(2)}) %collective-permute-start.17) | collective-permute-done | bytes 57376 | tf_op jit(solution)/shard_map/ppermute | solution.py:472
  72.8 2.2 %shard_map.108.mixed = bf16[8,512]{1,0:T(8,128)(2,1)S(1)} custom-call(s32[8]{0:T(128)S(1)} %copy-done.14, bf16[56,512]{1,0:T(8,128)(2,1)S(1)} %get-tuple-element.31.own, bf16[56,512]{1,0:T(8,128)(2,1)S(1)} %collective-permute-done.16.three, bf16[56,512]{1,0:T(8,128)(2,1)S(1)} %collective-permute-done.17.two, ...), custom_call_target="tpu_custom_call" | custom-call | flops 20000000000 | bytes 2285600 | tf_op jit(solution)/shard_map/pallas_call | solution.py:178
  75.0 0.5 shard_map.109
  75.5 2.4 %collective-permute-start.21 = (bf16[8,640]{1,0:T(8,128)(2,1)S(1)}, bf16[8,640]{1,0:T(8,128)(2,1)S(1)}, u32[]{:S(2)}, u32[]{:S(2)}) collective-permute-start(bf16[8,640]{1,0:T(8,128)(2,1)S(1)} %get-tuple-element.35), channel_id=1, source_target_pairs={{0,12},{1,13},{2,14},{3,15},{4,8},{5,9},{6,10},{7,11},{8,4},{9,5},... | collective-permute-start | bytes 30728 | tf_op jit(solution)/shard_map/ppermute | solution.py:472
  78.0 2.0 %collective-permute-start.19 = (bf16[8,640]{1,0:T(8,128)(2,1)S(1)}, bf16[8,640]{1,0:T(8,128)(2,1)S(1)}, u32[]{:S(2)}, u32[]{:S(2)}) collective-permute-start(bf16[8,640]{1,0:T(8,128)(2,1)S(1)} %get-tuple-element.33), channel_id=1, source_target_pairs={{0,4},{1,5},{2,6},{3,7},{4,0},{5,1},{6,2},{7,3},{8,12},{9,13},{10,... | collective-permute-start | bytes 30728 | tf_op jit(solution)/shard_map/ppermute | solution.py:472
  80.0 0.6 select_bitcast_fusion
  80.6 0.4 collective-permute-done.21
  81.0 1.5 %collective-permute-done.20 = bf16[8,640]{1,0:T(8,128)(2,1)S(1)} collective-permute-done((bf16[8,640]{1,0:T(8,128)(2,1)S(1)}, bf16[8,640]{1,0:T(8,128)(2,1)S(1)}, u32[]{:S(2)}, u32[]{:S(2)}) %collective-permute-start.20) | collective-permute-done | bytes 10272 | tf_op jit(solution)/shard_map/ppermute | solution.py:472
  82.5 0.6 fusion.1
  (38 shorter events, 0.2 us)
Async XLA Ops:
  0.6 10.3 %collective-permute-start = (bf16[192,640]{1,0:T(8,128)(2,1)}, bf16[192,640]{1,0:T(8,128)(2,1)S(1)}, u32[]{:S(2)}, u32[]{:S(2)}) collective-permute-start(bf16[192,640]{1,0:T(8,128)(2,1)} %prompt.3), channel_id=1, source_target_pairs={{0,16},{1,17},{2,18},{3,19},{4,20},{5,21},{6,22},{7,23},{8,24},{9,... | collective-permute-start | bytes 737288 | tf_op jit(solution)/shard_map/ppermute | solution.py:472
  4.2 6.7 %collective-permute-start.1 = (bf16[192,640]{1,0:T(8,128)(2,1)}, bf16[192,640]{1,0:T(8,128)(2,1)S(1)}, u32[]{:S(2)}, u32[]{:S(2)}) collective-permute-start(bf16[192,640]{1,0:T(8,128)(2,1)} %prompt.3), channel_id=1, source_target_pairs={{0,8},{1,9},{2,10},{3,11},{4,12},{5,13},{6,14},{7,15},{8,0},{9,1},... | collective-permute-start | bytes 737288 | tf_op jit(solution)/shard_map/ppermute | solution.py:472
  4.2 1.1 %copy-start.4 = (bf16[1,2560,136]{1,2,0:T(8,128)(2,1)S(1)}, bf16[1,2560,136]{1,2,0:T(8,128)(2,1)}, u32[]{:S(2)}) copy-start(bf16[1,2560,136]{1,2,0:T(8,128)(2,1)} %param.13) | copy-start | bytes 2088964
  5.3 0.9 %copy-start.10 = (bf16[192,640]{1,0:T(8,128)(2,1)S(1)}, bf16[192,640]{1,0:T(8,128)(2,1)}, u32[]{:S(2)}) copy-start(bf16[192,640]{1,0:T(8,128)(2,1)} %prompt.3) | copy-start | bytes 737284
  6.3 9.5 %copy-start.15 = (bf16[1,2560,192]{1,2,0:T(8,128)(2,1)S(1)}, bf16[1,2560,192]{1,2,0:T(8,128)(2,1)}, u32[]{:S(2)}) copy-start(bf16[1,2560,192]{1,2,0:T(8,128)(2,1)} %param.11) | copy-start | bytes 2949124
  6.3 9.5 %collective-permute-start.2 = (bf16[192,640]{1,0:T(8,128)(2,1)S(1)}, bf16[192,640]{1,0:T(8,128)(2,1)S(1)}, u32[]{:S(2)}, u32[]{:S(2)}) collective-permute-start(bf16[192,640]{1,0:T(8,128)(2,1)S(1)} %shard_map.104), channel_id=1, source_target_pairs={{0,4},{1,5},{2,6},{3,7},{4,0},{5,1},{6,2},{7,3},{8,12},{9,13},{10,... | collective-permute-start | bytes 737288 | tf_op jit(solution)/shard_map/ppermute | solution.py:472
  15.8 13.2 %copy-start = (bf16[1,512,2560]{2,1,0:T(8,128)(2,1)S(1)}, bf16[1,512,2560]{2,1,0:T(8,128)(2,1)}, u32[]{:S(2)}) copy-start(bf16[1,512,2560]{2,1,0:T(8,128)(2,1)} %param.16) | copy-start | bytes 7864324
  15.8 13.2 %copy-start.2 = (bf16[1,768,640]{2,1,0:T(8,128)(2,1)S(1)}, bf16[1,768,640]{2,1,0:T(8,128)(2,1)}, u32[]{:S(2)}) copy-start(bf16[1,768,640]{2,1,0:T(8,128)(2,1)} %param.12) | copy-start | bytes 2949124
  15.8 13.2 %copy-start.5 = (bf16[1,2560,136]{1,2,0:T(8,128)(2,1)S(1)}, bf16[1,2560,136]{1,2,0:T(8,128)(2,1)}, u32[]{:S(2)}) copy-start(bf16[1,2560,136]{1,2,0:T(8,128)(2,1)} %param.13) | copy-start | bytes 2088964
  15.8 13.2 %copy-start.6 = (bf16[1,512,512]{2,1,0:T(8,128)(2,1)S(1)}, bf16[1,512,512]{2,1,0:T(8,128)(2,1)}, u32[]{:S(2)}) copy-start(bf16[1,512,512]{2,1,0:T(8,128)(2,1)} %param.14) | copy-start | bytes 1572868
  15.8 13.2 %copy-start.8 = (bf16[1,512,512]{2,1,0:T(8,128)(2,1)S(1)}, bf16[1,512,512]{2,1,0:T(8,128)(2,1)}, u32[]{:S(2)}) copy-start(bf16[1,512,512]{2,1,0:T(8,128)(2,1)} %param.15) | copy-start | bytes 1572868
  15.9 13.2 %copy-start.11 = (bf16[192,640]{1,0:T(8,128)(2,1)S(1)}, bf16[192,640]{1,0:T(8,128)(2,1)}, u32[]{:S(2)}) copy-start(bf16[192,640]{1,0:T(8,128)(2,1)} %prompt.3) | copy-start | bytes 737284
  15.9 13.2 %copy-start.12 = (f32[192,32]{1,0:T(8,128)S(1)}, f32[192,32]{1,0:T(8,128)}, u32[]{:S(2)}) copy-start(f32[192,32]{1,0:T(8,128)} %constant.10.clone.angles) | copy-start | bytes 73732
  15.9 13.2 %copy-start.13 = (s32[8]{0:T(128)S(1)}, s32[8]{0:T(128)}, u32[]{:S(2)}) copy-start(s32[8]{0:T(128)} %sizes.3) | copy-start | bytes 100
  15.9 11.2 %collective-permute-start.3 = (bf16[256,256]{1,0:T(8,128)(2,1)S(1)}, bf16[256,256]{1,0:T(8,128)(2,1)S(1)}, u32[]{:S(2)}, u32[]{:S(2)}) collective-permute-start(bf16[256,256]{1,0:T(8,128)(2,1)S(1)} %shard_map.105.own), channel_id=1, source_target_pairs={{0,8},{1,9},{2,10},{3,11},{4,12},{5,13},{6,14},{7,15},{8,0},{9,1},... | collective-permute-start | bytes 393224 | tf_op jit(solution)/shard_map/ppermute | solution.py:472
  17.6 9.6 %collective-permute-start.4 = (bf16[256,256]{1,0:T(8,128)(2,1)S(1)}, bf16[256,256]{1,0:T(8,128)(2,1)S(1)}, u32[]{:S(2)}, u32[]{:S(2)}) collective-permute-start(bf16[256,256]{1,0:T(8,128)(2,1)S(1)} %shard_map.105.own), channel_id=1, source_target_pairs={{0,4},{1,5},{2,6},{3,7},{4,0},{5,1},{6,2},{7,3},{8,12},{9,13},{10,... | collective-permute-start | bytes 393224 | tf_op jit(solution)/shard_map/ppermute | solution.py:472
  20.0 8.9 %collective-permute-start.5 = (bf16[256,256]{1,0:T(8,128)(2,1)S(1)}, bf16[256,256]{1,0:T(8,128)(2,1)S(1)}, u32[]{:S(2)}, u32[]{:S(2)}) collective-permute-start(bf16[256,256]{1,0:T(8,128)(2,1)S(1)} %shard_map.105.own), channel_id=1, source_target_pairs={{0,12},{1,13},{2,14},{3,15},{4,8},{5,9},{6,10},{7,11},{8,4},{9,5},... | collective-permute-start | bytes 393224 | tf_op jit(solution)/shard_map/ppermute | solution.py:472
  29.7 27.1 %collective-permute-start.10 = (bf16[2,136,896]{2,1,0:T(8,128)(2,1)S(1)}, bf16[2,136,896]{2,1,0:T(8,128)(2,1)S(1)}, u32[]{:S(2)}, u32[]{:S(2)}) collective-permute-start(bf16[2,136,896]{2,1,0:T(8,128)(2,1)S(1)} %get-tuple-element.24), channel_id=1, source_target_pairs={{16,24},{17,25},{18,26},{19,27},{20,28},{21,29},{22,30},{23,31},{2... | collective-permute-start | bytes 1462280 | tf_op jit(solution)/shard_map/ppermute | solution.py:472
  35.0 21.8 %collective-permute-start.6 = (bf16[56,2560]{1,0:T(8,128)(2,1)S(1)}, bf16[56,2560]{1,0:T(8,128)(2,1)S(1)}, u32[]{:S(2)}, u32[]{:S(2)}) collective-permute-start(bf16[56,2560]{1,0:T(8,128)(2,1)S(1)} %get-tuple-element.20), channel_id=1, source_target_pairs={{0,24},{1,25},{2,26},{3,27},{4,28},{5,29},{6,30},{7,31},{8,16},{9,... | collective-permute-start | bytes 860168 | tf_op jit(solution)/shard_map/ppermute | solution.py:472
  35.5 21.9 %collective-permute-start.7 = (bf16[56,2560]{1,0:T(8,128)(2,1)S(1)}, bf16[56,2560]{1,0:T(8,128)(2,1)S(1)}, u32[]{:S(2)}, u32[]{:S(2)}) collective-permute-start(bf16[56,2560]{1,0:T(8,128)(2,1)S(1)} %get-tuple-element.21), channel_id=1, source_target_pairs={{0,20},{1,21},{2,22},{3,23},{4,16},{5,17},{6,18},{7,19},{8,28},{9,... | collective-permute-start | bytes 860168 | tf_op jit(solution)/shard_map/ppermute | solution.py:472
  36.6 21.1 %collective-permute-start.8 = (bf16[56,2560]{1,0:T(8,128)(2,1)S(1)}, bf16[56,2560]{1,0:T(8,128)(2,1)S(1)}, u32[]{:S(2)}, u32[]{:S(2)}) collective-permute-start(bf16[56,2560]{1,0:T(8,128)(2,1)S(1)} %get-tuple-element.22), channel_id=1, source_target_pairs={{0,28},{1,29},{2,30},{3,31},{4,24},{5,25},{6,26},{7,27},{8,20},{9,... | collective-permute-start | bytes 860168 | tf_op jit(solution)/shard_map/ppermute | solution.py:472
  39.3 23.7 %collective-permute-start.9 = (bf16[56,2560]{1,0:T(8,128)(2,1)S(1)}, bf16[56,2560]{1,0:T(8,128)(2,1)S(1)}, u32[]{:S(2)}, u32[]{:S(2)}) collective-permute-start(bf16[56,2560]{1,0:T(8,128)(2,1)S(1)} %get-tuple-element.23), channel_id=1, source_target_pairs={{0,16},{1,17},{2,18},{3,19},{4,20},{5,21},{6,22},{7,23},{8,24},{9,... | collective-permute-start | bytes 860168 | tf_op jit(solution)/shard_map/ppermute | solution.py:472
  56.8 6.2 %collective-permute-start.14 = (bf16[3,136,384]{2,1,0:T(8,128)(2,1)S(1)}, bf16[3,136,384]{2,1,0:T(8,128)(2,1)S(1)}, u32[]{:S(2)}, u32[]{:S(2)}) collective-permute-start(bf16[3,136,384]{2,1,0:T(8,128)(2,1)S(1)} %get-tuple-element.28.rest), channel_id=1, source_target_pairs={{0,1},{1,0},{2,3},{3,2},{4,5},{5,4},{6,7},{7,6},{8,9},{9,8},{10,11... | collective-permute-start | bytes 940040 | tf_op jit(solution)/shard_map/ppermute | solution.py:481
  56.8 6.1 %collective-permute-start.11 = (bf16[136,896]{1,0:T(8,128)(2,1)S(1)}, bf16[136,896]{1,0:T(8,128)(2,1)S(1)}, u32[]{:S(2)}, u32[]{:S(2)}) collective-permute-start(bf16[136,896]{1,0:T(8,128)(2,1)S(1)} %slice_bitcast_fusion.2.first1), channel_id=1, source_target_pairs={{0,1},{1,0},{2,3},{3,2},{4,5},{5,4},{6,7},{7,6},{8,9},{9,8},{10,11... | collective-permute-start | bytes 731144 | tf_op jit(solution)/shard_map/ppermute | solution.py:481
  57.4 5.6 %collective-permute-start.12 = (bf16[136,896]{1,0:T(8,128)(2,1)S(1)}, bf16[136,896]{1,0:T(8,128)(2,1)S(1)}, u32[]{:S(2)}, u32[]{:S(2)}) collective-permute-start(bf16[136,896]{1,0:T(8,128)(2,1)S(1)} %get-tuple-element.37.first2), channel_id=1, source_target_pairs={{0,1},{1,0},{2,3},{3,2},{4,5},{5,4},{6,7},{7,6},{8,9},{9,8},{10,11... | collective-permute-start | bytes 731144 | tf_op jit(solution)/shard_map/ppermute | solution.py:481
  57.7 5.3 %collective-permute-start.13 = (bf16[136,896]{1,0:T(8,128)(2,1)S(1)}, bf16[136,896]{1,0:T(8,128)(2,1)S(1)}, u32[]{:S(2)}, u32[]{:S(2)}) collective-permute-start(bf16[136,896]{1,0:T(8,128)(2,1)S(1)} %get-tuple-element.36.first3), channel_id=1, source_target_pairs={{0,1},{1,0},{2,3},{3,2},{4,5},{5,4},{6,7},{7,6},{8,9},{9,8},{10,11... | collective-permute-start | bytes 731144 | tf_op jit(solution)/shard_map/ppermute | solution.py:481
  63.0 9.8 %copy-start.3 = (bf16[1,768,640]{2,1,0:T(8,128)(2,1)S(1)}, bf16[1,768,640]{2,1,0:T(8,128)(2,1)}, u32[]{:S(2)}) copy-start(bf16[1,768,640]{2,1,0:T(8,128)(2,1)} %param.12) | copy-start | bytes 2949124
  63.0 9.8 %copy-start.7 = (bf16[1,512,512]{2,1,0:T(8,128)(2,1)S(1)}, bf16[1,512,512]{2,1,0:T(8,128)(2,1)}, u32[]{:S(2)}) copy-start(bf16[1,512,512]{2,1,0:T(8,128)(2,1)} %param.14) | copy-start | bytes 1572868
  63.0 9.8 %copy-start.9 = (bf16[1,512,512]{2,1,0:T(8,128)(2,1)S(1)}, bf16[1,512,512]{2,1,0:T(8,128)(2,1)}, u32[]{:S(2)}) copy-start(bf16[1,512,512]{2,1,0:T(8,128)(2,1)} %param.15) | copy-start | bytes 1572868
  63.0 9.8 %copy-start.14 = (s32[8]{0:T(128)S(1)}, s32[8]{0:T(128)}, u32[]{:S(2)}) copy-start(s32[8]{0:T(128)} %sizes.3) | copy-start | bytes 100
  64.7 6.6 %collective-permute-start.16 = (bf16[56,512]{1,0:T(8,128)(2,1)S(1)}, bf16[56,512]{1,0:T(8,128)(2,1)S(1)}, u32[]{:S(2)}, u32[]{:S(2)}) collective-permute-start(bf16[56,512]{1,0:T(8,128)(2,1)S(1)} %get-tuple-element.31.own), channel_id=1, source_target_pairs={{0,12},{1,13},{2,14},{3,15},{4,8},{5,9},{6,10},{7,11},{8,4},{9,5},... | collective-permute-start | bytes 172040 | tf_op jit(solution)/shard_map/ppermute | solution.py:472
  66.2 6.6 %collective-permute-start.17 = (bf16[56,512]{1,0:T(8,128)(2,1)S(1)}, bf16[56,512]{1,0:T(8,128)(2,1)S(1)}, u32[]{:S(2)}, u32[]{:S(2)}) collective-permute-start(bf16[56,512]{1,0:T(8,128)(2,1)S(1)} %get-tuple-element.31.own), channel_id=1, source_target_pairs={{0,8},{1,9},{2,10},{3,11},{4,12},{5,13},{6,14},{7,15},{8,0},{9,1},... | collective-permute-start | bytes 172040 | tf_op jit(solution)/shard_map/ppermute | solution.py:472
  66.9 5.9 %collective-permute-start.18 = (bf16[56,512]{1,0:T(8,128)(2,1)S(1)}, bf16[56,512]{1,0:T(8,128)(2,1)S(1)}, u32[]{:S(2)}, u32[]{:S(2)}) collective-permute-start(bf16[56,512]{1,0:T(8,128)(2,1)S(1)} %get-tuple-element.31.own), channel_id=1, source_target_pairs={{0,4},{1,5},{2,6},{3,7},{4,0},{5,1},{6,2},{7,3},{8,12},{9,13},{10,... | collective-permute-start | bytes 172040 | tf_op jit(solution)/shard_map/ppermute | solution.py:472
  69.1 5.9 %copy-start.1 = (bf16[1,512,2560]{2,1,0:T(8,128)(2,1)S(1)}, bf16[1,512,2560]{2,1,0:T(8,128)(2,1)}, u32[]{:S(2)}) copy-start(bf16[1,512,2560]{2,1,0:T(8,128)(2,1)} %param.16) | copy-start | bytes 7864324
  69.1 11.5 %collective-permute-start.15 = (bf16[8,640]{1,0:T(8,128)(2,1)S(1)}, bf16[8,640]{1,0:T(8,128)(2,1)S(1)}, u32[]{:S(2)}, u32[]{:S(2)}) collective-permute-start(bf16[8,640]{1,0:T(8,128)(2,1)S(1)} %get-tuple-element.30), channel_id=1, source_target_pairs={{0,16},{1,17},{2,18},{3,19},{4,20},{5,21},{6,22},{7,23},{8,24},{9,... | collective-permute-start | bytes 30728 | tf_op jit(solution)/shard_map/ppermute | solution.py:472
  75.5 5.5 %collective-permute-start.21 = (bf16[8,640]{1,0:T(8,128)(2,1)S(1)}, bf16[8,640]{1,0:T(8,128)(2,1)S(1)}, u32[]{:S(2)}, u32[]{:S(2)}) collective-permute-start(bf16[8,640]{1,0:T(8,128)(2,1)S(1)} %get-tuple-element.35), channel_id=1, source_target_pairs={{0,12},{1,13},{2,14},{3,15},{4,8},{5,9},{6,10},{7,11},{8,4},{9,5},... | collective-permute-start | bytes 30728 | tf_op jit(solution)/shard_map/ppermute | solution.py:472
  78.0 4.6 %collective-permute-start.20 = (bf16[8,640]{1,0:T(8,128)(2,1)S(1)}, bf16[8,640]{1,0:T(8,128)(2,1)S(1)}, u32[]{:S(2)}, u32[]{:S(2)}) collective-permute-start(bf16[8,640]{1,0:T(8,128)(2,1)S(1)} %get-tuple-element.34), channel_id=1, source_target_pairs={{0,8},{1,9},{2,10},{3,11},{4,12},{5,13},{6,14},{7,15},{8,0},{9,1},... | collective-permute-start | bytes 30728 | tf_op jit(solution)/shard_map/ppermute | solution.py:472
  78.0 4.6 %collective-permute-start.19 = (bf16[8,640]{1,0:T(8,128)(2,1)S(1)}, bf16[8,640]{1,0:T(8,128)(2,1)S(1)}, u32[]{:S(2)}, u32[]{:S(2)}) collective-permute-start(bf16[8,640]{1,0:T(8,128)(2,1)S(1)} %get-tuple-element.33), channel_id=1, source_target_pairs={{0,4},{1,5},{2,6},{3,7},{4,0},{5,1},{6,2},{7,3},{8,12},{9,13},{10,... | collective-permute-start | bytes 30728 | tf_op jit(solution)/shard_map/ppermute | solution.py:472

commit v11 on v10

--- a/solution.py
+++ b/solution.py
@@ -324,16 +324,17 @@
     section, tp, rep = (lax.axis_index(a) for a in ("section", "tp", "rep"))
     tokens, width = prompt.shape
     block = tokens // 4
-    cols, early = passed.shape[1:]
+    cols, late = rest.shape[1:]
     down_cols = w_query.shape[0] // 4
 
     @pl.when(section != 0)
     def _():
-        first = (rep & 1) * (early + rest.shape[2])
-        passed[0] = w_latent[:, pl.ds(pl.multiple_of(first, 128), early)]
-        passed[1] = unpack_share(share1[...], cols)
-        for k, ref in enumerate((one, two, three)):
-            rest[k] = unpack_rest(ref[...], cols)
+        long = passed.shape[1] - share1.shape[1] - 256
+        first = (rep & 1) * long
+        passed[:, :long] = w_latent[:, pl.ds(pl.multiple_of(first, 128), long)]
+        passed[:, long:] = unpack_share(share1[...], cols)
+        rest[0] = unpack_rest(one[...], cols)
+        rest[1] = unpack_rest(three[...], cols)
 
     @pl.when(section == 0)
     def _():
@@ -474,8 +475,8 @@
     def within(array, k):
         return route(array, (0, k), (1, k))
 
-    def onward(array, k):
-        return route(array, (1, k), (0, 0))
+    def onward(array, k, back=True):
+        return route(array, (1, k), (0, 0) if back else None)
 
     def over_rep(array, k):
         return lax.ppermute(array, "rep", [(i, i ^ k) for i in range(4)])
@@ -484,7 +485,7 @@
         send_kernel,
         jax.ShapeDtypeStruct((tokens, share), BF16),
         [prompt, w_lat],
-        grant=8,
+        grant=57,
         flops=2 * 10**10,
     )
     two = route(prompt, (0, 2), (1, 0, 1))
@@ -496,7 +497,7 @@
         [prompt, three, two, one, w_down, w_lat],
         flops=2 * 10**10,
     )
-    pieces = [parts] + [within(parts, k) for k in (1, 2, 3)]
+    pieces = [parts, within(parts, 1), route(parts, (0, 2), (1, 0, 1)), within(parts, 3)]
 
     message = jax.ShapeDtypeStruct((block + count, model), BF16)
     *blocks, first_cache, passed, rest = call(
@@ -504,8 +505,8 @@
         [message] * 4
         + [
             jax.ShapeDtypeStruct((block, ROW_WIDTH), BF16),
-            jax.ShapeDtypeStruct((2, latent_cols, model // 2 - 384), BF16),
-            jax.ShapeDtypeStruct((3, latent_cols, 384), BF16),
+            jax.ShapeDtypeStruct((latent_cols, model - 384), BF16),
+            jax.ShapeDtypeStruct((2, latent_cols, 384), BF16),
         ],
         [block_sizes, pieces[0], pieces[2], pieces[1], pieces[3], one, w_lat, prompt, angles, w_up, w_key, w_value, w_final],
         [
@@ -517,10 +518,12 @@
         scalars=1,
         grant=16,
     )
-    arrived = [onward(blocks[k], k) for k in (2, 1, 3, 0)]
+    arrived = [onward(blocks[k], k, k in (1, 2)) for k in (2, 1, 3, 0)]
     relayed = route(passed, None, (1, 2))
-    relayed, late, first = lax.optimization_barrier((relayed, rest, passed[1]))
-    weights = [first, relayed[0], relayed[1], late]
+    relayed, rest, beside = lax.optimization_barrier((relayed, rest, passed[:, model // 2 :]))
+    early = model // 2 - 384
+    late = jnp.stack([rest[0], relayed[:, early : model // 2], rest[1]])
+    weights = [beside, relayed[:, :early], relayed[:, model // 2 :], late]
     weights += [over_rep(w, 1) for w in weights]
     fresh, last_cache, ends_share = call(
         latent_kernel,

time: 83.5 us -> 82 us (0.982)
  waiting for transfers between devices: 46.3 us -> 43.6 us
  Pallas kernels: 5.01 us -> 7.05 us
  local copies, waits for them, and re-layouts: 2.18 us -> 0.17 us
    ppermute x18, waiting for transfers between devices: 46.3 us -> 43.6 us  [route(): return lax.ppermute(array, ('section', 'tp', 'rep'), pairs)]
    unnamed x32 -> x28, local copies, waits for them, and re-layouts: 2.12 us -> 0.08 us
    pallas_call x6, Pallas kernels: 5.01 us -> 7.05 us  [call(): pl.pallas_call(kernel, out_shape=out_shape, in_specs=[SMEM] * scalars + [...]
  transfers between devices with their start and end apart: 22 -> 22, of which waited for: 11 -> 11; matrix products, arithmetic and copies ran while one was open for 1% -> 1% of each run, Pallas kernels for 3% -> 6%
where the time goes in v11:
time: 82 us; the launch traced here: 81.3 us
  waiting for transfers between devices  43.6 us (53%)
  starting transfers between devices  28.3 us (35%)
  Pallas kernels  7.05 us (9%)
  other arithmetic  1.31 us (2%)
  between operations  0.89 us (1%)
    ppermute x18, waiting for transfers between devices, route(): return lax.ppermute(array, ('section', 'tp', 'rep'), pairs)  43.6 us
    ppermute x18, starting transfers between devices, route(): return lax.ppermute(array, ('section', 'tp', 'rep'), pairs)  27.2 us
    pallas_call x6, Pallas kernels, call(): pl.pallas_call(kernel, out_shape=out_shape, in_specs=[SMEM] * scalars + [...  7.05 us
  transfers between devices with their start and end apart: 22, of which 11 were waited for; matrix products, arithmetic and copies ran while one was open for 1% of the time, Pallas kernels for 6%

profile of v11, /device:TPU:4, one launch (start us, length us, event | category | flops | bytes accessed | tf_op | source)
XLA Modules:
  0.0 81.3 jit_solution(16473946096613859382)
XLA Ops:
  0.6 3.6 %collective-permute-start = (bf16[192,640]{1,0:T(8,128)(2,1)}, bf16[192,640]{1,0:T(8,128)(2,1)S(1)}, u32[]{:S(2)}, u32[]{:S(2)}) collective-permute-start(bf16[192,640]{1,0:T(8,128)(2,1)} %prompt.3), channel_id=1, source_target_pairs={{0,16},{1,17},{2,18},{3,19},{4,20},{5,21},{6,22},{7,23},{8,24},{9,... | collective-permute-start | bytes 737288 | tf_op jit(solution)/shard_map/ppermute | solution.py:473
  4.2 2.1 %shard_map.104 = bf16[192,640]{1,0:T(8,128)(2,1)} custom-call(bf16[192,640]{1,0:T(8,128)(2,1)} %prompt.3, bf16[136,2560]{1,0:T(8,128)(2,1)} %bitcast.20), custom_call_target="tpu_custom_call" | custom-call | flops 20000000000 | bytes 942080 | tf_op jit(solution)/shard_map/pallas_call | solution.py:178
  6.3 4.6 %collective-permute-done.three = bf16[192,640]{1,0:T(8,128)(2,1)S(1)} collective-permute-done((bf16[192,640]{1,0:T(8,128)(2,1)}, bf16[192,640]{1,0:T(8,128)(2,1)S(1)}, u32[]{:S(2)}, u32[]{:S(2)}) %collective-permute-start) | collective-permute-done | bytes 245792 | tf_op jit(solution)/shard_map/ppermute | solution.py:473
  11.0 4.9 %collective-permute-done.2.one.share1 = bf16[192,640]{1,0:T(8,128)(2,1)S(1)} collective-permute-done((bf16[192,640]{1,0:T(8,128)(2,1)}, bf16[192,640]{1,0:T(8,128)(2,1)S(1)}, u32[]{:S(2)}, u32[]{:S(2)}) %collective-permute-start.2) | collective-permute-done | bytes 245792 | tf_op jit(solution)/shard_map/ppermute | solution.py:473
  15.8 0.0 copy-start
  15.8 0.0 copy-start.2
  15.9 0.0 copy-start.5
  15.9 0.0 copy-start.7
  15.9 0.0 copy-start.10
  15.9 0.0 copy-start.11
  15.9 0.1 collective-permute-start.3
  16.0 1.7 %collective-permute-start.4 = (bf16[256,256]{1,0:T(8,128)(2,1)S(1)}, bf16[256,256]{1,0:T(8,128)(2,1)S(1)}, u32[]{:S(2)}, u32[]{:S(2)}) collective-permute-start(bf16[256,256]{1,0:T(8,128)(2,1)S(1)} %shard_map.105.own), channel_id=1, source_target_pairs={{0,4},{1,5},{2,6},{3,7},{4,0},{5,1},{6,2},{7,3},{8,12},{9,13},{10,... | collective-permute-start | bytes 393224 | tf_op jit(solution)/shard_map/ppermute | solution.py:473
  17.8 1.9 %collective-permute-start.5 = (bf16[256,256]{1,0:T(8,128)(2,1)S(1)}, bf16[256,256]{1,0:T(8,128)(2,1)S(1)}, u32[]{:S(2)}, u32[]{:S(2)}) collective-permute-start(bf16[256,256]{1,0:T(8,128)(2,1)S(1)} %shard_map.105.own), channel_id=1, source_target_pairs={{0,12},{1,13},{2,14},{3,15},{4,8},{5,9},{6,10},{7,11},{8,4},{9,5},... | collective-permute-start | bytes 393224 | tf_op jit(solution)/shard_map/ppermute | solution.py:473
  19.7 2.3 %collective-permute-done.4.one = bf16[256,256]{1,0:T(8,128)(2,1)S(1)} collective-permute-done((bf16[256,256]{1,0:T(8,128)(2,1)S(1)}, bf16[256,256]{1,0:T(8,128)(2,1)S(1)}, u32[]{:S(2)}, u32[]{:S(2)}) %collective-permute-start.4) | collective-permute-done | bytes 131104 | tf_op jit(solution)/shard_map/ppermute | solution.py:473
  21.9 4.6 %collective-permute-done.5.three = bf16[256,256]{1,0:T(8,128)(2,1)S(1)} collective-permute-done((bf16[256,256]{1,0:T(8,128)(2,1)S(1)}, bf16[256,256]{1,0:T(8,128)(2,1)S(1)}, u32[]{:S(2)}, u32[]{:S(2)}) %collective-permute-start.5) | collective-permute-done | bytes 131104 | tf_op jit(solution)/shard_map/ppermute | solution.py:473
  26.6 0.6 shard_map.106
  27.3 3.8 %collective-permute-start.10 = (bf16[136,2176]{1,0:T(8,128)(2,1)S(1)}, bf16[136,2176]{1,0:T(8,128)(2,1)S(1)}, u32[]{:S(2)}, u32[]{:S(2)}) collective-permute-start(bf16[136,2176]{1,0:T(8,128)(2,1)S(1)} %get-tuple-element.24), channel_id=1, source_target_pairs={{16,24},{17,25},{18,26},{19,27},{20,28},{21,29},{22,30},{23,31},{2... | collective-permute-start | bytes 1775624 | tf_op jit(solution)/shard_map/ppermute | solution.py:473
  31.1 4.5 %collective-permute-start.6 = (bf16[56,2560]{1,0:T(8,128)(2,1)S(1)}, bf16[56,2560]{1,0:T(8,128)(2,1)S(1)}, u32[]{:S(2)}, u32[]{:S(2)}) collective-permute-start(bf16[56,2560]{1,0:T(8,128)(2,1)S(1)} %get-tuple-element.20), channel_id=1, source_target_pairs={{0,24},{1,25},{2,26},{3,27},{4,28},{5,29},{6,30},{7,31},{8,16},{9,... | collective-permute-start | bytes 860168 | tf_op jit(solution)/shard_map/ppermute | solution.py:473
  35.6 0.1 collective-permute-start.7
  35.7 1.3 %collective-permute-start.8 = (bf16[56,2560]{1,0:T(8,128)(2,1)S(1)}, bf16[56,2560]{1,0:T(8,128)(2,1)S(1)}, u32[]{:S(2)}, u32[]{:S(2)}) collective-permute-start(bf16[56,2560]{1,0:T(8,128)(2,1)S(1)} %get-tuple-element.22), channel_id=1, source_target_pairs={{0,28},{1,29},{2,30},{3,31},{4,24},{5,25},{6,26},{7,27},{8,20},{9,... | collective-permute-start | bytes 860168 | tf_op jit(solution)/shard_map/ppermute | solution.py:473
  37.0 1.3 %collective-permute-start.9 = (bf16[56,2560]{1,0:T(8,128)(2,1)S(1)}, bf16[56,2560]{1,0:T(8,128)(2,1)S(1)}, u32[]{:S(2)}, u32[]{:S(2)}) collective-permute-start(bf16[56,2560]{1,0:T(8,128)(2,1)S(1)} %get-tuple-element.23), channel_id=1, source_target_pairs={{0,16},{1,17},{2,18},{3,19},{4,20},{5,21},{6,22},{7,23},{8,24},{9,... | collective-permute-start | bytes 860168 | tf_op jit(solution)/shard_map/ppermute | solution.py:473
  38.3 18.4 %collective-permute-done.10 = bf16[136,2176]{1,0:T(8,128)(2,1)S(1)} collective-permute-done((bf16[136,2176]{1,0:T(8,128)(2,1)S(1)}, bf16[136,2176]{1,0:T(8,128)(2,1)S(1)}, u32[]{:S(2)}, u32[]{:S(2)}) %collective-permute-start.10) | collective-permute-done | bytes 591904 | tf_op jit(solution)/shard_map/ppermute | solution.py:473
  56.8 0.1 pad_maximum_fusion.rest
  56.8 0.1 collective-permute-start.14
  57.0 0.6 collective-permute-start.11
  57.5 0.1 collective-permute-start.12
  57.6 0.4 collective-permute-start.13
  58.0 4.0 %collective-permute-done.9.four = bf16[56,2560]{1,0:T(8,128)(2,1)S(1)} collective-permute-done((bf16[56,2560]{1,0:T(8,128)(2,1)S(1)}, bf16[56,2560]{1,0:T(8,128)(2,1)S(1)}, u32[]{:S(2)}, u32[]{:S(2)}) %collective-permute-start.9) | collective-permute-done | bytes 286752 | tf_op jit(solution)/shard_map/ppermute | solution.py:473
  62.0 0.0 copy-start.3
  62.1 0.0 copy-start.6
  62.1 0.0 copy-start.8
  62.1 0.0 copy-start.12
  62.1 1.6 %shard_map.107 = (bf16[56,512]{1,0:T(8,128)(2,1)S(1)}, bf16[48,544]{1,0:T(8,128)(2,1)S(1)}, bf16[8,640]{1,0:T(8,128)(2,1)S(1)}) custom-call(bf16[56,2560]{1,0:T(8,128)(2,1)S(1)} %collective-permute-done.6.one, bf16[56,2560]{1,0:T(8,128)(2,1)S(1)} %collective-permute-done.7.two, bf16[56,2560]{1,0:T(8,128)(2,1)S(1)} %collective-permute-done.8.three, ...), custom_call_target="tpu_custom_call" | custom-call | flops 199999995904 | bytes 4939776 | tf_op jit(solution)/shard_map/pallas_call | solution.py:178
  63.7 1.4 %collective-permute-start.16 = (bf16[56,512]{1,0:T(8,128)(2,1)S(1)}, bf16[56,512]{1,0:T(8,128)(2,1)S(1)}, u32[]{:S(2)}, u32[]{:S(2)}) collective-permute-start(bf16[56,512]{1,0:T(8,128)(2,1)S(1)} %get-tuple-element.31.own), channel_id=1, source_target_pairs={{0,12},{1,13},{2,14},{3,15},{4,8},{5,9},{6,10},{7,11},{8,4},{9,5},... | collective-permute-start | bytes 172040 | tf_op jit(solution)/shard_map/ppermute | solution.py:473
  65.1 0.7 collective-permute-start.17
  65.8 2.3 %collective-permute-start.18 = (bf16[56,512]{1,0:T(8,128)(2,1)S(1)}, bf16[56,512]{1,0:T(8,128)(2,1)S(1)}, u32[]{:S(2)}, u32[]{:S(2)}) collective-permute-start(bf16[56,512]{1,0:T(8,128)(2,1)S(1)} %get-tuple-element.31.own), channel_id=1, source_target_pairs={{0,4},{1,5},{2,6},{3,7},{4,0},{5,1},{6,2},{7,3},{8,12},{9,13},{10,... | collective-permute-start | bytes 172040 | tf_op jit(solution)/shard_map/ppermute | solution.py:473
  68.1 2.2 %collective-permute-done.16.three = bf16[56,512]{1,0:T(8,128)(2,1)S(1)} collective-permute-done((bf16[56,512]{1,0:T(8,128)(2,1)S(1)}, bf16[56,512]{1,0:T(8,128)(2,1)S(1)}, u32[]{:S(2)}, u32[]{:S(2)}) %collective-permute-start.16) | collective-permute-done | bytes 57376 | tf_op jit(solution)/shard_map/ppermute | solution.py:473
  70.4 1.5 %collective-permute-done.17.two = bf16[56,512]{1,0:T(8,128)(2,1)S(1)} collective-permute-done((bf16[56,512]{1,0:T(8,128)(2,1)S(1)}, bf16[56,512]{1,0:T(8,128)(2,1)S(1)}, u32[]{:S(2)}, u32[]{:S(2)}) %collective-permute-start.17) | collective-permute-done | bytes 57376 | tf_op jit(solution)/shard_map/ppermute | solution.py:473
  71.9 2.2 %shard_map.108.mixed = bf16[8,512]{1,0:T(8,128)(2,1)S(1)} custom-call(s32[8]{0:T(128)S(1)} %copy-done.12, bf16[56,512]{1,0:T(8,128)(2,1)S(1)} %get-tuple-element.31.own, bf16[56,512]{1,0:T(8,128)(2,1)S(1)} %collective-permute-done.16.three, bf16[56,512]{1,0:T(8,128)(2,1)S(1)} %collective-permute-done.17.two, ...), custom_call_target="tpu_custom_call" | custom-call | flops 20000000000 | bytes 2285600 | tf_op jit(solution)/shard_map/pallas_call | solution.py:178
  74.0 0.5 shard_map.109
  74.6 1.4 %collective-permute-start.21 = (bf16[8,640]{1,0:T(8,128)(2,1)S(1)}, bf16[8,640]{1,0:T(8,128)(2,1)S(1)}, u32[]{:S(2)}, u32[]{:S(2)}) collective-permute-start(bf16[8,640]{1,0:T(8,128)(2,1)S(1)} %get-tuple-element.35), channel_id=1, source_target_pairs={{0,12},{1,13},{2,14},{3,15},{4,8},{5,9},{6,10},{7,11},{8,4},{9,5},... | collective-permute-start | bytes 30728 | tf_op jit(solution)/shard_map/ppermute | solution.py:473
  76.0 0.5 collective-permute-start.20
  76.5 2.5 %collective-permute-start.19 = (bf16[8,640]{1,0:T(8,128)(2,1)S(1)}, bf16[8,640]{1,0:T(8,128)(2,1)S(1)}, u32[]{:S(2)}, u32[]{:S(2)}) collective-permute-start(bf16[8,640]{1,0:T(8,128)(2,1)S(1)} %get-tuple-element.33), channel_id=1, source_target_pairs={{0,4},{1,5},{2,6},{3,7},{4,0},{5,1},{6,2},{7,3},{8,12},{9,13},{10,... | collective-permute-start | bytes 30728 | tf_op jit(solution)/shard_map/ppermute | solution.py:473
  79.0 0.6 select_bitcast_fusion
  79.6 0.4 collective-permute-done.21
  80.1 0.5 collective-permute-done.20
  80.6 0.1 collective-permute-done.19
  80.7 0.6 fusion.1
  (37 shorter events, 0.2 us)
Async XLA Ops:
  0.6 10.3 %collective-permute-start = (bf16[192,640]{1,0:T(8,128)(2,1)}, bf16[192,640]{1,0:T(8,128)(2,1)S(1)}, u32[]{:S(2)}, u32[]{:S(2)}) collective-permute-start(bf16[192,640]{1,0:T(8,128)(2,1)} %prompt.3), channel_id=1, source_target_pairs={{0,16},{1,17},{2,18},{3,19},{4,20},{5,21},{6,22},{7,23},{8,24},{9,... | collective-permute-start | bytes 737288 | tf_op jit(solution)/shard_map/ppermute | solution.py:473
  4.2 6.7 %collective-permute-start.1 = (bf16[192,640]{1,0:T(8,128)(2,1)}, bf16[192,640]{1,0:T(8,128)(2,1)S(1)}, u32[]{:S(2)}, u32[]{:S(2)}) collective-permute-start(bf16[192,640]{1,0:T(8,128)(2,1)} %prompt.3), channel_id=1, source_target_pairs={{0,8},{1,9},{2,10},{3,11},{4,12},{5,13},{6,14},{7,15},{8,0},{9,1},... | collective-permute-start | bytes 737288 | tf_op jit(solution)/shard_map/ppermute | solution.py:473
  4.2 11.6 %copy-start.4 = (bf16[1,2560,136]{1,2,0:T(8,128)(2,1)S(1)}, bf16[1,2560,136]{1,2,0:T(8,128)(2,1)}, u32[]{:S(2)}) copy-start(bf16[1,2560,136]{1,2,0:T(8,128)(2,1)} %param.13) | copy-start | bytes 2088964
  4.2 11.6 %copy-start.9 = (bf16[192,640]{1,0:T(8,128)(2,1)S(1)}, bf16[192,640]{1,0:T(8,128)(2,1)}, u32[]{:S(2)}) copy-start(bf16[192,640]{1,0:T(8,128)(2,1)} %prompt.3) | copy-start | bytes 737284
  4.2 11.6 %copy-start.13 = (bf16[1,2560,192]{1,2,0:T(8,128)(2,1)S(1)}, bf16[1,2560,192]{1,2,0:T(8,128)(2,1)}, u32[]{:S(2)}) copy-start(bf16[1,2560,192]{1,2,0:T(8,128)(2,1)} %param.11) | copy-start | bytes 2949124
  6.3 9.5 %collective-permute-start.2 = (bf16[192,640]{1,0:T(8,128)(2,1)}, bf16[192,640]{1,0:T(8,128)(2,1)S(1)}, u32[]{:S(2)}, u32[]{:S(2)}) collective-permute-start(bf16[192,640]{1,0:T(8,128)(2,1)} %shard_map.104), channel_id=1, source_target_pairs={{0,4},{1,5},{2,6},{3,7},{4,0},{5,1},{6,2},{7,3},{8,12},{9,13},{10,... | collective-permute-start | bytes 737288 | tf_op jit(solution)/shard_map/ppermute | solution.py:473
  15.8 10.7 %copy-start = (bf16[1,512,2560]{2,1,0:T(8,128)(2,1)S(1)}, bf16[1,512,2560]{2,1,0:T(8,128)(2,1)}, u32[]{:S(2)}) copy-start(bf16[1,512,2560]{2,1,0:T(8,128)(2,1)} %param.16) | copy-start | bytes 7864324
  15.8 10.7 %copy-start.2 = (bf16[1,768,640]{2,1,0:T(8,128)(2,1)S(1)}, bf16[1,768,640]{2,1,0:T(8,128)(2,1)}, u32[]{:S(2)}) copy-start(bf16[1,768,640]{2,1,0:T(8,128)(2,1)} %param.12) | copy-start | bytes 2949124
  15.9 10.7 %copy-start.5 = (bf16[1,512,512]{2,1,0:T(8,128)(2,1)S(1)}, bf16[1,512,512]{2,1,0:T(8,128)(2,1)}, u32[]{:S(2)}) copy-start(bf16[1,512,512]{2,1,0:T(8,128)(2,1)} %param.14) | copy-start | bytes 1572868
  15.9 10.7 %copy-start.7 = (bf16[1,512,512]{2,1,0:T(8,128)(2,1)S(1)}, bf16[1,512,512]{2,1,0:T(8,128)(2,1)}, u32[]{:S(2)}) copy-start(bf16[1,512,512]{2,1,0:T(8,128)(2,1)} %param.15) | copy-start | bytes 1572868
  15.9 10.7 %copy-start.10 = (f32[192,32]{1,0:T(8,128)S(1)}, f32[192,32]{1,0:T(8,128)}, u32[]{:S(2)}) copy-start(f32[192,32]{1,0:T(8,128)} %constant.10.clone.angles) | copy-start | bytes 73732
  15.9 10.7 %copy-start.11 = (s32[8]{0:T(128)S(1)}, s32[8]{0:T(128)}, u32[]{:S(2)}) copy-start(s32[8]{0:T(128)} %sizes.3) | copy-start | bytes 100
  15.9 3.7 %collective-permute-start.3 = (bf16[256,256]{1,0:T(8,128)(2,1)S(1)}, bf16[256,256]{1,0:T(8,128)(2,1)S(1)}, u32[]{:S(2)}, u32[]{:S(2)}) collective-permute-start(bf16[256,256]{1,0:T(8,128)(2,1)S(1)} %shard_map.105.own), channel_id=1, source_target_pairs={{0,8},{1,9},{2,10},{3,11},{4,12},{5,13},{6,14},{7,15},{8,0},{9,1},... | collective-permute-start | bytes 393224 | tf_op jit(solution)/shard_map/ppermute | solution.py:473
  16.0 5.9 %collective-permute-start.4 = (bf16[256,256]{1,0:T(8,128)(2,1)S(1)}, bf16[256,256]{1,0:T(8,128)(2,1)S(1)}, u32[]{:S(2)}, u32[]{:S(2)}) collective-permute-start(bf16[256,256]{1,0:T(8,128)(2,1)S(1)} %shard_map.105.own), channel_id=1, source_target_pairs={{0,4},{1,5},{2,6},{3,7},{4,0},{5,1},{6,2},{7,3},{8,12},{9,13},{10,... | collective-permute-start | bytes 393224 | tf_op jit(solution)/shard_map/ppermute | solution.py:473
  17.8 8.8 %collective-permute-start.5 = (bf16[256,256]{1,0:T(8,128)(2,1)S(1)}, bf16[256,256]{1,0:T(8,128)(2,1)S(1)}, u32[]{:S(2)}, u32[]{:S(2)}) collective-permute-start(bf16[256,256]{1,0:T(8,128)(2,1)S(1)} %shard_map.105.own), channel_id=1, source_target_pairs={{0,12},{1,13},{2,14},{3,15},{4,8},{5,9},{6,10},{7,11},{8,4},{9,5},... | collective-permute-start | bytes 393224 | tf_op jit(solution)/shard_map/ppermute | solution.py:473
  27.3 29.5 %collective-permute-start.10 = (bf16[136,2176]{1,0:T(8,128)(2,1)S(1)}, bf16[136,2176]{1,0:T(8,128)(2,1)S(1)}, u32[]{:S(2)}, u32[]{:S(2)}) collective-permute-start(bf16[136,2176]{1,0:T(8,128)(2,1)S(1)} %get-tuple-element.24), channel_id=1, source_target_pairs={{16,24},{17,25},{18,26},{19,27},{20,28},{21,29},{22,30},{23,31},{2... | collective-permute-start | bytes 1775624 | tf_op jit(solution)/shard_map/ppermute | solution.py:473
  31.1 25.8 %collective-permute-start.6 = (bf16[56,2560]{1,0:T(8,128)(2,1)S(1)}, bf16[56,2560]{1,0:T(8,128)(2,1)S(1)}, u32[]{:S(2)}, u32[]{:S(2)}) collective-permute-start(bf16[56,2560]{1,0:T(8,128)(2,1)S(1)} %get-tuple-element.20), channel_id=1, source_target_pairs={{0,24},{1,25},{2,26},{3,27},{4,28},{5,29},{6,30},{7,31},{8,16},{9,... | collective-permute-start | bytes 860168 | tf_op jit(solution)/shard_map/ppermute | solution.py:473
  35.6 21.9 %collective-permute-start.7 = (bf16[56,2560]{1,0:T(8,128)(2,1)S(1)}, bf16[56,2560]{1,0:T(8,128)(2,1)S(1)}, u32[]{:S(2)}, u32[]{:S(2)}) collective-permute-start(bf16[56,2560]{1,0:T(8,128)(2,1)S(1)} %get-tuple-element.21), channel_id=1, source_target_pairs={{0,20},{1,21},{2,22},{3,23},{4,16},{5,17},{6,18},{7,19},{8,28},{9,... | collective-permute-start | bytes 860168 | tf_op jit(solution)/shard_map/ppermute | solution.py:473
  35.7 21.9 %collective-permute-start.8 = (bf16[56,2560]{1,0:T(8,128)(2,1)S(1)}, bf16[56,2560]{1,0:T(8,128)(2,1)S(1)}, u32[]{:S(2)}, u32[]{:S(2)}) collective-permute-start(bf16[56,2560]{1,0:T(8,128)(2,1)S(1)} %get-tuple-element.22), channel_id=1, source_target_pairs={{0,28},{1,29},{2,30},{3,31},{4,24},{5,25},{6,26},{7,27},{8,20},{9,... | collective-permute-start | bytes 860168 | tf_op jit(solution)/shard_map/ppermute | solution.py:473
  37.0 25.0 %collective-permute-start.9 = (bf16[56,2560]{1,0:T(8,128)(2,1)S(1)}, bf16[56,2560]{1,0:T(8,128)(2,1)S(1)}, u32[]{:S(2)}, u32[]{:S(2)}) collective-permute-start(bf16[56,2560]{1,0:T(8,128)(2,1)S(1)} %get-tuple-element.23), channel_id=1, source_target_pairs={{0,16},{1,17},{2,18},{3,19},{4,20},{5,21},{6,22},{7,23},{8,24},{9,... | collective-permute-start | bytes 860168 | tf_op jit(solution)/shard_map/ppermute | solution.py:473
  56.8 5.2 %collective-permute-start.14 = (bf16[3,136,384]{2,1,0:T(8,128)(2,1)S(1)}, bf16[3,136,384]{2,1,0:T(8,128)(2,1)S(1)}, u32[]{:S(2)}, u32[]{:S(2)}) collective-permute-start(bf16[3,136,384]{2,1,0:T(8,128)(2,1)S(1)} %pad_maximum_fusion.rest), channel_id=1, source_target_pairs={{0,1},{1,0},{2,3},{3,2},{4,5},{5,4},{6,7},{7,6},{8,9},{9,8},{10,11... | collective-permute-start | bytes 940040 | tf_op jit(solution)/shard_map/ppermute | solution.py:482
  57.0 5.1 %collective-permute-start.11 = (bf16[136,896]{1,0:T(8,128)(2,1)S(1)}, bf16[136,896]{1,0:T(8,128)(2,1)S(1)}, u32[]{:S(2)}, u32[]{:S(2)}) collective-permute-start(bf16[136,896]{1,0:T(8,128)(2,1)S(1)} %slice.18.first1), channel_id=1, source_target_pairs={{0,1},{1,0},{2,3},{3,2},{4,5},{5,4},{6,7},{7,6},{8,9},{9,8},{10,11... | collective-permute-start | bytes 731144 | tf_op jit(solution)/shard_map/ppermute | solution.py:482
  57.5 4.5 %collective-permute-start.12 = (bf16[136,896]{1,0:T(8,128)(2,1)S(1)}, bf16[136,896]{1,0:T(8,128)(2,1)S(1)}, u32[]{:S(2)}, u32[]{:S(2)}) collective-permute-start(bf16[136,896]{1,0:T(8,128)(2,1)S(1)} %get-tuple-element.37.first2), channel_id=1, source_target_pairs={{0,1},{1,0},{2,3},{3,2},{4,5},{5,4},{6,7},{7,6},{8,9},{9,8},{10,11... | collective-permute-start | bytes 731144 | tf_op jit(solution)/shard_map/ppermute | solution.py:482
  57.6 4.4 %collective-permute-start.13 = (bf16[136,896]{1,0:T(8,128)(2,1)S(1)}, bf16[136,896]{1,0:T(8,128)(2,1)S(1)}, u32[]{:S(2)}, u32[]{:S(2)}) collective-permute-start(bf16[136,896]{1,0:T(8,128)(2,1)S(1)} %get-tuple-element.36.first3), channel_id=1, source_target_pairs={{0,1},{1,0},{2,3},{3,2},{4,5},{5,4},{6,7},{7,6},{8,9},{9,8},{10,11... | collective-permute-start | bytes 731144 | tf_op jit(solution)/shard_map/ppermute | solution.py:482
  62.0 9.8 %copy-start.3 = (bf16[1,768,640]{2,1,0:T(8,128)(2,1)S(1)}, bf16[1,768,640]{2,1,0:T(8,128)(2,1)}, u32[]{:S(2)}) copy-start(bf16[1,768,640]{2,1,0:T(8,128)(2,1)} %param.12) | copy-start | bytes 2949124
  62.1 9.8 %copy-start.6 = (bf16[1,512,512]{2,1,0:T(8,128)(2,1)S(1)}, bf16[1,512,512]{2,1,0:T(8,128)(2,1)}, u32[]{:S(2)}) copy-start(bf16[1,512,512]{2,1,0:T(8,128)(2,1)} %param.14) | copy-start | bytes 1572868
  62.1 9.8 %copy-start.8 = (bf16[1,512,512]{2,1,0:T(8,128)(2,1)S(1)}, bf16[1,512,512]{2,1,0:T(8,128)(2,1)}, u32[]{:S(2)}) copy-start(bf16[1,512,512]{2,1,0:T(8,128)(2,1)} %param.15) | copy-start | bytes 1572868
  62.1 9.8 %copy-start.12 = (s32[8]{0:T(128)S(1)}, s32[8]{0:T(128)}, u32[]{:S(2)}) copy-start(s32[8]{0:T(128)} %sizes.3) | copy-start | bytes 100
  63.7 6.7 %collective-permute-start.16 = (bf16[56,512]{1,0:T(8,128)(2,1)S(1)}, bf16[56,512]{1,0:T(8,128)(2,1)S(1)}, u32[]{:S(2)}, u32[]{:S(2)}) collective-permute-start(bf16[56,512]{1,0:T(8,128)(2,1)S(1)} %get-tuple-element.31.own), channel_id=1, source_target_pairs={{0,12},{1,13},{2,14},{3,15},{4,8},{5,9},{6,10},{7,11},{8,4},{9,5},... | collective-permute-start | bytes 172040 | tf_op jit(solution)/shard_map/ppermute | solution.py:473
  65.1 6.7 %collective-permute-start.17 = (bf16[56,512]{1,0:T(8,128)(2,1)S(1)}, bf16[56,512]{1,0:T(8,128)(2,1)S(1)}, u32[]{:S(2)}, u32[]{:S(2)}) collective-permute-start(bf16[56,512]{1,0:T(8,128)(2,1)S(1)} %get-tuple-element.31.own), channel_id=1, source_target_pairs={{0,8},{1,9},{2,10},{3,11},{4,12},{5,13},{6,14},{7,15},{8,0},{9,1},... | collective-permute-start | bytes 172040 | tf_op jit(solution)/shard_map/ppermute | solution.py:473
  65.8 6.0 %collective-permute-start.18 = (bf16[56,512]{1,0:T(8,128)(2,1)S(1)}, bf16[56,512]{1,0:T(8,128)(2,1)S(1)}, u32[]{:S(2)}, u32[]{:S(2)}) collective-permute-start(bf16[56,512]{1,0:T(8,128)(2,1)S(1)} %get-tuple-element.31.own), channel_id=1, source_target_pairs={{0,4},{1,5},{2,6},{3,7},{4,0},{5,1},{6,2},{7,3},{8,12},{9,13},{10,... | collective-permute-start | bytes 172040 | tf_op jit(solution)/shard_map/ppermute | solution.py:473
  68.1 5.9 %copy-start.1 = (bf16[1,512,2560]{2,1,0:T(8,128)(2,1)S(1)}, bf16[1,512,2560]{2,1,0:T(8,128)(2,1)}, u32[]{:S(2)}) copy-start(bf16[1,512,2560]{2,1,0:T(8,128)(2,1)} %param.16) | copy-start | bytes 7864324
  68.1 11.5 %collective-permute-start.15 = (bf16[8,640]{1,0:T(8,128)(2,1)S(1)}, bf16[8,640]{1,0:T(8,128)(2,1)S(1)}, u32[]{:S(2)}, u32[]{:S(2)}) collective-permute-start(bf16[8,640]{1,0:T(8,128)(2,1)S(1)} %get-tuple-element.30), channel_id=1, source_target_pairs={{0,16},{1,17},{2,18},{3,19},{4,20},{5,21},{6,22},{7,23},{8,24},{9,... | collective-permute-start | bytes 30728 | tf_op jit(solution)/shard_map/ppermute | solution.py:473
  74.6 5.5 %collective-permute-start.21 = (bf16[8,640]{1,0:T(8,128)(2,1)S(1)}, bf16[8,640]{1,0:T(8,128)(2,1)S(1)}, u32[]{:S(2)}, u32[]{:S(2)}) collective-permute-start(bf16[8,640]{1,0:T(8,128)(2,1)S(1)} %get-tuple-element.35), channel_id=1, source_target_pairs={{0,12},{1,13},{2,14},{3,15},{4,8},{5,9},{6,10},{7,11},{8,4},{9,5},... | collective-permute-start | bytes 30728 | tf_op jit(solution)/shard_map/ppermute | solution.py:473
  76.0 4.6 %collective-permute-start.20 = (bf16[8,640]{1,0:T(8,128)(2,1)S(1)}, bf16[8,640]{1,0:T(8,128)(2,1)S(1)}, u32[]{:S(2)}, u32[]{:S(2)}) collective-permute-start(bf16[8,640]{1,0:T(8,128)(2,1)S(1)} %get-tuple-element.34), channel_id=1, source_target_pairs={{0,8},{1,9},{2,10},{3,11},{4,12},{5,13},{6,14},{7,15},{8,0},{9,1},... | collective-permute-start | bytes 30728 | tf_op jit(solution)/shard_map/ppermute | solution.py:473
  76.5 4.1 %collective-permute-start.19 = (bf16[8,640]{1,0:T(8,128)(2,1)S(1)}, bf16[8,640]{1,0:T(8,128)(2,1)S(1)}, u32[]{:S(2)}, u32[]{:S(2)}) collective-permute-start(bf16[8,640]{1,0:T(8,128)(2,1)S(1)} %get-tuple-element.33), channel_id=1, source_target_pairs={{0,4},{1,5},{2,6},{3,7},{4,0},{5,1},{6,2},{7,3},{8,12},{9,13},{10,... | collective-permute-start | bytes 30728 | tf_op jit(solution)/shard_map/ppermute | solution.py:473
